TPU v7x, 512 devices: a whole 4x4x16 slice. The times are simulated.
512 devices in a mesh: row: 8 (over z_lo), col: 8 (over y, core), depth: 8 (over z_hi, x).
Axes of the slice: x: 4, y: 4, z: 16 (z_hi: 2, z_lo: 8; z = z_hi * 8 + z_lo), core: 2. Of those that a mesh axis runs over, the one named last changes fastest.
Arguments:
- tokens: bfloat16 [2048, 4096], P(('row', 'depth'), 'col'), may hold values from -6 to 6
- gate_weight: bfloat16 [4096, 14336], P('row', 'col'), may hold values from -0.09375 to 0.09375
- up_weight: bfloat16 [4096, 14336], P('row', 'col'), may hold values from -0.09375 to 0.09375
- grad_hidden: bfloat16 [2048, 14336], P(('row', 'depth'), 'col'), may hold values from -6 to 6
Outputs:
- hidden: bfloat16 [2048, 14336], P(('row', 'depth'), 'col')
- grad_tokens: bfloat16 [2048, 4096], P(('col', 'depth'), 'row')
- grad_gate_weight: float32 [4096, 14336], P('row', ('col', 'depth'))
- grad_up_weight: float32 [4096, 14336], P('row', ('col', 'depth'))
All inputs are finite; a program needn't handle non-finite values.
Results may differ from a plain program's by a relative error of at most 0.028.
Values may be sent and summed in bfloat16 or wider, within the bound.
No kernel may reach another device: no remote copies, remote signals or barrier semaphores. Data moves between devices by JAX's collectives and lax.ppermute only.
A program may use at most 64 MiB of HBM per device.

v0:
```python
import jax
import jax.numpy as jnp
from jax import lax
from jax.sharding import PartitionSpec as P


def from_root(value, axis, source):
    kept = jnp.where(lax.axis_index(axis) == source, value, 0).astype(value.dtype)
    return lax.psum(kept, axis)


def local_grads(gate_pre, up_pre, cotangent):
    sigmoid_gate = jax.nn.sigmoid(gate_pre)
    cotan_f32 = cotangent.astype(jnp.float32)
    grad_gate = (
        cotan_f32 * up_pre * sigmoid_gate * (1.0 + gate_pre * (1.0 - sigmoid_gate))
    ).astype(jnp.bfloat16)
    grad_up = (cotan_f32 * jax.nn.silu(gate_pre)).astype(jnp.bfloat16)
    return (grad_gate, grad_up)


def matmul_f32(left, right):
    return jnp.dot(left, right, preferred_element_type=jnp.float32)


def rounded_term(left, right):
    return matmul_f32(left, right).astype(jnp.bfloat16).astype(jnp.float32)


def local(tokens, gate_weight, up_weight, grad_hidden):
    hidden_cols = gate_weight.shape[1]
    row_tokens = lax.all_gather(tokens, "row", axis=0, tiled=True)
    diag_panel = from_root(row_tokens, "col", lax.axis_index("row"))
    summed = lax.psum_scatter(
        jnp.concatenate(
            [rounded_term(diag_panel, gate_weight), rounded_term(diag_panel, up_weight)], 1
        ).astype(jnp.bfloat16),
        "row",
        scatter_dimension=0,
        tiled=True,
    ).astype(jnp.float32)
    gate_sum = summed[:, :hidden_cols]
    up_sum = summed[:, hidden_cols:]
    hidden = (jax.nn.silu(gate_sum) * up_sum).astype(jnp.bfloat16)
    own_gate, own_up = local_grads(gate_sum, up_sum, grad_hidden)
    grad_gate, grad_up = (
        lax.all_gather(own_gate, "row", axis=0, tiled=True),
        lax.all_gather(own_up, "row", axis=0, tiled=True),
    )
    first_term = jnp.einsum("tf,df->td", grad_gate, gate_weight, preferred_element_type=jnp.float32)
    grad_tokens = lax.psum_scatter(
        (
            first_term
            + jnp.einsum("tf,df->td", grad_up, up_weight, preferred_element_type=jnp.float32)
        ).astype(jnp.bfloat16),
        "col",
        scatter_dimension=0,
        tiled=True,
    )
    gate_slices, up_slices = (
        lax.all_to_all(grad_gate, "depth", split_axis=1, concat_axis=0, tiled=True),
        lax.all_to_all(grad_up, "depth", split_axis=1, concat_axis=0, tiled=True),
    )
    every_tokens = lax.all_gather(diag_panel, "depth", axis=0, tiled=True)
    grad_gate_weight = jnp.einsum(
        "td,tf->df", every_tokens, gate_slices, preferred_element_type=jnp.float32
    )
    grad_up_weight = jnp.einsum(
        "td,tf->df", every_tokens, up_slices, preferred_element_type=jnp.float32
    )
    return (hidden, grad_tokens, grad_gate_weight, grad_up_weight)


def solution(mesh):
    return jax.shard_map(
        local,
        mesh=mesh,
        in_specs=(
            P(("row", "depth"), "col"),
            P("row", "col"),
            P("row", "col"),
            P(("row", "depth"), "col"),
        ),
        out_specs=(
            P(("row", "depth"), "col"),
            P(("col", "depth"), "row"),
            P("row", ("col", "depth")),
            P("row", ("col", "depth")),
        ),
        check_vma=False,
    )
```

profile of v0, /device:TPU:2, one launch (start us, length us, event | category | flops | bytes accessed | tf_op | source)
XLA Modules:
  0.0 493.0 jit_solution(6767275870360330926)
XLA Ops:
  7.2 0.0 copy-start
  7.2 0.0 all-reduce.2.cloned.1.call-start
  7.2 49.8 %all_gather.12 = bf16[256,512]{1,0:T(8,128)(2,1)S(1)} all-gather(bf16[32,512]{1,0:T(8,128)(2,1)} %param.4), channel_id=1, replica_groups=mesh['row'=8,'col'=8,'depth'=8] {'row'}, dimensions={0}, use_global_device_ids=true | all-gather | bytes 294912 | tf_op jit(solution)/shard_map/all_gather | solution.py:32
  57.0 0.7 broadcast_select_fusion
  57.8 0.0 all-reduce.2.cloned.1.call-update
  57.8 0.0 reduce-scatter.3.cloned.1.call-start
  57.8 77.2 %all-reduce.2.cloned.1.call-done = bf16[256,512]{1,0:T(8,128)(2,1)} async-done(((bf16[256,512]{1,0:T(8,128)(2,1)}), bf16[256,512]{1,0:T(8,128)(2,1)}) %all-reduce.2.cloned.1.call-update) | async-done | bytes 262160 | tf_op jit(solution)/shard_map/psum | solution.py:9
  135.1 0.0 copy-start.3
  135.1 2.3 convolution_convert_fusion
  137.3 0.0 copy-done
  137.4 0.0 copy-done.3
  137.4 0.6 convolution_convert_fusion.1
  138.0 1.4 pad_maximum_fusion
  139.4 0.0 copy-start.5
  139.4 0.0 reduce-scatter.3.cloned.1.call-update
  139.4 70.9 %reduce-scatter.3.cloned.1.call-done = bf16[32,3584]{1,0:T(8,128)(2,1)} async-done(((bf16[256,3584]{1,0:T(8,128)(2,1)}), bf16[32,3584]{1,0:T(8,128)(2,1)}) %reduce-scatter.3.cloned.1.call-update) | async-done | bytes 229392 | tf_op jit(solution)/shard_map/reduce_scatter | solution.py:34
  210.3 1.0 convert_element_type.31
  211.3 0.0 copy-done.5
  211.3 0.8 fusion.4
  212.1 49.0 %all_gather.13 = bf16[256,1792]{1,0:T(8,128)(2,1)S(1)} all-gather(bf16[32,1792]{1,0:T(8,128)(2,1)S(1)} %get-tuple-element.5), channel_id=1, replica_groups=mesh['row'=8,'col'=8,'depth'=8] {'row'}, dimensions={0}, use_global_device_ids=true | all-gather | bytes 1032192 | tf_op jit(solution)/shard_map/all_gather | solution.py:47
  261.1 1.3 copy.8
  262.4 24.2 %all-to-all-start = ((bf16[256,8,224]{0,2,1:T(8,128)(2,1)}), bf16[256,8,224]{0,2,1:T(8,128)(2,1)}, u32[]{:S(2)}, u32[]{:S(2)}) async-start(bf16[256,8,224]{0,2,1:T(8,128)(2,1)} %bitcast.21), calls=%async_computation.2 | async-start | bytes 1835008 | tf_op jit(solution)/shard_map/all_to_all | solution.py:61
  286.6 0.0 all-gather.2.cloned.1.call-start
  286.6 0.7 all-gather.2.cloned.1.call-update
  287.3 81.8 %all_gather.14 = bf16[256,1792]{1,0:T(8,128)(2,1)} all-gather(bf16[32,1792]{1,0:T(8,128)(2,1)S(1)} %get-tuple-element.4), channel_id=1, replica_groups=mesh['row'=8,'col'=8,'depth'=8] {'row'}, dimensions={0}, use_global_device_ids=true | all-gather | bytes 1032192 | tf_op jit(solution)/shard_map/all_gather | solution.py:48
  369.1 2.2 copy.10
  371.4 0.0 all-to-all-done
  371.4 4.6 all-to-all-start.1
  375.9 0.0 reduce-scatter.5.cloned.1.call-start
  375.9 0.0 copy-start.1
  376.0 0.0 copy-start.2
  376.0 0.7 fusion.6
  376.6 0.5 copy-done.1
  377.1 0.6 copy-done.2
  377.7 1.4 fusion
  379.1 0.0 reduce-scatter.5.cloned.1.call-update
  379.1 1.3 copy.12
  380.4 46.2 %all-to-all-done.1 = bf16[256,8,224]{0,2,1:T(8,128)(2,1)} async-done(((bf16[256,8,224]{0,2,1:T(8,128)(2,1)}), bf16[256,8,224]{0,2,1:T(8,128)(2,1)}, u32[]{:S(2)}, u32[]{:S(2)}) %all-to-all-start.1) | async-done | bytes 917536 | tf_op jit(solution)/shard_map/all_to_all | solution.py:62
  426.6 2.2 copy.13
  428.8 7.7 %all-gather.2.cloned.1.call-done = bf16[2048,512]{1,0:T(8,128)(2,1)} async-done(((bf16[256,512]{1,0:T(8,128)(2,1)}), bf16[2048,512]{1,0:T(8,128)(2,1)}) %all-gather.2.cloned.1.call-update) | async-done | bytes 2097168 | tf_op jit(solution)/shard_map/all_gather | solution.py:64
  436.5 0.0 copy-start.4
  436.5 0.0 copy-start.6
  436.5 3.1 fusion.7
  439.7 0.0 copy-done.4
  439.7 0.0 copy-done.6
  439.7 1.4 fusion.8
  441.1 45.4 %reduce-scatter.5.cloned.1.call-done = bf16[32,512]{1,0:T(8,128)(2,1)} async-done(((bf16[256,512]{1,0:T(8,128)(2,1)}), bf16[32,512]{1,0:T(8,128)(2,1)}) %reduce-scatter.5.cloned.1.call-update) | async-done | bytes 32784 | tf_op jit(solution)/shard_map/reduce_scatter | solution.py:51
Async XLA Ops:
  7.2 130.2 %copy-start = (bf16[512,1792]{1,0:T(8,128)(2,1)S(1)}, bf16[512,1792]{1,0:T(8,128)(2,1)}, u32[]{:S(2)}) copy-start(bf16[512,1792]{1,0:T(8,128)(2,1)} %param.5) | copy-start | bytes 5505028
  7.2 127.9 %all-reduce.2.cloned.1.call-start = ((), (), s32[]{:S(2)}) async-start(), calls=%async_computation.4 | async-start | bytes 524288 | tf_op jit(solution)/shard_map/psum | solution.py:9
  57.8 152.6 %reduce-scatter.3.cloned.1.call-start = ((), (), s32[]{:S(2)}) async-start(), calls=%async_computation.5 | async-start | bytes 2064384 | tf_op jit(solution)/shard_map/reduce_scatter | solution.py:34
  135.1 2.3 copy-start.3
  139.4 71.9 %copy-start.5 = (bf16[32,1792]{1,0:T(8,128)(2,1)S(1)}, bf16[32,1792]{1,0:T(8,128)(2,1)}, u32[]{:S(2)}) copy-start(bf16[32,1792]{1,0:T(8,128)(2,1)} %param.7) | copy-start | bytes 344068
  262.4 109.0 %all-to-all-start = ((bf16[256,8,224]{0,2,1:T(8,128)(2,1)}), bf16[256,8,224]{0,2,1:T(8,128)(2,1)}, u32[]{:S(2)}, u32[]{:S(2)}) async-start(bf16[256,8,224]{0,2,1:T(8,128)(2,1)} %bitcast.21), calls=%async_computation.2 | async-start | bytes 1835008 | tf_op jit(solution)/shard_map/all_to_all | solution.py:61
  286.6 149.9 %all-gather.2.cloned.1.call-start = ((), (), s32[]{:S(2)}) async-start(), calls=%async_computation.7 | async-start | bytes 2359296 | tf_op jit(solution)/shard_map/all_gather | solution.py:64
  371.4 55.2 %all-to-all-start.1 = ((bf16[256,8,224]{0,2,1:T(8,128)(2,1)}), bf16[256,8,224]{0,2,1:T(8,128)(2,1)}, u32[]{:S(2)}, u32[]{:S(2)}) async-start(bf16[256,8,224]{0,2,1:T(8,128)(2,1)} %bitcast.20), calls=%async_computation.3 | async-start | bytes 1835008 | tf_op jit(solution)/shard_map/all_to_all | solution.py:62
  375.9 110.5 %reduce-scatter.5.cloned.1.call-start = ((), (), s32[]{:S(2)}) async-start(), calls=%async_computation.6 | async-start | bytes 294912 | tf_op jit(solution)/shard_map/reduce_scatter | solution.py:51
  375.9 1.2 copy-start.1
  376.0 1.8 copy-start.2
  436.5 3.2 copy-start.4
  436.5 3.2 copy-start.6
Sparse Core Ops, SparseCore 0:
  57.9 77.1 all-reduce.1
  139.6 70.7 reduce-scatter.2
  291.1 145.3 all-gather.1
  440.0 46.4 reduce-scatter.4
where the time goes:
time: 493 us
  waiting for transfers between devices  248 us (50%)
  blocking collectives  181 us (37%)
  starting transfers between devices  28.9 us (6%)
  between operations  13.8 us (3%)
  matrix products  9.5 us (2%)
  local copies, waits for them, and re-layouts  8.16 us (2%)
    all_gather x1, blocking collectives, local(): lax.all_gather(own_up, 'row', axis=0, tiled=True)  81.8 us
    psum x1, waiting for transfers between devices, from_root(): return lax.psum(kept, axis)  77.2 us
    reduce_scatter x1, waiting for transfers between devices, local(): lax.psum_scatter(jnp.concatenate([rounded_term(diag_panel, gate_weight),...  70.9 us
    all_gather x1, blocking collectives, local(): row_tokens = lax.all_gather(tokens, 'row', axis=0, tiled=True)  49.8 us
    all_gather x1, blocking collectives, local(): lax.all_gather(own_gate, 'row', axis=0, tiled=True)  49 us
    all_to_all x1, waiting for transfers between devices, local(): lax.all_to_all(grad_up, 'depth', split_axis=1, concat_axis=0, tiled=True)  46.2 us
    reduce_scatter x1, waiting for transfers between devices, local(): lax.psum_scatter((first_term + jnp.einsum('tf,df->td', grad_up, up_weight...  45.4 us
    all_to_all x1, starting transfers between devices, local(): lax.all_to_all(grad_gate, 'depth', split_axis=1, concat_axis=0, tiled=True)  24.2 us
  transfers between devices with their start and end apart: 6, of which 5 were waited for; matrix products, arithmetic and copies ran while one was open for 2% of the time, Pallas kernels for 0%

commit v1 on v0

v1 whole, which is shorter than its diff:
```python
import jax
import jax.numpy as jnp
from jax import lax
from jax.sharding import Mesh, PartitionSpec as P

RING = 16
ROWS = 8
BEFORE = 3


def ring_index(z):
    z %= RING
    return (z % ROWS) * 2 + z // ROWS


def ring_shift(value, step):
    pairs = [(ring_index(z), ring_index(z + step)) for z in range(RING)]
    return lax.ppermute(value, ("r", "h"), pairs)


def place(z, col):
    z %= RING
    return ((z % ROWS) * ROWS + col) * 2 + z // ROWS


def token_pairs():
    pairs = []
    for z in range(RING):
        for offset in range(ROWS):
            pairs.append((place(z + offset - BEFORE, z % ROWS), place(z, offset)))
    return pairs


def result_pairs():
    pairs = []
    for z in range(RING):
        for offset in range(ROWS):
            tile = (z + offset - 4) % RING
            pairs.append((place(z, offset), place(z % ROWS + ROWS * (tile // ROWS), tile % ROWS)))
    return pairs


def dot_f32(left, right, dims):
    return lax.dot_general(left, right, (dims, ((), ())), preferred_element_type=jnp.float32)


def gather_plane(piece):
    copies = jnp.broadcast_to(piece[None], (32,) + piece.shape)
    all_pieces = lax.all_to_all(copies, ("y", "c", "x"), split_axis=0, concat_axis=0, tiled=True)
    return all_pieces.reshape(32 * piece.shape[0], piece.shape[1])


def local(tokens, gate_weight, up_weight, grad_hidden):
    own_x = lax.axis_index("x")
    own_h = lax.axis_index("h")
    features, hidden_cols = gate_weight.shape
    part = hidden_cols // 8

    def own_columns(weight):
        first = lax.dynamic_slice(weight, (0, own_x * part), (features, part))
        second = lax.dynamic_slice(weight, (0, 4 * part + own_x * part), (features, part))
        return [first, second]

    weights = jnp.concatenate(own_columns(gate_weight) + own_columns(up_weight), 1)

    piece = lax.ppermute(tokens, ("r", "y", "c", "h"), token_pairs())
    near_tokens = gather_plane(piece)
    far_tokens = gather_plane(lax.ppermute(piece, "h", [(0, 1), (1, 0)]))

    cotangent = lax.all_to_all(
        grad_hidden.reshape(-1, 2, 4, part), "x", split_axis=2, concat_axis=0, tiled=True
    ).reshape(-1, 2 * part)

    partial = dot_f32(near_tokens, weights, ((1,), (0,))).astype(jnp.bfloat16)
    partial = partial.reshape(ROWS, -1, 4 * part)
    total = partial[BEFORE].astype(jnp.float32)
    arrived = []
    for offset in (7, 0, 6, 1, 5, 2, 4):
        arrived.append(ring_shift(partial[offset], offset - BEFORE))
    for term in arrived:
        total = total + term.astype(jnp.float32)
    gate_pre = total[:, : 2 * part]
    up_pre = total[:, 2 * part :]

    sigmoid = jax.nn.sigmoid(gate_pre)
    silu = gate_pre * sigmoid
    hidden = (silu * up_pre).astype(jnp.bfloat16)
    cotangent = cotangent.astype(jnp.float32)
    grad_gate = (cotangent * up_pre * sigmoid * (1.0 + gate_pre * (1.0 - sigmoid))).astype(jnp.bfloat16)
    grad_up = (cotangent * silu).astype(jnp.bfloat16)
    grads = jnp.concatenate([grad_gate, grad_up], 1)

    hidden = lax.all_to_all(
        hidden.reshape(-1, 2, 1, part), "x", split_axis=0, concat_axis=2, tiled=True
    ).reshape(-1, 8 * part)

    tiles = {0: grads}
    right = left = grads
    for step in range(1, 9):
        right = ring_shift(right, 1)
        tiles[-step] = right
        if step < 8:
            left = ring_shift(left, -1)
            tiles[step] = left

    reach = jnp.concatenate([tiles[offset] for offset in range(-4, 4)], 0)
    terms = dot_f32(reach, weights, ((1,), (1,))).astype(jnp.bfloat16)
    terms = lax.all_to_all(
        terms.reshape(32, -1, features), ("y", "c", "x"), split_axis=0, concat_axis=0, tiled=True
    )
    grad_tokens = jnp.sum(terms.astype(jnp.float32), 0).astype(jnp.bfloat16)
    grad_tokens = lax.ppermute(grad_tokens, ("r", "y", "c", "h"), result_pairs())

    def own_half(offsets):
        both = jnp.concatenate([tiles[offset] for offset in offsets], 0)
        low = jnp.concatenate([both[:, :part], both[:, 2 * part : 3 * part]], 1)
        high = jnp.concatenate([both[:, part : 2 * part], both[:, 3 * part :]], 1)
        return jnp.where(own_h == 0, low, high)

    near = own_half(range(-3, 5))
    far = own_half((5, 6, 7, -8, -7, -6, -5, -4))
    weight_grads = dot_f32(near_tokens, near, ((0,), (0,))) + dot_f32(far_tokens, far, ((0,), (0,)))
    return hidden, grad_tokens, weight_grads[:, :part], weight_grads[:, part:]


def solution(mesh):
    fine = Mesh(mesh.devices.reshape(8, 4, 2, 2, 4), ("r", "y", "c", "h", "x"))
    return jax.shard_map(
        local,
        mesh=fine,
        in_specs=(
            P(("r", "h", "x"), ("y", "c")),
            P("r", ("y", "c")),
            P("r", ("y", "c")),
            P(("r", "h", "x"), ("y", "c")),
        ),
        out_specs=(
            P(("r", "h", "x"), ("y", "c")),
            P(("y", "c", "h", "x"), "r"),
            P("r", ("y", "c", "h", "x")),
            P("r", ("y", "c", "h", "x")),
        ),
        check_vma=False,
    )
```

time: 493 us -> 269 us (0.55)
  the two profiles are of different devices: /device:TPU:2 before, /device:TPU:16 now
where the time goes in v1:
time: 269 us; the launch traced here: 268 us
  starting transfers between devices  146 us (54%)
  waiting for transfers between devices  83.8 us (31%)
  local copies, waits for them, and re-layouts  27.5 us (10%)
  matrix products  6.94 us (3%)
    ppermute x22, starting transfers between devices, ring_shift(): return lax.ppermute(value, ('r', 'h'), pairs)  90.9 us
    ppermute x22, waiting for transfers between devices, ring_shift(): return lax.ppermute(value, ('r', 'h'), pairs)  38.5 us
    all_to_all x2, starting transfers between devices, gather_plane(): lax.all_to_all(copies, ('y', 'c', 'x'), split_axis=0, concat_axis=0, tile...  15.4 us
    unnamed x66, local copies, waits for them, and re-layouts  13.7 us
    all_to_all x2, waiting for transfers between devices, gather_plane(): lax.all_to_all(copies, ('y', 'c', 'x'), split_axis=0, concat_axis=0, tile...  13.1 us
    ppermute x1, starting transfers between devices, local(): piece = lax.ppermute(tokens, ('r', 'y', 'c', 'h'), token_pairs())  12.9 us
    ppermute x1, waiting for transfers between devices, local(): lax.ppermute(grad_tokens, ('r', 'y', 'c', 'h'), result_pairs())  12.4 us
    all_to_all x1, waiting for transfers between devices, local(): lax.all_to_all(terms.reshape(32, -1, features), ('y', 'c', 'x'), split_ax...  11 us
  transfers between devices with their start and end apart: 30, of which 17 were waited for; matrix products, arithmetic and copies ran while one was open for 10% of the time, Pallas kernels for 0%

profile of v1, /device:TPU:16, one launch (start us, length us, event | category | flops | bytes accessed | tf_op | source)
XLA Modules:
  0.0 267.8 jit_solution(1105198972007580585)
XLA Ops:
  0.6 12.9 %collective-permute-start = (bf16[32,512]{1,0:T(8,128)(2,1)}, bf16[32,512]{1,0:T(8,128)(2,1)S(1)}, u32[]{:S(2)}, u32[]{:S(2)}) collective-permute-start(bf16[32,512]{1,0:T(8,128)(2,1)} %param.4), channel_id=1, source_target_pairs={{324,0},{388,8},{452,16},{0,24},{64,32},{128,40},{192,48},{256,56}... | collective-permute-start | bytes 98312 | tf_op jit(solution)/shard_map/ppermute | solution.py:66
  13.5 2.0 collective-permute-done
  15.5 1.1 broadcast_in_dim.4
  16.7 7.4 %all-to-all-start = ((bf16[32,32,512]{2,1,0:T(8,128)(2,1)}), bf16[32,32,512]{2,1,0:T(8,128)(2,1)S(1)}, u32[]{:S(2)}, u32[]{:S(2)}) async-start(bf16[32,32,512]{2,1,0:T(8,128)(2,1)} %broadcast_in_dim.4), calls=%async_computation | async-start | bytes 2097152 | tf_op jit(solution)/shard_map/all_to_all | solution.py:49
  24.1 2.6 constant_dynamic-slice_fusion.1
  26.7 13.1 %all-to-all-done = bf16[32,32,512]{2,1,0:T(8,128)(2,1)S(1)} async-done(((bf16[32,32,512]{2,1,0:T(8,128)(2,1)}), bf16[32,32,512]{2,1,0:T(8,128)(2,1)S(1)}, u32[]{:S(2)}, u32[]{:S(2)}) %all-to-all-start) | async-done | bytes 1048608 | tf_op jit(solution)/shard_map/all_to_all | solution.py:49
  39.8 3.0 %convert_bitcast_fusion = bf16[1024,896]{0,1:T(8,128)(2,1)S(1)} fusion(bf16[1024,512]{1,0:T(8,128)(2,1)S(1)} %bitcast.24, bf16[512,224]{1,0:T(8,128)(2,1)S(1)} %get-tuple-element.22, bf16[512,224]{1,0:T(8,128)(2,1)S(1)} %get-tuple-element.21, bf16[512,224]{1,0:T(8,128)(2,1)} %get-tuple-element.44, bf16[512,224]{1,0:T(8,128)(2,1)} %get-tuple-element.45), kind=kOutput, calls=%fused_computation | convolution fusion | flops 944111616 | bytes 3801088 | tf_op jit(solution)/shard_map/dot_general | solution.py:44
  42.9 1.3 fusion.21
  44.1 2.8 %collective-permute-start.7 = (bf16[128,896]{0,1:T(8,128)(2,1)}, bf16[128,896]{0,1:T(8,128)(2,1)S(1)}, u32[]{:S(2)}, u32[]{:S(2)}) collective-permute-start(bf16[128,896]{0,1:T(8,128)(2,1)} %get-tuple-element.13), channel_id=1, source_target_pairs={{0,64},{64,128},{128,192},{192,256},{256,320},{320,384},{384,448},... | collective-permute-start | bytes 688136 | tf_op jit(solution)/shard_map/ppermute | solution.py:18
  47.0 4.2 %collective-permute-start.6 = (bf16[128,896]{0,1:T(8,128)(2,1)}, bf16[128,896]{0,1:T(8,128)(2,1)S(1)}, u32[]{:S(2)}, u32[]{:S(2)}) collective-permute-start(bf16[128,896]{0,1:T(8,128)(2,1)} %get-tuple-element.14), channel_id=1, source_target_pairs={{0,452},{64,0},{128,64},{192,128},{256,192},{320,256},{384,320},{4... | collective-permute-start | bytes 688136 | tf_op jit(solution)/shard_map/ppermute | solution.py:18
  52.2 3.3 %all-to-all-start.2 = ((bf16[32,2,4,224]{3,1,0,2:T(2,128)(2,1)}), bf16[32,2,4,224]{3,1,0,2:T(2,128)(2,1)S(1)}, u32[]{:S(2)}, u32[]{:S(2)}) async-start(bf16[32,2,4,224]{3,1,0,2:T(2,128)(2,1)} %copy.22), calls=%async_computation.2 | async-start | bytes 262144 | tf_op jit(solution)/shard_map/all_to_all | solution.py:70
  55.5 1.9 collective-permute-start.5
  57.4 6.0 %collective-permute-start.4 = (bf16[128,896]{0,1:T(8,128)(2,1)}, bf16[128,896]{0,1:T(8,128)(2,1)}, u32[]{:S(2)}, u32[]{:S(2)}) collective-permute-start(bf16[128,896]{0,1:T(8,128)(2,1)} %get-tuple-element.16), channel_id=1, source_target_pairs={{0,388},{64,452},{128,0},{192,64},{256,128},{320,192},{384,256},{4... | collective-permute-start | bytes 688136 | tf_op jit(solution)/shard_map/ppermute | solution.py:18
  63.5 1.9 collective-permute-start.3
  65.4 6.9 %collective-permute-start.2 = (bf16[128,896]{0,1:T(8,128)(2,1)}, bf16[128,896]{0,1:T(8,128)(2,1)}, u32[]{:S(2)}, u32[]{:S(2)}) collective-permute-start(bf16[128,896]{0,1:T(8,128)(2,1)} %get-tuple-element.18), channel_id=1, source_target_pairs={{0,324},{64,388},{128,452},{192,0},{256,64},{320,128},{384,192},{4... | collective-permute-start | bytes 688136 | tf_op jit(solution)/shard_map/ppermute | solution.py:18
  72.4 4.8 %collective-permute-start.1 = (bf16[128,896]{0,1:T(8,128)(2,1)}, bf16[128,896]{0,1:T(8,128)(2,1)}, u32[]{:S(2)}, u32[]{:S(2)}) collective-permute-start(bf16[128,896]{0,1:T(8,128)(2,1)} %get-tuple-element.12), channel_id=1, source_target_pairs={{0,256},{64,320},{128,384},{192,448},{256,4},{320,68},{384,132},{4... | collective-permute-start | bytes 688136 | tf_op jit(solution)/shard_map/ppermute | solution.py:18
  77.7 11.4 %collective-permute-done.3 = bf16[128,896]{0,1:T(8,128)(2,1)} collective-permute-done((bf16[128,896]{0,1:T(8,128)(2,1)}, bf16[128,896]{0,1:T(8,128)(2,1)}, u32[]{:S(2)}, u32[]{:S(2)}) %collective-permute-start.3) | collective-permute-done | bytes 229408 | tf_op jit(solution)/shard_map/ppermute | solution.py:18
  89.1 7.3 %collective-permute-done.1 = bf16[128,896]{0,1:T(8,128)(2,1)} collective-permute-done((bf16[128,896]{0,1:T(8,128)(2,1)}, bf16[128,896]{0,1:T(8,128)(2,1)}, u32[]{:S(2)}, u32[]{:S(2)}) %collective-permute-start.1) | collective-permute-done | bytes 229408 | tf_op jit(solution)/shard_map/ppermute | solution.py:18
  96.4 1.5 convert_add_fusion
  98.1 9.6 %collective-permute-start.8 = (bf16[128,896]{0,1:T(8,128)(2,1)S(1)}, bf16[128,896]{0,1:T(8,128)(2,1)S(1)}, u32[]{:S(2)}, u32[]{:S(2)}) collective-permute-start(bf16[128,896]{0,1:T(8,128)(2,1)S(1)} %pad_maximum_fusion.1), channel_id=1, source_target_pairs={{0,64},{64,128},{128,192},{192,256},{256,320},{320,384},{384,448},... | collective-permute-start | bytes 688136 | tf_op jit(solution)/shard_map/ppermute | solution.py:18
  107.7 1.9 collective-permute-start.12
  109.6 1.6 collective-permute-done.8
  111.2 7.4 %collective-permute-start.9 = (bf16[128,896]{0,1:T(8,128)(2,1)S(1)}, bf16[128,896]{0,1:T(8,128)(2,1)S(1)}, u32[]{:S(2)}, u32[]{:S(2)}) collective-permute-start(bf16[128,896]{0,1:T(8,128)(2,1)S(1)} %collective-permute-done.8), channel_id=1, source_target_pairs={{0,64},{64,128},{128,192},{192,256},{256,320},{320,384},{384,448},... | collective-permute-start | bytes 688136 | tf_op jit(solution)/shard_map/ppermute | solution.py:18
  119.2 5.6 %collective-permute-start.13 = (bf16[128,896]{0,1:T(8,128)(2,1)S(1)}, bf16[128,896]{0,1:T(8,128)(2,1)S(1)}, u32[]{:S(2)}, u32[]{:S(2)}) collective-permute-start(bf16[128,896]{0,1:T(8,128)(2,1)S(1)} %collective-permute-done.12), channel_id=1, source_target_pairs={{0,452},{64,0},{128,64},{192,128},{256,192},{320,256},{384,320},{4... | collective-permute-start | bytes 688136 | tf_op jit(solution)/shard_map/ppermute | solution.py:18
  124.7 2.4 collective-permute-done.9
  127.2 1.9 collective-permute-start.10
  129.1 5.1 %collective-permute-start.14 = (bf16[128,896]{0,1:T(8,128)(2,1)S(1)}, bf16[128,896]{0,1:T(8,128)(2,1)S(1)}, u32[]{:S(2)}, u32[]{:S(2)}) collective-permute-start(bf16[128,896]{0,1:T(8,128)(2,1)S(1)} %collective-permute-done.13), channel_id=1, source_target_pairs={{0,452},{64,0},{128,64},{192,128},{256,192},{320,256},{384,320},{4... | collective-permute-start | bytes 688136 | tf_op jit(solution)/shard_map/ppermute | solution.py:18
  134.2 2.0 collective-permute-done.10
  136.3 1.9 collective-permute-start.11
  138.2 5.1 %collective-permute-start.16 = (bf16[128,896]{0,1:T(8,128)(2,1)S(1)}, bf16[128,896]{0,1:T(8,128)(2,1)S(1)}, u32[]{:S(2)}, u32[]{:S(2)}) collective-permute-start(bf16[128,896]{0,1:T(8,128)(2,1)S(1)} %collective-permute-done.14), channel_id=1, source_target_pairs={{0,452},{64,0},{128,64},{192,128},{256,192},{320,256},{384,320},{4... | collective-permute-start | bytes 688136 | tf_op jit(solution)/shard_map/ppermute | solution.py:18
  143.4 2.0 collective-permute-done.11
  145.4 1.9 collective-permute-start.20
  148.0 5.1 %collective-permute-start.17 = (bf16[128,896]{0,1:T(8,128)(2,1)S(1)}, bf16[128,896]{0,1:T(8,128)(2,1)S(1)}, u32[]{:S(2)}, u32[]{:S(2)}) collective-permute-start(bf16[128,896]{0,1:T(8,128)(2,1)S(1)} %collective-permute-done.16), channel_id=1, source_target_pairs={{0,452},{64,0},{128,64},{192,128},{256,192},{320,256},{384,320},{4... | collective-permute-start | bytes 688136 | tf_op jit(solution)/shard_map/ppermute | solution.py:18
  153.2 1.3 collective-permute-done.20
  154.5 1.9 collective-permute-start.21
  156.7 5.6 %collective-permute-start.18 = (bf16[128,896]{0,1:T(8,128)(2,1)S(1)}, bf16[128,896]{0,1:T(8,128)(2,1)}, u32[]{:S(2)}, u32[]{:S(2)}) collective-permute-start(bf16[128,896]{0,1:T(8,128)(2,1)S(1)} %collective-permute-done.17), channel_id=1, source_target_pairs={{0,452},{64,0},{128,64},{192,128},{256,192},{320,256},{384,320},{4... | collective-permute-start | bytes 688136 | tf_op jit(solution)/shard_map/ppermute | solution.py:18
  162.3 2.0 collective-permute-done.21
  164.3 1.9 collective-permute-start.22
  166.2 0.8 copy.19
  167.0 4.5 %all-to-all-start.1 = ((bf16[128,2,1,224]{3,1,2,0:T(2,128)(2,1)}), bf16[128,2,1,224]{3,1,2,0:T(2,128)(2,1)S(1)}, u32[]{:S(2)}, u32[]{:S(2)}) async-start(bf16[128,2,1,224]{3,1,2,0:T(2,128)(2,1)} %copy.19), calls=%async_computation.1 | async-start | bytes 262144 | tf_op jit(solution)/shard_map/all_to_all | solution.py:93
  171.5 7.7 %collective-permute-start.24 = (bf16[32,512]{1,0:T(8,128)(2,1)S(1)}, bf16[32,512]{1,0:T(8,128)(2,1)S(1)}, u32[]{:S(2)}, u32[]{:S(2)}) collective-permute-start(bf16[32,512]{1,0:T(8,128)(2,1)S(1)} %collective-permute-done), channel_id=1, source_target_pairs={{0,4},{4,0},{1,5},{5,1},{2,6},{6,2},{3,7},{7,3},{8,12},{12,8},{9,1... | collective-permute-start | bytes 98312 | tf_op jit(solution)/shard_map/ppermute | solution.py:68
  179.2 6.8 %collective-permute-done.24 = bf16[32,512]{1,0:T(8,128)(2,1)S(1)} collective-permute-done((bf16[32,512]{1,0:T(8,128)(2,1)S(1)}, bf16[32,512]{1,0:T(8,128)(2,1)S(1)}, u32[]{:S(2)}, u32[]{:S(2)}) %collective-permute-start.24) | collective-permute-done | bytes 32800 | tf_op jit(solution)/shard_map/ppermute | solution.py:68
  186.0 1.1 broadcast_in_dim.5
  187.1 7.9 %all-to-all-start.4 = ((bf16[32,32,512]{2,1,0:T(8,128)(2,1)}), bf16[32,32,512]{2,1,0:T(8,128)(2,1)S(1)}, u32[]{:S(2)}, u32[]{:S(2)}) async-start(bf16[32,32,512]{2,1,0:T(8,128)(2,1)} %broadcast_in_dim.5), calls=%async_computation.4 | async-start | bytes 2097152 | tf_op jit(solution)/shard_map/all_to_all | solution.py:49
  195.2 0.8 reshape.54
  196.0 5.1 %collective-permute-start.19 = (bf16[128,896]{0,1:T(8,128)(2,1)}, bf16[128,896]{0,1:T(8,128)(2,1)S(1)}, u32[]{:S(2)}, u32[]{:S(2)}) collective-permute-start(bf16[128,896]{0,1:T(8,128)(2,1)} %collective-permute-done.18), channel_id=1, source_target_pairs={{0,452},{64,0},{128,64},{192,128},{256,192},{320,256},{384,320},{4... | collective-permute-start | bytes 688136 | tf_op jit(solution)/shard_map/ppermute | solution.py:18
  201.1 1.0 constant_dynamic-update-slice_fusion.23
  202.2 2.1 collective-permute-start.23
  204.2 1.0 constant_dynamic-update-slice_fusion.22
  205.3 1.4 collective-permute-done.19
  206.7 6.3 %collective-permute-done.23 = bf16[128,896]{0,1:T(8,128)(2,1)S(1)} collective-permute-done((bf16[128,896]{0,1:T(8,128)(2,1)}, bf16[128,896]{0,1:T(8,128)(2,1)S(1)}, u32[]{:S(2)}, u32[]{:S(2)}) %collective-permute-start.23) | collective-permute-done | bytes 229408 | tf_op jit(solution)/shard_map/ppermute | solution.py:18
  213.1 1.1 constant_dynamic-update-slice_fusion.19
  214.1 1.0 constant_dynamic-update-slice_fusion.18
  215.2 1.0 constant_dynamic-update-slice_fusion.17
  216.2 1.1 constant_dynamic-update-slice_fusion.16
  223.4 2.6 convolution_convert_fusion
  226.0 1.0 copy-done.2
  227.0 7.4 %all-to-all-start.3 = ((bf16[32,32,512]{2,1,0:T(8,128)(2,1)}), bf16[32,32,512]{2,1,0:T(8,128)(2,1)S(1)}, u32[]{:S(2)}, u32[]{:S(2)}) async-start(bf16[32,32,512]{2,1,0:T(8,128)(2,1)} %bitcast.27), calls=%async_computation.3 | async-start | bytes 2097152 | tf_op jit(solution)/shard_map/all_to_all | solution.py:108
  234.4 1.6 fusion.20
  236.2 1.1 copy-done.1
  239.1 11.0 %all-to-all-done.3 = bf16[32,32,512]{2,1,0:T(8,128)(2,1)S(1)} async-done(((bf16[32,32,512]{2,1,0:T(8,128)(2,1)}), bf16[32,32,512]{2,1,0:T(8,128)(2,1)S(1)}, u32[]{:S(2)}, u32[]{:S(2)}) %all-to-all-start.3) | async-done | bytes 1048608 | tf_op jit(solution)/shard_map/all_to_all | solution.py:108
  250.2 3.5 %collective-permute-start.15 = (bf16[32,512]{1,0:T(8,128)(2,1)S(1)}, bf16[32,512]{1,0:T(8,128)(2,1)S(1)}, u32[]{:S(2)}, u32[]{:S(2)}) collective-permute-start(bf16[32,512]{1,0:T(8,128)(2,1)S(1)} %reduce_sum.12), channel_id=1, source_target_pairs={{0,36},{8,44},{16,52},{24,60},{32,0},{40,8},{48,16},{56,24},{64,10... | collective-permute-start | bytes 98312 | tf_op jit(solution)/shard_map/ppermute | solution.py:112
  253.7 1.0 fusion.22
  254.7 12.4 %collective-permute-done.15 = bf16[32,512]{1,0:T(8,128)(2,1)S(1)} collective-permute-done((bf16[32,512]{1,0:T(8,128)(2,1)S(1)}, bf16[32,512]{1,0:T(8,128)(2,1)S(1)}, u32[]{:S(2)}, u32[]{:S(2)}) %collective-permute-start.15) | collective-permute-done | bytes 32800 | tf_op jit(solution)/shard_map/ppermute | solution.py:112
  (89 shorter events, 12.2 us)
Async XLA Ops:
  0.6 14.9 %collective-permute-start = (bf16[32,512]{1,0:T(8,128)(2,1)}, bf16[32,512]{1,0:T(8,128)(2,1)S(1)}, u32[]{:S(2)}, u32[]{:S(2)}) collective-permute-start(bf16[32,512]{1,0:T(8,128)(2,1)} %param.4), channel_id=1, source_target_pairs={{324,0},{388,8},{452,16},{0,24},{64,32},{128,40},{192,48},{256,56}... | collective-permute-start | bytes 98312 | tf_op jit(solution)/shard_map/ppermute | solution.py:66
  16.7 23.1 %all-to-all-start = ((bf16[32,32,512]{2,1,0:T(8,128)(2,1)}), bf16[32,32,512]{2,1,0:T(8,128)(2,1)S(1)}, u32[]{:S(2)}, u32[]{:S(2)}) async-start(bf16[32,32,512]{2,1,0:T(8,128)(2,1)} %broadcast_in_dim.4), calls=%async_computation | async-start | bytes 2097152 | tf_op jit(solution)/shard_map/all_to_all | solution.py:49
  26.7 16.1 %copy-start.4 = (bf16[512,224]{1,0:T(8,128)(2,1)}, bf16[512,224]{1,0:T(8,128)(2,1)S(1)}, u32[]{:S(2)}) copy-start(bf16[512,224]{1,0:T(8,128)(2,1)S(1)} %get-tuple-element.22) | copy-start | bytes 688132
  39.8 3.0 %copy-start = (bf16[32,32,512]{2,1,0:T(8,128)(2,1)}, bf16[32,32,512]{2,1,0:T(8,128)(2,1)S(1)}, u32[]{:S(2)}) copy-start(bf16[32,32,512]{2,1,0:T(8,128)(2,1)S(1)} %all-to-all-done) | copy-start | bytes 3145732
  42.8 8.4 %copy-start.25 = (bf16[32,1792]{1,0:T(8,128)(2,1)S(1)}, bf16[32,1792]{1,0:T(8,128)(2,1)}, u32[]{:S(2)}) copy-start(bf16[32,1792]{1,0:T(8,128)(2,1)} %param.7) | copy-start | bytes 344068
  44.1 21.3 %collective-permute-start.7 = (bf16[128,896]{0,1:T(8,128)(2,1)}, bf16[128,896]{0,1:T(8,128)(2,1)S(1)}, u32[]{:S(2)}, u32[]{:S(2)}) collective-permute-start(bf16[128,896]{0,1:T(8,128)(2,1)} %get-tuple-element.13), channel_id=1, source_target_pairs={{0,64},{64,128},{128,192},{192,256},{256,320},{320,384},{384,448},... | collective-permute-start | bytes 688136 | tf_op jit(solution)/shard_map/ppermute | solution.py:18
  47.0 25.4 %collective-permute-start.6 = (bf16[128,896]{0,1:T(8,128)(2,1)}, bf16[128,896]{0,1:T(8,128)(2,1)S(1)}, u32[]{:S(2)}, u32[]{:S(2)}) collective-permute-start(bf16[128,896]{0,1:T(8,128)(2,1)} %get-tuple-element.14), channel_id=1, source_target_pairs={{0,452},{64,0},{128,64},{192,128},{256,192},{320,256},{384,320},{4... | collective-permute-start | bytes 688136 | tf_op jit(solution)/shard_map/ppermute | solution.py:18
  52.2 25.0 %all-to-all-start.2 = ((bf16[32,2,4,224]{3,1,0,2:T(2,128)(2,1)}), bf16[32,2,4,224]{3,1,0,2:T(2,128)(2,1)S(1)}, u32[]{:S(2)}, u32[]{:S(2)}) async-start(bf16[32,2,4,224]{3,1,0,2:T(2,128)(2,1)} %copy.22), calls=%async_computation.2 | async-start | bytes 262144 | tf_op jit(solution)/shard_map/all_to_all | solution.py:70
  55.5 22.2 %collective-permute-start.5 = (bf16[128,896]{0,1:T(8,128)(2,1)}, bf16[128,896]{0,1:T(8,128)(2,1)S(1)}, u32[]{:S(2)}, u32[]{:S(2)}) collective-permute-start(bf16[128,896]{0,1:T(8,128)(2,1)} %get-tuple-element.15), channel_id=1, source_target_pairs={{0,128},{64,192},{128,256},{192,320},{256,384},{320,448},{384,4},{... | collective-permute-start | bytes 688136 | tf_op jit(solution)/shard_map/ppermute | solution.py:18
  57.4 20.3 %collective-permute-start.4 = (bf16[128,896]{0,1:T(8,128)(2,1)}, bf16[128,896]{0,1:T(8,128)(2,1)}, u32[]{:S(2)}, u32[]{:S(2)}) collective-permute-start(bf16[128,896]{0,1:T(8,128)(2,1)} %get-tuple-element.16), channel_id=1, source_target_pairs={{0,388},{64,452},{128,0},{192,64},{256,128},{320,192},{384,256},{4... | collective-permute-start | bytes 688136 | tf_op jit(solution)/shard_map/ppermute | solution.py:18
  63.5 25.7 %collective-permute-start.3 = (bf16[128,896]{0,1:T(8,128)(2,1)}, bf16[128,896]{0,1:T(8,128)(2,1)}, u32[]{:S(2)}, u32[]{:S(2)}) collective-permute-start(bf16[128,896]{0,1:T(8,128)(2,1)} %get-tuple-element.17), channel_id=1, source_target_pairs={{0,192},{64,256},{128,320},{192,384},{256,448},{320,4},{384,68},{4... | collective-permute-start | bytes 688136 | tf_op jit(solution)/shard_map/ppermute | solution.py:18
  65.4 23.7 %collective-permute-start.2 = (bf16[128,896]{0,1:T(8,128)(2,1)}, bf16[128,896]{0,1:T(8,128)(2,1)}, u32[]{:S(2)}, u32[]{:S(2)}) collective-permute-start(bf16[128,896]{0,1:T(8,128)(2,1)} %get-tuple-element.18), channel_id=1, source_target_pairs={{0,324},{64,388},{128,452},{192,0},{256,64},{320,128},{384,192},{4... | collective-permute-start | bytes 688136 | tf_op jit(solution)/shard_map/ppermute | solution.py:18
  72.4 24.1 %collective-permute-start.1 = (bf16[128,896]{0,1:T(8,128)(2,1)}, bf16[128,896]{0,1:T(8,128)(2,1)}, u32[]{:S(2)}, u32[]{:S(2)}) collective-permute-start(bf16[128,896]{0,1:T(8,128)(2,1)} %get-tuple-element.12), channel_id=1, source_target_pairs={{0,256},{64,320},{128,384},{192,448},{256,4},{320,68},{384,132},{4... | collective-permute-start | bytes 688136 | tf_op jit(solution)/shard_map/ppermute | solution.py:18
  98.1 13.1 %collective-permute-start.8 = (bf16[128,896]{0,1:T(8,128)(2,1)S(1)}, bf16[128,896]{0,1:T(8,128)(2,1)S(1)}, u32[]{:S(2)}, u32[]{:S(2)}) collective-permute-start(bf16[128,896]{0,1:T(8,128)(2,1)S(1)} %pad_maximum_fusion.1), channel_id=1, source_target_pairs={{0,64},{64,128},{128,192},{192,256},{256,320},{320,384},{384,448},... | collective-permute-start | bytes 688136 | tf_op jit(solution)/shard_map/ppermute | solution.py:18
  107.7 11.5 %collective-permute-start.12 = (bf16[128,896]{0,1:T(8,128)(2,1)S(1)}, bf16[128,896]{0,1:T(8,128)(2,1)S(1)}, u32[]{:S(2)}, u32[]{:S(2)}) collective-permute-start(bf16[128,896]{0,1:T(8,128)(2,1)S(1)} %pad_maximum_fusion.1), channel_id=1, source_target_pairs={{0,452},{64,0},{128,64},{192,128},{256,192},{320,256},{384,320},{4... | collective-permute-start | bytes 688136 | tf_op jit(solution)/shard_map/ppermute | solution.py:18
  111.2 53.1 %copy-start.16 = (bf16[128,896]{0,1:T(8,128)(2,1)}, bf16[128,896]{0,1:T(8,128)(2,1)S(1)}, u32[]{:S(2)}) copy-start(bf16[128,896]{0,1:T(8,128)(2,1)S(1)} %collective-permute-done.8) | copy-start | bytes 688132
  111.2 15.9 %collective-permute-start.9 = (bf16[128,896]{0,1:T(8,128)(2,1)S(1)}, bf16[128,896]{0,1:T(8,128)(2,1)S(1)}, u32[]{:S(2)}, u32[]{:S(2)}) collective-permute-start(bf16[128,896]{0,1:T(8,128)(2,1)S(1)} %collective-permute-done.8), channel_id=1, source_target_pairs={{0,64},{64,128},{128,192},{192,256},{256,320},{320,384},{384,448},... | collective-permute-start | bytes 688136 | tf_op jit(solution)/shard_map/ppermute | solution.py:18
  119.2 19.0 %copy-start.12 = (bf16[128,896]{0,1:T(8,128)(2,1)}, bf16[128,896]{0,1:T(8,128)(2,1)S(1)}, u32[]{:S(2)}) copy-start(bf16[128,896]{0,1:T(8,128)(2,1)S(1)} %collective-permute-done.12) | copy-start | bytes 688132
  119.2 9.9 %collective-permute-start.13 = (bf16[128,896]{0,1:T(8,128)(2,1)S(1)}, bf16[128,896]{0,1:T(8,128)(2,1)S(1)}, u32[]{:S(2)}, u32[]{:S(2)}) collective-permute-start(bf16[128,896]{0,1:T(8,128)(2,1)S(1)} %collective-permute-done.12), channel_id=1, source_target_pairs={{0,452},{64,0},{128,64},{192,128},{256,192},{320,256},{384,320},{4... | collective-permute-start | bytes 688136 | tf_op jit(solution)/shard_map/ppermute | solution.py:18
  127.1 39.1 %copy-start.20 = (bf16[128,896]{0,1:T(8,128)(2,1)}, bf16[128,896]{0,1:T(8,128)(2,1)S(1)}, u32[]{:S(2)}) copy-start(bf16[128,896]{0,1:T(8,128)(2,1)S(1)} %collective-permute-done.9) | copy-start | bytes 688132
  127.2 9.1 %collective-permute-start.10 = (bf16[128,896]{0,1:T(8,128)(2,1)S(1)}, bf16[128,896]{0,1:T(8,128)(2,1)S(1)}, u32[]{:S(2)}, u32[]{:S(2)}) collective-permute-start(bf16[128,896]{0,1:T(8,128)(2,1)S(1)} %collective-permute-done.9), channel_id=1, source_target_pairs={{0,64},{64,128},{128,192},{192,256},{256,320},{320,384},{384,448},... | collective-permute-start | bytes 688136 | tf_op jit(solution)/shard_map/ppermute | solution.py:18
  129.1 14.3 %copy-start.14 = (bf16[128,896]{0,1:T(8,128)(2,1)}, bf16[128,896]{0,1:T(8,128)(2,1)S(1)}, u32[]{:S(2)}) copy-start(bf16[128,896]{0,1:T(8,128)(2,1)S(1)} %collective-permute-done.13) | copy-start | bytes 688132
  129.1 9.1 %collective-permute-start.14 = (bf16[128,896]{0,1:T(8,128)(2,1)S(1)}, bf16[128,896]{0,1:T(8,128)(2,1)S(1)}, u32[]{:S(2)}, u32[]{:S(2)}) collective-permute-start(bf16[128,896]{0,1:T(8,128)(2,1)S(1)} %collective-permute-done.13), channel_id=1, source_target_pairs={{0,452},{64,0},{128,64},{192,128},{256,192},{320,256},{384,320},{4... | collective-permute-start | bytes 688136 | tf_op jit(solution)/shard_map/ppermute | solution.py:18
  136.3 30.0 %copy-start.22 = (bf16[128,896]{0,1:T(8,128)(2,1)}, bf16[128,896]{0,1:T(8,128)(2,1)S(1)}, u32[]{:S(2)}) copy-start(bf16[128,896]{0,1:T(8,128)(2,1)S(1)} %collective-permute-done.10) | copy-start | bytes 688132
  136.3 9.1 %collective-permute-start.11 = (bf16[128,896]{0,1:T(8,128)(2,1)S(1)}, bf16[128,896]{0,1:T(8,128)(2,1)S(1)}, u32[]{:S(2)}, u32[]{:S(2)}) collective-permute-start(bf16[128,896]{0,1:T(8,128)(2,1)S(1)} %collective-permute-done.10), channel_id=1, source_target_pairs={{0,64},{64,128},{128,192},{192,256},{256,320},{320,384},{384,448},... | collective-permute-start | bytes 688136 | tf_op jit(solution)/shard_map/ppermute | solution.py:18
  138.2 28.0 %copy-start.18 = (bf16[128,896]{0,1:T(8,128)(2,1)}, bf16[128,896]{0,1:T(8,128)(2,1)S(1)}, u32[]{:S(2)}) copy-start(bf16[128,896]{0,1:T(8,128)(2,1)S(1)} %collective-permute-done.14) | copy-start | bytes 688132
  138.2 9.1 %collective-permute-start.16 = (bf16[128,896]{0,1:T(8,128)(2,1)S(1)}, bf16[128,896]{0,1:T(8,128)(2,1)S(1)}, u32[]{:S(2)}, u32[]{:S(2)}) collective-permute-start(bf16[128,896]{0,1:T(8,128)(2,1)S(1)} %collective-permute-done.14), channel_id=1, source_target_pairs={{0,452},{64,0},{128,64},{192,128},{256,192},{320,256},{384,320},{4... | collective-permute-start | bytes 688136 | tf_op jit(solution)/shard_map/ppermute | solution.py:18
  145.4 41.7 %copy-start.24 = (bf16[128,896]{0,1:T(8,128)(2,1)}, bf16[128,896]{0,1:T(8,128)(2,1)S(1)}, u32[]{:S(2)}) copy-start(bf16[128,896]{0,1:T(8,128)(2,1)S(1)} %collective-permute-done.11) | copy-start | bytes 688132
  145.4 9.1 %collective-permute-start.20 = (bf16[128,896]{0,1:T(8,128)(2,1)S(1)}, bf16[128,896]{0,1:T(8,128)(2,1)S(1)}, u32[]{:S(2)}, u32[]{:S(2)}) collective-permute-start(bf16[128,896]{0,1:T(8,128)(2,1)S(1)} %collective-permute-done.11), channel_id=1, source_target_pairs={{0,64},{64,128},{128,192},{192,256},{256,320},{320,384},{384,448},... | collective-permute-start | bytes 688136 | tf_op jit(solution)/shard_map/ppermute | solution.py:18
  147.3 0.7 copy-start.8
  148.0 8.7 %collective-permute-start.17 = (bf16[128,896]{0,1:T(8,128)(2,1)S(1)}, bf16[128,896]{0,1:T(8,128)(2,1)S(1)}, u32[]{:S(2)}, u32[]{:S(2)}) collective-permute-start(bf16[128,896]{0,1:T(8,128)(2,1)S(1)} %collective-permute-done.16), channel_id=1, source_target_pairs={{0,452},{64,0},{128,64},{192,128},{256,192},{320,256},{384,320},{4... | collective-permute-start | bytes 688136 | tf_op jit(solution)/shard_map/ppermute | solution.py:18
  154.5 2.2 copy-start.10
  154.5 9.8 %collective-permute-start.21 = (bf16[128,896]{0,1:T(8,128)(2,1)S(1)}, bf16[128,896]{0,1:T(8,128)(2,1)}, u32[]{:S(2)}, u32[]{:S(2)}) collective-permute-start(bf16[128,896]{0,1:T(8,128)(2,1)S(1)} %collective-permute-done.20), channel_id=1, source_target_pairs={{0,64},{64,128},{128,192},{192,256},{256,320},{320,384},{384,448},... | collective-permute-start | bytes 688136 | tf_op jit(solution)/shard_map/ppermute | solution.py:18
  156.7 30.4 %copy-start.11 = (bf16[128,896]{0,1:T(8,128)(2,1)}, bf16[128,896]{0,1:T(8,128)(2,1)S(1)}, u32[]{:S(2)}) copy-start(bf16[128,896]{0,1:T(8,128)(2,1)S(1)} %collective-permute-done.17) | copy-start | bytes 688132
  156.7 39.3 %collective-permute-start.18 = (bf16[128,896]{0,1:T(8,128)(2,1)S(1)}, bf16[128,896]{0,1:T(8,128)(2,1)}, u32[]{:S(2)}, u32[]{:S(2)}) collective-permute-start(bf16[128,896]{0,1:T(8,128)(2,1)S(1)} %collective-permute-done.17), channel_id=1, source_target_pairs={{0,452},{64,0},{128,64},{192,128},{256,192},{320,256},{384,320},{4... | collective-permute-start | bytes 688136 | tf_op jit(solution)/shard_map/ppermute | solution.py:18
  164.3 37.9 %collective-permute-start.22 = (bf16[128,896]{0,1:T(8,128)(2,1)}, bf16[128,896]{0,1:T(8,128)(2,1)}, u32[]{:S(2)}, u32[]{:S(2)}) collective-permute-start(bf16[128,896]{0,1:T(8,128)(2,1)} %collective-permute-done.21), channel_id=1, source_target_pairs={{0,64},{64,128},{128,192},{192,256},{256,320},{320,384},{384,448},... | collective-permute-start | bytes 688136 | tf_op jit(solution)/shard_map/ppermute | solution.py:18
  167.0 19.0 %all-to-all-start.1 = ((bf16[128,2,1,224]{3,1,2,0:T(2,128)(2,1)}), bf16[128,2,1,224]{3,1,2,0:T(2,128)(2,1)S(1)}, u32[]{:S(2)}, u32[]{:S(2)}) async-start(bf16[128,2,1,224]{3,1,2,0:T(2,128)(2,1)} %copy.19), calls=%async_computation.1 | async-start | bytes 262144 | tf_op jit(solution)/shard_map/all_to_all | solution.py:93
  171.5 14.5 %collective-permute-start.24 = (bf16[32,512]{1,0:T(8,128)(2,1)S(1)}, bf16[32,512]{1,0:T(8,128)(2,1)S(1)}, u32[]{:S(2)}, u32[]{:S(2)}) collective-permute-start(bf16[32,512]{1,0:T(8,128)(2,1)S(1)} %collective-permute-done), channel_id=1, source_target_pairs={{0,4},{4,0},{1,5},{5,1},{2,6},{6,2},{3,7},{7,3},{8,12},{12,8},{9,1... | collective-permute-start | bytes 98312 | tf_op jit(solution)/shard_map/ppermute | solution.py:68
  187.1 38.9 %all-to-all-start.4 = ((bf16[32,32,512]{2,1,0:T(8,128)(2,1)}), bf16[32,32,512]{2,1,0:T(8,128)(2,1)S(1)}, u32[]{:S(2)}, u32[]{:S(2)}) async-start(bf16[32,32,512]{2,1,0:T(8,128)(2,1)} %broadcast_in_dim.5), calls=%async_computation.4 | async-start | bytes 2097152 | tf_op jit(solution)/shard_map/all_to_all | solution.py:49
  196.0 10.6 %collective-permute-start.19 = (bf16[128,896]{0,1:T(8,128)(2,1)}, bf16[128,896]{0,1:T(8,128)(2,1)S(1)}, u32[]{:S(2)}, u32[]{:S(2)}) collective-permute-start(bf16[128,896]{0,1:T(8,128)(2,1)} %collective-permute-done.18), channel_id=1, source_target_pairs={{0,452},{64,0},{128,64},{192,128},{256,192},{320,256},{384,320},{4... | collective-permute-start | bytes 688136 | tf_op jit(solution)/shard_map/ppermute | solution.py:18
  202.2 15.2 %copy-start.23 = (bf16[128,896]{0,1:T(8,128)(2,1)S(1)}, bf16[128,896]{0,1:T(8,128)(2,1)}, u32[]{:S(2)}) copy-start(bf16[128,896]{0,1:T(8,128)(2,1)} %copy-done.22) | copy-start | bytes 688132
  202.2 10.8 %collective-permute-start.23 = (bf16[128,896]{0,1:T(8,128)(2,1)}, bf16[128,896]{0,1:T(8,128)(2,1)S(1)}, u32[]{:S(2)}, u32[]{:S(2)}) collective-permute-start(bf16[128,896]{0,1:T(8,128)(2,1)} %collective-permute-done.22), channel_id=1, source_target_pairs={{0,64},{64,128},{128,192},{192,256},{256,320},{320,384},{384,448},... | collective-permute-start | bytes 688136 | tf_op jit(solution)/shard_map/ppermute | solution.py:18
  205.2 12.9 %copy-start.21 = (bf16[128,896]{0,1:T(8,128)(2,1)S(1)}, bf16[128,896]{0,1:T(8,128)(2,1)}, u32[]{:S(2)}) copy-start(bf16[128,896]{0,1:T(8,128)(2,1)} %copy-done.20) | copy-start | bytes 688132
  213.1 5.8 %copy-start.17 = (bf16[128,896]{0,1:T(8,128)(2,1)S(1)}, bf16[128,896]{0,1:T(8,128)(2,1)}, u32[]{:S(2)}) copy-start(bf16[128,896]{0,1:T(8,128)(2,1)} %copy-done.16) | copy-start | bytes 688132
  216.2 4.2 %copy-start.13 = (bf16[128,896]{0,1:T(8,128)(2,1)S(1)}, bf16[128,896]{0,1:T(8,128)(2,1)}, u32[]{:S(2)}) copy-start(bf16[128,896]{0,1:T(8,128)(2,1)} %copy-done.12) | copy-start | bytes 688132
  217.3 3.8 %copy-start.15 = (bf16[128,896]{0,1:T(8,128)(2,1)S(1)}, bf16[128,896]{0,1:T(8,128)(2,1)}, u32[]{:S(2)}) copy-start(bf16[128,896]{0,1:T(8,128)(2,1)} %copy-done.14) | copy-start | bytes 688132
  218.1 3.7 %copy-start.19 = (bf16[128,896]{0,1:T(8,128)(2,1)S(1)}, bf16[128,896]{0,1:T(8,128)(2,1)}, u32[]{:S(2)}) copy-start(bf16[128,896]{0,1:T(8,128)(2,1)} %copy-done.18) | copy-start | bytes 688132
  218.9 3.7 %copy-start.9 = (bf16[128,896]{0,1:T(8,128)(2,1)S(1)}, bf16[128,896]{0,1:T(8,128)(2,1)}, u32[]{:S(2)}) copy-start(bf16[128,896]{0,1:T(8,128)(2,1)} %copy-done.8) | copy-start | bytes 688132
  218.9 4.5 %copy-start.5 = (bf16[512,224]{1,0:T(8,128)(2,1)S(1)}, bf16[512,224]{1,0:T(8,128)(2,1)}, u32[]{:S(2)}) copy-start(bf16[512,224]{1,0:T(8,128)(2,1)} %copy-done.4) | copy-start | bytes 688132
  218.9 4.5 %copy-start.6 = (bf16[512,224]{1,0:T(8,128)(2,1)S(1)}, bf16[512,224]{1,0:T(8,128)(2,1)}, u32[]{:S(2)}) copy-start(bf16[512,224]{1,0:T(8,128)(2,1)} %get-tuple-element.44) | copy-start | bytes 688132
  218.9 4.5 %copy-start.7 = (bf16[512,224]{1,0:T(8,128)(2,1)S(1)}, bf16[512,224]{1,0:T(8,128)(2,1)}, u32[]{:S(2)}) copy-start(bf16[512,224]{1,0:T(8,128)(2,1)} %get-tuple-element.45) | copy-start | bytes 688132
  226.0 1.0 copy-start.2
  227.0 23.1 %all-to-all-start.3 = ((bf16[32,32,512]{2,1,0:T(8,128)(2,1)}), bf16[32,32,512]{2,1,0:T(8,128)(2,1)S(1)}, u32[]{:S(2)}, u32[]{:S(2)}) async-start(bf16[32,32,512]{2,1,0:T(8,128)(2,1)} %bitcast.27), calls=%async_computation.3 | async-start | bytes 2097152 | tf_op jit(solution)/shard_map/all_to_all | solution.py:108
  236.0 1.2 copy-start.1
  237.2 1.2 copy-start.3
  250.2 16.9 %collective-permute-start.15 = (bf16[32,512]{1,0:T(8,128)(2,1)S(1)}, bf16[32,512]{1,0:T(8,128)(2,1)S(1)}, u32[]{:S(2)}, u32[]{:S(2)}) collective-permute-start(bf16[32,512]{1,0:T(8,128)(2,1)S(1)} %reduce_sum.12), channel_id=1, source_target_pairs={{0,36},{8,44},{16,52},{24,60},{32,0},{40,8},{48,16},{56,24},{64,10... | collective-permute-start | bytes 98312 | tf_op jit(solution)/shard_map/ppermute | solution.py:112

commit v2 on v1

v2 whole, which is shorter than its diff:
```python
import jax
import jax.numpy as jnp
from jax import lax
from jax.experimental import pallas as pl
from jax.experimental.pallas import tpu as pltpu
from jax.sharding import Mesh, PartitionSpec as P

RING = 16
ROWS = 8
BEFORE = 3


def ring_index(z):
    z %= RING
    return (z % ROWS) * 2 + z // ROWS


def ring_shift(value, step):
    pairs = [(ring_index(z), ring_index(z + step)) for z in range(RING)]
    return lax.ppermute(value, ("r", "h"), pairs)


def place(z, col):
    z %= RING
    return ((z % ROWS) * ROWS + col) * 2 + z // ROWS


def token_pairs():
    pairs = []
    for z in range(RING):
        for offset in range(ROWS):
            pairs.append((place(z + offset - BEFORE, z % ROWS), place(z, offset)))
    return pairs


def result_pairs():
    pairs = []
    for z in range(RING):
        for offset in range(ROWS):
            tile = (z + offset - 4) % RING
            pairs.append((place(z, offset), place(z % ROWS + ROWS * (tile // ROWS), tile % ROWS)))
    return pairs


def dot_f32(left, right, dims=((1,), (0,))):
    return lax.dot_general(left, right, (dims, ((), ())), preferred_element_type=jnp.float32)


def gather_plane(piece):
    copies = jnp.broadcast_to(piece[None], (32,) + piece.shape)
    all_pieces = lax.all_to_all(copies, ("y", "c", "x"), split_axis=0, concat_axis=0, tiled=True)
    return all_pieces.reshape(32 * piece.shape[0], piece.shape[1])


def forward_kernel(tokens_ref, weights_ref, *tile_refs):
    for at, tile_ref in enumerate(tile_refs):
        product = dot_f32(tokens_ref[at * 128 : (at + 1) * 128, :], weights_ref[...])
        tile_ref[...] = product.T.astype(jnp.bfloat16)


def forward_tiles(tokens, weights):
    cols = weights.shape[1]
    return pl.pallas_call(
        forward_kernel,
        out_shape=[jax.ShapeDtypeStruct((cols, 128), jnp.bfloat16)] * ROWS,
        compiler_params=pltpu.CompilerParams(vmem_limit_bytes=32 << 20),
    )(tokens, weights)


def terms_kernel(weights_ref, *refs):
    out_ref = refs[-1]
    for at, tile_ref in enumerate(refs[:-1]):
        product = dot_f32(weights_ref[...], tile_ref[...])
        out_ref[at * 128 : (at + 1) * 128, :] = product.T.astype(jnp.bfloat16)


def token_terms(weights, tiles):
    return pl.pallas_call(
        terms_kernel,
        out_shape=jax.ShapeDtypeStruct((128 * len(tiles), weights.shape[0]), jnp.bfloat16),
        compiler_params=pltpu.CompilerParams(vmem_limit_bytes=32 << 20),
    )(weights, *tiles)


def own_half_product(half_ref, tokens_ref, tile_refs, wide_ref):
    rows = wide_ref.shape[0]
    first = pl.multiple_of(half_ref[0] * rows, 16)
    for at, tile_ref in enumerate(tile_refs):
        wide_ref[:, at * 128 : (at + 1) * 128] = tile_ref[pl.ds(first, rows), :]
    return dot_f32(wide_ref[...], tokens_ref[...])


def near_kernel(half_ref, tokens_ref, *refs):
    out_ref, wide_ref = refs[-2:]
    out_ref[...] = own_half_product(half_ref, tokens_ref, refs[:-2], wide_ref)


def far_kernel(half_ref, tokens_ref, near_ref, *refs):
    gate_ref, up_ref, wide_ref = refs[-3:]
    total = near_ref[...] + own_half_product(half_ref, tokens_ref, refs[:-3], wide_ref)
    part = gate_ref.shape[0]
    gate_ref[...] = total[:part, :]
    up_ref[...] = total[part:, :]


SMEM_SPEC = pl.BlockSpec(memory_space=pltpu.SMEM)
VMEM_SPEC = pl.BlockSpec(memory_space=pltpu.VMEM)


def near_product(half, tokens, tiles):
    rows = tiles[0].shape[0] // 2
    return pl.pallas_call(
        near_kernel,
        in_specs=[SMEM_SPEC] + [VMEM_SPEC] * (1 + len(tiles)),
        out_specs=VMEM_SPEC,
        out_shape=jax.ShapeDtypeStruct((rows, tokens.shape[1]), jnp.float32),
        scratch_shapes=[pltpu.VMEM((rows, tokens.shape[0]), jnp.bfloat16)],
        compiler_params=pltpu.CompilerParams(vmem_limit_bytes=32 << 20),
    )(half, tokens, *tiles)


def far_product(half, tokens, near, tiles):
    rows = tiles[0].shape[0] // 2
    return pl.pallas_call(
        far_kernel,
        in_specs=[SMEM_SPEC] + [VMEM_SPEC] * (2 + len(tiles)),
        out_specs=[VMEM_SPEC] * 2,
        out_shape=[jax.ShapeDtypeStruct((rows // 2, tokens.shape[1]), jnp.float32)] * 2,
        scratch_shapes=[pltpu.VMEM((rows, tokens.shape[0]), jnp.bfloat16)],
        compiler_params=pltpu.CompilerParams(vmem_limit_bytes=32 << 20),
    )(half, tokens, near, *tiles)


def local(tokens, gate_weight, up_weight, grad_hidden):
    own_x = lax.axis_index("x")
    half = lax.axis_index("h").astype(jnp.int32).reshape(1)
    features, hidden_cols = gate_weight.shape
    part = hidden_cols // 8

    def own_columns(weight, which):
        return lax.dynamic_slice(weight, (0, (which * 4 + own_x) * part), (features, part))

    weights = jnp.concatenate(
        [own_columns(weight, which) for which in (0, 1) for weight in (gate_weight, up_weight)], 1
    )

    piece = lax.ppermute(tokens, ("r", "y", "c", "h"), token_pairs())
    cotangent = lax.all_to_all(
        grad_hidden.reshape(-1, 2, 4, part), "x", split_axis=2, concat_axis=0, tiled=True
    )
    piece, cotangent = lax.optimization_barrier((piece, cotangent))
    near_tokens = gather_plane(piece)
    far_piece = lax.ppermute(piece, "h", [(0, 1), (1, 0)])
    near_tokens, far_piece, weights = lax.optimization_barrier((near_tokens, far_piece, weights))
    cotangent = cotangent.reshape(-1, 2 * part).T.astype(jnp.float32)

    partial = forward_tiles(near_tokens, weights)
    far_tokens = gather_plane(far_piece)
    arrived = [partial[BEFORE]]
    for offset in (7, 0, 6, 1, 5, 2, 4):
        arrived.append(ring_shift(partial[offset], offset - BEFORE))
    *arrived, far_tokens = lax.optimization_barrier((*arrived, far_tokens))
    total = arrived[0].astype(jnp.float32)
    for term in arrived[1:]:
        total = total + term.astype(jnp.float32)
    gate_pre = jnp.concatenate([total[:part], total[2 * part : 3 * part]], 0)
    up_pre = jnp.concatenate([total[part : 2 * part], total[3 * part :]], 0)

    sigmoid = jax.nn.sigmoid(gate_pre)
    silu = gate_pre * sigmoid
    hidden = (silu * up_pre).astype(jnp.bfloat16)
    grad_gate = (cotangent * up_pre * sigmoid * (1.0 + gate_pre * (1.0 - sigmoid))).astype(jnp.bfloat16)
    grad_up = (cotangent * silu).astype(jnp.bfloat16)
    grads = jnp.concatenate([grad_gate[:part], grad_up[:part], grad_gate[part:], grad_up[part:]], 0)

    hidden = lax.all_to_all(
        hidden.T.reshape(-1, 2, 1, part), "x", split_axis=0, concat_axis=2, tiled=True
    )

    tiles = {0: grads}
    right = left = grads
    for step in range(1, 9):
        right = ring_shift(right, 1)
        tiles[-step] = right
        if step < 8:
            left = ring_shift(left, -1)
            tiles[step] = left
        if step == 4:
            terms = token_terms(weights, [tiles[offset] for offset in range(-4, 4)])
            right, left, terms, hidden = lax.optimization_barrier((right, left, terms, hidden))
            terms = lax.all_to_all(
                terms.reshape(32, -1, features), ("y", "c", "x"), split_axis=0, concat_axis=0, tiled=True
            )
            near = near_product(half, near_tokens, [tiles[offset] for offset in range(-3, 5)])
        if step == 6:
            right, left, terms = lax.optimization_barrier((right, left, terms))
            grad_tokens = jnp.sum(terms.astype(jnp.float32), 0).astype(jnp.bfloat16)
            right, left, grad_tokens = lax.optimization_barrier((right, left, grad_tokens))
            grad_tokens = lax.ppermute(grad_tokens, ("r", "y", "c", "h"), result_pairs())

    far_tiles = [tiles[offset] for offset in (5, 6, 7, -8, -7, -6, -5, -4)]
    gate_grad, up_grad = far_product(half, far_tokens, near, far_tiles)
    return hidden.reshape(-1, hidden_cols), grad_tokens, gate_grad.T, up_grad.T


def solution(mesh):
    fine = Mesh(mesh.devices.reshape(8, 4, 2, 2, 4), ("r", "y", "c", "h", "x"))
    return jax.shard_map(
        local,
        mesh=fine,
        in_specs=(
            P(("r", "h", "x"), ("y", "c")),
            P("r", ("y", "c")),
            P("r", ("y", "c")),
            P(("r", "h", "x"), ("y", "c")),
        ),
        out_specs=(
            P(("r", "h", "x"), ("y", "c")),
            P(("y", "c", "h", "x"), "r"),
            P("r", ("y", "c", "h", "x")),
            P("r", ("y", "c", "h", "x")),
        ),
        check_vma=False,
    )
```

time: 269 us -> 240 us (0.89)
  the two profiles are of different devices: /device:TPU:16 before, /device:TPU:2 now
where the time goes in v2:
time: 240 us; the launch traced here: 238 us
  starting transfers between devices  148 us (62%)
  waiting for transfers between devices  42.8 us (18%)
  local copies, waits for them, and re-layouts  22.5 us (9%)
  Pallas kernels  10 us (4%)
  blocking collectives  9.35 us (4%)
  other arithmetic  4.38 us (2%)
    ppermute x22, starting transfers between devices, ring_shift(): return lax.ppermute(value, ('r', 'h'), pairs)  88.1 us
    ppermute x22, waiting for transfers between devices, ring_shift(): return lax.ppermute(value, ('r', 'h'), pairs)  33.2 us
    ppermute x1, starting transfers between devices, local(): lax.ppermute(grad_tokens, ('r', 'y', 'c', 'h'), result_pairs())  15.3 us
    all_to_all x2, starting transfers between devices, gather_plane(): lax.all_to_all(copies, ('y', 'c', 'x'), split_axis=0, concat_axis=0, tile...  15.1 us
    ppermute x1, starting transfers between devices, local(): far_piece = lax.ppermute(piece, 'h', [(0, 1), (1, 0)])  12 us
    all_to_all x1, blocking collectives, local(): lax.all_to_all(hidden.T.reshape(-1, 2, 1, part), 'x', split_axis=0, conca...  9.35 us
    all_to_all x1, starting transfers between devices, local(): lax.all_to_all(grad_hidden.reshape(-1, 2, 4, part), 'x', split_axis=2, co...  9.2 us
    unnamed x35, local copies, waits for them, and re-layouts  8.57 us
  transfers between devices with their start and end apart: 29, of which 14 were waited for; matrix products, arithmetic and copies ran while one was open for 4% of the time, Pallas kernels for 3%

profile of v2, /device:TPU:2, one launch (start us, length us, event | category | flops | bytes accessed | tf_op | source)
XLA Modules:
  0.0 238.3 jit_solution(3533946684722391395)
XLA Ops:
  0.6 1.1 reshape.34
  2.4 9.2 %all-to-all-start = ((bf16[32,2,4,224]{3,0,1,2:T(8,128)(2,1)}), bf16[32,2,4,224]{3,0,1,2:T(8,128)(2,1)S(1)}, u32[]{:S(2)}, u32[]{:S(2)}) async-start(bf16[32,2,4,224]{3,0,1,2:T(8,128)(2,1)} %copy.22), calls=%async_computation | async-start | bytes 262144 | tf_op jit(solution)/shard_map/all_to_all | solution.py:148
  11.6 1.9 collective-permute-start
  13.5 2.6 %all-to-all-done = bf16[32,2,4,224]{3,0,1,2:T(8,128)(2,1)S(1)} async-done(((bf16[32,2,4,224]{3,0,1,2:T(8,128)(2,1)}), bf16[32,2,4,224]{3,0,1,2:T(8,128)(2,1)S(1)}, u32[]{:S(2)}, u32[]{:S(2)}) %all-to-all-start) | async-done | bytes 114720 | tf_op jit(solution)/shard_map/all_to_all | solution.py:148
  16.8 4.8 %collective-permute-done = bf16[32,512]{1,0:T(8,128)(2,1)S(1)} collective-permute-done((bf16[32,512]{1,0:T(8,128)(2,1)}, bf16[32,512]{1,0:T(8,128)(2,1)S(1)}, u32[]{:S(2)}, u32[]{:S(2)}) %collective-permute-start) | collective-permute-done | bytes 32800 | tf_op jit(solution)/shard_map/ppermute | solution.py:147
  21.6 1.1 broadcast_in_dim.4
  22.7 7.7 %all-to-all-start.1 = ((bf16[32,32,512]{2,1,0:T(8,128)(2,1)}), bf16[32,32,512]{2,1,0:T(8,128)(2,1)S(1)}, u32[]{:S(2)}, u32[]{:S(2)}) async-start(bf16[32,32,512]{2,1,0:T(8,128)(2,1)} %broadcast_in_dim.4), calls=%async_computation.1 | async-start | bytes 2097152 | tf_op jit(solution)/shard_map/all_to_all | solution.py:51
  30.5 1.8 constant_dynamic-slice_fusion.2
  32.3 12.0 %collective-permute-start.1 = (bf16[32,512]{1,0:T(8,128)(2,1)S(1)}, bf16[32,512]{1,0:T(8,128)(2,1)S(1)}, u32[]{:S(2)}, u32[]{:S(2)}) collective-permute-start(bf16[32,512]{1,0:T(8,128)(2,1)S(1)} %collective-permute-done), channel_id=1, source_target_pairs={{0,4},{4,0},{1,5},{5,1},{2,6},{6,2},{3,7},{7,3},{8,12},{12,8},{9,1... | collective-permute-start | bytes 98312 | tf_op jit(solution)/shard_map/ppermute | solution.py:153
  44.7 2.1 collective-permute-done.1
  46.8 1.1 broadcast_in_dim.5
  47.9 7.4 %all-to-all-start.2 = ((bf16[32,32,512]{2,1,0:T(8,128)(2,1)}), bf16[32,32,512]{2,1,0:T(8,128)(2,1)S(1)}, u32[]{:S(2)}, u32[]{:S(2)}) async-start(bf16[32,32,512]{2,1,0:T(8,128)(2,1)} %broadcast_in_dim.5), calls=%async_computation.2 | async-start | bytes 2097152 | tf_op jit(solution)/shard_map/all_to_all | solution.py:51
  55.3 2.0 shard_map.75
  57.3 5.2 %collective-permute-start.2 = (bf16[896,128]{1,0:T(8,128)(2,1)S(1)}, bf16[896,128]{1,0:T(8,128)(2,1)S(1)}, u32[]{:S(2)}, u32[]{:S(2)}) collective-permute-start(bf16[896,128]{1,0:T(8,128)(2,1)S(1)} %get-tuple-element.43), channel_id=1, source_target_pairs={{0,256},{64,320},{128,384},{192,448},{256,4},{320,68},{384,132},{4... | collective-permute-start | bytes 688136 | tf_op jit(solution)/shard_map/ppermute | solution.py:20
  62.5 5.4 %collective-permute-start.3 = (bf16[896,128]{1,0:T(8,128)(2,1)S(1)}, bf16[896,128]{1,0:T(8,128)(2,1)S(1)}, u32[]{:S(2)}, u32[]{:S(2)}) collective-permute-start(bf16[896,128]{1,0:T(8,128)(2,1)S(1)} %get-tuple-element.44), channel_id=1, source_target_pairs={{0,324},{64,388},{128,452},{192,0},{256,64},{320,128},{384,192},{4... | collective-permute-start | bytes 688136 | tf_op jit(solution)/shard_map/ppermute | solution.py:20
  67.9 2.2 collective-permute-start.4
  70.1 5.9 %collective-permute-start.5 = (bf16[896,128]{1,0:T(8,128)(2,1)}, bf16[896,128]{1,0:T(8,128)(2,1)}, u32[]{:S(2)}, u32[]{:S(2)}) collective-permute-start(bf16[896,128]{1,0:T(8,128)(2,1)} %get-tuple-element.46), channel_id=1, source_target_pairs={{0,388},{64,452},{128,0},{192,64},{256,128},{320,192},{384,256},{4... | collective-permute-start | bytes 688136 | tf_op jit(solution)/shard_map/ppermute | solution.py:20
  76.1 3.2 %collective-permute-start.6 = (bf16[896,128]{1,0:T(8,128)(2,1)}, bf16[896,128]{1,0:T(8,128)(2,1)}, u32[]{:S(2)}, u32[]{:S(2)}) collective-permute-start(bf16[896,128]{1,0:T(8,128)(2,1)} %get-tuple-element.47), channel_id=1, source_target_pairs={{0,128},{64,192},{128,256},{192,320},{256,384},{320,448},{384,4},{... | collective-permute-start | bytes 688136 | tf_op jit(solution)/shard_map/ppermute | solution.py:20
  79.3 11.8 %collective-permute-start.7 = (bf16[896,128]{1,0:T(8,128)(2,1)}, bf16[896,128]{1,0:T(8,128)(2,1)}, u32[]{:S(2)}, u32[]{:S(2)}) collective-permute-start(bf16[896,128]{1,0:T(8,128)(2,1)} %get-tuple-element.48), channel_id=1, source_target_pairs={{0,452},{64,0},{128,64},{192,128},{256,192},{320,256},{384,320},{4... | collective-permute-start | bytes 688136 | tf_op jit(solution)/shard_map/ppermute | solution.py:20
  91.2 0.7 copy-done.16
  91.8 1.9 collective-permute-start.8
  93.8 1.7 copy.24
  95.5 6.0 %collective-permute-done.4 = bf16[896,128]{1,0:T(8,128)(2,1)} collective-permute-done((bf16[896,128]{1,0:T(8,128)(2,1)}, bf16[896,128]{1,0:T(8,128)(2,1)}, u32[]{:S(2)}, u32[]{:S(2)}) %collective-permute-start.4) | collective-permute-done | bytes 229408 | tf_op jit(solution)/shard_map/ppermute | solution.py:20
  101.5 9.1 %collective-permute-done.6 = bf16[896,128]{1,0:T(8,128)(2,1)} collective-permute-done((bf16[896,128]{1,0:T(8,128)(2,1)}, bf16[896,128]{1,0:T(8,128)(2,1)}, u32[]{:S(2)}, u32[]{:S(2)}) %collective-permute-start.6) | collective-permute-done | bytes 229408 | tf_op jit(solution)/shard_map/ppermute | solution.py:20
  110.6 3.7 %collective-permute-done.8 = bf16[896,128]{1,0:T(8,128)(2,1)} collective-permute-done((bf16[896,128]{1,0:T(8,128)(2,1)S(1)}, bf16[896,128]{1,0:T(8,128)(2,1)}, u32[]{:S(2)}, u32[]{:S(2)}) %collective-permute-start.8) | collective-permute-done | bytes 229408 | tf_op jit(solution)/shard_map/ppermute | solution.py:20
  114.3 1.7 convert_add_fusion
  116.1 0.8 multiply_convert_fusion
  117.0 2.9 %collective-permute-start.9 = (bf16[896,128]{1,0:T(8,128)(2,1)S(1)}, bf16[896,128]{1,0:T(8,128)(2,1)S(1)}, u32[]{:S(2)}, u32[]{:S(2)}) collective-permute-start(bf16[896,128]{1,0:T(8,128)(2,1)S(1)} %pad_maximum_fusion.3.refs_4_.refs_3_), channel_id=1, source_target_pairs={{0,64},{64,128},{128,192},{192,256},{256,320},{320,384},{384,448},... | collective-permute-start | bytes 688136 | tf_op jit(solution)/shard_map/ppermute | solution.py:20
  119.9 4.2 %collective-permute-start.13 = (bf16[896,128]{1,0:T(8,128)(2,1)S(1)}, bf16[896,128]{1,0:T(8,128)(2,1)S(1)}, u32[]{:S(2)}, u32[]{:S(2)}) collective-permute-start(bf16[896,128]{1,0:T(8,128)(2,1)S(1)} %pad_maximum_fusion.3.refs_4_.refs_3_), channel_id=1, source_target_pairs={{0,452},{64,0},{128,64},{192,128},{256,192},{320,256},{384,320},{4... | collective-permute-start | bytes 688136 | tf_op jit(solution)/shard_map/ppermute | solution.py:20
  124.0 3.0 %collective-permute-done.9.refs_3_.refs_2_ = bf16[896,128]{1,0:T(8,128)(2,1)S(1)} collective-permute-done((bf16[896,128]{1,0:T(8,128)(2,1)S(1)}, bf16[896,128]{1,0:T(8,128)(2,1)S(1)}, u32[]{:S(2)}, u32[]{:S(2)}) %collective-permute-start.9) | collective-permute-done | bytes 229408 | tf_op jit(solution)/shard_map/ppermute | solution.py:20
  127.1 1.9 collective-permute-start.10
  129.0 5.1 %collective-permute-start.14 = (bf16[896,128]{1,0:T(8,128)(2,1)S(1)}, bf16[896,128]{1,0:T(8,128)(2,1)S(1)}, u32[]{:S(2)}, u32[]{:S(2)}) collective-permute-start(bf16[896,128]{1,0:T(8,128)(2,1)S(1)} %collective-permute-done.13.refs_5_.refs_4_), channel_id=1, source_target_pairs={{0,452},{64,0},{128,64},{192,128},{256,192},{320,256},{384,320},{4... | collective-permute-start | bytes 688136 | tf_op jit(solution)/shard_map/ppermute | solution.py:20
  134.8 1.4 collective-permute-done.10.refs_2_.refs_1_
  136.2 1.9 collective-permute-start.11
  138.8 5.1 %collective-permute-start.15 = (bf16[896,128]{1,0:T(8,128)(2,1)S(1)}, bf16[896,128]{1,0:T(8,128)(2,1)}, u32[]{:S(2)}, u32[]{:S(2)}) collective-permute-start(bf16[896,128]{1,0:T(8,128)(2,1)S(1)} %collective-permute-done.14.refs_6_.refs_5_), channel_id=1, source_target_pairs={{0,452},{64,0},{128,64},{192,128},{256,192},{320,256},{384,320},{4... | collective-permute-start | bytes 688136 | tf_op jit(solution)/shard_map/ppermute | solution.py:20
  144.0 0.7 copy-done.7
  144.7 0.8 collective-permute-done.11.refs_1_.refs_0_
  145.4 1.9 collective-permute-start.12
  147.5 5.7 %collective-permute-start.16 = (bf16[896,128]{1,0:T(8,128)(2,1)}, bf16[896,128]{1,0:T(8,128)(2,1)}, u32[]{:S(2)}, u32[]{:S(2)}) collective-permute-start(bf16[896,128]{1,0:T(8,128)(2,1)} %collective-permute-done.15.refs_7_.refs_6_), channel_id=1, source_target_pairs={{0,452},{64,0},{128,64},{192,128},{256,192},{320,256},{384,320},{4... | collective-permute-start | bytes 688136 | tf_op jit(solution)/shard_map/ppermute | solution.py:20
  153.2 1.7 copy.25
  154.8 9.3 %all_to_all.51 = bf16[128,2,1,224]{3,1,2,0:T(2,128)(2,1)S(1)} all-to-all(bf16[128,2,1,224]{3,1,2,0:T(2,128)(2,1)} %copy.25), channel_id=1, replica_groups=mesh['r'=8,'y'=4,'c'=2,'h'=2,'x'=4] {'x'}, dimensions={0} | all-to-all | bytes 229376 | tf_op jit(solution)/shard_map/all_to_all | solution.py:176
  164.9 0.9 copy-done.2
  165.8 0.9 copy-done.5
  166.7 0.9 copy-done.8
  167.7 3.3 %shard_map.76 = bf16[1024,512]{1,0:T(8,128)(2,1)S(1)} custom-call(bf16[512,896]{1,0:T(8,128)(2,1)S(1)} %pad_maximum_fusion.weights_ref, bf16[896,128]{1,0:T(8,128)(2,1)} %collective-permute-done.12.refs_0_.refs_7_, bf16[896,128]{1,0:T(8,128)(2,1)} %collective-permute-done.11.refs_1_.refs_0_, bf16[896,128]{1,0:T(8,128)(2,1)S(1)} %copy-done.5, ...), custom_call_target="tpu_custom_call" | custom-call | tf_op jit(solution)/shard_map/pallas_call | solution.py:78
  171.0 1.0 copy-done
  172.0 6.7 %all-to-all-start.4 = ((bf16[32,32,512]{2,1,0:T(8,128)(2,1)}), bf16[32,32,512]{2,1,0:T(8,128)(2,1)}, u32[]{:S(2)}, u32[]{:S(2)}) async-start(bf16[32,32,512]{2,1,0:T(8,128)(2,1)} %bitcast.34), calls=%async_computation.4 | async-start | bytes 2097152 | tf_op jit(solution)/shard_map/all_to_all | solution.py:191
  178.6 1.9 collective-permute-start.17
  180.6 5.1 %collective-permute-start.19 = (bf16[896,128]{1,0:T(8,128)(2,1)}, bf16[896,128]{1,0:T(8,128)(2,1)S(1)}, u32[]{:S(2)}, u32[]{:S(2)}) collective-permute-start(bf16[896,128]{1,0:T(8,128)(2,1)} %collective-permute-done.16.refs_7_), channel_id=1, source_target_pairs={{0,452},{64,0},{128,64},{192,128},{256,192},{320,256},{384,320},{4... | collective-permute-start | bytes 688136 | tf_op jit(solution)/shard_map/ppermute | solution.py:20
  185.7 3.9 %collective-permute-done.17.refs_6_ = bf16[896,128]{1,0:T(8,128)(2,1)S(1)} collective-permute-done((bf16[896,128]{1,0:T(8,128)(2,1)}, bf16[896,128]{1,0:T(8,128)(2,1)S(1)}, u32[]{:S(2)}, u32[]{:S(2)}) %collective-permute-start.17) | collective-permute-done | bytes 229408 | tf_op jit(solution)/shard_map/ppermute | solution.py:20
  189.6 1.9 collective-permute-start.18
  191.5 5.1 %collective-permute-start.20 = (bf16[896,128]{1,0:T(8,128)(2,1)S(1)}, bf16[896,128]{1,0:T(8,128)(2,1)}, u32[]{:S(2)}, u32[]{:S(2)}) collective-permute-start(bf16[896,128]{1,0:T(8,128)(2,1)S(1)} %collective-permute-done.19.refs_0_), channel_id=1, source_target_pairs={{0,452},{64,0},{128,64},{192,128},{256,192},{320,256},{384,320},{4... | collective-permute-start | bytes 688136 | tf_op jit(solution)/shard_map/ppermute | solution.py:20
  197.4 2.3 collective-permute-done.18.refs_5_
  199.6 0.7 copy-done.12
  200.8 1.4 reduce_sum.12
  202.2 2.8 %collective-permute-start.23 = (bf16[896,128]{1,0:T(8,128)(2,1)}, bf16[896,128]{1,0:T(8,128)(2,1)}, u32[]{:S(2)}, u32[]{:S(2)}) collective-permute-start(bf16[896,128]{1,0:T(8,128)(2,1)} %copy-done.12), channel_id=1, source_target_pairs={{0,64},{64,128},{128,192},{192,256},{256,320},{320,384},{384,448},... | collective-permute-start | bytes 688136 | tf_op jit(solution)/shard_map/ppermute | solution.py:20
  205.0 4.8 %collective-permute-start.22 = (bf16[896,128]{1,0:T(8,128)(2,1)}, bf16[896,128]{1,0:T(8,128)(2,1)}, u32[]{:S(2)}, u32[]{:S(2)}) collective-permute-start(bf16[896,128]{1,0:T(8,128)(2,1)} %collective-permute-done.20.refs_1_), channel_id=1, source_target_pairs={{0,452},{64,0},{128,64},{192,128},{256,192},{320,256},{384,320},{4... | collective-permute-start | bytes 688136 | tf_op jit(solution)/shard_map/ppermute | solution.py:20
  209.9 2.4 collective-permute-done.23.refs_4_
  212.2 1.9 collective-permute-start.24
  214.2 15.3 %collective-permute-start.21 = (bf16[32,512]{1,0:T(8,128)(2,1)S(1)}, bf16[32,512]{1,0:T(8,128)(2,1)S(1)}, u32[]{:S(2)}, u32[]{:S(2)}) collective-permute-start(bf16[32,512]{1,0:T(8,128)(2,1)S(1)} %reduce_sum.12), channel_id=1, source_target_pairs={{0,36},{8,44},{16,52},{24,60},{32,0},{40,8},{48,16},{56,24},{64,10... | collective-permute-start | bytes 98312 | tf_op jit(solution)/shard_map/ppermute | solution.py:199
  229.5 1.7 copy.27
  231.1 1.7 reshape.38
  232.9 1.9 shard_map.77.near_ref
  234.8 2.9 %shard_map.78 = (f32[224,512]{1,0:T(8,128)}, f32[224,512]{1,0:T(8,128)}) custom-call(s32[1]{0:T(128)} %bitcast.14.half_ref, bf16[1024,512]{1,0:T(8,128)(2,1)S(1)} %bitcast.33, f32[448,512]{1,0:T(8,128)S(1)} %shard_map.77.near_ref, bf16[896,128]{1,0:T(8,128)(2,1)S(1)} %copy-done.11, bf16[896,128]{1,0:T(8,128)(2,1)} %collective-permute-done.20.refs_1_, ...), custom_call_target="tpu_custom_call" | custom-call | tf_op jit(solution)/shard_map/pallas_call | solution.py:124
  (53 shorter events, 5.9 us)
Async XLA Ops:
  2.4 13.7 %all-to-all-start = ((bf16[32,2,4,224]{3,0,1,2:T(8,128)(2,1)}), bf16[32,2,4,224]{3,0,1,2:T(8,128)(2,1)S(1)}, u32[]{:S(2)}, u32[]{:S(2)}) async-start(bf16[32,2,4,224]{3,0,1,2:T(8,128)(2,1)} %copy.22), calls=%async_computation | async-start | bytes 262144 | tf_op jit(solution)/shard_map/all_to_all | solution.py:148
  11.6 10.0 %collective-permute-start = (bf16[32,512]{1,0:T(8,128)(2,1)}, bf16[32,512]{1,0:T(8,128)(2,1)S(1)}, u32[]{:S(2)}, u32[]{:S(2)}) collective-permute-start(bf16[32,512]{1,0:T(8,128)(2,1)} %param.4), channel_id=1, source_target_pairs={{324,0},{388,8},{452,16},{0,24},{64,32},{128,40},{192,48},{256,56}... | collective-permute-start | bytes 98312 | tf_op jit(solution)/shard_map/ppermute | solution.py:147
  22.7 24.1 %all-to-all-start.1 = ((bf16[32,32,512]{2,1,0:T(8,128)(2,1)}), bf16[32,32,512]{2,1,0:T(8,128)(2,1)S(1)}, u32[]{:S(2)}, u32[]{:S(2)}) async-start(bf16[32,32,512]{2,1,0:T(8,128)(2,1)} %broadcast_in_dim.4), calls=%async_computation.1 | async-start | bytes 2097152 | tf_op jit(solution)/shard_map/all_to_all | solution.py:51
  32.3 14.5 %collective-permute-start.1 = (bf16[32,512]{1,0:T(8,128)(2,1)S(1)}, bf16[32,512]{1,0:T(8,128)(2,1)S(1)}, u32[]{:S(2)}, u32[]{:S(2)}) collective-permute-start(bf16[32,512]{1,0:T(8,128)(2,1)S(1)} %collective-permute-done), channel_id=1, source_target_pairs={{0,4},{4,0},{1,5},{5,1},{2,6},{6,2},{3,7},{7,3},{8,12},{12,8},{9,1... | collective-permute-start | bytes 98312 | tf_op jit(solution)/shard_map/ppermute | solution.py:153
  47.9 66.4 %all-to-all-start.2 = ((bf16[32,32,512]{2,1,0:T(8,128)(2,1)}), bf16[32,32,512]{2,1,0:T(8,128)(2,1)S(1)}, u32[]{:S(2)}, u32[]{:S(2)}) async-start(bf16[32,32,512]{2,1,0:T(8,128)(2,1)} %broadcast_in_dim.5), calls=%async_computation.2 | async-start | bytes 2097152 | tf_op jit(solution)/shard_map/all_to_all | solution.py:51
  57.3 22.0 %collective-permute-start.2 = (bf16[896,128]{1,0:T(8,128)(2,1)S(1)}, bf16[896,128]{1,0:T(8,128)(2,1)S(1)}, u32[]{:S(2)}, u32[]{:S(2)}) collective-permute-start(bf16[896,128]{1,0:T(8,128)(2,1)S(1)} %get-tuple-element.43), channel_id=1, source_target_pairs={{0,256},{64,320},{128,384},{192,448},{256,4},{320,68},{384,132},{4... | collective-permute-start | bytes 688136 | tf_op jit(solution)/shard_map/ppermute | solution.py:20
  62.5 28.6 %collective-permute-start.3 = (bf16[896,128]{1,0:T(8,128)(2,1)S(1)}, bf16[896,128]{1,0:T(8,128)(2,1)S(1)}, u32[]{:S(2)}, u32[]{:S(2)}) collective-permute-start(bf16[896,128]{1,0:T(8,128)(2,1)S(1)} %get-tuple-element.44), channel_id=1, source_target_pairs={{0,324},{64,388},{128,452},{192,0},{256,64},{320,128},{384,192},{4... | collective-permute-start | bytes 688136 | tf_op jit(solution)/shard_map/ppermute | solution.py:20
  67.9 33.6 %collective-permute-start.4 = (bf16[896,128]{1,0:T(8,128)(2,1)}, bf16[896,128]{1,0:T(8,128)(2,1)}, u32[]{:S(2)}, u32[]{:S(2)}) collective-permute-start(bf16[896,128]{1,0:T(8,128)(2,1)} %get-tuple-element.45), channel_id=1, source_target_pairs={{0,192},{64,256},{128,320},{192,384},{256,448},{320,4},{384,68},{4... | collective-permute-start | bytes 688136 | tf_op jit(solution)/shard_map/ppermute | solution.py:20
  70.1 31.3 %collective-permute-start.5 = (bf16[896,128]{1,0:T(8,128)(2,1)}, bf16[896,128]{1,0:T(8,128)(2,1)}, u32[]{:S(2)}, u32[]{:S(2)}) collective-permute-start(bf16[896,128]{1,0:T(8,128)(2,1)} %get-tuple-element.46), channel_id=1, source_target_pairs={{0,388},{64,452},{128,0},{192,64},{256,128},{320,192},{384,256},{4... | collective-permute-start | bytes 688136 | tf_op jit(solution)/shard_map/ppermute | solution.py:20
  76.1 34.5 %collective-permute-start.6 = (bf16[896,128]{1,0:T(8,128)(2,1)}, bf16[896,128]{1,0:T(8,128)(2,1)}, u32[]{:S(2)}, u32[]{:S(2)}) collective-permute-start(bf16[896,128]{1,0:T(8,128)(2,1)} %get-tuple-element.47), channel_id=1, source_target_pairs={{0,128},{64,192},{128,256},{192,320},{256,384},{320,448},{384,4},{... | collective-permute-start | bytes 688136 | tf_op jit(solution)/shard_map/ppermute | solution.py:20
  79.3 11.9 %copy-start.15 = (bf16[896,128]{1,0:T(8,128)(2,1)}, bf16[896,128]{1,0:T(8,128)(2,1)S(1)}, u32[]{:S(2)}) copy-start(bf16[896,128]{1,0:T(8,128)(2,1)S(1)} %collective-permute-done.2) | copy-start | bytes 688132
  79.3 31.3 %collective-permute-start.7 = (bf16[896,128]{1,0:T(8,128)(2,1)}, bf16[896,128]{1,0:T(8,128)(2,1)}, u32[]{:S(2)}, u32[]{:S(2)}) collective-permute-start(bf16[896,128]{1,0:T(8,128)(2,1)} %get-tuple-element.48), channel_id=1, source_target_pairs={{0,452},{64,0},{128,64},{192,128},{256,192},{320,256},{384,320},{4... | collective-permute-start | bytes 688136 | tf_op jit(solution)/shard_map/ppermute | solution.py:20
  91.1 0.7 copy-start.16
  91.8 22.5 %collective-permute-start.8 = (bf16[896,128]{1,0:T(8,128)(2,1)S(1)}, bf16[896,128]{1,0:T(8,128)(2,1)}, u32[]{:S(2)}, u32[]{:S(2)}) collective-permute-start(bf16[896,128]{1,0:T(8,128)(2,1)S(1)} %get-tuple-element.49), channel_id=1, source_target_pairs={{0,64},{64,128},{128,192},{192,256},{256,320},{320,384},{384,448},... | collective-permute-start | bytes 688136 | tf_op jit(solution)/shard_map/ppermute | solution.py:20
  114.3 1.8 copy-start.14
  117.0 10.1 %collective-permute-start.9 = (bf16[896,128]{1,0:T(8,128)(2,1)S(1)}, bf16[896,128]{1,0:T(8,128)(2,1)S(1)}, u32[]{:S(2)}, u32[]{:S(2)}) collective-permute-start(bf16[896,128]{1,0:T(8,128)(2,1)S(1)} %pad_maximum_fusion.3.refs_4_.refs_3_), channel_id=1, source_target_pairs={{0,64},{64,128},{128,192},{192,256},{256,320},{320,384},{384,448},... | collective-permute-start | bytes 688136 | tf_op jit(solution)/shard_map/ppermute | solution.py:20
  119.9 9.1 %collective-permute-start.13 = (bf16[896,128]{1,0:T(8,128)(2,1)S(1)}, bf16[896,128]{1,0:T(8,128)(2,1)S(1)}, u32[]{:S(2)}, u32[]{:S(2)}) collective-permute-start(bf16[896,128]{1,0:T(8,128)(2,1)S(1)} %pad_maximum_fusion.3.refs_4_.refs_3_), channel_id=1, source_target_pairs={{0,452},{64,0},{128,64},{192,128},{256,192},{320,256},{384,320},{4... | collective-permute-start | bytes 688136 | tf_op jit(solution)/shard_map/ppermute | solution.py:20
  127.1 9.1 %collective-permute-start.10 = (bf16[896,128]{1,0:T(8,128)(2,1)S(1)}, bf16[896,128]{1,0:T(8,128)(2,1)S(1)}, u32[]{:S(2)}, u32[]{:S(2)}) collective-permute-start(bf16[896,128]{1,0:T(8,128)(2,1)S(1)} %collective-permute-done.9.refs_3_.refs_2_), channel_id=1, source_target_pairs={{0,64},{64,128},{128,192},{192,256},{256,320},{320,384},{384,448},... | collective-permute-start | bytes 688136 | tf_op jit(solution)/shard_map/ppermute | solution.py:20
  129.0 9.8 %collective-permute-start.14 = (bf16[896,128]{1,0:T(8,128)(2,1)S(1)}, bf16[896,128]{1,0:T(8,128)(2,1)S(1)}, u32[]{:S(2)}, u32[]{:S(2)}) collective-permute-start(bf16[896,128]{1,0:T(8,128)(2,1)S(1)} %collective-permute-done.13.refs_5_.refs_4_), channel_id=1, source_target_pairs={{0,452},{64,0},{128,64},{192,128},{256,192},{320,256},{384,320},{4... | collective-permute-start | bytes 688136 | tf_op jit(solution)/shard_map/ppermute | solution.py:20
  134.1 0.7 copy-start.1
  136.2 9.2 %collective-permute-start.11 = (bf16[896,128]{1,0:T(8,128)(2,1)S(1)}, bf16[896,128]{1,0:T(8,128)(2,1)}, u32[]{:S(2)}, u32[]{:S(2)}) collective-permute-start(bf16[896,128]{1,0:T(8,128)(2,1)S(1)} %collective-permute-done.10.refs_2_.refs_1_), channel_id=1, source_target_pairs={{0,64},{64,128},{128,192},{192,256},{256,320},{320,384},{384,448},... | collective-permute-start | bytes 688136 | tf_op jit(solution)/shard_map/ppermute | solution.py:20
  138.1 0.7 copy-start.4
  138.8 8.6 %collective-permute-start.15 = (bf16[896,128]{1,0:T(8,128)(2,1)S(1)}, bf16[896,128]{1,0:T(8,128)(2,1)}, u32[]{:S(2)}, u32[]{:S(2)}) collective-permute-start(bf16[896,128]{1,0:T(8,128)(2,1)S(1)} %collective-permute-done.14.refs_6_.refs_5_), channel_id=1, source_target_pairs={{0,452},{64,0},{128,64},{192,128},{256,192},{320,256},{384,320},{4... | collective-permute-start | bytes 688136 | tf_op jit(solution)/shard_map/ppermute | solution.py:20
  143.9 0.7 copy-start.7
  145.4 19.4 %collective-permute-start.12 = (bf16[896,128]{1,0:T(8,128)(2,1)}, bf16[896,128]{1,0:T(8,128)(2,1)}, u32[]{:S(2)}, u32[]{:S(2)}) collective-permute-start(bf16[896,128]{1,0:T(8,128)(2,1)} %collective-permute-done.11.refs_1_.refs_0_), channel_id=1, source_target_pairs={{0,64},{64,128},{128,192},{192,256},{256,320},{320,384},{384,448},... | collective-permute-start | bytes 688136 | tf_op jit(solution)/shard_map/ppermute | solution.py:20
  147.5 24.5 %collective-permute-start.16 = (bf16[896,128]{1,0:T(8,128)(2,1)}, bf16[896,128]{1,0:T(8,128)(2,1)}, u32[]{:S(2)}, u32[]{:S(2)}) collective-permute-start(bf16[896,128]{1,0:T(8,128)(2,1)} %collective-permute-done.15.refs_7_.refs_6_), channel_id=1, source_target_pairs={{0,452},{64,0},{128,64},{192,128},{256,192},{320,256},{384,320},{4... | collective-permute-start | bytes 688136 | tf_op jit(solution)/shard_map/ppermute | solution.py:20
  164.9 0.9 copy-start.2
  165.8 0.9 copy-start.5
  166.7 0.9 copy-start.8
  171.0 1.0 copy-start
  172.0 60.9 %copy-start.3 = (bf16[896,128]{1,0:T(8,128)(2,1)S(1)}, bf16[896,128]{1,0:T(8,128)(2,1)}, u32[]{:S(2)}) copy-start(bf16[896,128]{1,0:T(8,128)(2,1)} %copy-done.1) | copy-start | bytes 688132
  172.0 60.9 %copy-start.6 = (bf16[896,128]{1,0:T(8,128)(2,1)S(1)}, bf16[896,128]{1,0:T(8,128)(2,1)}, u32[]{:S(2)}) copy-start(bf16[896,128]{1,0:T(8,128)(2,1)} %copy-done.4) | copy-start | bytes 688132
  172.0 60.9 %copy-start.9 = (bf16[896,128]{1,0:T(8,128)(2,1)S(1)}, bf16[896,128]{1,0:T(8,128)(2,1)}, u32[]{:S(2)}) copy-start(bf16[896,128]{1,0:T(8,128)(2,1)} %copy-done.7) | copy-start | bytes 688132
  172.0 28.9 %all-to-all-start.4 = ((bf16[32,32,512]{2,1,0:T(8,128)(2,1)}), bf16[32,32,512]{2,1,0:T(8,128)(2,1)}, u32[]{:S(2)}, u32[]{:S(2)}) async-start(bf16[32,32,512]{2,1,0:T(8,128)(2,1)} %bitcast.34), calls=%async_computation.4 | async-start | bytes 2097152 | tf_op jit(solution)/shard_map/all_to_all | solution.py:191
  178.6 11.0 %collective-permute-start.17 = (bf16[896,128]{1,0:T(8,128)(2,1)}, bf16[896,128]{1,0:T(8,128)(2,1)S(1)}, u32[]{:S(2)}, u32[]{:S(2)}) collective-permute-start(bf16[896,128]{1,0:T(8,128)(2,1)} %collective-permute-done.12.refs_0_.refs_7_), channel_id=1, source_target_pairs={{0,64},{64,128},{128,192},{192,256},{256,320},{320,384},{384,448},... | collective-permute-start | bytes 688136 | tf_op jit(solution)/shard_map/ppermute | solution.py:20
  180.6 11.0 %collective-permute-start.19 = (bf16[896,128]{1,0:T(8,128)(2,1)}, bf16[896,128]{1,0:T(8,128)(2,1)S(1)}, u32[]{:S(2)}, u32[]{:S(2)}) collective-permute-start(bf16[896,128]{1,0:T(8,128)(2,1)} %collective-permute-done.16.refs_7_), channel_id=1, source_target_pairs={{0,452},{64,0},{128,64},{192,128},{256,192},{320,256},{384,320},{4... | collective-permute-start | bytes 688136 | tf_op jit(solution)/shard_map/ppermute | solution.py:20
  189.6 10.0 %collective-permute-start.18 = (bf16[896,128]{1,0:T(8,128)(2,1)S(1)}, bf16[896,128]{1,0:T(8,128)(2,1)S(1)}, u32[]{:S(2)}, u32[]{:S(2)}) collective-permute-start(bf16[896,128]{1,0:T(8,128)(2,1)S(1)} %collective-permute-done.17.refs_6_), channel_id=1, source_target_pairs={{0,64},{64,128},{128,192},{192,256},{256,320},{320,384},{384,448},... | collective-permute-start | bytes 688136 | tf_op jit(solution)/shard_map/ppermute | solution.py:20
  191.5 9.3 %collective-permute-start.20 = (bf16[896,128]{1,0:T(8,128)(2,1)S(1)}, bf16[896,128]{1,0:T(8,128)(2,1)}, u32[]{:S(2)}, u32[]{:S(2)}) collective-permute-start(bf16[896,128]{1,0:T(8,128)(2,1)S(1)} %collective-permute-done.19.refs_0_), channel_id=1, source_target_pairs={{0,452},{64,0},{128,64},{192,128},{256,192},{320,256},{384,320},{4... | collective-permute-start | bytes 688136 | tf_op jit(solution)/shard_map/ppermute | solution.py:20
  196.7 0.7 copy-start.10
  199.6 0.7 copy-start.12
  202.2 10.0 %collective-permute-start.23 = (bf16[896,128]{1,0:T(8,128)(2,1)}, bf16[896,128]{1,0:T(8,128)(2,1)}, u32[]{:S(2)}, u32[]{:S(2)}) collective-permute-start(bf16[896,128]{1,0:T(8,128)(2,1)} %copy-done.12), channel_id=1, source_target_pairs={{0,64},{64,128},{128,192},{192,256},{256,320},{320,384},{384,448},... | collective-permute-start | bytes 688136 | tf_op jit(solution)/shard_map/ppermute | solution.py:20
  205.0 29.7 %collective-permute-start.22 = (bf16[896,128]{1,0:T(8,128)(2,1)}, bf16[896,128]{1,0:T(8,128)(2,1)}, u32[]{:S(2)}, u32[]{:S(2)}) collective-permute-start(bf16[896,128]{1,0:T(8,128)(2,1)} %collective-permute-done.20.refs_1_), channel_id=1, source_target_pairs={{0,452},{64,0},{128,64},{192,128},{256,192},{320,256},{384,320},{4... | collective-permute-start | bytes 688136 | tf_op jit(solution)/shard_map/ppermute | solution.py:20
  212.2 22.5 %collective-permute-start.24 = (bf16[896,128]{1,0:T(8,128)(2,1)}, bf16[896,128]{1,0:T(8,128)(2,1)}, u32[]{:S(2)}, u32[]{:S(2)}) collective-permute-start(bf16[896,128]{1,0:T(8,128)(2,1)} %collective-permute-done.23.refs_4_), channel_id=1, source_target_pairs={{0,64},{64,128},{128,192},{192,256},{256,320},{320,384},{384,448},... | collective-permute-start | bytes 688136 | tf_op jit(solution)/shard_map/ppermute | solution.py:20
  214.2 20.6 %collective-permute-start.21 = (bf16[32,512]{1,0:T(8,128)(2,1)S(1)}, bf16[32,512]{1,0:T(8,128)(2,1)S(1)}, u32[]{:S(2)}, u32[]{:S(2)}) collective-permute-start(bf16[32,512]{1,0:T(8,128)(2,1)S(1)} %reduce_sum.12), channel_id=1, source_target_pairs={{0,36},{8,44},{16,52},{24,60},{32,0},{40,8},{48,16},{56,24},{64,10... | collective-permute-start | bytes 98312 | tf_op jit(solution)/shard_map/ppermute | solution.py:199
  232.9 1.9 copy-start.11
  232.9 1.9 copy-start.13

commit v3 on v1

v3 whole, which is shorter than its diff:
```python
import functools

import jax
import jax.numpy as jnp
from jax import lax
from jax.experimental import pallas as pl
from jax.experimental.pallas import tpu as pltpu
from jax.sharding import Mesh, PartitionSpec as P

RING = 16
ROWS = 8
BEFORE = 3


def ring_index(z):
    z %= RING
    return (z % ROWS) * 2 + z // ROWS


def ring_shift(value, step):
    pairs = [(ring_index(z), ring_index(z + step)) for z in range(RING)]
    return lax.ppermute(value, ("r", "h"), pairs)


def place(z, col):
    z %= RING
    return ((z % ROWS) * ROWS + col) * 2 + z // ROWS


def slot(offset):
    return (offset % 4) * 2 + offset // 4


def token_pairs():
    pairs = []
    for z in range(RING):
        for offset in range(ROWS):
            pairs.append((place(z + offset - BEFORE, z % ROWS), place(z, slot(offset))))
    return pairs


def result_pairs():
    pairs = []
    for z in range(RING):
        for offset in range(ROWS):
            tile = (z + offset - BEFORE) % RING
            pairs.append((place(z, slot(offset)), place(z % ROWS + ROWS * (tile // ROWS), tile % ROWS)))
    return pairs


def dot_f32(left, right, dims=((1,), (0,))):
    return lax.dot_general(left, right, (dims, ((), ())), preferred_element_type=jnp.float32)


SMEM_SPEC = pl.BlockSpec(memory_space=pltpu.SMEM)
VMEM_SPEC = pl.BlockSpec(memory_space=pltpu.VMEM)
PARAMS = pltpu.CompilerParams(vmem_limit_bytes=32 << 20)


def swap_cores(value):
    return lax.ppermute(value, "c", [(0, 1), (1, 0)])


def join_cores(core, own_ref, other_ref, both_ref):
    rows = own_ref.shape[0]
    both_ref[pl.ds(pl.multiple_of(core * rows, rows), rows), :] = own_ref[...]
    both_ref[pl.ds(pl.multiple_of((1 - core) * rows, rows), rows), :] = other_ref[...]


def forward_kernel(offsets, core_ref, own_ref, other_ref, weights_ref, *refs):
    tokens_ref = refs[-1]
    join_cores(core_ref[0], own_ref, other_ref, tokens_ref)
    for offset, tile_ref in zip(offsets, refs):
        product = dot_f32(tokens_ref[offset * 128 : (offset + 1) * 128, :], weights_ref[...])
        tile_ref[...] = product.T.astype(jnp.bfloat16)


def forward_tiles(offsets, core, own, other, weights):
    features, cols = weights.shape
    return pl.pallas_call(
        functools.partial(forward_kernel, offsets),
        in_specs=[SMEM_SPEC] + [VMEM_SPEC] * 3,
        out_specs=[VMEM_SPEC] * len(offsets),
        out_shape=[jax.ShapeDtypeStruct((cols, 128), jnp.bfloat16)] * len(offsets),
        scratch_shapes=[pltpu.VMEM((ROWS * 128, features), jnp.bfloat16)],
        compiler_params=PARAMS,
    )(core, own, other, weights)


def terms_kernel(core_ref, weights_ref, *refs):
    tile_refs = refs[:ROWS]
    keep_ref, send_ref, all_ref = refs[ROWS:]
    for at, tile_ref in enumerate(tile_refs):
        product = dot_f32(weights_ref[...], tile_ref[...])
        all_ref[at * 128 : (at + 1) * 128, :] = product.T
    rows = keep_ref.shape[0]
    core = core_ref[0]
    keep_ref[...] = all_ref[pl.ds(pl.multiple_of(core * rows, rows), rows), :]
    send = all_ref[pl.ds(pl.multiple_of((1 - core) * rows, rows), rows), :]
    send_ref[...] = send.astype(jnp.bfloat16)


def token_terms(core, weights, tiles):
    shape = (ROWS * 64, weights.shape[0])
    return pl.pallas_call(
        terms_kernel,
        in_specs=[SMEM_SPEC] + [VMEM_SPEC] * (1 + ROWS),
        out_specs=[VMEM_SPEC] * 2,
        out_shape=[jax.ShapeDtypeStruct(shape, jnp.float32), jax.ShapeDtypeStruct(shape, jnp.bfloat16)],
        scratch_shapes=[pltpu.VMEM((ROWS * 128, shape[1]), jnp.float32)],
        compiler_params=PARAMS,
    )(core, weights, *tiles)


def weight_grad_kernel(core_ref, half_ref, own_ref, other_ref, *refs):
    tile_refs = refs[:ROWS]
    keep_ref, send_ref, tokens_ref, wide_ref = refs[ROWS:]
    join_cores(core_ref[0], own_ref, other_ref, tokens_ref)
    rows = wide_ref.shape[0]

    def product(half):
        first = pl.multiple_of(half * rows, 16)
        for at, tile_ref in enumerate(tile_refs):
            wide_ref[:, at * 128 : (at + 1) * 128] = tile_ref[pl.ds(first, rows), :]
        return dot_f32(wide_ref[...], tokens_ref[...])

    send_ref[...] = product(1 - half_ref[0]).astype(jnp.bfloat16)
    keep_ref[...] = product(half_ref[0])


def weight_grads(core, half, own, other, tiles):
    rows = tiles[0].shape[0] // 2
    features = own.shape[1]
    return pl.pallas_call(
        weight_grad_kernel,
        in_specs=[SMEM_SPEC] * 2 + [VMEM_SPEC] * (2 + ROWS),
        out_specs=[VMEM_SPEC] * 2,
        out_shape=[
            jax.ShapeDtypeStruct((rows, features), jnp.float32),
            jax.ShapeDtypeStruct((rows, features), jnp.bfloat16),
        ],
        scratch_shapes=[
            pltpu.VMEM((ROWS * 128, features), jnp.bfloat16),
            pltpu.VMEM((rows, ROWS * 128), jnp.bfloat16),
        ],
        compiler_params=PARAMS,
    )(core, half, own, other, *tiles)


def add_tiles(left, right):
    return (left.astype(jnp.float32) + right.astype(jnp.float32)).astype(jnp.bfloat16)


def local(tokens, gate_weight, up_weight, grad_hidden):
    own_x = lax.axis_index("x")
    core = lax.axis_index("c").astype(jnp.int32).reshape(1)
    half = lax.axis_index("h").astype(jnp.int32).reshape(1)
    features, hidden_cols = gate_weight.shape
    part = hidden_cols // 8

    def own_columns(weight, which):
        return lax.dynamic_slice(weight, (0, (which * 4 + own_x) * part), (features, part))

    weights = jnp.concatenate(
        [own_columns(weight, which) for which in (0, 1) for weight in (gate_weight, up_weight)], 1
    )

    piece = lax.ppermute(tokens, ("r", "y", "c", "h"), token_pairs())
    piece, grad_hidden = lax.optimization_barrier((piece, grad_hidden))
    copies = jnp.broadcast_to(piece[None], (16,) + piece.shape)
    own_tokens = lax.all_to_all(copies, ("y", "x"), split_axis=0, concat_axis=0, tiled=True)
    own_tokens = own_tokens.reshape(-1, features)
    cotangent = lax.all_to_all(
        grad_hidden.reshape(-1, 2, 4, part), "x", split_axis=2, concat_axis=0, tiled=True
    )
    own_tokens, cotangent, weights = lax.optimization_barrier((own_tokens, cotangent, weights))
    other_tokens = swap_cores(own_tokens)
    cotangent = cotangent.reshape(-1, 2 * part).T.astype(jnp.float32)

    partial = {}
    for offsets in ((7, 0), (6, 1, 5, 2, 4, 3)):
        partial.update(zip(offsets, forward_tiles(offsets, core, own_tokens, other_tokens, weights)))
    right, left = partial[7], partial[0]
    for step in range(4):
        right = ring_shift(right, 1)
        if step < 3:
            left = ring_shift(left, -1)
            right = add_tiles(right, partial[6 - step])
            if step < 2:
                left = add_tiles(left, partial[step + 1])
    total = partial[BEFORE].astype(jnp.float32) + left.astype(jnp.float32) + right.astype(jnp.float32)
    gate_pre = jnp.concatenate([total[:part], total[2 * part : 3 * part]], 0)
    up_pre = jnp.concatenate([total[part : 2 * part], total[3 * part :]], 0)

    sigmoid = jax.nn.sigmoid(gate_pre)
    silu = gate_pre * sigmoid
    hidden = (silu * up_pre).astype(jnp.bfloat16)
    grad_gate = (cotangent * up_pre * sigmoid * (1.0 + gate_pre * (1.0 - sigmoid))).astype(jnp.bfloat16)
    grad_up = (cotangent * silu).astype(jnp.bfloat16)
    grads = jnp.concatenate([grad_gate[:part], grad_up[:part], grad_gate[part:], grad_up[part:]], 0)

    tiles = {BEFORE: grads}
    right = left = grads
    for step in range(1, 5):
        left = ring_shift(left, -1)
        tiles[BEFORE + step] = left
        if step < 4:
            right = ring_shift(right, 1)
            tiles[BEFORE - step] = right
    tiles = [tiles[offset] for offset in range(ROWS)]

    keep, send = token_terms(core, weights, tiles)
    terms = keep + swap_cores(send).astype(jnp.float32)
    terms = lax.all_to_all(
        terms.astype(jnp.bfloat16).reshape(16, -1, features), ("y", "x"), split_axis=0, concat_axis=0, tiled=True
    )
    grad_tokens = jnp.sum(terms.astype(jnp.float32), 0).astype(jnp.bfloat16)
    grad_tokens = lax.ppermute(grad_tokens, ("r", "y", "c", "h"), result_pairs())

    keep, send = weight_grads(core, half, own_tokens, other_tokens, tiles)
    send, hidden = lax.optimization_barrier((send, hidden))
    hidden = lax.all_to_all(
        hidden.T.reshape(-1, 2, 1, part), "x", split_axis=0, concat_axis=2, tiled=True
    ).reshape(-1, hidden_cols)
    grad_weights = keep + lax.ppermute(send, "h", [(0, 1), (1, 0)]).astype(jnp.float32)
    return hidden, grad_tokens, grad_weights[:part].T, grad_weights[part:].T


def solution(mesh):
    fine = Mesh(mesh.devices.reshape(8, 4, 2, 2, 4), ("r", "y", "c", "h", "x"))
    return jax.shard_map(
        local,
        mesh=fine,
        in_specs=(
            P(("r", "h", "x"), ("y", "c")),
            P("r", ("y", "c")),
            P("r", ("y", "c")),
            P(("r", "h", "x"), ("y", "c")),
        ),
        out_specs=(
            P(("r", "h", "x"), ("y", "c")),
            P(("y", "c", "h", "x"), "r"),
            P("r", ("y", "c", "h", "x")),
            P("r", ("y", "c", "h", "x")),
        ),
        check_vma=False,
    )
```

time: 269 us -> 205 us (0.76)
  the two profiles are of different devices: /device:TPU:16 before, /device:TPU:128 now
where the time goes in v3:
time: 205 us; the launch traced here: 203 us
  waiting for transfers between devices  95.1 us (46%)
  starting transfers between devices  72.1 us (35%)
  local copies, waits for them, and re-layouts  13.8 us (7%)
  blocking collectives  10.1 us (5%)
  Pallas kernels  6.36 us (3%)
  other arithmetic  4.88 us (2%)
    ppermute x14, starting transfers between devices, ring_shift(): return lax.ppermute(value, ('r', 'h'), pairs)  43.2 us
    ppermute x14, waiting for transfers between devices, ring_shift(): return lax.ppermute(value, ('r', 'h'), pairs)  29.8 us
    ppermute x1, waiting for transfers between devices, local(): lax.ppermute(send, 'h', [(0, 1), (1, 0)]).astype(jnp.float32)  28.2 us
    ppermute x1, waiting for transfers between devices, local(): lax.ppermute(grad_tokens, ('r', 'y', 'c', 'h'), result_pairs())  13.1 us
    ppermute x1, starting transfers between devices, local(): lax.ppermute(send, 'h', [(0, 1), (1, 0)]).astype(jnp.float32)  10.1 us
    all_to_all x1, blocking collectives, local(): lax.all_to_all(grad_hidden.reshape(-1, 2, 4, part), 'x', split_axis=2, co...  10.1 us
    all_to_all x1, waiting for transfers between devices, local(): lax.all_to_all(copies, ('y', 'x'), split_axis=0, concat_axis=0, tiled=True)  9.11 us
    ppermute x1, waiting for transfers between devices, local(): piece = lax.ppermute(tokens, ('r', 'y', 'c', 'h'), token_pairs())  8.98 us
  transfers between devices with their start and end apart: 22, of which 17 were waited for; matrix products, arithmetic and copies ran while one was open for 5% of the time, Pallas kernels for 1%

profile of v3, /device:TPU:128, one launch (start us, length us, event | category | flops | bytes accessed | tf_op | source)
XLA Modules:
  0.0 203.4 jit_solution(11740316168170957040)
XLA Ops:
  0.6 2.5 %collective-permute-start = (bf16[32,512]{1,0:T(8,128)(2,1)}, bf16[32,512]{1,0:T(8,128)(2,1)S(1)}, u32[]{:S(2)}, u32[]{:S(2)}) collective-permute-start(bf16[32,512]{1,0:T(8,128)(2,1)} %param.4), channel_id=1, source_target_pairs={{324,0},{388,16},{452,32},{0,48},{64,8},{128,24},{192,40},{256,56}... | collective-permute-start | bytes 98312 | tf_op jit(solution)/shard_map/ppermute | solution.py:168
  3.2 9.0 %collective-permute-done = bf16[32,512]{1,0:T(8,128)(2,1)S(1)} collective-permute-done((bf16[32,512]{1,0:T(8,128)(2,1)}, bf16[32,512]{1,0:T(8,128)(2,1)S(1)}, u32[]{:S(2)}, u32[]{:S(2)}) %collective-permute-start) | collective-permute-done | bytes 32800 | tf_op jit(solution)/shard_map/ppermute | solution.py:168
  12.2 1.1 reshape.37
  13.3 10.1 %all_to_all.43 = bf16[32,2,4,224]{3,0,1,2:T(8,128)(2,1)S(1)} all-to-all(bf16[32,2,4,224]{3,0,1,2:T(8,128)(2,1)S(1)} %copy.22), channel_id=1, replica_groups=mesh['r'=8,'y'=4,'c'=2,'h'=2,'x'=4] {'x'}, dimensions={2} | all-to-all | bytes 229376 | tf_op jit(solution)/shard_map/all_to_all | solution.py:173
  23.4 0.8 broadcast_in_dim.2
  24.2 3.6 %all-to-all-start = ((bf16[16,32,512]{2,1,0:T(8,128)(2,1)}), bf16[16,32,512]{2,1,0:T(8,128)(2,1)S(1)}, u32[]{:S(2)}, u32[]{:S(2)}) async-start(bf16[16,32,512]{2,1,0:T(8,128)(2,1)} %broadcast_in_dim.2), calls=%async_computation | async-start | bytes 1048576 | tf_op jit(solution)/shard_map/all_to_all | solution.py:171
  27.8 1.8 constant_dynamic-slice_fusion.2
  29.6 0.4 pad_maximum_fusion.weights_ref
  30.1 9.1 %all-to-all-done = bf16[16,32,512]{2,1,0:T(8,128)(2,1)S(1)} async-done(((bf16[16,32,512]{2,1,0:T(8,128)(2,1)}), bf16[16,32,512]{2,1,0:T(8,128)(2,1)S(1)}, u32[]{:S(2)}, u32[]{:S(2)}) %all-to-all-start) | async-done | bytes 524320 | tf_op jit(solution)/shard_map/all_to_all | solution.py:171
  39.2 1.9 collective-permute-start.1
  41.1 1.9 collective-permute-done.1.other_ref
  43.0 0.6 shard_map.76
  43.6 2.2 %collective-permute-start.5 = (bf16[896,128]{1,0:T(8,128)(2,1)S(1)}, bf16[896,128]{1,0:T(8,128)(2,1)S(1)}, u32[]{:S(2)}, u32[]{:S(2)}) collective-permute-start(bf16[896,128]{1,0:T(8,128)(2,1)S(1)} %get-tuple-element.32), channel_id=1, source_target_pairs={{0,64},{64,128},{128,192},{192,256},{256,320},{320,384},{384,448},... | collective-permute-start | bytes 688136 | tf_op jit(solution)/shard_map/ppermute | solution.py:22
  45.7 4.9 %collective-permute-start.2 = (bf16[896,128]{1,0:T(8,128)(2,1)S(1)}, bf16[896,128]{1,0:T(8,128)(2,1)S(1)}, u32[]{:S(2)}, u32[]{:S(2)}) collective-permute-start(bf16[896,128]{1,0:T(8,128)(2,1)S(1)} %get-tuple-element.29), channel_id=1, source_target_pairs={{0,452},{64,0},{128,64},{192,128},{256,192},{320,256},{384,320},{4... | collective-permute-start | bytes 688136 | tf_op jit(solution)/shard_map/ppermute | solution.py:22
  50.6 1.1 shard_map.75
  51.7 2.6 %collective-permute-done.5 = bf16[896,128]{1,0:T(8,128)(2,1)S(1)} collective-permute-done((bf16[896,128]{1,0:T(8,128)(2,1)S(1)}, bf16[896,128]{1,0:T(8,128)(2,1)S(1)}, u32[]{:S(2)}, u32[]{:S(2)}) %collective-permute-start.5) | collective-permute-done | bytes 229408 | tf_op jit(solution)/shard_map/ppermute | solution.py:22
  54.4 1.9 collective-permute-start.6
  56.3 0.3 collective-permute-done.2
  56.7 4.9 %collective-permute-start.3 = (bf16[896,128]{1,0:T(8,128)(2,1)S(1)}, bf16[896,128]{1,0:T(8,128)(2,1)S(1)}, u32[]{:S(2)}, u32[]{:S(2)}) collective-permute-start(bf16[896,128]{1,0:T(8,128)(2,1)S(1)} %add_convert_fusion.5), channel_id=1, source_target_pairs={{0,452},{64,0},{128,64},{192,128},{256,192},{320,256},{384,320},{4... | collective-permute-start | bytes 688136 | tf_op jit(solution)/shard_map/ppermute | solution.py:22
  61.5 2.8 %collective-permute-done.6 = bf16[896,128]{1,0:T(8,128)(2,1)S(1)} collective-permute-done((bf16[896,128]{1,0:T(8,128)(2,1)S(1)}, bf16[896,128]{1,0:T(8,128)(2,1)S(1)}, u32[]{:S(2)}, u32[]{:S(2)}) %collective-permute-start.6) | collective-permute-done | bytes 229408 | tf_op jit(solution)/shard_map/ppermute | solution.py:22
  64.4 1.9 collective-permute-start.7
  66.4 5.1 %collective-permute-start.4 = (bf16[896,128]{1,0:T(8,128)(2,1)S(1)}, bf16[896,128]{1,0:T(8,128)(2,1)S(1)}, u32[]{:S(2)}, u32[]{:S(2)}) collective-permute-start(bf16[896,128]{1,0:T(8,128)(2,1)S(1)} %add_convert_fusion.4), channel_id=1, source_target_pairs={{0,452},{64,0},{128,64},{192,128},{256,192},{320,256},{384,320},{4... | collective-permute-start | bytes 688136 | tf_op jit(solution)/shard_map/ppermute | solution.py:22
  71.5 2.0 collective-permute-done.7
  73.5 1.9 collective-permute-start.8
  75.5 0.1 copy.24
  75.7 7.0 %collective-permute-done.8 = bf16[896,128]{1,0:T(8,128)(2,1)S(1)} collective-permute-done((bf16[896,128]{1,0:T(8,128)(2,1)S(1)}, bf16[896,128]{1,0:T(8,128)(2,1)S(1)}, u32[]{:S(2)}, u32[]{:S(2)}) %collective-permute-start.8) | collective-permute-done | bytes 229408 | tf_op jit(solution)/shard_map/ppermute | solution.py:22
  82.7 0.1 convert_add_fusion.1
  82.8 0.8 multiply_convert_fusion
  83.7 1.9 collective-permute-start.12
  85.6 3.9 %collective-permute-start.9 = (bf16[896,128]{1,0:T(8,128)(2,1)S(1)}, bf16[896,128]{1,0:T(8,128)(2,1)S(1)}, u32[]{:S(2)}, u32[]{:S(2)}) collective-permute-start(bf16[896,128]{1,0:T(8,128)(2,1)S(1)} %pad_maximum_fusion.3.refs_3_), channel_id=1, source_target_pairs={{0,64},{64,128},{128,192},{192,256},{256,320},{320,384},{384,448},... | collective-permute-start | bytes 688136 | tf_op jit(solution)/shard_map/ppermute | solution.py:22
  89.5 2.6 %collective-permute-done.12.refs_4_ = bf16[896,128]{1,0:T(8,128)(2,1)S(1)} collective-permute-done((bf16[896,128]{1,0:T(8,128)(2,1)S(1)}, bf16[896,128]{1,0:T(8,128)(2,1)S(1)}, u32[]{:S(2)}, u32[]{:S(2)}) %collective-permute-start.12) | collective-permute-done | bytes 229408 | tf_op jit(solution)/shard_map/ppermute | solution.py:22
  92.1 2.6 %collective-permute-start.13 = (bf16[896,128]{1,0:T(8,128)(2,1)S(1)}, bf16[896,128]{1,0:T(8,128)(2,1)S(1)}, u32[]{:S(2)}, u32[]{:S(2)}) collective-permute-start(bf16[896,128]{1,0:T(8,128)(2,1)S(1)} %collective-permute-done.12.refs_4_), channel_id=1, source_target_pairs={{0,452},{64,0},{128,64},{192,128},{256,192},{320,256},{384,320},{4... | collective-permute-start | bytes 688136 | tf_op jit(solution)/shard_map/ppermute | solution.py:22
  94.7 3.2 %collective-permute-start.10 = (bf16[896,128]{1,0:T(8,128)(2,1)S(1)}, bf16[896,128]{1,0:T(8,128)(2,1)S(1)}, u32[]{:S(2)}, u32[]{:S(2)}) collective-permute-start(bf16[896,128]{1,0:T(8,128)(2,1)S(1)} %collective-permute-done.9.refs_2_), channel_id=1, source_target_pairs={{0,64},{64,128},{128,192},{192,256},{256,320},{320,384},{384,448},... | collective-permute-start | bytes 688136 | tf_op jit(solution)/shard_map/ppermute | solution.py:22
  98.0 3.4 %collective-permute-done.13.refs_5_ = bf16[896,128]{1,0:T(8,128)(2,1)S(1)} collective-permute-done((bf16[896,128]{1,0:T(8,128)(2,1)S(1)}, bf16[896,128]{1,0:T(8,128)(2,1)S(1)}, u32[]{:S(2)}, u32[]{:S(2)}) %collective-permute-start.13) | collective-permute-done | bytes 229408 | tf_op jit(solution)/shard_map/ppermute | solution.py:22
  101.3 2.6 %collective-permute-start.14 = (bf16[896,128]{1,0:T(8,128)(2,1)S(1)}, bf16[896,128]{1,0:T(8,128)(2,1)S(1)}, u32[]{:S(2)}, u32[]{:S(2)}) collective-permute-start(bf16[896,128]{1,0:T(8,128)(2,1)S(1)} %collective-permute-done.13.refs_5_), channel_id=1, source_target_pairs={{0,452},{64,0},{128,64},{192,128},{256,192},{320,256},{384,320},{4... | collective-permute-start | bytes 688136 | tf_op jit(solution)/shard_map/ppermute | solution.py:22
  104.0 0.3 collective-permute-done.10.refs_1_
  104.3 3.1 %collective-permute-start.11 = (bf16[896,128]{1,0:T(8,128)(2,1)S(1)}, bf16[896,128]{1,0:T(8,128)(2,1)S(1)}, u32[]{:S(2)}, u32[]{:S(2)}) collective-permute-start(bf16[896,128]{1,0:T(8,128)(2,1)S(1)} %collective-permute-done.10.refs_1_), channel_id=1, source_target_pairs={{0,64},{64,128},{128,192},{192,256},{256,320},{320,384},{384,448},... | collective-permute-start | bytes 688136 | tf_op jit(solution)/shard_map/ppermute | solution.py:22
  107.4 4.0 %collective-permute-done.14.refs_6_ = bf16[896,128]{1,0:T(8,128)(2,1)S(1)} collective-permute-done((bf16[896,128]{1,0:T(8,128)(2,1)S(1)}, bf16[896,128]{1,0:T(8,128)(2,1)S(1)}, u32[]{:S(2)}, u32[]{:S(2)}) %collective-permute-start.14) | collective-permute-done | bytes 229408 | tf_op jit(solution)/shard_map/ppermute | solution.py:22
  111.4 3.0 %collective-permute-start.15 = (bf16[896,128]{1,0:T(8,128)(2,1)S(1)}, bf16[896,128]{1,0:T(8,128)(2,1)S(1)}, u32[]{:S(2)}, u32[]{:S(2)}) collective-permute-start(bf16[896,128]{1,0:T(8,128)(2,1)S(1)} %collective-permute-done.14.refs_6_), channel_id=1, source_target_pairs={{0,452},{64,0},{128,64},{192,128},{256,192},{320,256},{384,320},{4... | collective-permute-start | bytes 688136 | tf_op jit(solution)/shard_map/ppermute | solution.py:22
  114.4 4.9 %collective-permute-done.15.refs_7_ = bf16[896,128]{1,0:T(8,128)(2,1)S(1)} collective-permute-done((bf16[896,128]{1,0:T(8,128)(2,1)S(1)}, bf16[896,128]{1,0:T(8,128)(2,1)S(1)}, u32[]{:S(2)}, u32[]{:S(2)}) %collective-permute-start.15) | collective-permute-done | bytes 229408 | tf_op jit(solution)/shard_map/ppermute | solution.py:22
  119.3 3.1 %shard_map.78 = (f32[512,512]{1,0:T(8,128)S(1)}, bf16[512,512]{1,0:T(8,128)(2,1)}) custom-call(s32[1]{0:T(128)} %bitcast.core_ref, bf16[512,896]{1,0:T(8,128)(2,1)S(1)} %pad_maximum_fusion.weights_ref, bf16[896,128]{1,0:T(8,128)(2,1)S(1)} %collective-permute-done.11.refs_0_, bf16[896,128]{1,0:T(8,128)(2,1)S(1)} %collective-permute-done.10.refs_1_, ...), custom_call_target="tpu_custom_call" | custom-call | tf_op jit(solution)/shard_map/pallas_call | solution.py:105
  122.4 1.9 collective-permute-start.16
  124.4 0.9 copy-done.1
  125.3 0.9 copy-done.3
  126.2 0.9 copy-done.5
  127.2 0.9 copy-done.7
  128.1 0.9 copy-done.9
  129.1 0.9 copy-done.11
  130.0 1.6 shard_map.77
  131.6 10.1 %collective-permute-start.18 = (bf16[448,512]{1,0:T(8,128)(2,1)}, bf16[448,512]{1,0:T(8,128)(2,1)}, u32[]{:S(2)}, u32[]{:S(2)}) collective-permute-start(bf16[448,512]{1,0:T(8,128)(2,1)} %get-tuple-element.41), channel_id=1, source_target_pairs={{0,4},{4,0},{1,5},{5,1},{2,6},{6,2},{3,7},{7,3},{8,12},{12,8},{9,1... | collective-permute-start | bytes 1376264 | tf_op jit(solution)/shard_map/ppermute | solution.py:225
  141.7 1.7 copy.25
  143.4 3.3 %all-to-all-start.2 = ((bf16[128,2,1,224]{3,1,2,0:T(2,128)(2,1)}), bf16[128,2,1,224]{3,1,2,0:T(2,128)(2,1)S(1)}, u32[]{:S(2)}, u32[]{:S(2)}) async-start(bf16[128,2,1,224]{3,1,2,0:T(2,128)(2,1)} %copy.25), calls=%async_computation.2 | async-start | bytes 262144 | tf_op jit(solution)/shard_map/all_to_all | solution.py:222
  146.7 2.0 add_convert_fusion
  148.8 3.9 %all-to-all-done.2 = bf16[128,2,1,224]{3,1,2,0:T(2,128)(2,1)S(1)} async-done(((bf16[128,2,1,224]{3,1,2,0:T(2,128)(2,1)}), bf16[128,2,1,224]{3,1,2,0:T(2,128)(2,1)S(1)}, u32[]{:S(2)}, u32[]{:S(2)}) %all-to-all-start.2) | async-done | bytes 114720 | tf_op jit(solution)/shard_map/all_to_all | solution.py:222
  152.7 3.6 %all-to-all-start.3 = ((bf16[16,32,512]{2,1,0:T(8,128)(2,1)}), bf16[16,32,512]{2,1,0:T(8,128)(2,1)S(1)}, u32[]{:S(2)}, u32[]{:S(2)}) async-start(bf16[16,32,512]{2,1,0:T(8,128)(2,1)} %bitcast.13), calls=%async_computation.3 | async-start | bytes 1048576 | tf_op jit(solution)/shard_map/all_to_all | solution.py:214
  156.3 0.1 copy.27
  156.4 0.8 reshape.39
  157.2 28.2 %collective-permute-done.18 = bf16[448,512]{1,0:T(8,128)(2,1)} collective-permute-done((bf16[448,512]{1,0:T(8,128)(2,1)}, bf16[448,512]{1,0:T(8,128)(2,1)}, u32[]{:S(2)}, u32[]{:S(2)}) %collective-permute-start.18) | collective-permute-done | bytes 458784 | tf_op jit(solution)/shard_map/ppermute | solution.py:225
  185.4 1.2 convert_add_fusion
  186.6 0.1 reduce_sum.12
  186.7 1.9 collective-permute-start.17
  188.6 1.0 slice_bitcast_fusion
  189.6 13.1 %collective-permute-done.17 = bf16[32,512]{1,0:T(8,128)(2,1)S(1)} collective-permute-done((bf16[32,512]{1,0:T(8,128)(2,1)S(1)}, bf16[32,512]{1,0:T(8,128)(2,1)S(1)}, u32[]{:S(2)}, u32[]{:S(2)}) %collective-permute-start.17) | collective-permute-done | bytes 32800 | tf_op jit(solution)/shard_map/ppermute | solution.py:218
  202.7 0.6 copy.29
  (36 shorter events, 0.6 us)
Async XLA Ops:
  0.6 11.5 %collective-permute-start = (bf16[32,512]{1,0:T(8,128)(2,1)}, bf16[32,512]{1,0:T(8,128)(2,1)S(1)}, u32[]{:S(2)}, u32[]{:S(2)}) collective-permute-start(bf16[32,512]{1,0:T(8,128)(2,1)} %param.4), channel_id=1, source_target_pairs={{324,0},{388,16},{452,32},{0,48},{64,8},{128,24},{192,40},{256,56}... | collective-permute-start | bytes 98312 | tf_op jit(solution)/shard_map/ppermute | solution.py:168
  24.2 15.0 %all-to-all-start = ((bf16[16,32,512]{2,1,0:T(8,128)(2,1)}), bf16[16,32,512]{2,1,0:T(8,128)(2,1)S(1)}, u32[]{:S(2)}, u32[]{:S(2)}) async-start(bf16[16,32,512]{2,1,0:T(8,128)(2,1)} %broadcast_in_dim.2), calls=%async_computation | async-start | bytes 1048576 | tf_op jit(solution)/shard_map/all_to_all | solution.py:171
  39.2 3.8 %collective-permute-start.1 = (bf16[512,512]{1,0:T(8,128)(2,1)S(1)}, bf16[512,512]{1,0:T(8,128)(2,1)S(1)}, u32[]{:S(2)}, u32[]{:S(2)}) collective-permute-start(bf16[512,512]{1,0:T(8,128)(2,1)S(1)} %bitcast.33), channel_id=1, source_target_pairs={{0,8},{8,0},{1,9},{9,1},{2,10},{10,2},{3,11},{11,3},{4,12},{12,4},... | collective-permute-start | bytes 1572872 | tf_op jit(solution)/shard_map/ppermute | solution.py:61
  43.6 10.7 %collective-permute-start.5 = (bf16[896,128]{1,0:T(8,128)(2,1)S(1)}, bf16[896,128]{1,0:T(8,128)(2,1)S(1)}, u32[]{:S(2)}, u32[]{:S(2)}) collective-permute-start(bf16[896,128]{1,0:T(8,128)(2,1)S(1)} %get-tuple-element.32), channel_id=1, source_target_pairs={{0,64},{64,128},{128,192},{192,256},{256,320},{320,384},{384,448},... | collective-permute-start | bytes 688136 | tf_op jit(solution)/shard_map/ppermute | solution.py:22
  45.7 10.9 %collective-permute-start.2 = (bf16[896,128]{1,0:T(8,128)(2,1)S(1)}, bf16[896,128]{1,0:T(8,128)(2,1)S(1)}, u32[]{:S(2)}, u32[]{:S(2)}) collective-permute-start(bf16[896,128]{1,0:T(8,128)(2,1)S(1)} %get-tuple-element.29), channel_id=1, source_target_pairs={{0,452},{64,0},{128,64},{192,128},{256,192},{320,256},{384,320},{4... | collective-permute-start | bytes 688136 | tf_op jit(solution)/shard_map/ppermute | solution.py:22
  54.4 9.9 %collective-permute-start.6 = (bf16[896,128]{1,0:T(8,128)(2,1)S(1)}, bf16[896,128]{1,0:T(8,128)(2,1)S(1)}, u32[]{:S(2)}, u32[]{:S(2)}) collective-permute-start(bf16[896,128]{1,0:T(8,128)(2,1)S(1)} %add_convert_fusion.3), channel_id=1, source_target_pairs={{0,64},{64,128},{128,192},{192,256},{256,320},{320,384},{384,448},... | collective-permute-start | bytes 688136 | tf_op jit(solution)/shard_map/ppermute | solution.py:22
  56.7 9.6 %collective-permute-start.3 = (bf16[896,128]{1,0:T(8,128)(2,1)S(1)}, bf16[896,128]{1,0:T(8,128)(2,1)S(1)}, u32[]{:S(2)}, u32[]{:S(2)}) collective-permute-start(bf16[896,128]{1,0:T(8,128)(2,1)S(1)} %add_convert_fusion.5), channel_id=1, source_target_pairs={{0,452},{64,0},{128,64},{192,128},{256,192},{320,256},{384,320},{4... | collective-permute-start | bytes 688136 | tf_op jit(solution)/shard_map/ppermute | solution.py:22
  64.4 9.1 %collective-permute-start.7 = (bf16[896,128]{1,0:T(8,128)(2,1)S(1)}, bf16[896,128]{1,0:T(8,128)(2,1)S(1)}, u32[]{:S(2)}, u32[]{:S(2)}) collective-permute-start(bf16[896,128]{1,0:T(8,128)(2,1)S(1)} %add_convert_fusion.2), channel_id=1, source_target_pairs={{0,64},{64,128},{128,192},{192,256},{256,320},{320,384},{384,448},... | collective-permute-start | bytes 688136 | tf_op jit(solution)/shard_map/ppermute | solution.py:22
  66.4 9.3 %collective-permute-start.4 = (bf16[896,128]{1,0:T(8,128)(2,1)S(1)}, bf16[896,128]{1,0:T(8,128)(2,1)S(1)}, u32[]{:S(2)}, u32[]{:S(2)}) collective-permute-start(bf16[896,128]{1,0:T(8,128)(2,1)S(1)} %add_convert_fusion.4), channel_id=1, source_target_pairs={{0,452},{64,0},{128,64},{192,128},{256,192},{320,256},{384,320},{4... | collective-permute-start | bytes 688136 | tf_op jit(solution)/shard_map/ppermute | solution.py:22
  73.5 9.1 %collective-permute-start.8 = (bf16[896,128]{1,0:T(8,128)(2,1)S(1)}, bf16[896,128]{1,0:T(8,128)(2,1)S(1)}, u32[]{:S(2)}, u32[]{:S(2)}) collective-permute-start(bf16[896,128]{1,0:T(8,128)(2,1)S(1)} %add_convert_fusion.1), channel_id=1, source_target_pairs={{0,64},{64,128},{128,192},{192,256},{256,320},{320,384},{384,448},... | collective-permute-start | bytes 688136 | tf_op jit(solution)/shard_map/ppermute | solution.py:22
  83.7 8.4 %collective-permute-start.12 = (bf16[896,128]{1,0:T(8,128)(2,1)S(1)}, bf16[896,128]{1,0:T(8,128)(2,1)S(1)}, u32[]{:S(2)}, u32[]{:S(2)}) collective-permute-start(bf16[896,128]{1,0:T(8,128)(2,1)S(1)} %pad_maximum_fusion.3.refs_3_), channel_id=1, source_target_pairs={{0,452},{64,0},{128,64},{192,128},{256,192},{320,256},{384,320},{4... | collective-permute-start | bytes 688136 | tf_op jit(solution)/shard_map/ppermute | solution.py:22
  85.6 9.1 %collective-permute-start.9 = (bf16[896,128]{1,0:T(8,128)(2,1)S(1)}, bf16[896,128]{1,0:T(8,128)(2,1)S(1)}, u32[]{:S(2)}, u32[]{:S(2)}) collective-permute-start(bf16[896,128]{1,0:T(8,128)(2,1)S(1)} %pad_maximum_fusion.3.refs_3_), channel_id=1, source_target_pairs={{0,64},{64,128},{128,192},{192,256},{256,320},{320,384},{384,448},... | collective-permute-start | bytes 688136 | tf_op jit(solution)/shard_map/ppermute | solution.py:22
  92.1 9.2 %collective-permute-start.13 = (bf16[896,128]{1,0:T(8,128)(2,1)S(1)}, bf16[896,128]{1,0:T(8,128)(2,1)S(1)}, u32[]{:S(2)}, u32[]{:S(2)}) collective-permute-start(bf16[896,128]{1,0:T(8,128)(2,1)S(1)} %collective-permute-done.12.refs_4_), channel_id=1, source_target_pairs={{0,452},{64,0},{128,64},{192,128},{256,192},{320,256},{384,320},{4... | collective-permute-start | bytes 688136 | tf_op jit(solution)/shard_map/ppermute | solution.py:22
  94.7 27.7 %copy-start = (bf16[896,128]{1,0:T(8,128)(2,1)}, bf16[896,128]{1,0:T(8,128)(2,1)S(1)}, u32[]{:S(2)}) copy-start(bf16[896,128]{1,0:T(8,128)(2,1)S(1)} %collective-permute-done.9.refs_2_) | copy-start | bytes 688132
  94.7 9.6 %collective-permute-start.10 = (bf16[896,128]{1,0:T(8,128)(2,1)S(1)}, bf16[896,128]{1,0:T(8,128)(2,1)S(1)}, u32[]{:S(2)}, u32[]{:S(2)}) collective-permute-start(bf16[896,128]{1,0:T(8,128)(2,1)S(1)} %collective-permute-done.9.refs_2_), channel_id=1, source_target_pairs={{0,64},{64,128},{128,192},{192,256},{256,320},{320,384},{384,448},... | collective-permute-start | bytes 688136 | tf_op jit(solution)/shard_map/ppermute | solution.py:22
  101.3 21.1 %copy-start.2 = (bf16[896,128]{1,0:T(8,128)(2,1)}, bf16[896,128]{1,0:T(8,128)(2,1)S(1)}, u32[]{:S(2)}) copy-start(bf16[896,128]{1,0:T(8,128)(2,1)S(1)} %collective-permute-done.13.refs_5_) | copy-start | bytes 688132
  101.3 10.1 %collective-permute-start.14 = (bf16[896,128]{1,0:T(8,128)(2,1)S(1)}, bf16[896,128]{1,0:T(8,128)(2,1)S(1)}, u32[]{:S(2)}, u32[]{:S(2)}) collective-permute-start(bf16[896,128]{1,0:T(8,128)(2,1)S(1)} %collective-permute-done.13.refs_5_), channel_id=1, source_target_pairs={{0,452},{64,0},{128,64},{192,128},{256,192},{320,256},{384,320},{4... | collective-permute-start | bytes 688136 | tf_op jit(solution)/shard_map/ppermute | solution.py:22
  104.3 18.1 %copy-start.4 = (bf16[896,128]{1,0:T(8,128)(2,1)}, bf16[896,128]{1,0:T(8,128)(2,1)S(1)}, u32[]{:S(2)}) copy-start(bf16[896,128]{1,0:T(8,128)(2,1)S(1)} %collective-permute-done.10.refs_1_) | copy-start | bytes 688132
  104.3 10.1 %collective-permute-start.11 = (bf16[896,128]{1,0:T(8,128)(2,1)S(1)}, bf16[896,128]{1,0:T(8,128)(2,1)S(1)}, u32[]{:S(2)}, u32[]{:S(2)}) collective-permute-start(bf16[896,128]{1,0:T(8,128)(2,1)S(1)} %collective-permute-done.10.refs_1_), channel_id=1, source_target_pairs={{0,64},{64,128},{128,192},{192,256},{256,320},{320,384},{384,448},... | collective-permute-start | bytes 688136 | tf_op jit(solution)/shard_map/ppermute | solution.py:22
  111.4 11.0 %copy-start.6 = (bf16[896,128]{1,0:T(8,128)(2,1)}, bf16[896,128]{1,0:T(8,128)(2,1)S(1)}, u32[]{:S(2)}) copy-start(bf16[896,128]{1,0:T(8,128)(2,1)S(1)} %collective-permute-done.14.refs_6_) | copy-start | bytes 688132
  111.4 7.9 %collective-permute-start.15 = (bf16[896,128]{1,0:T(8,128)(2,1)S(1)}, bf16[896,128]{1,0:T(8,128)(2,1)S(1)}, u32[]{:S(2)}, u32[]{:S(2)}) collective-permute-start(bf16[896,128]{1,0:T(8,128)(2,1)S(1)} %collective-permute-done.14.refs_6_), channel_id=1, source_target_pairs={{0,452},{64,0},{128,64},{192,128},{256,192},{320,256},{384,320},{4... | collective-permute-start | bytes 688136 | tf_op jit(solution)/shard_map/ppermute | solution.py:22
  114.4 8.0 %copy-start.8 = (bf16[896,128]{1,0:T(8,128)(2,1)}, bf16[896,128]{1,0:T(8,128)(2,1)S(1)}, u32[]{:S(2)}) copy-start(bf16[896,128]{1,0:T(8,128)(2,1)S(1)} %collective-permute-done.11.refs_0_) | copy-start | bytes 688132
  119.3 3.1 %copy-start.10 = (bf16[896,128]{1,0:T(8,128)(2,1)}, bf16[896,128]{1,0:T(8,128)(2,1)S(1)}, u32[]{:S(2)}) copy-start(bf16[896,128]{1,0:T(8,128)(2,1)S(1)} %collective-permute-done.15.refs_7_) | copy-start | bytes 688132
  122.4 24.3 %collective-permute-start.16 = (bf16[512,512]{1,0:T(8,128)(2,1)}, bf16[512,512]{1,0:T(8,128)(2,1)}, u32[]{:S(2)}, u32[]{:S(2)}) collective-permute-start(bf16[512,512]{1,0:T(8,128)(2,1)} %get-tuple-element.39), channel_id=1, source_target_pairs={{0,8},{8,0},{1,9},{9,1},{2,10},{10,2},{3,11},{11,3},{4,12},{12,4},... | collective-permute-start | bytes 1572872 | tf_op jit(solution)/shard_map/ppermute | solution.py:61
  124.4 0.9 copy-start.1
  125.3 0.9 copy-start.3
  126.2 0.9 copy-start.5
  127.2 0.9 copy-start.7
  128.1 0.9 copy-start.9
  129.1 0.9 copy-start.11
  131.6 53.8 %collective-permute-start.18 = (bf16[448,512]{1,0:T(8,128)(2,1)}, bf16[448,512]{1,0:T(8,128)(2,1)}, u32[]{:S(2)}, u32[]{:S(2)}) collective-permute-start(bf16[448,512]{1,0:T(8,128)(2,1)} %get-tuple-element.41), channel_id=1, source_target_pairs={{0,4},{4,0},{1,5},{5,1},{2,6},{6,2},{3,7},{7,3},{8,12},{12,8},{9,1... | collective-permute-start | bytes 1376264 | tf_op jit(solution)/shard_map/ppermute | solution.py:225
  143.4 9.3 %all-to-all-start.2 = ((bf16[128,2,1,224]{3,1,2,0:T(2,128)(2,1)}), bf16[128,2,1,224]{3,1,2,0:T(2,128)(2,1)S(1)}, u32[]{:S(2)}, u32[]{:S(2)}) async-start(bf16[128,2,1,224]{3,1,2,0:T(2,128)(2,1)} %copy.25), calls=%async_computation.2 | async-start | bytes 262144 | tf_op jit(solution)/shard_map/all_to_all | solution.py:222
  152.7 33.9 %all-to-all-start.3 = ((bf16[16,32,512]{2,1,0:T(8,128)(2,1)}), bf16[16,32,512]{2,1,0:T(8,128)(2,1)S(1)}, u32[]{:S(2)}, u32[]{:S(2)}) async-start(bf16[16,32,512]{2,1,0:T(8,128)(2,1)} %bitcast.13), calls=%async_computation.3 | async-start | bytes 1048576 | tf_op jit(solution)/shard_map/all_to_all | solution.py:214
  186.7 16.1 %collective-permute-start.17 = (bf16[32,512]{1,0:T(8,128)(2,1)S(1)}, bf16[32,512]{1,0:T(8,128)(2,1)S(1)}, u32[]{:S(2)}, u32[]{:S(2)}) collective-permute-start(bf16[32,512]{1,0:T(8,128)(2,1)S(1)} %reduce_sum.12), channel_id=1, source_target_pairs={{0,44},{16,52},{32,60},{48,0},{8,8},{24,16},{40,24},{56,32},{64,11... | collective-permute-start | bytes 98312 | tf_op jit(solution)/shard_map/ppermute | solution.py:218

commit v4 on v3

--- a/solution.py
+++ b/solution.py
@@ -87,68 +87,82 @@
     )(core, own, other, weights)
 
 
-def terms_kernel(core_ref, weights_ref, *refs):
-    tile_refs = refs[:ROWS]
-    keep_ref, send_ref, all_ref = refs[ROWS:]
+def near_kernel(core_ref, own_ref, other_ref, weights_ref, *refs):
+    tile_refs = refs[:5]
+    terms_ref, sums_ref, tokens_ref, wide_ref = refs[5:]
+    join_cores(core_ref[0], own_ref, other_ref, tokens_ref)
     for at, tile_ref in enumerate(tile_refs):
+        wide_ref[:, at * 128 : (at + 1) * 128] = tile_ref[...]
         product = dot_f32(weights_ref[...], tile_ref[...])
-        all_ref[at * 128 : (at + 1) * 128, :] = product.T
-    rows = keep_ref.shape[0]
-    core = core_ref[0]
-    keep_ref[...] = all_ref[pl.ds(pl.multiple_of(core * rows, rows), rows), :]
-    send = all_ref[pl.ds(pl.multiple_of((1 - core) * rows, rows), rows), :]
-    send_ref[...] = send.astype(jnp.bfloat16)
-
-
-def token_terms(core, weights, tiles):
-    shape = (ROWS * 64, weights.shape[0])
+        terms_ref[at * 128 : (at + 1) * 128, :] = product.T.astype(jnp.bfloat16)
+    sums_ref[...] = dot_f32(wide_ref[...], tokens_ref[128:768, :])
+
+
+def near_products(core, own, other, weights, tiles):
+    features, cols = weights.shape
     return pl.pallas_call(
-        terms_kernel,
-        in_specs=[SMEM_SPEC] + [VMEM_SPEC] * (1 + ROWS),
-        out_specs=[VMEM_SPEC] * 2,
-        out_shape=[jax.ShapeDtypeStruct(shape, jnp.float32), jax.ShapeDtypeStruct(shape, jnp.bfloat16)],
-        scratch_shapes=[pltpu.VMEM((ROWS * 128, shape[1]), jnp.float32)],
-        compiler_params=PARAMS,
-    )(core, weights, *tiles)
-
-
-def weight_grad_kernel(core_ref, half_ref, own_ref, other_ref, *refs):
-    tile_refs = refs[:ROWS]
-    keep_ref, send_ref, tokens_ref, wide_ref = refs[ROWS:]
-    join_cores(core_ref[0], own_ref, other_ref, tokens_ref)
-    rows = wide_ref.shape[0]
-
-    def product(half):
-        first = pl.multiple_of(half * rows, 16)
-        for at, tile_ref in enumerate(tile_refs):
-            wide_ref[:, at * 128 : (at + 1) * 128] = tile_ref[pl.ds(first, rows), :]
-        return dot_f32(wide_ref[...], tokens_ref[...])
-
-    send_ref[...] = product(1 - half_ref[0]).astype(jnp.bfloat16)
-    keep_ref[...] = product(half_ref[0])
-
-
-def weight_grads(core, half, own, other, tiles):
-    rows = tiles[0].shape[0] // 2
-    features = own.shape[1]
-    return pl.pallas_call(
-        weight_grad_kernel,
-        in_specs=[SMEM_SPEC] * 2 + [VMEM_SPEC] * (2 + ROWS),
+        near_kernel,
+        in_specs=[SMEM_SPEC] + [VMEM_SPEC] * 8,
         out_specs=[VMEM_SPEC] * 2,
         out_shape=[
-            jax.ShapeDtypeStruct((rows, features), jnp.float32),
-            jax.ShapeDtypeStruct((rows, features), jnp.bfloat16),
+            jax.ShapeDtypeStruct((5 * 128, features), jnp.bfloat16),
+            jax.ShapeDtypeStruct((cols, features), jnp.float32),
         ],
         scratch_shapes=[
             pltpu.VMEM((ROWS * 128, features), jnp.bfloat16),
-            pltpu.VMEM((rows, ROWS * 128), jnp.bfloat16),
+            pltpu.VMEM((cols, 5 * 128), jnp.bfloat16),
         ],
         compiler_params=PARAMS,
-    )(core, half, own, other, *tiles)
-
-
-def add_tiles(left, right):
-    return (left.astype(jnp.float32) + right.astype(jnp.float32)).astype(jnp.bfloat16)
+    )(core, own, other, weights, *tiles)
+
+
+def last_kernel(core_ref, half_ref, own_ref, other_ref, weights_ref, terms_ref, sums_ref, *refs):
+    tile_refs = refs[:3]
+    keep_terms_ref, send_terms_ref, keep_ref, send_ref = refs[3:7]
+    tokens_ref, wide_ref, all_terms_ref, all_sums_ref = refs[7:]
+    core = core_ref[0]
+    half = half_ref[0]
+    join_cores(core, own_ref, other_ref, tokens_ref)
+    all_terms_ref[128:768, :] = terms_ref[...]
+    for at, (offset, tile_ref) in enumerate(zip((0, 6, 7), tile_refs)):
+        wide_ref[:, at * 128 : (at + 1) * 128] = tile_ref[...]
+        product = dot_f32(weights_ref[...], tile_ref[...])
+        all_terms_ref[offset * 128 : (offset + 1) * 128, :] = product.T.astype(jnp.bfloat16)
+    tokens_ref[640:768, :] = tokens_ref[0:128, :]
+    all_sums_ref[...] = sums_ref[...] + dot_f32(wide_ref[...], tokens_ref[640:1024, :])
+    rows = keep_terms_ref.shape[0]
+    keep_terms_ref[...] = all_terms_ref[pl.ds(pl.multiple_of(core * rows, rows), rows), :]
+    send_terms_ref[...] = all_terms_ref[pl.ds(pl.multiple_of((1 - core) * rows, rows), rows), :]
+    rows = keep_ref.shape[0]
+    keep_ref[...] = all_sums_ref[pl.ds(pl.multiple_of(half * rows, 16), rows), :]
+    send = all_sums_ref[pl.ds(pl.multiple_of((1 - half) * rows, 16), rows), :]
+    send_ref[...] = send.astype(jnp.bfloat16)
+
+
+def last_products(core, half, own, other, weights, terms, sums, tiles):
+    features, cols = weights.shape
+    return pl.pallas_call(
+        last_kernel,
+        in_specs=[SMEM_SPEC] * 2 + [VMEM_SPEC] * 8,
+        out_specs=[VMEM_SPEC] * 4,
+        out_shape=[
+            jax.ShapeDtypeStruct((ROWS * 64, features), jnp.bfloat16),
+            jax.ShapeDtypeStruct((ROWS * 64, features), jnp.bfloat16),
+            jax.ShapeDtypeStruct((cols // 2, features), jnp.float32),
+            jax.ShapeDtypeStruct((cols // 2, features), jnp.bfloat16),
+        ],
+        scratch_shapes=[
+            pltpu.VMEM((ROWS * 128, features), jnp.bfloat16),
+            pltpu.VMEM((cols, 3 * 128), jnp.bfloat16),
+            pltpu.VMEM((ROWS * 128, features), jnp.bfloat16),
+            pltpu.VMEM((cols, features), jnp.float32),
+        ],
+        compiler_params=PARAMS,
+    )(core, half, own, other, weights, terms, sums, *tiles)
+
+
+def add_tiles(*tiles):
+    return sum(tile.astype(jnp.float32) for tile in tiles).astype(jnp.bfloat16)
 
 
 def local(tokens, gate_weight, up_weight, grad_hidden):
@@ -166,28 +180,26 @@
     )
 
     piece = lax.ppermute(tokens, ("r", "y", "c", "h"), token_pairs())
-    piece, grad_hidden = lax.optimization_barrier((piece, grad_hidden))
     copies = jnp.broadcast_to(piece[None], (16,) + piece.shape)
     own_tokens = lax.all_to_all(copies, ("y", "x"), split_axis=0, concat_axis=0, tiled=True)
     own_tokens = own_tokens.reshape(-1, features)
-    cotangent = lax.all_to_all(
-        grad_hidden.reshape(-1, 2, 4, part), "x", split_axis=2, concat_axis=0, tiled=True
-    )
+    cotangent = grad_hidden.reshape(-1, 2, 4, part).transpose(2, 0, 1, 3)
     own_tokens, cotangent, weights = lax.optimization_barrier((own_tokens, cotangent, weights))
     other_tokens = swap_cores(own_tokens)
+    cotangent = lax.all_to_all(cotangent, "x", split_axis=0, concat_axis=0, tiled=True)
     cotangent = cotangent.reshape(-1, 2 * part).T.astype(jnp.float32)
 
     partial = {}
-    for offsets in ((7, 0), (6, 1, 5, 2, 4, 3)):
+    for offsets in ((6, 7, 0), (5, 1, 4, 2, 3)):
         partial.update(zip(offsets, forward_tiles(offsets, core, own_tokens, other_tokens, weights)))
-    right, left = partial[7], partial[0]
-    for step in range(4):
-        right = ring_shift(right, 1)
-        if step < 3:
-            left = ring_shift(left, -1)
-            right = add_tiles(right, partial[6 - step])
-            if step < 2:
-                left = add_tiles(left, partial[step + 1])
+    right = ring_shift(partial[6], 1)
+    left = ring_shift(partial[0], -1)
+    right = add_tiles(right, ring_shift(partial[7], 2), partial[5])
+    left = add_tiles(left, partial[1])
+    right = add_tiles(ring_shift(right, 1), partial[4])
+    left = add_tiles(ring_shift(left, -1), partial[2])
+    right = ring_shift(right, 1)
+    left = ring_shift(left, -1)
     total = partial[BEFORE].astype(jnp.float32) + left.astype(jnp.float32) + right.astype(jnp.float32)
     gate_pre = jnp.concatenate([total[:part], total[2 * part : 3 * part]], 0)
     up_pre = jnp.concatenate([total[part : 2 * part], total[3 * part :]], 0)
@@ -199,30 +211,33 @@
     grad_up = (cotangent * silu).astype(jnp.bfloat16)
     grads = jnp.concatenate([grad_gate[:part], grad_up[:part], grad_gate[part:], grad_up[part:]], 0)
 
-    tiles = {BEFORE: grads}
-    right = left = grads
-    for step in range(1, 5):
-        left = ring_shift(left, -1)
-        tiles[BEFORE + step] = left
-        if step < 4:
-            right = ring_shift(right, 1)
-            tiles[BEFORE - step] = right
-    tiles = [tiles[offset] for offset in range(ROWS)]
-
-    keep, send = token_terms(core, weights, tiles)
-    terms = keep + swap_cores(send).astype(jnp.float32)
+    left_1 = ring_shift(grads, -1)
+    right_1 = ring_shift(grads, 1)
+    left_2 = ring_shift(left_1, -1)
+    right_2 = ring_shift(right_1, 1)
+    left_3 = ring_shift(left_2, -1)
+    right_3 = ring_shift(right_2, 1)
+    left_4 = ring_shift(left_2, -2)
+    terms, sums = near_products(
+        core, own_tokens, other_tokens, weights, [right_2, right_1, grads, left_1, left_2]
+    )
+    keep_terms, send_terms, keep, send = last_products(
+        core, half, own_tokens, other_tokens, weights, terms, sums, [right_3, left_3, left_4]
+    )
+
+    terms = add_tiles(keep_terms, swap_cores(send_terms))
+    received = lax.ppermute(send, "h", [(0, 1), (1, 0)])
     terms = lax.all_to_all(
-        terms.astype(jnp.bfloat16).reshape(16, -1, features), ("y", "x"), split_axis=0, concat_axis=0, tiled=True
+        terms.reshape(16, -1, features), ("y", "x"), split_axis=0, concat_axis=0, tiled=True
     )
     grad_tokens = jnp.sum(terms.astype(jnp.float32), 0).astype(jnp.bfloat16)
+    grad_tokens, hidden = lax.optimization_barrier((grad_tokens, hidden))
     grad_tokens = lax.ppermute(grad_tokens, ("r", "y", "c", "h"), result_pairs())
-
-    keep, send = weight_grads(core, half, own_tokens, other_tokens, tiles)
-    send, hidden = lax.optimization_barrier((send, hidden))
     hidden = lax.all_to_all(
         hidden.T.reshape(-1, 2, 1, part), "x", split_axis=0, concat_axis=2, tiled=True
     ).reshape(-1, hidden_cols)
-    grad_weights = keep + lax.ppermute(send, "h", [(0, 1), (1, 0)]).astype(jnp.float32)
+    grad_tokens, hidden, keep = lax.optimization_barrier((grad_tokens, hidden, keep))
+    grad_weights = keep + received.astype(jnp.float32)
     return hidden, grad_tokens, grad_weights[:part].T, grad_weights[part:].T
 
 

time: 205 us -> 190 us (0.927)
  the two profiles are of different devices: /device:TPU:128 before, /device:TPU:73 now
where the time goes in v4:
time: 190 us; the launch traced here: 189 us
  starting transfers between devices  96.6 us (51%)
  waiting for transfers between devices  66.4 us (35%)
  blocking collectives  7.92 us (4%)
  local copies, waits for them, and re-layouts  7.48 us (4%)
  Pallas kernels  6.34 us (3%)
  other arithmetic  2.78 us (1%)
    ppermute x14, starting transfers between devices, ring_shift(): return lax.ppermute(value, ('r', 'h'), pairs)  44.9 us
    ppermute x1, waiting for transfers between devices, local(): received = lax.ppermute(send, 'h', [(0, 1), (1, 0)])  31.1 us
    ppermute x2, starting transfers between devices, swap_cores(): return lax.ppermute(value, 'c', [(0, 1), (1, 0)])  20.9 us
    ppermute x14, waiting for transfers between devices, ring_shift(): return lax.ppermute(value, ('r', 'h'), pairs)  18 us
    all_to_all x1, starting transfers between devices, local(): lax.all_to_all(copies, ('y', 'x'), split_axis=0, concat_axis=0, tiled=True)  10 us
    all_to_all x1, blocking collectives, local(): lax.all_to_all(cotangent, 'x', split_axis=0, concat_axis=0, tiled=True)  7.92 us
    all_to_all x1, waiting for transfers between devices, local(): lax.all_to_all(terms.reshape(16, -1, features), ('y', 'x'), split_axis=0,...  5.36 us
    ppermute x1, starting transfers between devices, local(): piece = lax.ppermute(tokens, ('r', 'y', 'c', 'h'), token_pairs())  5.12 us
  transfers between devices with their start and end apart: 22, of which 13 were waited for; matrix products, arithmetic and copies ran while one was open for 3% of the time, Pallas kernels for 2%

profile of v4, /device:TPU:73, one launch (start us, length us, event | category | flops | bytes accessed | tf_op | source)
XLA Modules:
  0.0 188.6 jit_solution(183699177495494760)
XLA Ops:
  0.6 5.1 %collective-permute-start = (bf16[32,512]{1,0:T(8,128)(2,1)}, bf16[32,512]{1,0:T(8,128)(2,1)S(1)}, u32[]{:S(2)}, u32[]{:S(2)}) collective-permute-start(bf16[32,512]{1,0:T(8,128)(2,1)} %param.4), channel_id=1, source_target_pairs={{324,0},{388,16},{452,32},{0,48},{64,8},{128,24},{192,40},{256,56}... | collective-permute-start | bytes 98312 | tf_op jit(solution)/shard_map/ppermute | solution.py:182
  5.8 3.3 %collective-permute-done = bf16[32,512]{1,0:T(8,128)(2,1)S(1)} collective-permute-done((bf16[32,512]{1,0:T(8,128)(2,1)}, bf16[32,512]{1,0:T(8,128)(2,1)S(1)}, u32[]{:S(2)}, u32[]{:S(2)}) %collective-permute-start) | collective-permute-done | bytes 32800 | tf_op jit(solution)/shard_map/ppermute | solution.py:182
  9.1 0.8 broadcast_in_dim.2
  9.9 10.0 %all-to-all-start = ((bf16[16,32,512]{2,1,0:T(8,128)(2,1)}), bf16[16,32,512]{2,1,0:T(8,128)(2,1)S(1)}, u32[]{:S(2)}, u32[]{:S(2)}) async-start(bf16[16,32,512]{2,1,0:T(8,128)(2,1)} %broadcast_in_dim.2), calls=%async_computation | async-start | bytes 1048576 | tf_op jit(solution)/shard_map/all_to_all | solution.py:184
  20.0 1.1 reshape.37
  21.1 0.1 copy.23
  21.2 1.8 constant_dynamic-slice_fusion.2
  23.0 0.4 pad_maximum_fusion.weights_ref
  23.4 4.7 %all-to-all-done = bf16[16,32,512]{2,1,0:T(8,128)(2,1)S(1)} async-done(((bf16[16,32,512]{2,1,0:T(8,128)(2,1)}), bf16[16,32,512]{2,1,0:T(8,128)(2,1)S(1)}, u32[]{:S(2)}, u32[]{:S(2)}) %all-to-all-start) | async-done | bytes 524320 | tf_op jit(solution)/shard_map/all_to_all | solution.py:184
  28.1 4.1 %collective-permute-start.1 = (bf16[512,512]{1,0:T(8,128)(2,1)S(1)}, bf16[512,512]{1,0:T(8,128)(2,1)S(1)}, u32[]{:S(2)}, u32[]{:S(2)}) collective-permute-start(bf16[512,512]{1,0:T(8,128)(2,1)S(1)} %bitcast.30), channel_id=1, source_target_pairs={{0,8},{8,0},{1,9},{9,1},{2,10},{10,2},{3,11},{11,3},{4,12},{12,4},... | collective-permute-start | bytes 1572872 | tf_op jit(solution)/shard_map/ppermute | solution.py:61
  32.2 1.5 collective-permute-done.1.other_ref
  33.8 0.7 shard_map.76
  34.5 3.6 %collective-permute-start.2 = (bf16[896,128]{1,0:T(8,128)(2,1)S(1)}, bf16[896,128]{1,0:T(8,128)(2,1)S(1)}, u32[]{:S(2)}, u32[]{:S(2)}) collective-permute-start(bf16[896,128]{1,0:T(8,128)(2,1)S(1)} %get-tuple-element.30), channel_id=1, source_target_pairs={{0,452},{64,0},{128,64},{192,128},{256,192},{320,256},{384,320},{4... | collective-permute-start | bytes 688136 | tf_op jit(solution)/shard_map/ppermute | solution.py:22
  38.0 1.9 %collective-permute-start.5 = (bf16[896,128]{1,0:T(8,128)(2,1)S(1)}, bf16[896,128]{1,0:T(8,128)(2,1)S(1)}, u32[]{:S(2)}, u32[]{:S(2)}) collective-permute-start(bf16[896,128]{1,0:T(8,128)(2,1)S(1)} %get-tuple-element.33), channel_id=1, source_target_pairs={{0,64},{64,128},{128,192},{192,256},{256,320},{320,384},{384,448},... | collective-permute-start | bytes 688136 | tf_op jit(solution)/shard_map/ppermute | solution.py:22
  40.0 4.1 %collective-permute-start.6 = (bf16[896,128]{1,0:T(8,128)(2,1)S(1)}, bf16[896,128]{1,0:T(8,128)(2,1)S(1)}, u32[]{:S(2)}, u32[]{:S(2)}) collective-permute-start(bf16[896,128]{1,0:T(8,128)(2,1)S(1)} %get-tuple-element.34), channel_id=1, source_target_pairs={{0,128},{64,192},{128,256},{192,320},{256,384},{320,448},{384,4},{... | collective-permute-start | bytes 688136 | tf_op jit(solution)/shard_map/ppermute | solution.py:22
  44.0 1.0 shard_map.75
  45.0 0.0 collective-permute-done.2
  45.0 0.1 add_convert_fusion.4
  45.1 2.0 %collective-permute-start.3 = (bf16[896,128]{1,0:T(8,128)(2,1)S(1)}, bf16[896,128]{1,0:T(8,128)(2,1)S(1)}, u32[]{:S(2)}, u32[]{:S(2)}) collective-permute-start(bf16[896,128]{1,0:T(8,128)(2,1)S(1)} %add_convert_fusion.4), channel_id=1, source_target_pairs={{0,452},{64,0},{128,64},{192,128},{256,192},{320,256},{384,320},{4... | collective-permute-start | bytes 688136 | tf_op jit(solution)/shard_map/ppermute | solution.py:22
  47.1 0.0 collective-permute-done.5
  47.1 9.4 %collective-permute-done.6 = bf16[896,128]{1,0:T(8,128)(2,1)S(1)} collective-permute-done((bf16[896,128]{1,0:T(8,128)(2,1)S(1)}, bf16[896,128]{1,0:T(8,128)(2,1)S(1)}, u32[]{:S(2)}, u32[]{:S(2)}) %collective-permute-start.6) | collective-permute-done | bytes 229408 | tf_op jit(solution)/shard_map/ppermute | solution.py:22
  56.5 0.1 add_convert_fusion.2
  56.6 1.9 %collective-permute-start.7 = (bf16[896,128]{1,0:T(8,128)(2,1)S(1)}, bf16[896,128]{1,0:T(8,128)(2,1)S(1)}, u32[]{:S(2)}, u32[]{:S(2)}) collective-permute-start(bf16[896,128]{1,0:T(8,128)(2,1)S(1)} %add_convert_fusion.2), channel_id=1, source_target_pairs={{0,64},{64,128},{128,192},{192,256},{256,320},{320,384},{384,448},... | collective-permute-start | bytes 688136 | tf_op jit(solution)/shard_map/ppermute | solution.py:22
  58.5 0.1 add_convert_fusion.3
  58.6 7.2 %collective-permute-start.4 = (bf16[896,128]{1,0:T(8,128)(2,1)S(1)}, bf16[896,128]{1,0:T(8,128)(2,1)S(1)}, u32[]{:S(2)}, u32[]{:S(2)}) collective-permute-start(bf16[896,128]{1,0:T(8,128)(2,1)S(1)} %add_convert_fusion.3), channel_id=1, source_target_pairs={{0,452},{64,0},{128,64},{192,128},{256,192},{320,256},{384,320},{4... | collective-permute-start | bytes 688136 | tf_op jit(solution)/shard_map/ppermute | solution.py:22
  65.8 2.4 %collective-permute-done.7 = bf16[896,128]{1,0:T(8,128)(2,1)S(1)} collective-permute-done((bf16[896,128]{1,0:T(8,128)(2,1)S(1)}, bf16[896,128]{1,0:T(8,128)(2,1)S(1)}, u32[]{:S(2)}, u32[]{:S(2)}) %collective-permute-start.7) | collective-permute-done | bytes 229408 | tf_op jit(solution)/shard_map/ppermute | solution.py:22
  68.1 0.8 add_convert_fusion.1
  68.9 1.9 %collective-permute-start.8 = (bf16[896,128]{1,0:T(8,128)(2,1)}, bf16[896,128]{1,0:T(8,128)(2,1)S(1)}, u32[]{:S(2)}, u32[]{:S(2)}) collective-permute-start(bf16[896,128]{1,0:T(8,128)(2,1)} %add_convert_fusion.1), channel_id=1, source_target_pairs={{0,64},{64,128},{128,192},{192,256},{256,320},{320,384},{384,448},... | collective-permute-start | bytes 688136 | tf_op jit(solution)/shard_map/ppermute | solution.py:22
  70.8 7.9 %all_to_all.30 = bf16[4,32,2,224]{3,2,1,0:T(2,128)(2,1)S(1)} all-to-all(bf16[4,32,2,224]{3,2,1,0:T(2,128)(2,1)S(1)} %bitcast.35), channel_id=1, replica_groups=mesh['r'=8,'y'=4,'c'=2,'h'=2,'x'=4] {'x'}, dimensions={0} | all-to-all | bytes 229376 | tf_op jit(solution)/shard_map/all_to_all | solution.py:189
  78.7 0.1 reshape.41
  78.8 0.1 copy.18
  79.0 0.1 convert_add_fusion.1
  79.1 0.2 multiply_convert_fusion
  79.3 3.4 %collective-permute-start.11 = (bf16[896,128]{1,0:T(8,128)(2,1)S(1)}, bf16[896,128]{1,0:T(8,128)(2,1)S(1)}, u32[]{:S(2)}, u32[]{:S(2)}) collective-permute-start(bf16[896,128]{1,0:T(8,128)(2,1)S(1)} %pad_maximum_fusion.3.refs_2_), channel_id=1, source_target_pairs={{0,452},{64,0},{128,64},{192,128},{256,192},{320,256},{384,320},{4... | collective-permute-start | bytes 688136 | tf_op jit(solution)/shard_map/ppermute | solution.py:22
  82.7 1.9 %collective-permute-start.9 = (bf16[896,128]{1,0:T(8,128)(2,1)S(1)}, bf16[896,128]{1,0:T(8,128)(2,1)S(1)}, u32[]{:S(2)}, u32[]{:S(2)}) collective-permute-start(bf16[896,128]{1,0:T(8,128)(2,1)S(1)} %pad_maximum_fusion.3.refs_2_), channel_id=1, source_target_pairs={{0,64},{64,128},{128,192},{192,256},{256,320},{320,384},{384,448},... | collective-permute-start | bytes 688136 | tf_op jit(solution)/shard_map/ppermute | solution.py:22
  84.6 1.5 collective-permute-done.11.refs_3_
  86.1 3.4 %collective-permute-start.12 = (bf16[896,128]{1,0:T(8,128)(2,1)S(1)}, bf16[896,128]{1,0:T(8,128)(2,1)S(1)}, u32[]{:S(2)}, u32[]{:S(2)}) collective-permute-start(bf16[896,128]{1,0:T(8,128)(2,1)S(1)} %collective-permute-done.11.refs_3_), channel_id=1, source_target_pairs={{0,452},{64,0},{128,64},{192,128},{256,192},{320,256},{384,320},{4... | collective-permute-start | bytes 688136 | tf_op jit(solution)/shard_map/ppermute | solution.py:22
  89.5 0.3 collective-permute-done.9.refs_1_
  89.8 1.9 %collective-permute-start.10 = (bf16[896,128]{1,0:T(8,128)(2,1)S(1)}, bf16[896,128]{1,0:T(8,128)(2,1)S(1)}, u32[]{:S(2)}, u32[]{:S(2)}) collective-permute-start(bf16[896,128]{1,0:T(8,128)(2,1)S(1)} %collective-permute-done.9.refs_1_), channel_id=1, source_target_pairs={{0,64},{64,128},{128,192},{192,256},{256,320},{320,384},{384,448},... | collective-permute-start | bytes 688136 | tf_op jit(solution)/shard_map/ppermute | solution.py:22
  91.7 1.5 collective-permute-done.12.refs_4_
  93.2 4.9 %collective-permute-start.15 = (bf16[896,128]{1,0:T(8,128)(2,1)S(1)}, bf16[896,128]{1,0:T(8,128)(2,1)S(1)}, u32[]{:S(2)}, u32[]{:S(2)}) collective-permute-start(bf16[896,128]{1,0:T(8,128)(2,1)S(1)} %collective-permute-done.12.refs_4_), channel_id=1, source_target_pairs={{0,388},{64,452},{128,0},{192,64},{256,128},{320,192},{384,256},{4... | collective-permute-start | bytes 688136 | tf_op jit(solution)/shard_map/ppermute | solution.py:22
  98.1 5.0 %collective-permute-start.14 = (bf16[896,128]{1,0:T(8,128)(2,1)S(1)}, bf16[896,128]{1,0:T(8,128)(2,1)}, u32[]{:S(2)}, u32[]{:S(2)}) collective-permute-start(bf16[896,128]{1,0:T(8,128)(2,1)S(1)} %collective-permute-done.12.refs_4_), channel_id=1, source_target_pairs={{0,452},{64,0},{128,64},{192,128},{256,192},{320,256},{384,320},{4... | collective-permute-start | bytes 688136 | tf_op jit(solution)/shard_map/ppermute | solution.py:22
  103.1 1.9 %collective-permute-start.13 = (bf16[896,128]{1,0:T(8,128)(2,1)S(1)}, bf16[896,128]{1,0:T(8,128)(2,1)}, u32[]{:S(2)}, u32[]{:S(2)}) collective-permute-start(bf16[896,128]{1,0:T(8,128)(2,1)S(1)} %collective-permute-done.10.refs_0_), channel_id=1, source_target_pairs={{0,64},{64,128},{128,192},{192,256},{256,320},{320,384},{384,448},... | collective-permute-start | bytes 688136 | tf_op jit(solution)/shard_map/ppermute | solution.py:22
  105.1 2.1 %shard_map.77 = (bf16[640,512]{1,0:T(8,128)(2,1)S(1)}, f32[896,512]{1,0:T(8,128)S(1)}) custom-call(s32[1]{0:T(128)} %bitcast.core_ref, bf16[512,512]{1,0:T(8,128)(2,1)S(1)} %bitcast.33, bf16[512,512]{1,0:T(8,128)(2,1)S(1)} %collective-permute-done.1.other_ref, bf16[512,896]{1,0:T(8,128)(2,1)S(1)} %pad_maximum_fusion.weights_ref, ...), custom_call_target="tpu_custom_call" | custom-call | tf_op jit(solution)/shard_map/pallas_call | solution.py:103
  107.2 3.0 %collective-permute-done.13.refs_0_ = bf16[896,128]{1,0:T(8,128)(2,1)} collective-permute-done((bf16[896,128]{1,0:T(8,128)(2,1)S(1)}, bf16[896,128]{1,0:T(8,128)(2,1)}, u32[]{:S(2)}, u32[]{:S(2)}) %collective-permute-start.13) | collective-permute-done | bytes 229408 | tf_op jit(solution)/shard_map/ppermute | solution.py:22
  110.2 2.6 %shard_map.78 = (bf16[512,512]{1,0:T(8,128)(2,1)S(1)}, bf16[512,512]{1,0:T(8,128)(2,1)S(1)}, f32[448,512]{1,0:T(8,128)S(1)}, bf16[448,512]{1,0:T(8,128)(2,1)S(1)}) custom-call(s32[1]{0:T(128)} %bitcast.core_ref, s32[1]{0:T(128)} %bitcast.1.half_ref, bf16[512,512]{1,0:T(8,128)(2,1)S(1)} %bitcast.34, bf16[512,512]{1,0:T(8,128)(2,1)S(1)} %collective-permute-done.1.other_ref, ...), custom_call_target="tpu_custom_call" | custom-call | tf_op jit(solution)/shard_map/pallas_call | solution.py:144
  112.8 0.0 copy-start
  112.8 16.8 %collective-permute-start.16 = (bf16[512,512]{1,0:T(8,128)(2,1)S(1)}, bf16[512,512]{1,0:T(8,128)(2,1)S(1)}, u32[]{:S(2)}, u32[]{:S(2)}) collective-permute-start(bf16[512,512]{1,0:T(8,128)(2,1)S(1)} %get-tuple-element.40), channel_id=1, source_target_pairs={{0,8},{8,0},{1,9},{9,1},{2,10},{10,2},{3,11},{11,3},{4,12},{12,4},... | collective-permute-start | bytes 1572872 | tf_op jit(solution)/shard_map/ppermute | solution.py:61
  129.6 1.5 collective-permute-done.16
  131.1 0.9 add_convert_fusion
  132.0 4.5 %all-to-all-start.2 = ((bf16[16,32,512]{2,1,0:T(8,128)(2,1)}), bf16[16,32,512]{2,1,0:T(8,128)(2,1)S(1)}, u32[]{:S(2)}, u32[]{:S(2)}) async-start(bf16[16,32,512]{2,1,0:T(8,128)(2,1)} %bitcast.5), calls=%async_computation.2 | async-start | bytes 1048576 | tf_op jit(solution)/shard_map/all_to_all | solution.py:230
  136.5 3.6 %collective-permute-start.18 = (bf16[448,512]{1,0:T(8,128)(2,1)}, bf16[448,512]{1,0:T(8,128)(2,1)S(1)}, u32[]{:S(2)}, u32[]{:S(2)}) collective-permute-start(bf16[448,512]{1,0:T(8,128)(2,1)} %copy-done), channel_id=1, source_target_pairs={{0,4},{4,0},{1,5},{5,1},{2,6},{6,2},{3,7},{7,3},{8,12},{12,8},{9,1... | collective-permute-start | bytes 1376264 | tf_op jit(solution)/shard_map/ppermute | solution.py:229
  140.1 5.4 %all-to-all-done.2 = bf16[16,32,512]{2,1,0:T(8,128)(2,1)S(1)} async-done(((bf16[16,32,512]{2,1,0:T(8,128)(2,1)}), bf16[16,32,512]{2,1,0:T(8,128)(2,1)S(1)}, u32[]{:S(2)}, u32[]{:S(2)}) %all-to-all-start.2) | async-done | bytes 524320 | tf_op jit(solution)/shard_map/all_to_all | solution.py:230
  145.5 0.1 reduce_sum.12
  145.6 0.8 copy.19
  146.4 3.3 %all-to-all-start.3 = ((bf16[128,2,1,224]{3,1,2,0:T(2,128)(2,1)}), bf16[128,2,1,224]{3,1,2,0:T(2,128)(2,1)S(1)}, u32[]{:S(2)}, u32[]{:S(2)}) async-start(bf16[128,2,1,224]{3,1,2,0:T(2,128)(2,1)} %copy.19), calls=%async_computation.3 | async-start | bytes 262144 | tf_op jit(solution)/shard_map/all_to_all | solution.py:236
  149.7 4.2 %collective-permute-start.17 = (bf16[32,512]{1,0:T(8,128)(2,1)S(1)}, bf16[32,512]{1,0:T(8,128)(2,1)S(1)}, u32[]{:S(2)}, u32[]{:S(2)}) collective-permute-start(bf16[32,512]{1,0:T(8,128)(2,1)S(1)} %reduce_sum.12), channel_id=1, source_target_pairs={{0,44},{16,52},{32,60},{48,0},{8,8},{24,16},{40,24},{56,32},{64,11... | collective-permute-start | bytes 98312 | tf_op jit(solution)/shard_map/ppermute | solution.py:235
  153.9 0.9 all-to-all-done.3
  154.8 0.1 copy.21
  154.9 0.8 reshape.40
  155.7 31.1 %collective-permute-done.18 = bf16[448,512]{1,0:T(8,128)(2,1)S(1)} collective-permute-done((bf16[448,512]{1,0:T(8,128)(2,1)}, bf16[448,512]{1,0:T(8,128)(2,1)S(1)}, u32[]{:S(2)}, u32[]{:S(2)}) %collective-permute-start.18) | collective-permute-done | bytes 458784 | tf_op jit(solution)/shard_map/ppermute | solution.py:229
  186.8 0.1 convert_add_fusion
  187.0 1.0 slice_bitcast_fusion
  187.9 0.6 copy.25
  (13 shorter events, 0.1 us)
Async XLA Ops:
  0.6 8.5 %collective-permute-start = (bf16[32,512]{1,0:T(8,128)(2,1)}, bf16[32,512]{1,0:T(8,128)(2,1)S(1)}, u32[]{:S(2)}, u32[]{:S(2)}) collective-permute-start(bf16[32,512]{1,0:T(8,128)(2,1)} %param.4), channel_id=1, source_target_pairs={{324,0},{388,16},{452,32},{0,48},{64,8},{128,24},{192,40},{256,56}... | collective-permute-start | bytes 98312 | tf_op jit(solution)/shard_map/ppermute | solution.py:182
  9.9 18.2 %all-to-all-start = ((bf16[16,32,512]{2,1,0:T(8,128)(2,1)}), bf16[16,32,512]{2,1,0:T(8,128)(2,1)S(1)}, u32[]{:S(2)}, u32[]{:S(2)}) async-start(bf16[16,32,512]{2,1,0:T(8,128)(2,1)} %broadcast_in_dim.2), calls=%async_computation | async-start | bytes 1048576 | tf_op jit(solution)/shard_map/all_to_all | solution.py:184
  28.1 5.6 %collective-permute-start.1 = (bf16[512,512]{1,0:T(8,128)(2,1)S(1)}, bf16[512,512]{1,0:T(8,128)(2,1)S(1)}, u32[]{:S(2)}, u32[]{:S(2)}) collective-permute-start(bf16[512,512]{1,0:T(8,128)(2,1)S(1)} %bitcast.30), channel_id=1, source_target_pairs={{0,8},{8,0},{1,9},{9,1},{2,10},{10,2},{3,11},{11,3},{4,12},{12,4},... | collective-permute-start | bytes 1572872 | tf_op jit(solution)/shard_map/ppermute | solution.py:61
  34.5 10.6 %collective-permute-start.2 = (bf16[896,128]{1,0:T(8,128)(2,1)S(1)}, bf16[896,128]{1,0:T(8,128)(2,1)S(1)}, u32[]{:S(2)}, u32[]{:S(2)}) collective-permute-start(bf16[896,128]{1,0:T(8,128)(2,1)S(1)} %get-tuple-element.30), channel_id=1, source_target_pairs={{0,452},{64,0},{128,64},{192,128},{256,192},{320,256},{384,320},{4... | collective-permute-start | bytes 688136 | tf_op jit(solution)/shard_map/ppermute | solution.py:22
  38.0 9.0 %collective-permute-start.5 = (bf16[896,128]{1,0:T(8,128)(2,1)S(1)}, bf16[896,128]{1,0:T(8,128)(2,1)S(1)}, u32[]{:S(2)}, u32[]{:S(2)}) collective-permute-start(bf16[896,128]{1,0:T(8,128)(2,1)S(1)} %get-tuple-element.33), channel_id=1, source_target_pairs={{0,64},{64,128},{128,192},{192,256},{256,320},{320,384},{384,448},... | collective-permute-start | bytes 688136 | tf_op jit(solution)/shard_map/ppermute | solution.py:22
  40.0 16.5 %collective-permute-start.6 = (bf16[896,128]{1,0:T(8,128)(2,1)S(1)}, bf16[896,128]{1,0:T(8,128)(2,1)S(1)}, u32[]{:S(2)}, u32[]{:S(2)}) collective-permute-start(bf16[896,128]{1,0:T(8,128)(2,1)S(1)} %get-tuple-element.34), channel_id=1, source_target_pairs={{0,128},{64,192},{128,256},{192,320},{256,384},{320,448},{384,4},{... | collective-permute-start | bytes 688136 | tf_op jit(solution)/shard_map/ppermute | solution.py:22
  45.1 13.4 %collective-permute-start.3 = (bf16[896,128]{1,0:T(8,128)(2,1)S(1)}, bf16[896,128]{1,0:T(8,128)(2,1)S(1)}, u32[]{:S(2)}, u32[]{:S(2)}) collective-permute-start(bf16[896,128]{1,0:T(8,128)(2,1)S(1)} %add_convert_fusion.4), channel_id=1, source_target_pairs={{0,452},{64,0},{128,64},{192,128},{256,192},{320,256},{384,320},{4... | collective-permute-start | bytes 688136 | tf_op jit(solution)/shard_map/ppermute | solution.py:22
  56.6 11.6 %collective-permute-start.7 = (bf16[896,128]{1,0:T(8,128)(2,1)S(1)}, bf16[896,128]{1,0:T(8,128)(2,1)S(1)}, u32[]{:S(2)}, u32[]{:S(2)}) collective-permute-start(bf16[896,128]{1,0:T(8,128)(2,1)S(1)} %add_convert_fusion.2), channel_id=1, source_target_pairs={{0,64},{64,128},{128,192},{192,256},{256,320},{320,384},{384,448},... | collective-permute-start | bytes 688136 | tf_op jit(solution)/shard_map/ppermute | solution.py:22
  58.6 20.4 %collective-permute-start.4 = (bf16[896,128]{1,0:T(8,128)(2,1)S(1)}, bf16[896,128]{1,0:T(8,128)(2,1)S(1)}, u32[]{:S(2)}, u32[]{:S(2)}) collective-permute-start(bf16[896,128]{1,0:T(8,128)(2,1)S(1)} %add_convert_fusion.3), channel_id=1, source_target_pairs={{0,452},{64,0},{128,64},{192,128},{256,192},{320,256},{384,320},{4... | collective-permute-start | bytes 688136 | tf_op jit(solution)/shard_map/ppermute | solution.py:22
  68.9 10.1 %collective-permute-start.8 = (bf16[896,128]{1,0:T(8,128)(2,1)}, bf16[896,128]{1,0:T(8,128)(2,1)S(1)}, u32[]{:S(2)}, u32[]{:S(2)}) collective-permute-start(bf16[896,128]{1,0:T(8,128)(2,1)} %add_convert_fusion.1), channel_id=1, source_target_pairs={{0,64},{64,128},{128,192},{192,256},{256,320},{320,384},{384,448},... | collective-permute-start | bytes 688136 | tf_op jit(solution)/shard_map/ppermute | solution.py:22
  79.3 6.8 %collective-permute-start.11 = (bf16[896,128]{1,0:T(8,128)(2,1)S(1)}, bf16[896,128]{1,0:T(8,128)(2,1)S(1)}, u32[]{:S(2)}, u32[]{:S(2)}) collective-permute-start(bf16[896,128]{1,0:T(8,128)(2,1)S(1)} %pad_maximum_fusion.3.refs_2_), channel_id=1, source_target_pairs={{0,452},{64,0},{128,64},{192,128},{256,192},{320,256},{384,320},{4... | collective-permute-start | bytes 688136 | tf_op jit(solution)/shard_map/ppermute | solution.py:22
  82.7 7.1 %collective-permute-start.9 = (bf16[896,128]{1,0:T(8,128)(2,1)S(1)}, bf16[896,128]{1,0:T(8,128)(2,1)S(1)}, u32[]{:S(2)}, u32[]{:S(2)}) collective-permute-start(bf16[896,128]{1,0:T(8,128)(2,1)S(1)} %pad_maximum_fusion.3.refs_2_), channel_id=1, source_target_pairs={{0,64},{64,128},{128,192},{192,256},{256,320},{320,384},{384,448},... | collective-permute-start | bytes 688136 | tf_op jit(solution)/shard_map/ppermute | solution.py:22
  86.1 7.0 %collective-permute-start.12 = (bf16[896,128]{1,0:T(8,128)(2,1)S(1)}, bf16[896,128]{1,0:T(8,128)(2,1)S(1)}, u32[]{:S(2)}, u32[]{:S(2)}) collective-permute-start(bf16[896,128]{1,0:T(8,128)(2,1)S(1)} %collective-permute-done.11.refs_3_), channel_id=1, source_target_pairs={{0,452},{64,0},{128,64},{192,128},{256,192},{320,256},{384,320},{4... | collective-permute-start | bytes 688136 | tf_op jit(solution)/shard_map/ppermute | solution.py:22
  89.8 13.4 %collective-permute-start.10 = (bf16[896,128]{1,0:T(8,128)(2,1)S(1)}, bf16[896,128]{1,0:T(8,128)(2,1)S(1)}, u32[]{:S(2)}, u32[]{:S(2)}) collective-permute-start(bf16[896,128]{1,0:T(8,128)(2,1)S(1)} %collective-permute-done.9.refs_1_), channel_id=1, source_target_pairs={{0,64},{64,128},{128,192},{192,256},{256,320},{320,384},{384,448},... | collective-permute-start | bytes 688136 | tf_op jit(solution)/shard_map/ppermute | solution.py:22
  93.2 14.0 %collective-permute-start.15 = (bf16[896,128]{1,0:T(8,128)(2,1)S(1)}, bf16[896,128]{1,0:T(8,128)(2,1)S(1)}, u32[]{:S(2)}, u32[]{:S(2)}) collective-permute-start(bf16[896,128]{1,0:T(8,128)(2,1)S(1)} %collective-permute-done.12.refs_4_), channel_id=1, source_target_pairs={{0,388},{64,452},{128,0},{192,64},{256,128},{320,192},{384,256},{4... | collective-permute-start | bytes 688136 | tf_op jit(solution)/shard_map/ppermute | solution.py:22
  98.1 9.1 %collective-permute-start.14 = (bf16[896,128]{1,0:T(8,128)(2,1)S(1)}, bf16[896,128]{1,0:T(8,128)(2,1)}, u32[]{:S(2)}, u32[]{:S(2)}) collective-permute-start(bf16[896,128]{1,0:T(8,128)(2,1)S(1)} %collective-permute-done.12.refs_4_), channel_id=1, source_target_pairs={{0,452},{64,0},{128,64},{192,128},{256,192},{320,256},{384,320},{4... | collective-permute-start | bytes 688136 | tf_op jit(solution)/shard_map/ppermute | solution.py:22
  103.1 7.1 %collective-permute-start.13 = (bf16[896,128]{1,0:T(8,128)(2,1)S(1)}, bf16[896,128]{1,0:T(8,128)(2,1)}, u32[]{:S(2)}, u32[]{:S(2)}) collective-permute-start(bf16[896,128]{1,0:T(8,128)(2,1)S(1)} %collective-permute-done.10.refs_0_), channel_id=1, source_target_pairs={{0,64},{64,128},{128,192},{192,256},{256,320},{320,384},{384,448},... | collective-permute-start | bytes 688136 | tf_op jit(solution)/shard_map/ppermute | solution.py:22
  112.8 19.2 %copy-start = (bf16[448,512]{1,0:T(8,128)(2,1)}, bf16[448,512]{1,0:T(8,128)(2,1)S(1)}, u32[]{:S(2)}) copy-start(bf16[448,512]{1,0:T(8,128)(2,1)S(1)} %get-tuple-element.47) | copy-start | bytes 1376260
  112.8 18.3 %collective-permute-start.16 = (bf16[512,512]{1,0:T(8,128)(2,1)S(1)}, bf16[512,512]{1,0:T(8,128)(2,1)S(1)}, u32[]{:S(2)}, u32[]{:S(2)}) collective-permute-start(bf16[512,512]{1,0:T(8,128)(2,1)S(1)} %get-tuple-element.40), channel_id=1, source_target_pairs={{0,8},{8,0},{1,9},{9,1},{2,10},{10,2},{3,11},{11,3},{4,12},{12,4},... | collective-permute-start | bytes 1572872 | tf_op jit(solution)/shard_map/ppermute | solution.py:61
  132.0 13.5 %all-to-all-start.2 = ((bf16[16,32,512]{2,1,0:T(8,128)(2,1)}), bf16[16,32,512]{2,1,0:T(8,128)(2,1)S(1)}, u32[]{:S(2)}, u32[]{:S(2)}) async-start(bf16[16,32,512]{2,1,0:T(8,128)(2,1)} %bitcast.5), calls=%async_computation.2 | async-start | bytes 1048576 | tf_op jit(solution)/shard_map/all_to_all | solution.py:230
  136.5 50.3 %collective-permute-start.18 = (bf16[448,512]{1,0:T(8,128)(2,1)}, bf16[448,512]{1,0:T(8,128)(2,1)S(1)}, u32[]{:S(2)}, u32[]{:S(2)}) collective-permute-start(bf16[448,512]{1,0:T(8,128)(2,1)} %copy-done), channel_id=1, source_target_pairs={{0,4},{4,0},{1,5},{5,1},{2,6},{6,2},{3,7},{7,3},{8,12},{12,8},{9,1... | collective-permute-start | bytes 1376264 | tf_op jit(solution)/shard_map/ppermute | solution.py:229
  146.4 8.4 %all-to-all-start.3 = ((bf16[128,2,1,224]{3,1,2,0:T(2,128)(2,1)}), bf16[128,2,1,224]{3,1,2,0:T(2,128)(2,1)S(1)}, u32[]{:S(2)}, u32[]{:S(2)}) async-start(bf16[128,2,1,224]{3,1,2,0:T(2,128)(2,1)} %copy.19), calls=%async_computation.3 | async-start | bytes 262144 | tf_op jit(solution)/shard_map/all_to_all | solution.py:236
  149.7 6.0 %collective-permute-start.17 = (bf16[32,512]{1,0:T(8,128)(2,1)S(1)}, bf16[32,512]{1,0:T(8,128)(2,1)S(1)}, u32[]{:S(2)}, u32[]{:S(2)}) collective-permute-start(bf16[32,512]{1,0:T(8,128)(2,1)S(1)} %reduce_sum.12), channel_id=1, source_target_pairs={{0,44},{16,52},{32,60},{48,0},{8,8},{24,16},{40,24},{56,32},{64,11... | collective-permute-start | bytes 98312 | tf_op jit(solution)/shard_map/ppermute | solution.py:235

commit v5 on v4

--- a/solution.py
+++ b/solution.py
@@ -88,77 +88,88 @@
 
 
 def near_kernel(core_ref, own_ref, other_ref, weights_ref, *refs):
-    tile_refs = refs[:5]
-    terms_ref, sums_ref, tokens_ref, wide_ref = refs[5:]
+    tile_refs = refs[:7]
+    terms_ref, sums_ref, tokens_ref, wide_ref = refs[7:]
     join_cores(core_ref[0], own_ref, other_ref, tokens_ref)
     for at, tile_ref in enumerate(tile_refs):
         wide_ref[:, at * 128 : (at + 1) * 128] = tile_ref[...]
         product = dot_f32(weights_ref[...], tile_ref[...])
         terms_ref[at * 128 : (at + 1) * 128, :] = product.T.astype(jnp.bfloat16)
-    sums_ref[...] = dot_f32(wide_ref[...], tokens_ref[128:768, :])
+    sums_ref[...] = dot_f32(wide_ref[...], tokens_ref[0:896, :])
 
 
 def near_products(core, own, other, weights, tiles):
     features, cols = weights.shape
     return pl.pallas_call(
         near_kernel,
-        in_specs=[SMEM_SPEC] + [VMEM_SPEC] * 8,
+        in_specs=[SMEM_SPEC] + [VMEM_SPEC] * 10,
         out_specs=[VMEM_SPEC] * 2,
         out_shape=[
-            jax.ShapeDtypeStruct((5 * 128, features), jnp.bfloat16),
+            jax.ShapeDtypeStruct((7 * 128, features), jnp.bfloat16),
             jax.ShapeDtypeStruct((cols, features), jnp.float32),
         ],
         scratch_shapes=[
             pltpu.VMEM((ROWS * 128, features), jnp.bfloat16),
-            pltpu.VMEM((cols, 5 * 128), jnp.bfloat16),
+            pltpu.VMEM((cols, 7 * 128), jnp.bfloat16),
         ],
         compiler_params=PARAMS,
     )(core, own, other, weights, *tiles)
 
 
-def last_kernel(core_ref, half_ref, own_ref, other_ref, weights_ref, terms_ref, sums_ref, *refs):
-    tile_refs = refs[:3]
-    keep_terms_ref, send_terms_ref, keep_ref, send_ref = refs[3:7]
-    tokens_ref, wide_ref, all_terms_ref, all_sums_ref = refs[7:]
-    core = core_ref[0]
+def last_sums_kernel(core_ref, half_ref, own_ref, other_ref, sums_ref, tile_ref, keep_ref, send_ref, last_ref):
+    rows = own_ref.shape[0]
+
+    @pl.when(core_ref[0] == 0)
+    def _():
+        last_ref[...] = other_ref[rows - 128 :, :]
+
+    @pl.when(core_ref[0] == 1)
+    def _():
+        last_ref[...] = own_ref[rows - 128 :, :]
+
+    rows = keep_ref.shape[0]
     half = half_ref[0]
-    join_cores(core, own_ref, other_ref, tokens_ref)
-    all_terms_ref[128:768, :] = terms_ref[...]
-    for at, (offset, tile_ref) in enumerate(zip((0, 6, 7), tile_refs)):
-        wide_ref[:, at * 128 : (at + 1) * 128] = tile_ref[...]
-        product = dot_f32(weights_ref[...], tile_ref[...])
-        all_terms_ref[offset * 128 : (offset + 1) * 128, :] = product.T.astype(jnp.bfloat16)
-    tokens_ref[640:768, :] = tokens_ref[0:128, :]
-    all_sums_ref[...] = sums_ref[...] + dot_f32(wide_ref[...], tokens_ref[640:1024, :])
-    rows = keep_terms_ref.shape[0]
-    keep_terms_ref[...] = all_terms_ref[pl.ds(pl.multiple_of(core * rows, rows), rows), :]
-    send_terms_ref[...] = all_terms_ref[pl.ds(pl.multiple_of((1 - core) * rows, rows), rows), :]
-    rows = keep_ref.shape[0]
-    keep_ref[...] = all_sums_ref[pl.ds(pl.multiple_of(half * rows, 16), rows), :]
-    send = all_sums_ref[pl.ds(pl.multiple_of((1 - half) * rows, 16), rows), :]
+    send_rows = pl.ds(pl.multiple_of((1 - half) * rows, 16), rows)
+    keep_rows = pl.ds(pl.multiple_of(half * rows, 16), rows)
+    send = sums_ref[send_rows, :] + dot_f32(tile_ref[send_rows, :], last_ref[...])
     send_ref[...] = send.astype(jnp.bfloat16)
-
-
-def last_products(core, half, own, other, weights, terms, sums, tiles):
-    features, cols = weights.shape
-    return pl.pallas_call(
-        last_kernel,
-        in_specs=[SMEM_SPEC] * 2 + [VMEM_SPEC] * 8,
-        out_specs=[VMEM_SPEC] * 4,
+    keep_ref[...] = sums_ref[keep_rows, :] + dot_f32(tile_ref[keep_rows, :], last_ref[...])
+
+
+def last_sums(core, half, own, other, sums, tile):
+    cols, features = sums.shape
+    return pl.pallas_call(
+        last_sums_kernel,
+        in_specs=[SMEM_SPEC] * 2 + [VMEM_SPEC] * 4,
+        out_specs=[VMEM_SPEC] * 2,
         out_shape=[
-            jax.ShapeDtypeStruct((ROWS * 64, features), jnp.bfloat16),
-            jax.ShapeDtypeStruct((ROWS * 64, features), jnp.bfloat16),
             jax.ShapeDtypeStruct((cols // 2, features), jnp.float32),
             jax.ShapeDtypeStruct((cols // 2, features), jnp.bfloat16),
         ],
-        scratch_shapes=[
-            pltpu.VMEM((ROWS * 128, features), jnp.bfloat16),
-            pltpu.VMEM((cols, 3 * 128), jnp.bfloat16),
-            pltpu.VMEM((ROWS * 128, features), jnp.bfloat16),
-            pltpu.VMEM((cols, features), jnp.float32),
-        ],
-        compiler_params=PARAMS,
-    )(core, half, own, other, weights, terms, sums, *tiles)
+        scratch_shapes=[pltpu.VMEM((128, features), jnp.bfloat16)],
+        compiler_params=PARAMS,
+    )(core, half, own, other, sums, tile)
+
+
+def last_terms_kernel(core_ref, weights_ref, terms_ref, tile_ref, keep_ref, send_ref, all_ref):
+    all_ref[0:896, :] = terms_ref[...]
+    all_ref[896:1024, :] = dot_f32(weights_ref[...], tile_ref[...]).T.astype(jnp.bfloat16)
+    core = core_ref[0]
+    rows = keep_ref.shape[0]
+    keep_ref[...] = all_ref[pl.ds(pl.multiple_of(core * rows, rows), rows), :]
+    send_ref[...] = all_ref[pl.ds(pl.multiple_of((1 - core) * rows, rows), rows), :]
+
+
+def last_terms(core, weights, terms, tile):
+    shape = (ROWS * 64, weights.shape[0])
+    return pl.pallas_call(
+        last_terms_kernel,
+        in_specs=[SMEM_SPEC] + [VMEM_SPEC] * 3,
+        out_specs=[VMEM_SPEC] * 2,
+        out_shape=[jax.ShapeDtypeStruct(shape, jnp.bfloat16)] * 2,
+        scratch_shapes=[pltpu.VMEM((ROWS * 128, shape[1]), jnp.bfloat16)],
+        compiler_params=PARAMS,
+    )(core, weights, terms, tile)
 
 
 def add_tiles(*tiles):
@@ -187,19 +198,20 @@
     own_tokens, cotangent, weights = lax.optimization_barrier((own_tokens, cotangent, weights))
     other_tokens = swap_cores(own_tokens)
     cotangent = lax.all_to_all(cotangent, "x", split_axis=0, concat_axis=0, tiled=True)
+    partial = {}
+    for offsets in ((7, 0), (6, 1, 5, 2, 4, 3)):
+        partial.update(zip(offsets, forward_tiles(offsets, core, own_tokens, other_tokens, weights)))
+    right = ring_shift(partial[7], 1)
+    left = ring_shift(partial[0], -1)
+    right, left, cotangent = lax.optimization_barrier((right, left, cotangent))
+    right = add_tiles(right, partial[6])
+    left = add_tiles(left, partial[1])
+    right = add_tiles(ring_shift(right, 1), partial[5])
+    left = add_tiles(ring_shift(left, -1), partial[2])
+    right = add_tiles(ring_shift(right, 1), partial[4])
+    left = ring_shift(left, -1)
+    right = ring_shift(right, 1)
     cotangent = cotangent.reshape(-1, 2 * part).T.astype(jnp.float32)
-
-    partial = {}
-    for offsets in ((6, 7, 0), (5, 1, 4, 2, 3)):
-        partial.update(zip(offsets, forward_tiles(offsets, core, own_tokens, other_tokens, weights)))
-    right = ring_shift(partial[6], 1)
-    left = ring_shift(partial[0], -1)
-    right = add_tiles(right, ring_shift(partial[7], 2), partial[5])
-    left = add_tiles(left, partial[1])
-    right = add_tiles(ring_shift(right, 1), partial[4])
-    left = add_tiles(ring_shift(left, -1), partial[2])
-    right = ring_shift(right, 1)
-    left = ring_shift(left, -1)
     total = partial[BEFORE].astype(jnp.float32) + left.astype(jnp.float32) + right.astype(jnp.float32)
     gate_pre = jnp.concatenate([total[:part], total[2 * part : 3 * part]], 0)
     up_pre = jnp.concatenate([total[part : 2 * part], total[3 * part :]], 0)
@@ -217,13 +229,13 @@
     right_2 = ring_shift(right_1, 1)
     left_3 = ring_shift(left_2, -1)
     right_3 = ring_shift(right_2, 1)
-    left_4 = ring_shift(left_2, -2)
+    left_4 = ring_shift(left_3, -1)
     terms, sums = near_products(
-        core, own_tokens, other_tokens, weights, [right_2, right_1, grads, left_1, left_2]
-    )
-    keep_terms, send_terms, keep, send = last_products(
-        core, half, own_tokens, other_tokens, weights, terms, sums, [right_3, left_3, left_4]
-    )
+        core, own_tokens, other_tokens, weights, [right_3, right_2, right_1, grads, left_1, left_2, left_3]
+    )
+    keep, send = last_sums(core, half, own_tokens, other_tokens, sums, left_4)
+    terms, send = lax.optimization_barrier((terms, send))
+    keep_terms, send_terms = last_terms(core, weights, terms, left_4)
 
     terms = add_tiles(keep_terms, swap_cores(send_terms))
     received = lax.ppermute(send, "h", [(0, 1), (1, 0)])

time: 190 us -> 191 us (level)
  the two profiles are of different devices: /device:TPU:73 before, /device:TPU:233 now
where the time goes in v5:
time: 191 us; the launch traced here: 189 us
  starting transfers between devices  90.2 us (47%)
  waiting for transfers between devices  77.1 us (40%)
  local copies, waits for them, and re-layouts  8.12 us (4%)
  Pallas kernels  7.25 us (4%)
  other arithmetic  5.65 us (3%)
    ppermute x14, starting transfers between devices, ring_shift(): return lax.ppermute(value, ('r', 'h'), pairs)  49.1 us
    ppermute x1, waiting for transfers between devices, local(): lax.ppermute(grad_tokens, ('r', 'y', 'c', 'h'), result_pairs())  33.2 us
    ppermute x14, waiting for transfers between devices, ring_shift(): return lax.ppermute(value, ('r', 'h'), pairs)  15.6 us
    ppermute x2, starting transfers between devices, swap_cores(): return lax.ppermute(value, 'c', [(0, 1), (1, 0)])  14.4 us
    ppermute x1, waiting for transfers between devices, local(): piece = lax.ppermute(tokens, ('r', 'y', 'c', 'h'), token_pairs())  8.6 us
    all_to_all x1, waiting for transfers between devices, local(): lax.all_to_all(terms.reshape(16, -1, features), ('y', 'x'), split_axis=0,...  7.06 us
    all_to_all x1, waiting for transfers between devices, local(): lax.all_to_all(copies, ('y', 'x'), split_axis=0, concat_axis=0, tiled=True)  6 us
    ppermute x1, starting transfers between devices, local(): lax.ppermute(grad_tokens, ('r', 'y', 'c', 'h'), result_pairs())  5.63 us
  transfers between devices with their start and end apart: 23, of which 13 were waited for; matrix products, arithmetic and copies ran while one was open for 4% of the time, Pallas kernels for 3%

profile of v5, /device:TPU:233, one launch (start us, length us, event | category | flops | bytes accessed | tf_op | source)
XLA Modules:
  0.0 189.4 jit_solution(14514450788095110599)
XLA Ops:
  0.6 2.1 %collective-permute-start = (bf16[32,512]{1,0:T(8,128)(2,1)}, bf16[32,512]{1,0:T(8,128)(2,1)S(1)}, u32[]{:S(2)}, u32[]{:S(2)}) collective-permute-start(bf16[32,512]{1,0:T(8,128)(2,1)} %param.4), channel_id=1, source_target_pairs={{324,0},{388,16},{452,32},{0,48},{64,8},{128,24},{192,40},{256,56}... | collective-permute-start | bytes 98312 | tf_op jit(solution)/shard_map/ppermute | solution.py:193
  2.7 8.6 %collective-permute-done = bf16[32,512]{1,0:T(8,128)(2,1)S(1)} collective-permute-done((bf16[32,512]{1,0:T(8,128)(2,1)}, bf16[32,512]{1,0:T(8,128)(2,1)S(1)}, u32[]{:S(2)}, u32[]{:S(2)}) %collective-permute-start) | collective-permute-done | bytes 32800 | tf_op jit(solution)/shard_map/ppermute | solution.py:193
  11.3 0.8 broadcast_in_dim.2
  12.2 5.3 %all-to-all-start = ((bf16[16,32,512]{2,1,0:T(8,128)(2,1)}), bf16[16,32,512]{2,1,0:T(8,128)(2,1)S(1)}, u32[]{:S(2)}, u32[]{:S(2)}) async-start(bf16[16,32,512]{2,1,0:T(8,128)(2,1)} %broadcast_in_dim.2), calls=%async_computation | async-start | bytes 1048576 | tf_op jit(solution)/shard_map/all_to_all | solution.py:195
  17.5 1.1 reshape.36
  18.6 0.7 copy.23
  19.4 1.8 constant_dynamic-slice_fusion.2
  21.2 0.4 pad_maximum_fusion.weights_ref
  21.6 6.0 %all-to-all-done = bf16[16,32,512]{2,1,0:T(8,128)(2,1)S(1)} async-done(((bf16[16,32,512]{2,1,0:T(8,128)(2,1)}), bf16[16,32,512]{2,1,0:T(8,128)(2,1)S(1)}, u32[]{:S(2)}, u32[]{:S(2)}) %all-to-all-start) | async-done | bytes 524320 | tf_op jit(solution)/shard_map/all_to_all | solution.py:195
  27.6 2.4 %collective-permute-start.1 = (bf16[512,512]{1,0:T(8,128)(2,1)S(1)}, bf16[512,512]{1,0:T(8,128)(2,1)S(1)}, u32[]{:S(2)}, u32[]{:S(2)}) collective-permute-start(bf16[512,512]{1,0:T(8,128)(2,1)S(1)} %bitcast.30), channel_id=1, source_target_pairs={{0,8},{8,0},{1,9},{9,1},{2,10},{10,2},{3,11},{11,3},{4,12},{12,4},... | collective-permute-start | bytes 1572872 | tf_op jit(solution)/shard_map/ppermute | solution.py:61
  30.0 1.5 collective-permute-done.1.other_ref
  31.5 1.3 shard_map.75
  32.8 6.6 %collective-permute-start.2 = (bf16[896,128]{1,0:T(8,128)(2,1)}, bf16[896,128]{1,0:T(8,128)(2,1)}, u32[]{:S(2)}, u32[]{:S(2)}) collective-permute-start(bf16[896,128]{1,0:T(8,128)(2,1)} %get-tuple-element.33), channel_id=1, source_target_pairs={{0,64},{64,128},{128,192},{192,256},{256,320},{320,384},{384,448},... | collective-permute-start | bytes 688136 | tf_op jit(solution)/shard_map/ppermute | solution.py:22
  39.4 1.9 %collective-permute-start.3 = (bf16[896,128]{1,0:T(8,128)(2,1)}, bf16[896,128]{1,0:T(8,128)(2,1)}, u32[]{:S(2)}, u32[]{:S(2)}) collective-permute-start(bf16[896,128]{1,0:T(8,128)(2,1)} %get-tuple-element.34), channel_id=1, source_target_pairs={{0,452},{64,0},{128,64},{192,128},{256,192},{320,256},{384,320},{4... | collective-permute-start | bytes 688136 | tf_op jit(solution)/shard_map/ppermute | solution.py:22
  41.3 3.6 %all-to-all-start.1 = ((bf16[4,32,2,224]{3,2,1,0:T(2,128)(2,1)}), bf16[4,32,2,224]{3,2,1,0:T(2,128)(2,1)S(1)}, u32[]{:S(2)}, u32[]{:S(2)}) async-start(bf16[4,32,2,224]{3,2,1,0:T(2,128)(2,1)} %bitcast.29), calls=%async_computation.1 | async-start | bytes 262144 | tf_op jit(solution)/shard_map/all_to_all | solution.py:200
  44.9 1.1 shard_map.76
  46.0 3.7 %all-to-all-done.1 = bf16[4,32,2,224]{3,2,1,0:T(2,128)(2,1)S(1)} async-done(((bf16[4,32,2,224]{3,2,1,0:T(2,128)(2,1)}), bf16[4,32,2,224]{3,2,1,0:T(2,128)(2,1)S(1)}, u32[]{:S(2)}, u32[]{:S(2)}) %all-to-all-start.1) | async-done | bytes 114720 | tf_op jit(solution)/shard_map/all_to_all | solution.py:200
  49.7 1.0 add_convert_fusion.3
  50.7 4.6 %collective-permute-start.6 = (bf16[896,128]{1,0:T(8,128)(2,1)S(1)}, bf16[896,128]{1,0:T(8,128)(2,1)S(1)}, u32[]{:S(2)}, u32[]{:S(2)}) collective-permute-start(bf16[896,128]{1,0:T(8,128)(2,1)S(1)} %add_convert_fusion.3), channel_id=1, source_target_pairs={{0,64},{64,128},{128,192},{192,256},{256,320},{320,384},{384,448},... | collective-permute-start | bytes 688136 | tf_op jit(solution)/shard_map/ppermute | solution.py:22
  55.3 1.0 add_convert_fusion.5
  56.3 1.9 %collective-permute-start.4 = (bf16[896,128]{1,0:T(8,128)(2,1)S(1)}, bf16[896,128]{1,0:T(8,128)(2,1)S(1)}, u32[]{:S(2)}, u32[]{:S(2)}) collective-permute-start(bf16[896,128]{1,0:T(8,128)(2,1)S(1)} %add_convert_fusion.5), channel_id=1, source_target_pairs={{0,452},{64,0},{128,64},{192,128},{256,192},{320,256},{384,320},{4... | collective-permute-start | bytes 688136 | tf_op jit(solution)/shard_map/ppermute | solution.py:22
  58.2 0.1 add_convert_fusion.2
  58.3 5.0 %collective-permute-start.7 = (bf16[896,128]{1,0:T(8,128)(2,1)S(1)}, bf16[896,128]{1,0:T(8,128)(2,1)S(1)}, u32[]{:S(2)}, u32[]{:S(2)}) collective-permute-start(bf16[896,128]{1,0:T(8,128)(2,1)S(1)} %add_convert_fusion.2), channel_id=1, source_target_pairs={{0,64},{64,128},{128,192},{192,256},{256,320},{320,384},{384,448},... | collective-permute-start | bytes 688136 | tf_op jit(solution)/shard_map/ppermute | solution.py:22
  63.3 0.9 collective-permute-done.4
  64.3 0.1 add_convert_fusion.4
  64.4 1.9 %collective-permute-start.5 = (bf16[896,128]{1,0:T(8,128)(2,1)S(1)}, bf16[896,128]{1,0:T(8,128)(2,1)S(1)}, u32[]{:S(2)}, u32[]{:S(2)}) collective-permute-start(bf16[896,128]{1,0:T(8,128)(2,1)S(1)} %add_convert_fusion.4), channel_id=1, source_target_pairs={{0,452},{64,0},{128,64},{192,128},{256,192},{320,256},{384,320},{4... | collective-permute-start | bytes 688136 | tf_op jit(solution)/shard_map/ppermute | solution.py:22
  66.3 0.8 add_convert_fusion.1
  67.0 5.0 %collective-permute-start.8 = (bf16[896,128]{1,0:T(8,128)(2,1)}, bf16[896,128]{1,0:T(8,128)(2,1)}, u32[]{:S(2)}, u32[]{:S(2)}) collective-permute-start(bf16[896,128]{1,0:T(8,128)(2,1)} %add_convert_fusion.1), channel_id=1, source_target_pairs={{0,64},{64,128},{128,192},{192,256},{256,320},{320,384},{384,448},... | collective-permute-start | bytes 688136 | tf_op jit(solution)/shard_map/ppermute | solution.py:22
  72.1 0.1 reshape.41
  72.2 0.1 copy.18
  72.3 0.0 collective-permute-done.5
  72.3 3.0 %collective-permute-done.8 = bf16[896,128]{1,0:T(8,128)(2,1)} collective-permute-done((bf16[896,128]{1,0:T(8,128)(2,1)}, bf16[896,128]{1,0:T(8,128)(2,1)}, u32[]{:S(2)}, u32[]{:S(2)}) %collective-permute-start.8) | collective-permute-done | bytes 229408 | tf_op jit(solution)/shard_map/ppermute | solution.py:22
  75.3 1.0 convert_add_fusion.1
  76.4 0.2 multiply_convert_fusion
  76.6 1.9 %collective-permute-start.12 = (bf16[896,128]{1,0:T(8,128)(2,1)S(1)}, bf16[896,128]{1,0:T(8,128)(2,1)S(1)}, u32[]{:S(2)}, u32[]{:S(2)}) collective-permute-start(bf16[896,128]{1,0:T(8,128)(2,1)S(1)} %pad_maximum_fusion.3.refs_3_), channel_id=1, source_target_pairs={{0,452},{64,0},{128,64},{192,128},{256,192},{320,256},{384,320},{4... | collective-permute-start | bytes 688136 | tf_op jit(solution)/shard_map/ppermute | solution.py:22
  78.5 5.0 %collective-permute-start.9 = (bf16[896,128]{1,0:T(8,128)(2,1)S(1)}, bf16[896,128]{1,0:T(8,128)(2,1)S(1)}, u32[]{:S(2)}, u32[]{:S(2)}) collective-permute-start(bf16[896,128]{1,0:T(8,128)(2,1)S(1)} %pad_maximum_fusion.3.refs_3_), channel_id=1, source_target_pairs={{0,64},{64,128},{128,192},{192,256},{256,320},{320,384},{384,448},... | collective-permute-start | bytes 688136 | tf_op jit(solution)/shard_map/ppermute | solution.py:22
  83.6 1.5 collective-permute-done.12.refs_4_
  85.0 1.9 %collective-permute-start.13 = (bf16[896,128]{1,0:T(8,128)(2,1)S(1)}, bf16[896,128]{1,0:T(8,128)(2,1)S(1)}, u32[]{:S(2)}, u32[]{:S(2)}) collective-permute-start(bf16[896,128]{1,0:T(8,128)(2,1)S(1)} %collective-permute-done.12.refs_4_), channel_id=1, source_target_pairs={{0,452},{64,0},{128,64},{192,128},{256,192},{320,256},{384,320},{4... | collective-permute-start | bytes 688136 | tf_op jit(solution)/shard_map/ppermute | solution.py:22
  87.0 4.6 %collective-permute-start.10 = (bf16[896,128]{1,0:T(8,128)(2,1)S(1)}, bf16[896,128]{1,0:T(8,128)(2,1)S(1)}, u32[]{:S(2)}, u32[]{:S(2)}) collective-permute-start(bf16[896,128]{1,0:T(8,128)(2,1)S(1)} %collective-permute-done.9.refs_2_), channel_id=1, source_target_pairs={{0,64},{64,128},{128,192},{192,256},{256,320},{320,384},{384,448},... | collective-permute-start | bytes 688136 | tf_op jit(solution)/shard_map/ppermute | solution.py:22
  91.5 1.9 %collective-permute-done.13.refs_5_ = bf16[896,128]{1,0:T(8,128)(2,1)S(1)} collective-permute-done((bf16[896,128]{1,0:T(8,128)(2,1)S(1)}, bf16[896,128]{1,0:T(8,128)(2,1)S(1)}, u32[]{:S(2)}, u32[]{:S(2)}) %collective-permute-start.13) | collective-permute-done | bytes 229408 | tf_op jit(solution)/shard_map/ppermute | solution.py:22
  93.5 1.9 %collective-permute-start.14 = (bf16[896,128]{1,0:T(8,128)(2,1)S(1)}, bf16[896,128]{1,0:T(8,128)(2,1)}, u32[]{:S(2)}, u32[]{:S(2)}) collective-permute-start(bf16[896,128]{1,0:T(8,128)(2,1)S(1)} %collective-permute-done.13.refs_5_), channel_id=1, source_target_pairs={{0,452},{64,0},{128,64},{192,128},{256,192},{320,256},{384,320},{4... | collective-permute-start | bytes 688136 | tf_op jit(solution)/shard_map/ppermute | solution.py:22
  95.4 4.8 %collective-permute-start.11 = (bf16[896,128]{1,0:T(8,128)(2,1)S(1)}, bf16[896,128]{1,0:T(8,128)(2,1)}, u32[]{:S(2)}, u32[]{:S(2)}) collective-permute-start(bf16[896,128]{1,0:T(8,128)(2,1)S(1)} %collective-permute-done.10.refs_1_), channel_id=1, source_target_pairs={{0,64},{64,128},{128,192},{192,256},{256,320},{320,384},{384,448},... | collective-permute-start | bytes 688136 | tf_op jit(solution)/shard_map/ppermute | solution.py:22
  100.3 3.3 %collective-permute-done.14.refs_6_ = bf16[896,128]{1,0:T(8,128)(2,1)} collective-permute-done((bf16[896,128]{1,0:T(8,128)(2,1)S(1)}, bf16[896,128]{1,0:T(8,128)(2,1)}, u32[]{:S(2)}, u32[]{:S(2)}) %collective-permute-start.14) | collective-permute-done | bytes 229408 | tf_op jit(solution)/shard_map/ppermute | solution.py:22
  103.5 1.9 %collective-permute-start.15 = (bf16[896,128]{1,0:T(8,128)(2,1)}, bf16[896,128]{1,0:T(8,128)(2,1)S(1)}, u32[]{:S(2)}, u32[]{:S(2)}) collective-permute-start(bf16[896,128]{1,0:T(8,128)(2,1)} %collective-permute-done.14.refs_6_), channel_id=1, source_target_pairs={{0,452},{64,0},{128,64},{192,128},{256,192},{320,256},{384,320},{4... | collective-permute-start | bytes 688136 | tf_op jit(solution)/shard_map/ppermute | solution.py:22
  105.5 3.8 %shard_map.77 = (bf16[896,512]{1,0:T(8,128)(2,1)S(1)}, f32[896,512]{1,0:T(8,128)S(1)}) custom-call(s32[1]{0:T(128)} %bitcast.core_ref, bf16[512,512]{1,0:T(8,128)(2,1)S(1)} %bitcast.33, bf16[512,512]{1,0:T(8,128)(2,1)S(1)} %collective-permute-done.1.other_ref, bf16[512,896]{1,0:T(8,128)(2,1)S(1)} %pad_maximum_fusion.weights_ref, ...), custom_call_target="tpu_custom_call" | custom-call | tf_op jit(solution)/shard_map/pallas_call | solution.py:103
  109.3 4.9 %collective-permute-done.15.tile_ref = bf16[896,128]{1,0:T(8,128)(2,1)S(1)} collective-permute-done((bf16[896,128]{1,0:T(8,128)(2,1)}, bf16[896,128]{1,0:T(8,128)(2,1)S(1)}, u32[]{:S(2)}, u32[]{:S(2)}) %collective-permute-start.15) | collective-permute-done | bytes 229408 | tf_op jit(solution)/shard_map/ppermute | solution.py:22
  114.2 0.4 shard_map.78
  114.6 0.6 shard_map.79
  115.3 12.0 %collective-permute-start.16 = (bf16[512,512]{1,0:T(8,128)(2,1)S(1)}, bf16[512,512]{1,0:T(8,128)(2,1)S(1)}, u32[]{:S(2)}, u32[]{:S(2)}) collective-permute-start(bf16[512,512]{1,0:T(8,128)(2,1)S(1)} %get-tuple-element.50), channel_id=1, source_target_pairs={{0,8},{8,0},{1,9},{9,1},{2,10},{10,2},{3,11},{11,3},{4,12},{12,4},... | collective-permute-start | bytes 1572872 | tf_op jit(solution)/shard_map/ppermute | solution.py:61
  127.3 1.5 collective-permute-done.16
  128.8 0.9 add_convert_fusion
  129.7 5.0 %all-to-all-start.2 = ((bf16[16,32,512]{2,1,0:T(8,128)(2,1)}), bf16[16,32,512]{2,1,0:T(8,128)(2,1)S(1)}, u32[]{:S(2)}, u32[]{:S(2)}) async-start(bf16[16,32,512]{2,1,0:T(8,128)(2,1)} %bitcast.5), calls=%async_computation.2 | async-start | bytes 1048576 | tf_op jit(solution)/shard_map/all_to_all | solution.py:242
  134.7 1.9 %collective-permute-start.18 = (bf16[448,512]{1,0:T(8,128)(2,1)}, bf16[448,512]{1,0:T(8,128)(2,1)S(1)}, u32[]{:S(2)}, u32[]{:S(2)}) collective-permute-start(bf16[448,512]{1,0:T(8,128)(2,1)} %copy-done), channel_id=1, source_target_pairs={{0,4},{4,0},{1,5},{5,1},{2,6},{6,2},{3,7},{7,3},{8,12},{12,8},{9,1... | collective-permute-start | bytes 1376264 | tf_op jit(solution)/shard_map/ppermute | solution.py:241
  136.6 7.1 %all-to-all-done.2 = bf16[16,32,512]{2,1,0:T(8,128)(2,1)S(1)} async-done(((bf16[16,32,512]{2,1,0:T(8,128)(2,1)}), bf16[16,32,512]{2,1,0:T(8,128)(2,1)S(1)}, u32[]{:S(2)}, u32[]{:S(2)}) %all-to-all-start.2) | async-done | bytes 524320 | tf_op jit(solution)/shard_map/all_to_all | solution.py:242
  143.7 0.1 reduce_sum.12
  143.7 0.8 copy.19
  144.5 3.3 %all-to-all-start.3 = ((bf16[128,2,1,224]{3,1,2,0:T(2,128)(2,1)}), bf16[128,2,1,224]{3,1,2,0:T(2,128)(2,1)S(1)}, u32[]{:S(2)}, u32[]{:S(2)}) async-start(bf16[128,2,1,224]{3,1,2,0:T(2,128)(2,1)} %copy.19), calls=%async_computation.3 | async-start | bytes 262144 | tf_op jit(solution)/shard_map/all_to_all | solution.py:248
  147.9 5.6 %collective-permute-start.17 = (bf16[32,512]{1,0:T(8,128)(2,1)S(1)}, bf16[32,512]{1,0:T(8,128)(2,1)S(1)}, u32[]{:S(2)}, u32[]{:S(2)}) collective-permute-start(bf16[32,512]{1,0:T(8,128)(2,1)S(1)} %reduce_sum.12), channel_id=1, source_target_pairs={{0,44},{16,52},{32,60},{48,0},{8,8},{24,16},{40,24},{56,32},{64,11... | collective-permute-start | bytes 98312 | tf_op jit(solution)/shard_map/ppermute | solution.py:247
  153.5 0.1 copy.21
  153.6 0.8 reshape.40
  154.5 33.2 %collective-permute-done.17 = bf16[32,512]{1,0:T(8,128)(2,1)S(1)} collective-permute-done((bf16[32,512]{1,0:T(8,128)(2,1)S(1)}, bf16[32,512]{1,0:T(8,128)(2,1)S(1)}, u32[]{:S(2)}, u32[]{:S(2)}) %collective-permute-start.17) | collective-permute-done | bytes 32800 | tf_op jit(solution)/shard_map/ppermute | solution.py:247
  187.6 0.1 convert_add_fusion
  187.8 1.0 slice_bitcast_fusion
  188.7 0.6 copy.25
  (16 shorter events, 0.1 us)
Async XLA Ops:
  0.6 10.7 %collective-permute-start = (bf16[32,512]{1,0:T(8,128)(2,1)}, bf16[32,512]{1,0:T(8,128)(2,1)S(1)}, u32[]{:S(2)}, u32[]{:S(2)}) collective-permute-start(bf16[32,512]{1,0:T(8,128)(2,1)} %param.4), channel_id=1, source_target_pairs={{324,0},{388,16},{452,32},{0,48},{64,8},{128,24},{192,40},{256,56}... | collective-permute-start | bytes 98312 | tf_op jit(solution)/shard_map/ppermute | solution.py:193
  12.2 15.4 %all-to-all-start = ((bf16[16,32,512]{2,1,0:T(8,128)(2,1)}), bf16[16,32,512]{2,1,0:T(8,128)(2,1)S(1)}, u32[]{:S(2)}, u32[]{:S(2)}) async-start(bf16[16,32,512]{2,1,0:T(8,128)(2,1)} %broadcast_in_dim.2), calls=%async_computation | async-start | bytes 1048576 | tf_op jit(solution)/shard_map/all_to_all | solution.py:195
  27.6 3.9 %collective-permute-start.1 = (bf16[512,512]{1,0:T(8,128)(2,1)S(1)}, bf16[512,512]{1,0:T(8,128)(2,1)S(1)}, u32[]{:S(2)}, u32[]{:S(2)}) collective-permute-start(bf16[512,512]{1,0:T(8,128)(2,1)S(1)} %bitcast.30), channel_id=1, source_target_pairs={{0,8},{8,0},{1,9},{9,1},{2,10},{10,2},{3,11},{11,3},{4,12},{12,4},... | collective-permute-start | bytes 1572872 | tf_op jit(solution)/shard_map/ppermute | solution.py:61
  32.8 16.9 %collective-permute-start.2 = (bf16[896,128]{1,0:T(8,128)(2,1)}, bf16[896,128]{1,0:T(8,128)(2,1)}, u32[]{:S(2)}, u32[]{:S(2)}) collective-permute-start(bf16[896,128]{1,0:T(8,128)(2,1)} %get-tuple-element.33), channel_id=1, source_target_pairs={{0,64},{64,128},{128,192},{192,256},{256,320},{320,384},{384,448},... | collective-permute-start | bytes 688136 | tf_op jit(solution)/shard_map/ppermute | solution.py:22
  39.4 10.3 %collective-permute-start.3 = (bf16[896,128]{1,0:T(8,128)(2,1)}, bf16[896,128]{1,0:T(8,128)(2,1)}, u32[]{:S(2)}, u32[]{:S(2)}) collective-permute-start(bf16[896,128]{1,0:T(8,128)(2,1)} %get-tuple-element.34), channel_id=1, source_target_pairs={{0,452},{64,0},{128,64},{192,128},{256,192},{320,256},{384,320},{4... | collective-permute-start | bytes 688136 | tf_op jit(solution)/shard_map/ppermute | solution.py:22
  41.3 8.4 %all-to-all-start.1 = ((bf16[4,32,2,224]{3,2,1,0:T(2,128)(2,1)}), bf16[4,32,2,224]{3,2,1,0:T(2,128)(2,1)S(1)}, u32[]{:S(2)}, u32[]{:S(2)}) async-start(bf16[4,32,2,224]{3,2,1,0:T(2,128)(2,1)} %bitcast.29), calls=%async_computation.1 | async-start | bytes 262144 | tf_op jit(solution)/shard_map/all_to_all | solution.py:200
  50.7 7.5 %collective-permute-start.6 = (bf16[896,128]{1,0:T(8,128)(2,1)S(1)}, bf16[896,128]{1,0:T(8,128)(2,1)S(1)}, u32[]{:S(2)}, u32[]{:S(2)}) collective-permute-start(bf16[896,128]{1,0:T(8,128)(2,1)S(1)} %add_convert_fusion.3), channel_id=1, source_target_pairs={{0,64},{64,128},{128,192},{192,256},{256,320},{320,384},{384,448},... | collective-permute-start | bytes 688136 | tf_op jit(solution)/shard_map/ppermute | solution.py:22
  56.3 8.0 %collective-permute-start.4 = (bf16[896,128]{1,0:T(8,128)(2,1)S(1)}, bf16[896,128]{1,0:T(8,128)(2,1)S(1)}, u32[]{:S(2)}, u32[]{:S(2)}) collective-permute-start(bf16[896,128]{1,0:T(8,128)(2,1)S(1)} %add_convert_fusion.5), channel_id=1, source_target_pairs={{0,452},{64,0},{128,64},{192,128},{256,192},{320,256},{384,320},{4... | collective-permute-start | bytes 688136 | tf_op jit(solution)/shard_map/ppermute | solution.py:22
  58.3 8.0 %collective-permute-start.7 = (bf16[896,128]{1,0:T(8,128)(2,1)S(1)}, bf16[896,128]{1,0:T(8,128)(2,1)S(1)}, u32[]{:S(2)}, u32[]{:S(2)}) collective-permute-start(bf16[896,128]{1,0:T(8,128)(2,1)S(1)} %add_convert_fusion.2), channel_id=1, source_target_pairs={{0,64},{64,128},{128,192},{192,256},{256,320},{320,384},{384,448},... | collective-permute-start | bytes 688136 | tf_op jit(solution)/shard_map/ppermute | solution.py:22
  64.4 8.0 %collective-permute-start.5 = (bf16[896,128]{1,0:T(8,128)(2,1)S(1)}, bf16[896,128]{1,0:T(8,128)(2,1)S(1)}, u32[]{:S(2)}, u32[]{:S(2)}) collective-permute-start(bf16[896,128]{1,0:T(8,128)(2,1)S(1)} %add_convert_fusion.4), channel_id=1, source_target_pairs={{0,452},{64,0},{128,64},{192,128},{256,192},{320,256},{384,320},{4... | collective-permute-start | bytes 688136 | tf_op jit(solution)/shard_map/ppermute | solution.py:22
  67.0 8.3 %collective-permute-start.8 = (bf16[896,128]{1,0:T(8,128)(2,1)}, bf16[896,128]{1,0:T(8,128)(2,1)}, u32[]{:S(2)}, u32[]{:S(2)}) collective-permute-start(bf16[896,128]{1,0:T(8,128)(2,1)} %add_convert_fusion.1), channel_id=1, source_target_pairs={{0,64},{64,128},{128,192},{192,256},{256,320},{320,384},{384,448},... | collective-permute-start | bytes 688136 | tf_op jit(solution)/shard_map/ppermute | solution.py:22
  76.6 8.4 %collective-permute-start.12 = (bf16[896,128]{1,0:T(8,128)(2,1)S(1)}, bf16[896,128]{1,0:T(8,128)(2,1)S(1)}, u32[]{:S(2)}, u32[]{:S(2)}) collective-permute-start(bf16[896,128]{1,0:T(8,128)(2,1)S(1)} %pad_maximum_fusion.3.refs_3_), channel_id=1, source_target_pairs={{0,452},{64,0},{128,64},{192,128},{256,192},{320,256},{384,320},{4... | collective-permute-start | bytes 688136 | tf_op jit(solution)/shard_map/ppermute | solution.py:22
  78.5 8.4 %collective-permute-start.9 = (bf16[896,128]{1,0:T(8,128)(2,1)S(1)}, bf16[896,128]{1,0:T(8,128)(2,1)S(1)}, u32[]{:S(2)}, u32[]{:S(2)}) collective-permute-start(bf16[896,128]{1,0:T(8,128)(2,1)S(1)} %pad_maximum_fusion.3.refs_3_), channel_id=1, source_target_pairs={{0,64},{64,128},{128,192},{192,256},{256,320},{320,384},{384,448},... | collective-permute-start | bytes 688136 | tf_op jit(solution)/shard_map/ppermute | solution.py:22
  85.0 8.4 %collective-permute-start.13 = (bf16[896,128]{1,0:T(8,128)(2,1)S(1)}, bf16[896,128]{1,0:T(8,128)(2,1)S(1)}, u32[]{:S(2)}, u32[]{:S(2)}) collective-permute-start(bf16[896,128]{1,0:T(8,128)(2,1)S(1)} %collective-permute-done.12.refs_4_), channel_id=1, source_target_pairs={{0,452},{64,0},{128,64},{192,128},{256,192},{320,256},{384,320},{4... | collective-permute-start | bytes 688136 | tf_op jit(solution)/shard_map/ppermute | solution.py:22
  87.0 8.4 %collective-permute-start.10 = (bf16[896,128]{1,0:T(8,128)(2,1)S(1)}, bf16[896,128]{1,0:T(8,128)(2,1)S(1)}, u32[]{:S(2)}, u32[]{:S(2)}) collective-permute-start(bf16[896,128]{1,0:T(8,128)(2,1)S(1)} %collective-permute-done.9.refs_2_), channel_id=1, source_target_pairs={{0,64},{64,128},{128,192},{192,256},{256,320},{320,384},{384,448},... | collective-permute-start | bytes 688136 | tf_op jit(solution)/shard_map/ppermute | solution.py:22
  93.5 10.1 %collective-permute-start.14 = (bf16[896,128]{1,0:T(8,128)(2,1)S(1)}, bf16[896,128]{1,0:T(8,128)(2,1)}, u32[]{:S(2)}, u32[]{:S(2)}) collective-permute-start(bf16[896,128]{1,0:T(8,128)(2,1)S(1)} %collective-permute-done.13.refs_5_), channel_id=1, source_target_pairs={{0,452},{64,0},{128,64},{192,128},{256,192},{320,256},{384,320},{4... | collective-permute-start | bytes 688136 | tf_op jit(solution)/shard_map/ppermute | solution.py:22
  95.4 10.1 %collective-permute-start.11 = (bf16[896,128]{1,0:T(8,128)(2,1)S(1)}, bf16[896,128]{1,0:T(8,128)(2,1)}, u32[]{:S(2)}, u32[]{:S(2)}) collective-permute-start(bf16[896,128]{1,0:T(8,128)(2,1)S(1)} %collective-permute-done.10.refs_1_), channel_id=1, source_target_pairs={{0,64},{64,128},{128,192},{192,256},{256,320},{320,384},{384,448},... | collective-permute-start | bytes 688136 | tf_op jit(solution)/shard_map/ppermute | solution.py:22
  103.5 10.7 %collective-permute-start.15 = (bf16[896,128]{1,0:T(8,128)(2,1)}, bf16[896,128]{1,0:T(8,128)(2,1)S(1)}, u32[]{:S(2)}, u32[]{:S(2)}) collective-permute-start(bf16[896,128]{1,0:T(8,128)(2,1)} %collective-permute-done.14.refs_6_), channel_id=1, source_target_pairs={{0,452},{64,0},{128,64},{192,128},{256,192},{320,256},{384,320},{4... | collective-permute-start | bytes 688136 | tf_op jit(solution)/shard_map/ppermute | solution.py:22
  114.6 15.1 %copy-start = (bf16[448,512]{1,0:T(8,128)(2,1)}, bf16[448,512]{1,0:T(8,128)(2,1)S(1)}, u32[]{:S(2)}) copy-start(bf16[448,512]{1,0:T(8,128)(2,1)S(1)} %get-tuple-element.57) | copy-start | bytes 1376260
  115.3 13.5 %collective-permute-start.16 = (bf16[512,512]{1,0:T(8,128)(2,1)S(1)}, bf16[512,512]{1,0:T(8,128)(2,1)S(1)}, u32[]{:S(2)}, u32[]{:S(2)}) collective-permute-start(bf16[512,512]{1,0:T(8,128)(2,1)S(1)} %get-tuple-element.50), channel_id=1, source_target_pairs={{0,8},{8,0},{1,9},{9,1},{2,10},{10,2},{3,11},{11,3},{4,12},{12,4},... | collective-permute-start | bytes 1572872 | tf_op jit(solution)/shard_map/ppermute | solution.py:61
  129.7 14.0 %all-to-all-start.2 = ((bf16[16,32,512]{2,1,0:T(8,128)(2,1)}), bf16[16,32,512]{2,1,0:T(8,128)(2,1)S(1)}, u32[]{:S(2)}, u32[]{:S(2)}) async-start(bf16[16,32,512]{2,1,0:T(8,128)(2,1)} %bitcast.5), calls=%async_computation.2 | async-start | bytes 1048576 | tf_op jit(solution)/shard_map/all_to_all | solution.py:242
  134.7 52.9 %collective-permute-start.18 = (bf16[448,512]{1,0:T(8,128)(2,1)}, bf16[448,512]{1,0:T(8,128)(2,1)S(1)}, u32[]{:S(2)}, u32[]{:S(2)}) collective-permute-start(bf16[448,512]{1,0:T(8,128)(2,1)} %copy-done), channel_id=1, source_target_pairs={{0,4},{4,0},{1,5},{5,1},{2,6},{6,2},{3,7},{7,3},{8,12},{12,8},{9,1... | collective-permute-start | bytes 1376264 | tf_op jit(solution)/shard_map/ppermute | solution.py:241
  144.5 9.0 %all-to-all-start.3 = ((bf16[128,2,1,224]{3,1,2,0:T(2,128)(2,1)}), bf16[128,2,1,224]{3,1,2,0:T(2,128)(2,1)S(1)}, u32[]{:S(2)}, u32[]{:S(2)}) async-start(bf16[128,2,1,224]{3,1,2,0:T(2,128)(2,1)} %copy.19), calls=%async_computation.3 | async-start | bytes 262144 | tf_op jit(solution)/shard_map/all_to_all | solution.py:248
  147.9 39.8 %collective-permute-start.17 = (bf16[32,512]{1,0:T(8,128)(2,1)S(1)}, bf16[32,512]{1,0:T(8,128)(2,1)S(1)}, u32[]{:S(2)}, u32[]{:S(2)}) collective-permute-start(bf16[32,512]{1,0:T(8,128)(2,1)S(1)} %reduce_sum.12), channel_id=1, source_target_pairs={{0,44},{16,52},{32,60},{48,0},{8,8},{24,16},{40,24},{56,32},{64,11... | collective-permute-start | bytes 98312 | tf_op jit(solution)/shard_map/ppermute | solution.py:247

commit v6 on v5

--- a/solution.py
+++ b/solution.py
@@ -54,7 +54,7 @@
 
 SMEM_SPEC = pl.BlockSpec(memory_space=pltpu.SMEM)
 VMEM_SPEC = pl.BlockSpec(memory_space=pltpu.VMEM)
-PARAMS = pltpu.CompilerParams(vmem_limit_bytes=32 << 20)
+PARAMS = pltpu.CompilerParams(vmem_limit_bytes=16 << 20)
 
 
 def swap_cores(value):
@@ -203,13 +203,13 @@
         partial.update(zip(offsets, forward_tiles(offsets, core, own_tokens, other_tokens, weights)))
     right = ring_shift(partial[7], 1)
     left = ring_shift(partial[0], -1)
-    right, left, cotangent = lax.optimization_barrier((right, left, cotangent))
     right = add_tiles(right, partial[6])
     left = add_tiles(left, partial[1])
     right = add_tiles(ring_shift(right, 1), partial[5])
     left = add_tiles(ring_shift(left, -1), partial[2])
     right = add_tiles(ring_shift(right, 1), partial[4])
     left = ring_shift(left, -1)
+    right, cotangent = lax.optimization_barrier((right, cotangent))
     right = ring_shift(right, 1)
     cotangent = cotangent.reshape(-1, 2 * part).T.astype(jnp.float32)
     total = partial[BEFORE].astype(jnp.float32) + left.astype(jnp.float32) + right.astype(jnp.float32)
@@ -235,22 +235,21 @@
     )
     keep, send = last_sums(core, half, own_tokens, other_tokens, sums, left_4)
     terms, send = lax.optimization_barrier((terms, send))
+    received = lax.ppermute(send, "h", [(0, 1), (1, 0)])
     keep_terms, send_terms = last_terms(core, weights, terms, left_4)
-
     terms = add_tiles(keep_terms, swap_cores(send_terms))
-    received = lax.ppermute(send, "h", [(0, 1), (1, 0)])
     terms = lax.all_to_all(
         terms.reshape(16, -1, features), ("y", "x"), split_axis=0, concat_axis=0, tiled=True
     )
     grad_tokens = jnp.sum(terms.astype(jnp.float32), 0).astype(jnp.bfloat16)
     grad_tokens, hidden = lax.optimization_barrier((grad_tokens, hidden))
-    grad_tokens = lax.ppermute(grad_tokens, ("r", "y", "c", "h"), result_pairs())
     hidden = lax.all_to_all(
         hidden.T.reshape(-1, 2, 1, part), "x", split_axis=0, concat_axis=2, tiled=True
-    ).reshape(-1, hidden_cols)
+    )
+    grad_tokens = lax.ppermute(grad_tokens, ("r", "y", "c", "h"), result_pairs())
     grad_tokens, hidden, keep = lax.optimization_barrier((grad_tokens, hidden, keep))
     grad_weights = keep + received.astype(jnp.float32)
-    return hidden, grad_tokens, grad_weights[:part].T, grad_weights[part:].T
+    return hidden.reshape(-1, hidden_cols), grad_tokens, grad_weights[:part].T, grad_weights[part:].T
 
 
 def solution(mesh):

time: 191 us -> 184 us (0.963)
  waiting for transfers between devices: 77.1 us -> 73.2 us
  other arithmetic: 5.65 us -> 3.08 us
    all_to_all x1, waiting for transfers between devices: 3.71 us -> 0.01 us  [local(): lax.all_to_all(cotangent, 'x', split_axis=0, concat_axis=0, tiled=True)]
    convert_element_type x6, other arithmetic: 3.81 us -> 1.25 us  [add_tiles(): sum((tile.astype(jnp.float32) for tile in tiles)).astype(jnp.bfloat16)]
    ppermute x1, waiting for transfers between devices: 33.2 us -> 35.7 us  [local(): lax.ppermute(grad_tokens, ('r', 'y', 'c', 'h'), result_pairs())]
    ppermute x14, waiting for transfers between devices: 15.6 us -> 13.5 us  [ring_shift(): return lax.ppermute(value, ('r', 'h'), pairs)]
  transfers between devices with their start and end apart: 23 -> 23, of which waited for: 13 -> 15; matrix products, arithmetic and copies ran while one was open for 4% -> 4% of each run, Pallas kernels for 3% -> 3%
where the time goes in v6:
time: 184 us; the launch traced here: 183 us
  starting transfers between devices  91.4 us (50%)
  waiting for transfers between devices  73.2 us (40%)
  local copies, waits for them, and re-layouts  8.13 us (4%)
  Pallas kernels  6.54 us (4%)
  other arithmetic  3.08 us (2%)
    ppermute x14, starting transfers between devices, ring_shift(): return lax.ppermute(value, ('r', 'h'), pairs)  49.2 us
    ppermute x1, waiting for transfers between devices, local(): lax.ppermute(grad_tokens, ('r', 'y', 'c', 'h'), result_pairs())  35.7 us
    ppermute x14, waiting for transfers between devices, ring_shift(): return lax.ppermute(value, ('r', 'h'), pairs)  13.5 us
    ppermute x2, starting transfers between devices, swap_cores(): return lax.ppermute(value, 'c', [(0, 1), (1, 0)])  12.9 us
    ppermute x1, waiting for transfers between devices, local(): piece = lax.ppermute(tokens, ('r', 'y', 'c', 'h'), token_pairs())  8.6 us
    all_to_all x1, starting transfers between devices, local(): lax.all_to_all(terms.reshape(16, -1, features), ('y', 'x'), split_axis=0,...  6.77 us
    all_to_all x1, waiting for transfers between devices, local(): lax.all_to_all(terms.reshape(16, -1, features), ('y', 'x'), split_axis=0,...  6.4 us
    all_to_all x1, waiting for transfers between devices, local(): lax.all_to_all(copies, ('y', 'x'), split_axis=0, concat_axis=0, tiled=True)  5.99 us
  transfers between devices with their start and end apart: 23, of which 15 were waited for; matrix products, arithmetic and copies ran while one was open for 4% of the time, Pallas kernels for 3%

profile of v6, /device:TPU:233, one launch (start us, length us, event | category | flops | bytes accessed | tf_op | source)
XLA Modules:
  0.0 183.3 jit_solution(3810597755215330504)
XLA Ops:
  0.6 2.1 %collective-permute-start = (bf16[32,512]{1,0:T(8,128)(2,1)}, bf16[32,512]{1,0:T(8,128)(2,1)S(1)}, u32[]{:S(2)}, u32[]{:S(2)}) collective-permute-start(bf16[32,512]{1,0:T(8,128)(2,1)} %param.4), channel_id=1, source_target_pairs={{324,0},{388,16},{452,32},{0,48},{64,8},{128,24},{192,40},{256,56}... | collective-permute-start | bytes 98312 | tf_op jit(solution)/shard_map/ppermute | solution.py:193
  2.7 8.6 %collective-permute-done = bf16[32,512]{1,0:T(8,128)(2,1)S(1)} collective-permute-done((bf16[32,512]{1,0:T(8,128)(2,1)}, bf16[32,512]{1,0:T(8,128)(2,1)S(1)}, u32[]{:S(2)}, u32[]{:S(2)}) %collective-permute-start) | collective-permute-done | bytes 32800 | tf_op jit(solution)/shard_map/ppermute | solution.py:193
  11.3 0.8 broadcast_in_dim.2
  12.2 5.3 %all-to-all-start = ((bf16[16,32,512]{2,1,0:T(8,128)(2,1)}), bf16[16,32,512]{2,1,0:T(8,128)(2,1)S(1)}, u32[]{:S(2)}, u32[]{:S(2)}) async-start(bf16[16,32,512]{2,1,0:T(8,128)(2,1)} %broadcast_in_dim.2), calls=%async_computation | async-start | bytes 1048576 | tf_op jit(solution)/shard_map/all_to_all | solution.py:195
  17.5 1.1 reshape.35
  18.6 0.8 copy.23
  19.4 1.8 constant_dynamic-slice_fusion.2
  21.2 0.4 pad_maximum_fusion.weights_ref
  21.6 6.0 %all-to-all-done = bf16[16,32,512]{2,1,0:T(8,128)(2,1)S(1)} async-done(((bf16[16,32,512]{2,1,0:T(8,128)(2,1)}), bf16[16,32,512]{2,1,0:T(8,128)(2,1)S(1)}, u32[]{:S(2)}, u32[]{:S(2)}) %all-to-all-start) | async-done | bytes 524320 | tf_op jit(solution)/shard_map/all_to_all | solution.py:195
  27.6 2.4 %collective-permute-start.1 = (bf16[512,512]{1,0:T(8,128)(2,1)S(1)}, bf16[512,512]{1,0:T(8,128)(2,1)S(1)}, u32[]{:S(2)}, u32[]{:S(2)}) collective-permute-start(bf16[512,512]{1,0:T(8,128)(2,1)S(1)} %bitcast.30), channel_id=1, source_target_pairs={{0,8},{8,0},{1,9},{9,1},{2,10},{10,2},{3,11},{11,3},{4,12},{12,4},... | collective-permute-start | bytes 1572872 | tf_op jit(solution)/shard_map/ppermute | solution.py:61
  30.0 1.5 collective-permute-done.1.other_ref
  31.5 0.6 shard_map.75
  32.1 6.6 %collective-permute-start.2 = (bf16[896,128]{1,0:T(8,128)(2,1)S(1)}, bf16[896,128]{1,0:T(8,128)(2,1)S(1)}, u32[]{:S(2)}, u32[]{:S(2)}) collective-permute-start(bf16[896,128]{1,0:T(8,128)(2,1)S(1)} %get-tuple-element.32), channel_id=1, source_target_pairs={{0,64},{64,128},{128,192},{192,256},{256,320},{320,384},{384,448},... | collective-permute-start | bytes 688136 | tf_op jit(solution)/shard_map/ppermute | solution.py:22
  38.7 3.6 %all-to-all-start.1 = ((bf16[4,32,2,224]{3,2,1,0:T(2,128)(2,1)}), bf16[4,32,2,224]{3,2,1,0:T(2,128)(2,1)S(1)}, u32[]{:S(2)}, u32[]{:S(2)}) async-start(bf16[4,32,2,224]{3,2,1,0:T(2,128)(2,1)} %bitcast.29), calls=%async_computation.1 | async-start | bytes 262144 | tf_op jit(solution)/shard_map/all_to_all | solution.py:200
  42.3 1.9 %collective-permute-start.5 = (bf16[896,128]{1,0:T(8,128)(2,1)S(1)}, bf16[896,128]{1,0:T(8,128)(2,1)S(1)}, u32[]{:S(2)}, u32[]{:S(2)}) collective-permute-start(bf16[896,128]{1,0:T(8,128)(2,1)S(1)} %get-tuple-element.39), channel_id=1, source_target_pairs={{0,452},{64,0},{128,64},{192,128},{256,192},{320,256},{384,320},{4... | collective-permute-start | bytes 688136 | tf_op jit(solution)/shard_map/ppermute | solution.py:22
  44.2 1.1 shard_map.76
  45.3 0.1 add_convert_fusion.5
  45.4 4.6 %collective-permute-start.3 = (bf16[896,128]{1,0:T(8,128)(2,1)S(1)}, bf16[896,128]{1,0:T(8,128)(2,1)S(1)}, u32[]{:S(2)}, u32[]{:S(2)}) collective-permute-start(bf16[896,128]{1,0:T(8,128)(2,1)S(1)} %add_convert_fusion.5), channel_id=1, source_target_pairs={{0,64},{64,128},{128,192},{192,256},{256,320},{320,384},{384,448},... | collective-permute-start | bytes 688136 | tf_op jit(solution)/shard_map/ppermute | solution.py:22
  50.0 1.6 collective-permute-done.5
  51.5 0.1 add_convert_fusion.2
  51.6 1.9 %collective-permute-start.6 = (bf16[896,128]{1,0:T(8,128)(2,1)S(1)}, bf16[896,128]{1,0:T(8,128)(2,1)S(1)}, u32[]{:S(2)}, u32[]{:S(2)}) collective-permute-start(bf16[896,128]{1,0:T(8,128)(2,1)S(1)} %add_convert_fusion.2), channel_id=1, source_target_pairs={{0,452},{64,0},{128,64},{192,128},{256,192},{320,256},{384,320},{4... | collective-permute-start | bytes 688136 | tf_op jit(solution)/shard_map/ppermute | solution.py:22
  53.5 0.1 collective-permute-done.3
  53.6 0.1 add_convert_fusion.4
  53.7 5.3 %collective-permute-start.4 = (bf16[896,128]{1,0:T(8,128)(2,1)S(1)}, bf16[896,128]{1,0:T(8,128)(2,1)S(1)}, u32[]{:S(2)}, u32[]{:S(2)}) collective-permute-start(bf16[896,128]{1,0:T(8,128)(2,1)S(1)} %add_convert_fusion.4), channel_id=1, source_target_pairs={{0,64},{64,128},{128,192},{192,256},{256,320},{320,384},{384,448},... | collective-permute-start | bytes 688136 | tf_op jit(solution)/shard_map/ppermute | solution.py:22
  59.0 0.9 collective-permute-done.6
  59.9 0.1 add_convert_fusion.1
  60.0 1.9 %collective-permute-start.7 = (bf16[896,128]{1,0:T(8,128)(2,1)S(1)}, bf16[896,128]{1,0:T(8,128)(2,1)S(1)}, u32[]{:S(2)}, u32[]{:S(2)}) collective-permute-start(bf16[896,128]{1,0:T(8,128)(2,1)S(1)} %add_convert_fusion.1), channel_id=1, source_target_pairs={{0,452},{64,0},{128,64},{192,128},{256,192},{320,256},{384,320},{4... | collective-permute-start | bytes 688136 | tf_op jit(solution)/shard_map/ppermute | solution.py:22
  62.0 5.0 %collective-permute-start.8 = (bf16[896,128]{1,0:T(8,128)(2,1)S(1)}, bf16[896,128]{1,0:T(8,128)(2,1)}, u32[]{:S(2)}, u32[]{:S(2)}) collective-permute-start(bf16[896,128]{1,0:T(8,128)(2,1)S(1)} %add_convert_fusion.3), channel_id=1, source_target_pairs={{0,64},{64,128},{128,192},{192,256},{256,320},{320,384},{384,448},... | collective-permute-start | bytes 688136 | tf_op jit(solution)/shard_map/ppermute | solution.py:22
  67.1 0.1 reshape.40
  67.2 0.1 copy.18
  67.3 0.7 collective-permute-done.7
  68.0 2.0 %collective-permute-done.8 = bf16[896,128]{1,0:T(8,128)(2,1)} collective-permute-done((bf16[896,128]{1,0:T(8,128)(2,1)S(1)}, bf16[896,128]{1,0:T(8,128)(2,1)}, u32[]{:S(2)}, u32[]{:S(2)}) %collective-permute-start.8) | collective-permute-done | bytes 229408 | tf_op jit(solution)/shard_map/ppermute | solution.py:22
  70.0 1.0 convert_add_fusion.1
  71.1 0.2 multiply_convert_fusion
  71.3 1.9 %collective-permute-start.12 = (bf16[896,128]{1,0:T(8,128)(2,1)S(1)}, bf16[896,128]{1,0:T(8,128)(2,1)S(1)}, u32[]{:S(2)}, u32[]{:S(2)}) collective-permute-start(bf16[896,128]{1,0:T(8,128)(2,1)S(1)} %pad_maximum_fusion.3.refs_3_), channel_id=1, source_target_pairs={{0,452},{64,0},{128,64},{192,128},{256,192},{320,256},{384,320},{4... | collective-permute-start | bytes 688136 | tf_op jit(solution)/shard_map/ppermute | solution.py:22
  73.2 5.1 %collective-permute-start.9 = (bf16[896,128]{1,0:T(8,128)(2,1)S(1)}, bf16[896,128]{1,0:T(8,128)(2,1)S(1)}, u32[]{:S(2)}, u32[]{:S(2)}) collective-permute-start(bf16[896,128]{1,0:T(8,128)(2,1)S(1)} %pad_maximum_fusion.3.refs_3_), channel_id=1, source_target_pairs={{0,64},{64,128},{128,192},{192,256},{256,320},{320,384},{384,448},... | collective-permute-start | bytes 688136 | tf_op jit(solution)/shard_map/ppermute | solution.py:22
  78.4 1.5 collective-permute-done.12.refs_4_
  79.8 1.9 %collective-permute-start.13 = (bf16[896,128]{1,0:T(8,128)(2,1)S(1)}, bf16[896,128]{1,0:T(8,128)(2,1)S(1)}, u32[]{:S(2)}, u32[]{:S(2)}) collective-permute-start(bf16[896,128]{1,0:T(8,128)(2,1)S(1)} %collective-permute-done.12.refs_4_), channel_id=1, source_target_pairs={{0,452},{64,0},{128,64},{192,128},{256,192},{320,256},{384,320},{4... | collective-permute-start | bytes 688136 | tf_op jit(solution)/shard_map/ppermute | solution.py:22
  81.8 4.6 %collective-permute-start.10 = (bf16[896,128]{1,0:T(8,128)(2,1)S(1)}, bf16[896,128]{1,0:T(8,128)(2,1)S(1)}, u32[]{:S(2)}, u32[]{:S(2)}) collective-permute-start(bf16[896,128]{1,0:T(8,128)(2,1)S(1)} %collective-permute-done.9.refs_2_), channel_id=1, source_target_pairs={{0,64},{64,128},{128,192},{192,256},{256,320},{320,384},{384,448},... | collective-permute-start | bytes 688136 | tf_op jit(solution)/shard_map/ppermute | solution.py:22
  86.3 1.5 collective-permute-done.13.refs_5_
  87.8 1.9 %collective-permute-start.14 = (bf16[896,128]{1,0:T(8,128)(2,1)S(1)}, bf16[896,128]{1,0:T(8,128)(2,1)}, u32[]{:S(2)}, u32[]{:S(2)}) collective-permute-start(bf16[896,128]{1,0:T(8,128)(2,1)S(1)} %collective-permute-done.13.refs_5_), channel_id=1, source_target_pairs={{0,452},{64,0},{128,64},{192,128},{256,192},{320,256},{384,320},{4... | collective-permute-start | bytes 688136 | tf_op jit(solution)/shard_map/ppermute | solution.py:22
  89.7 4.6 %collective-permute-start.11 = (bf16[896,128]{1,0:T(8,128)(2,1)S(1)}, bf16[896,128]{1,0:T(8,128)(2,1)}, u32[]{:S(2)}, u32[]{:S(2)}) collective-permute-start(bf16[896,128]{1,0:T(8,128)(2,1)S(1)} %collective-permute-done.10.refs_1_), channel_id=1, source_target_pairs={{0,64},{64,128},{128,192},{192,256},{256,320},{320,384},{384,448},... | collective-permute-start | bytes 688136 | tf_op jit(solution)/shard_map/ppermute | solution.py:22
  94.3 1.8 collective-permute-done.14.refs_6_
  96.1 1.9 %collective-permute-start.15 = (bf16[896,128]{1,0:T(8,128)(2,1)}, bf16[896,128]{1,0:T(8,128)(2,1)S(1)}, u32[]{:S(2)}, u32[]{:S(2)}) collective-permute-start(bf16[896,128]{1,0:T(8,128)(2,1)} %collective-permute-done.14.refs_6_), channel_id=1, source_target_pairs={{0,452},{64,0},{128,64},{192,128},{256,192},{320,256},{384,320},{4... | collective-permute-start | bytes 688136 | tf_op jit(solution)/shard_map/ppermute | solution.py:22
  98.1 3.8 %shard_map.77 = (bf16[896,512]{1,0:T(8,128)(2,1)S(1)}, f32[896,512]{1,0:T(8,128)S(1)}) custom-call(s32[1]{0:T(128)} %bitcast.core_ref, bf16[512,512]{1,0:T(8,128)(2,1)S(1)} %bitcast.33, bf16[512,512]{1,0:T(8,128)(2,1)S(1)} %collective-permute-done.1.other_ref, bf16[512,896]{1,0:T(8,128)(2,1)S(1)} %pad_maximum_fusion.weights_ref, ...), custom_call_target="tpu_custom_call" | custom-call | tf_op jit(solution)/shard_map/pallas_call | solution.py:103
  101.9 3.4 %collective-permute-done.15.tile_ref = bf16[896,128]{1,0:T(8,128)(2,1)S(1)} collective-permute-done((bf16[896,128]{1,0:T(8,128)(2,1)}, bf16[896,128]{1,0:T(8,128)(2,1)S(1)}, u32[]{:S(2)}, u32[]{:S(2)}) %collective-permute-start.15) | collective-permute-done | bytes 229408 | tf_op jit(solution)/shard_map/ppermute | solution.py:22
  105.3 0.4 shard_map.78
  105.7 0.6 shard_map.79
  106.4 10.5 %collective-permute-start.16 = (bf16[512,512]{1,0:T(8,128)(2,1)S(1)}, bf16[512,512]{1,0:T(8,128)(2,1)S(1)}, u32[]{:S(2)}, u32[]{:S(2)}) collective-permute-start(bf16[512,512]{1,0:T(8,128)(2,1)S(1)} %get-tuple-element.48), channel_id=1, source_target_pairs={{0,8},{8,0},{1,9},{9,1},{2,10},{10,2},{3,11},{11,3},{4,12},{12,4},... | collective-permute-start | bytes 1572872 | tf_op jit(solution)/shard_map/ppermute | solution.py:61
  116.9 1.5 collective-permute-done.16
  118.4 0.9 add_convert_fusion
  119.3 6.8 %all-to-all-start.2 = ((bf16[16,32,512]{2,1,0:T(8,128)(2,1)}), bf16[16,32,512]{2,1,0:T(8,128)(2,1)S(1)}, u32[]{:S(2)}, u32[]{:S(2)}) async-start(bf16[16,32,512]{2,1,0:T(8,128)(2,1)} %bitcast.5), calls=%async_computation.2 | async-start | bytes 1048576 | tf_op jit(solution)/shard_map/all_to_all | solution.py:241
  126.1 2.3 %collective-permute-start.18 = (bf16[448,512]{1,0:T(8,128)(2,1)}, bf16[448,512]{1,0:T(8,128)(2,1)S(1)}, u32[]{:S(2)}, u32[]{:S(2)}) collective-permute-start(bf16[448,512]{1,0:T(8,128)(2,1)} %copy-done), channel_id=1, source_target_pairs={{0,4},{4,0},{1,5},{5,1},{2,6},{6,2},{3,7},{7,3},{8,12},{12,8},{9,1... | collective-permute-start | bytes 1376264 | tf_op jit(solution)/shard_map/ppermute | solution.py:238
  128.4 6.4 %all-to-all-done.2 = bf16[16,32,512]{2,1,0:T(8,128)(2,1)S(1)} async-done(((bf16[16,32,512]{2,1,0:T(8,128)(2,1)}), bf16[16,32,512]{2,1,0:T(8,128)(2,1)S(1)}, u32[]{:S(2)}, u32[]{:S(2)}) %all-to-all-start.2) | async-done | bytes 524320 | tf_op jit(solution)/shard_map/all_to_all | solution.py:241
  134.8 0.1 reduce_sum.12
  134.9 0.8 copy.19
  135.7 3.3 %all-to-all-start.3 = ((bf16[128,2,1,224]{3,1,2,0:T(2,128)(2,1)}), bf16[128,2,1,224]{3,1,2,0:T(2,128)(2,1)S(1)}, u32[]{:S(2)}, u32[]{:S(2)}) async-start(bf16[128,2,1,224]{3,1,2,0:T(2,128)(2,1)} %copy.19), calls=%async_computation.3 | async-start | bytes 262144 | tf_op jit(solution)/shard_map/all_to_all | solution.py:246
  139.0 5.9 %collective-permute-start.17 = (bf16[32,512]{1,0:T(8,128)(2,1)S(1)}, bf16[32,512]{1,0:T(8,128)(2,1)S(1)}, u32[]{:S(2)}, u32[]{:S(2)}) collective-permute-start(bf16[32,512]{1,0:T(8,128)(2,1)S(1)} %reduce_sum.12), channel_id=1, source_target_pairs={{0,44},{16,52},{32,60},{48,0},{8,8},{24,16},{40,24},{56,32},{64,11... | collective-permute-start | bytes 98312 | tf_op jit(solution)/shard_map/ppermute | solution.py:249
  145.0 35.7 %collective-permute-done.17 = bf16[32,512]{1,0:T(8,128)(2,1)S(1)} collective-permute-done((bf16[32,512]{1,0:T(8,128)(2,1)S(1)}, bf16[32,512]{1,0:T(8,128)(2,1)S(1)}, u32[]{:S(2)}, u32[]{:S(2)}) %collective-permute-start.17) | collective-permute-done | bytes 32800 | tf_op jit(solution)/shard_map/ppermute | solution.py:249
  180.6 0.1 copy.21
  180.7 0.8 reshape.39
  181.6 0.1 convert_add_fusion
  181.7 1.0 slice_bitcast_fusion
  182.7 0.6 copy.25
  (16 shorter events, 0.2 us)
Async XLA Ops:
  0.6 10.7 %collective-permute-start = (bf16[32,512]{1,0:T(8,128)(2,1)}, bf16[32,512]{1,0:T(8,128)(2,1)S(1)}, u32[]{:S(2)}, u32[]{:S(2)}) collective-permute-start(bf16[32,512]{1,0:T(8,128)(2,1)} %param.4), channel_id=1, source_target_pairs={{324,0},{388,16},{452,32},{0,48},{64,8},{128,24},{192,40},{256,56}... | collective-permute-start | bytes 98312 | tf_op jit(solution)/shard_map/ppermute | solution.py:193
  12.2 15.4 %all-to-all-start = ((bf16[16,32,512]{2,1,0:T(8,128)(2,1)}), bf16[16,32,512]{2,1,0:T(8,128)(2,1)S(1)}, u32[]{:S(2)}, u32[]{:S(2)}) async-start(bf16[16,32,512]{2,1,0:T(8,128)(2,1)} %broadcast_in_dim.2), calls=%async_computation | async-start | bytes 1048576 | tf_op jit(solution)/shard_map/all_to_all | solution.py:195
  27.6 3.9 %collective-permute-start.1 = (bf16[512,512]{1,0:T(8,128)(2,1)S(1)}, bf16[512,512]{1,0:T(8,128)(2,1)S(1)}, u32[]{:S(2)}, u32[]{:S(2)}) collective-permute-start(bf16[512,512]{1,0:T(8,128)(2,1)S(1)} %bitcast.30), channel_id=1, source_target_pairs={{0,8},{8,0},{1,9},{9,1},{2,10},{10,2},{3,11},{11,3},{4,12},{12,4},... | collective-permute-start | bytes 1572872 | tf_op jit(solution)/shard_map/ppermute | solution.py:61
  32.1 13.2 %collective-permute-start.2 = (bf16[896,128]{1,0:T(8,128)(2,1)S(1)}, bf16[896,128]{1,0:T(8,128)(2,1)S(1)}, u32[]{:S(2)}, u32[]{:S(2)}) collective-permute-start(bf16[896,128]{1,0:T(8,128)(2,1)S(1)} %get-tuple-element.32), channel_id=1, source_target_pairs={{0,64},{64,128},{128,192},{192,256},{256,320},{320,384},{384,448},... | collective-permute-start | bytes 688136 | tf_op jit(solution)/shard_map/ppermute | solution.py:22
  38.7 23.3 %all-to-all-start.1 = ((bf16[4,32,2,224]{3,2,1,0:T(2,128)(2,1)}), bf16[4,32,2,224]{3,2,1,0:T(2,128)(2,1)S(1)}, u32[]{:S(2)}, u32[]{:S(2)}) async-start(bf16[4,32,2,224]{3,2,1,0:T(2,128)(2,1)} %bitcast.29), calls=%async_computation.1 | async-start | bytes 262144 | tf_op jit(solution)/shard_map/all_to_all | solution.py:200
  42.3 9.3 %collective-permute-start.5 = (bf16[896,128]{1,0:T(8,128)(2,1)S(1)}, bf16[896,128]{1,0:T(8,128)(2,1)S(1)}, u32[]{:S(2)}, u32[]{:S(2)}) collective-permute-start(bf16[896,128]{1,0:T(8,128)(2,1)S(1)} %get-tuple-element.39), channel_id=1, source_target_pairs={{0,452},{64,0},{128,64},{192,128},{256,192},{320,256},{384,320},{4... | collective-permute-start | bytes 688136 | tf_op jit(solution)/shard_map/ppermute | solution.py:22
  45.4 8.2 %collective-permute-start.3 = (bf16[896,128]{1,0:T(8,128)(2,1)S(1)}, bf16[896,128]{1,0:T(8,128)(2,1)S(1)}, u32[]{:S(2)}, u32[]{:S(2)}) collective-permute-start(bf16[896,128]{1,0:T(8,128)(2,1)S(1)} %add_convert_fusion.5), channel_id=1, source_target_pairs={{0,64},{64,128},{128,192},{192,256},{256,320},{320,384},{384,448},... | collective-permute-start | bytes 688136 | tf_op jit(solution)/shard_map/ppermute | solution.py:22
  51.6 8.4 %collective-permute-start.6 = (bf16[896,128]{1,0:T(8,128)(2,1)S(1)}, bf16[896,128]{1,0:T(8,128)(2,1)S(1)}, u32[]{:S(2)}, u32[]{:S(2)}) collective-permute-start(bf16[896,128]{1,0:T(8,128)(2,1)S(1)} %add_convert_fusion.2), channel_id=1, source_target_pairs={{0,452},{64,0},{128,64},{192,128},{256,192},{320,256},{384,320},{4... | collective-permute-start | bytes 688136 | tf_op jit(solution)/shard_map/ppermute | solution.py:22
  53.7 8.3 %collective-permute-start.4 = (bf16[896,128]{1,0:T(8,128)(2,1)S(1)}, bf16[896,128]{1,0:T(8,128)(2,1)S(1)}, u32[]{:S(2)}, u32[]{:S(2)}) collective-permute-start(bf16[896,128]{1,0:T(8,128)(2,1)S(1)} %add_convert_fusion.4), channel_id=1, source_target_pairs={{0,64},{64,128},{128,192},{192,256},{256,320},{320,384},{384,448},... | collective-permute-start | bytes 688136 | tf_op jit(solution)/shard_map/ppermute | solution.py:22
  60.0 8.0 %collective-permute-start.7 = (bf16[896,128]{1,0:T(8,128)(2,1)S(1)}, bf16[896,128]{1,0:T(8,128)(2,1)S(1)}, u32[]{:S(2)}, u32[]{:S(2)}) collective-permute-start(bf16[896,128]{1,0:T(8,128)(2,1)S(1)} %add_convert_fusion.1), channel_id=1, source_target_pairs={{0,452},{64,0},{128,64},{192,128},{256,192},{320,256},{384,320},{4... | collective-permute-start | bytes 688136 | tf_op jit(solution)/shard_map/ppermute | solution.py:22
  62.0 8.0 %collective-permute-start.8 = (bf16[896,128]{1,0:T(8,128)(2,1)S(1)}, bf16[896,128]{1,0:T(8,128)(2,1)}, u32[]{:S(2)}, u32[]{:S(2)}) collective-permute-start(bf16[896,128]{1,0:T(8,128)(2,1)S(1)} %add_convert_fusion.3), channel_id=1, source_target_pairs={{0,64},{64,128},{128,192},{192,256},{256,320},{320,384},{384,448},... | collective-permute-start | bytes 688136 | tf_op jit(solution)/shard_map/ppermute | solution.py:22
  71.3 8.5 %collective-permute-start.12 = (bf16[896,128]{1,0:T(8,128)(2,1)S(1)}, bf16[896,128]{1,0:T(8,128)(2,1)S(1)}, u32[]{:S(2)}, u32[]{:S(2)}) collective-permute-start(bf16[896,128]{1,0:T(8,128)(2,1)S(1)} %pad_maximum_fusion.3.refs_3_), channel_id=1, source_target_pairs={{0,452},{64,0},{128,64},{192,128},{256,192},{320,256},{384,320},{4... | collective-permute-start | bytes 688136 | tf_op jit(solution)/shard_map/ppermute | solution.py:22
  73.2 8.5 %collective-permute-start.9 = (bf16[896,128]{1,0:T(8,128)(2,1)S(1)}, bf16[896,128]{1,0:T(8,128)(2,1)S(1)}, u32[]{:S(2)}, u32[]{:S(2)}) collective-permute-start(bf16[896,128]{1,0:T(8,128)(2,1)S(1)} %pad_maximum_fusion.3.refs_3_), channel_id=1, source_target_pairs={{0,64},{64,128},{128,192},{192,256},{256,320},{320,384},{384,448},... | collective-permute-start | bytes 688136 | tf_op jit(solution)/shard_map/ppermute | solution.py:22
  79.8 8.0 %collective-permute-start.13 = (bf16[896,128]{1,0:T(8,128)(2,1)S(1)}, bf16[896,128]{1,0:T(8,128)(2,1)S(1)}, u32[]{:S(2)}, u32[]{:S(2)}) collective-permute-start(bf16[896,128]{1,0:T(8,128)(2,1)S(1)} %collective-permute-done.12.refs_4_), channel_id=1, source_target_pairs={{0,452},{64,0},{128,64},{192,128},{256,192},{320,256},{384,320},{4... | collective-permute-start | bytes 688136 | tf_op jit(solution)/shard_map/ppermute | solution.py:22
  81.8 8.0 %collective-permute-start.10 = (bf16[896,128]{1,0:T(8,128)(2,1)S(1)}, bf16[896,128]{1,0:T(8,128)(2,1)S(1)}, u32[]{:S(2)}, u32[]{:S(2)}) collective-permute-start(bf16[896,128]{1,0:T(8,128)(2,1)S(1)} %collective-permute-done.9.refs_2_), channel_id=1, source_target_pairs={{0,64},{64,128},{128,192},{192,256},{256,320},{320,384},{384,448},... | collective-permute-start | bytes 688136 | tf_op jit(solution)/shard_map/ppermute | solution.py:22
  87.8 8.3 %collective-permute-start.14 = (bf16[896,128]{1,0:T(8,128)(2,1)S(1)}, bf16[896,128]{1,0:T(8,128)(2,1)}, u32[]{:S(2)}, u32[]{:S(2)}) collective-permute-start(bf16[896,128]{1,0:T(8,128)(2,1)S(1)} %collective-permute-done.13.refs_5_), channel_id=1, source_target_pairs={{0,452},{64,0},{128,64},{192,128},{256,192},{320,256},{384,320},{4... | collective-permute-start | bytes 688136 | tf_op jit(solution)/shard_map/ppermute | solution.py:22
  89.7 8.3 %collective-permute-start.11 = (bf16[896,128]{1,0:T(8,128)(2,1)S(1)}, bf16[896,128]{1,0:T(8,128)(2,1)}, u32[]{:S(2)}, u32[]{:S(2)}) collective-permute-start(bf16[896,128]{1,0:T(8,128)(2,1)S(1)} %collective-permute-done.10.refs_1_), channel_id=1, source_target_pairs={{0,64},{64,128},{128,192},{192,256},{256,320},{320,384},{384,448},... | collective-permute-start | bytes 688136 | tf_op jit(solution)/shard_map/ppermute | solution.py:22
  96.1 9.2 %collective-permute-start.15 = (bf16[896,128]{1,0:T(8,128)(2,1)}, bf16[896,128]{1,0:T(8,128)(2,1)S(1)}, u32[]{:S(2)}, u32[]{:S(2)}) collective-permute-start(bf16[896,128]{1,0:T(8,128)(2,1)} %collective-permute-done.14.refs_6_), channel_id=1, source_target_pairs={{0,452},{64,0},{128,64},{192,128},{256,192},{320,256},{384,320},{4... | collective-permute-start | bytes 688136 | tf_op jit(solution)/shard_map/ppermute | solution.py:22
  105.7 13.6 %copy-start = (bf16[448,512]{1,0:T(8,128)(2,1)}, bf16[448,512]{1,0:T(8,128)(2,1)S(1)}, u32[]{:S(2)}) copy-start(bf16[448,512]{1,0:T(8,128)(2,1)S(1)} %get-tuple-element.55) | copy-start | bytes 1376260
  106.4 12.1 %collective-permute-start.16 = (bf16[512,512]{1,0:T(8,128)(2,1)S(1)}, bf16[512,512]{1,0:T(8,128)(2,1)S(1)}, u32[]{:S(2)}, u32[]{:S(2)}) collective-permute-start(bf16[512,512]{1,0:T(8,128)(2,1)S(1)} %get-tuple-element.48), channel_id=1, source_target_pairs={{0,8},{8,0},{1,9},{9,1},{2,10},{10,2},{3,11},{11,3},{4,12},{12,4},... | collective-permute-start | bytes 1572872 | tf_op jit(solution)/shard_map/ppermute | solution.py:61
  119.3 15.5 %all-to-all-start.2 = ((bf16[16,32,512]{2,1,0:T(8,128)(2,1)}), bf16[16,32,512]{2,1,0:T(8,128)(2,1)S(1)}, u32[]{:S(2)}, u32[]{:S(2)}) async-start(bf16[16,32,512]{2,1,0:T(8,128)(2,1)} %bitcast.5), calls=%async_computation.2 | async-start | bytes 1048576 | tf_op jit(solution)/shard_map/all_to_all | solution.py:241
  126.1 55.5 %collective-permute-start.18 = (bf16[448,512]{1,0:T(8,128)(2,1)}, bf16[448,512]{1,0:T(8,128)(2,1)S(1)}, u32[]{:S(2)}, u32[]{:S(2)}) collective-permute-start(bf16[448,512]{1,0:T(8,128)(2,1)} %copy-done), channel_id=1, source_target_pairs={{0,4},{4,0},{1,5},{5,1},{2,6},{6,2},{3,7},{7,3},{8,12},{12,8},{9,1... | collective-permute-start | bytes 1376264 | tf_op jit(solution)/shard_map/ppermute | solution.py:238
  135.7 9.3 %all-to-all-start.3 = ((bf16[128,2,1,224]{3,1,2,0:T(2,128)(2,1)}), bf16[128,2,1,224]{3,1,2,0:T(2,128)(2,1)S(1)}, u32[]{:S(2)}, u32[]{:S(2)}) async-start(bf16[128,2,1,224]{3,1,2,0:T(2,128)(2,1)} %copy.19), calls=%async_computation.3 | async-start | bytes 262144 | tf_op jit(solution)/shard_map/all_to_all | solution.py:246
  139.0 41.6 %collective-permute-start.17 = (bf16[32,512]{1,0:T(8,128)(2,1)S(1)}, bf16[32,512]{1,0:T(8,128)(2,1)S(1)}, u32[]{:S(2)}, u32[]{:S(2)}) collective-permute-start(bf16[32,512]{1,0:T(8,128)(2,1)S(1)} %reduce_sum.12), channel_id=1, source_target_pairs={{0,44},{16,52},{32,60},{48,0},{8,8},{24,16},{40,24},{56,32},{64,11... | collective-permute-start | bytes 98312 | tf_op jit(solution)/shard_map/ppermute | solution.py:249

commit v7 on v6

v7 whole, which is shorter than its diff:
```python
import functools

import jax
import jax.numpy as jnp
from jax import lax
from jax.experimental import pallas as pl
from jax.experimental.pallas import tpu as pltpu
from jax.sharding import Mesh, PartitionSpec as P

RING = 16
ROWS = 8
BEFORE = 3


def ring_index(z):
    z %= RING
    return (z % ROWS) * 2 + z // ROWS


def ring_shift(value, step):
    pairs = [(ring_index(z), ring_index(z + step)) for z in range(RING)]
    return lax.ppermute(value, ("r", "h"), pairs)


def place(z, col):
    z %= RING
    return ((z % ROWS) * ROWS + col) * 2 + z // ROWS


def slot(offset):
    return (offset % 4) * 2 + offset // 4


def token_pairs(away):
    pairs = []
    for z in range(RING):
        for offset in range(ROWS):
            pairs.append((place(z + offset - BEFORE, z % ROWS), place(z + away, slot(offset))))
    return pairs


def result_pairs():
    pairs = []
    for z in range(RING):
        for offset in range(ROWS):
            tile = (z + offset - BEFORE) % RING
            pairs.append((place(z, slot(offset)), place(z % ROWS + ROWS * (tile // ROWS), tile % ROWS)))
    return pairs


def dot_f32(left, right, dims=((1,), (0,))):
    return lax.dot_general(left, right, (dims, ((), ())), preferred_element_type=jnp.float32)


SMEM_SPEC = pl.BlockSpec(memory_space=pltpu.SMEM)
VMEM_SPEC = pl.BlockSpec(memory_space=pltpu.VMEM)
PARAMS = pltpu.CompilerParams(vmem_limit_bytes=16 << 20)


def swap_cores(value):
    return lax.ppermute(value, "c", [(0, 1), (1, 0)])


def join_cores(core, own_ref, other_ref, both_ref):
    rows = own_ref.shape[0]
    both_ref[pl.ds(pl.multiple_of(core * rows, rows), rows), :] = own_ref[...]
    both_ref[pl.ds(pl.multiple_of((1 - core) * rows, rows), rows), :] = other_ref[...]


def forward_kernel(offsets, core_ref, own_ref, other_ref, weights_ref, tokens_ref, *refs):
    join_cores(core_ref[0], own_ref, other_ref, tokens_ref)
    for offset, tile_ref in zip(offsets, refs):
        product = dot_f32(tokens_ref[offset * 128 : (offset + 1) * 128, :], weights_ref[...])
        tile_ref[...] = product.T.astype(jnp.bfloat16)


def forward_tiles(offsets, core, own, other, weights):
    features, cols = weights.shape
    tokens = jax.ShapeDtypeStruct((ROWS * 128, features), jnp.bfloat16)
    return pl.pallas_call(
        functools.partial(forward_kernel, offsets),
        in_specs=[SMEM_SPEC] + [VMEM_SPEC] * 3,
        out_specs=[VMEM_SPEC] * (1 + len(offsets)),
        out_shape=[tokens] + [jax.ShapeDtypeStruct((cols, 128), jnp.bfloat16)] * len(offsets),
        compiler_params=PARAMS,
    )(core, own, other, weights)


def step_kernel(rows_at, has_terms, has_sums, outs, half_ref, *refs):
    count = len(rows_at)
    refs = list(refs)
    weights_ref = refs.pop(0) if has_terms else None
    sums_ref = refs.pop(0) if has_sums else None
    token_refs, tile_refs = refs[:count], refs[count : 2 * count]
    tokens_ref, wide_ref = refs[-2:]
    out_refs = refs[2 * count : -2]
    rows = wide_ref.shape[0]
    own_rows = pl.ds(pl.multiple_of(half_ref[0] * rows, 16), rows)
    for at, (first, token_ref, tile_ref) in enumerate(zip(rows_at, token_refs, tile_refs)):
        tokens_ref[at * 128 : (at + 1) * 128, :] = token_ref[first : first + 128, :]
        wide_ref[:, at * 128 : (at + 1) * 128] = tile_ref[own_rows, :]
        if has_terms:
            product = dot_f32(weights_ref[...], tile_ref[...])
            out_refs[outs][at * 128 : (at + 1) * 128, :] = product.T.astype(jnp.bfloat16)
    total = dot_f32(wide_ref[...], tokens_ref[...])
    if has_sums:
        total = total + sums_ref[...]
    rows = rows // outs
    for at, out_ref in enumerate(out_refs[:outs]):
        out_ref[...] = total[at * rows : (at + 1) * rows, :]


def step_products(half, parts, weights=None, sums=None, outs=1):
    tokens = [part[0] for part in parts]
    tiles = [part[2] for part in parts]
    features = tokens[0].shape[1]
    rows = tiles[0].shape[0] // 2
    more = [value for value in (weights, sums) if value is not None]
    shapes = [jax.ShapeDtypeStruct((rows // outs, features), jnp.float32)] * outs
    if weights is not None:
        shapes.append(jax.ShapeDtypeStruct((128 * len(parts), features), jnp.bfloat16))
    rows_at = tuple(part[1] for part in parts)
    return pl.pallas_call(
        functools.partial(step_kernel, rows_at, weights is not None, sums is not None, outs),
        in_specs=[SMEM_SPEC] + [VMEM_SPEC] * (len(more) + 2 * len(parts)),
        out_specs=[VMEM_SPEC] * len(shapes),
        out_shape=shapes,
        scratch_shapes=[
            pltpu.VMEM((128 * len(parts), features), jnp.bfloat16),
            pltpu.VMEM((rows, 128 * len(parts)), jnp.bfloat16),
        ],
        compiler_params=PARAMS,
    )(half, *more, *tokens, *tiles)


def last_terms_kernel(offsets, weights_ref, tile_ref, *refs):
    all_ref = refs[-1]
    for term_ref, term_offsets in zip(refs, offsets):
        for at, offset in enumerate(term_offsets):
            all_ref[slot(offset) * 128 : (slot(offset) + 1) * 128, :] = term_ref[at * 128 : (at + 1) * 128, :]
    all_ref[896:1024, :] = dot_f32(weights_ref[...], tile_ref[...]).T.astype(jnp.bfloat16)


def last_terms(weights, tile, terms, offsets):
    return pl.pallas_call(
        functools.partial(last_terms_kernel, offsets),
        in_specs=[VMEM_SPEC] * (2 + len(terms)),
        out_specs=VMEM_SPEC,
        out_shape=jax.ShapeDtypeStruct((ROWS * 128, weights.shape[0]), jnp.bfloat16),
        compiler_params=PARAMS,
    )(weights, tile, *terms)


def gather_plane(piece):
    copies = jnp.broadcast_to(piece[None], (16,) + piece.shape)
    pieces = lax.all_to_all(copies, ("y", "x"), split_axis=0, concat_axis=0, tiled=True)
    return pieces.reshape(16 * piece.shape[0], piece.shape[1])


def add_tiles(*tiles):
    return sum(tile.astype(jnp.float32) for tile in tiles).astype(jnp.bfloat16)


def local(tokens, gate_weight, up_weight, grad_hidden):
    own_x = lax.axis_index("x")
    core = lax.axis_index("c").astype(jnp.int32).reshape(1)
    half = lax.axis_index("h").astype(jnp.int32).reshape(1)
    features, hidden_cols = gate_weight.shape
    part = hidden_cols // 8

    def own_columns(weight, which):
        return lax.dynamic_slice(weight, (0, (which * 4 + own_x) * part), (features, part))

    weights = jnp.concatenate(
        [own_columns(weight, which) for which in (0, 1) for weight in (gate_weight, up_weight)], 1
    )

    piece = lax.ppermute(tokens, ("r", "y", "c", "h"), token_pairs(0))
    far_piece = lax.ppermute(tokens, ("r", "y", "c", "h"), token_pairs(8))
    own_tokens = gather_plane(piece)
    cotangent = grad_hidden.reshape(-1, 2, 4, part).transpose(2, 0, 1, 3)
    own_tokens, far_piece, cotangent, weights = lax.optimization_barrier(
        (own_tokens, far_piece, cotangent, weights)
    )
    other_tokens = swap_cores(own_tokens)
    cotangent = lax.all_to_all(cotangent, "x", split_axis=0, concat_axis=0, tiled=True)
    partial = {}
    for offsets in ((7, 0), (6, 1, 5, 2, 4, 3)):
        near_tokens, *products = forward_tiles(offsets, core, own_tokens, other_tokens, weights)
        partial.update(zip(offsets, products))
    right = ring_shift(partial[7], 1)
    left = ring_shift(partial[0], -1)
    right = add_tiles(right, partial[6])
    left = add_tiles(left, partial[1])
    right = add_tiles(ring_shift(right, 1), partial[5])
    left = add_tiles(ring_shift(left, -1), partial[2])
    right = add_tiles(ring_shift(right, 1), partial[4])
    left = ring_shift(left, -1)
    far_own = gather_plane(far_piece)
    right, cotangent = lax.optimization_barrier((right, cotangent))
    right = ring_shift(right, 1)
    right, left, far_own = lax.optimization_barrier((right, left, far_own))
    far_other = swap_cores(far_own)
    cotangent = cotangent.reshape(-1, 2 * part).T.astype(jnp.float32)
    total = partial[BEFORE].astype(jnp.float32) + left.astype(jnp.float32) + right.astype(jnp.float32)
    gate_pre = jnp.concatenate([total[:part], total[2 * part : 3 * part]], 0)
    up_pre = jnp.concatenate([total[part : 2 * part], total[3 * part :]], 0)

    sigmoid = jax.nn.sigmoid(gate_pre)
    silu = gate_pre * sigmoid
    hidden = (silu * up_pre).astype(jnp.bfloat16)
    grad_gate = (cotangent * up_pre * sigmoid * (1.0 + gate_pre * (1.0 - sigmoid))).astype(jnp.bfloat16)
    grad_up = (cotangent * silu).astype(jnp.bfloat16)
    grads = jnp.concatenate([grad_gate[:part], grad_up[:part], grad_gate[part:], grad_up[part:]], 0)

    far_tokens = jnp.where(
        core[0] == 0, jnp.concatenate([far_own, far_other], 0), jnp.concatenate([far_other, far_own], 0)
    )
    left = right = grads
    parts = [(near_tokens, BEFORE * 128, grads)]
    terms = []
    offsets = ((3, 4, 2), (5, 1), (6, 0))
    sums = None
    for step in range(1, 4):
        left = ring_shift(left, -1)
        right = ring_shift(right, 1)
        parts += [(near_tokens, (BEFORE + step) * 128, left), (near_tokens, (BEFORE - step) * 128, right)]
        sums, step_terms = step_products(half, parts, weights, sums)
        terms.append(step_terms)
        parts = []
    left = ring_shift(left, -1)
    right = ring_shift(right, 1)
    parts = [(near_tokens, 7 * 128, left), (far_tokens, 7 * 128, right)]
    terms = last_terms(weights, left, terms, offsets)
    left, right, terms = lax.optimization_barrier((left, right, terms))
    terms = lax.all_to_all(
        terms.reshape(32, -1, features), ("y", "c", "x"), split_axis=0, concat_axis=0, tiled=True
    )
    for step in range(5, 9):
        left = ring_shift(left, -1)
        parts.append((far_tokens, (step - 5) * 128, left))
        if step < 8:
            right = ring_shift(right, 1)
            parts.append((far_tokens, (11 - step) * 128, right))
        if step < 7:
            (sums,) = step_products(half, parts, sums=sums)
            parts = []
        if step == 6:
            left, right, terms = lax.optimization_barrier((left, right, terms))
            grad_tokens = jnp.sum(terms.astype(jnp.float32), 0).astype(jnp.bfloat16)
            grad_tokens = lax.ppermute(grad_tokens, ("r", "y", "c", "h"), result_pairs())
            left, hidden = lax.optimization_barrier((left, hidden))
            hidden = lax.all_to_all(
                hidden.T.reshape(-1, 2, 1, part), "x", split_axis=0, concat_axis=2, tiled=True
            )
    gate_grad, up_grad = step_products(half, parts, sums=sums, outs=2)
    return hidden.reshape(-1, hidden_cols), grad_tokens, gate_grad.T, up_grad.T


def solution(mesh):
    fine = Mesh(mesh.devices.reshape(8, 4, 2, 2, 4), ("r", "y", "c", "h", "x"))
    return jax.shard_map(
        local,
        mesh=fine,
        in_specs=(
            P(("r", "h", "x"), ("y", "c")),
            P("r", ("y", "c")),
            P("r", ("y", "c")),
            P(("r", "h", "x"), ("y", "c")),
        ),
        out_specs=(
            P(("r", "h", "x"), ("y", "c")),
            P(("y", "c", "h", "x"), "r"),
            P("r", ("y", "c", "h", "x")),
            P("r", ("y", "c", "h", "x")),
        ),
        check_vma=False,
    )
```

time: 184 us -> 217 us (1.18)
  the two profiles are of different devices: /device:TPU:233 before, /device:TPU:10 now
where the time goes in v7:
time: 217 us; the launch traced here: 215 us
  starting transfers between devices  132 us (61%)
  waiting for transfers between devices  44.9 us (21%)
  local copies, waits for them, and re-layouts  13.9 us (6%)
  Pallas kernels  11.8 us (5%)
  other arithmetic  11.5 us (5%)
    ppermute x22, starting transfers between devices, ring_shift(): return lax.ppermute(value, ('r', 'h'), pairs)  67.7 us
    ppermute x22, waiting for transfers between devices, ring_shift(): return lax.ppermute(value, ('r', 'h'), pairs)  32 us
    all_to_all x2, starting transfers between devices, gather_plane(): lax.all_to_all(copies, ('y', 'x'), split_axis=0, concat_axis=0, tiled=True)  18.7 us
    ppermute x1, starting transfers between devices, local(): lax.ppermute(grad_tokens, ('r', 'y', 'c', 'h'), result_pairs())  12.1 us
    ppermute x1, waiting for transfers between devices, local(): piece = lax.ppermute(tokens, ('r', 'y', 'c', 'h'), token_pairs(0))  8.64 us
    pallas_call x6, Pallas kernels, step_products(): pl.pallas_call(functools.partial(step_kernel, rows_at, weights is not Non...  7.71 us
    all_to_all x1, starting transfers between devices, local(): lax.all_to_all(terms.reshape(32, -1, features), ('y', 'c', 'x'), split_ax...  7.42 us
    ppermute x1, starting transfers between devices, local(): far_piece = lax.ppermute(tokens, ('r', 'y', 'c', 'h'), token_pairs(8))  6.99 us
  transfers between devices with their start and end apart: 32, of which 15 were waited for; matrix products, arithmetic and copies ran while one was open for 8% of the time, Pallas kernels for 4%

profile of v7, /device:TPU:10, one launch (start us, length us, event | category | flops | bytes accessed | tf_op | source)
XLA Modules:
  0.0 214.8 jit_solution(6755448435145073197)
XLA Ops:
  0.6 5.2 %collective-permute-start = (bf16[32,512]{1,0:T(8,128)(2,1)}, bf16[32,512]{1,0:T(8,128)(2,1)S(1)}, u32[]{:S(2)}, u32[]{:S(2)}) collective-permute-start(bf16[32,512]{1,0:T(8,128)(2,1)} %param.4), channel_id=1, source_target_pairs={{324,0},{388,16},{452,32},{0,48},{64,8},{128,24},{192,40},{256,56}... | collective-permute-start | bytes 98312 | tf_op jit(solution)/shard_map/ppermute | solution.py:178
  5.8 8.6 %collective-permute-done = bf16[32,512]{1,0:T(8,128)(2,1)S(1)} collective-permute-done((bf16[32,512]{1,0:T(8,128)(2,1)}, bf16[32,512]{1,0:T(8,128)(2,1)S(1)}, u32[]{:S(2)}, u32[]{:S(2)}) %collective-permute-start) | collective-permute-done | bytes 32800 | tf_op jit(solution)/shard_map/ppermute | solution.py:178
  14.5 0.9 broadcast_in_dim.4
  15.3 8.7 %all-to-all-start = ((bf16[16,32,512]{2,1,0:T(8,128)(2,1)}), bf16[16,32,512]{2,1,0:T(8,128)(2,1)S(1)}, u32[]{:S(2)}, u32[]{:S(2)}) async-start(bf16[16,32,512]{2,1,0:T(8,128)(2,1)} %broadcast_in_dim.4), calls=%async_computation | async-start | bytes 1048576 | tf_op jit(solution)/shard_map/all_to_all | solution.py:156
  24.0 7.0 %collective-permute-start.1 = (bf16[32,512]{1,0:T(8,128)(2,1)}, bf16[32,512]{1,0:T(8,128)(2,1)S(1)}, u32[]{:S(2)}, u32[]{:S(2)}) collective-permute-start(bf16[32,512]{1,0:T(8,128)(2,1)} %param.4), channel_id=1, source_target_pairs={{324,4},{388,20},{452,36},{0,52},{64,12},{128,28},{192,44},{256,60... | collective-permute-start | bytes 98312 | tf_op jit(solution)/shard_map/ppermute | solution.py:179
  31.0 1.8 constant_dynamic-slice_fusion.2
  34.3 2.4 %collective-permute-done.1 = bf16[32,512]{1,0:T(8,128)(2,1)S(1)} collective-permute-done((bf16[32,512]{1,0:T(8,128)(2,1)}, bf16[32,512]{1,0:T(8,128)(2,1)S(1)}, u32[]{:S(2)}, u32[]{:S(2)}) %collective-permute-start.1) | collective-permute-done | bytes 32800 | tf_op jit(solution)/shard_map/ppermute | solution.py:179
  36.7 1.9 collective-permute-start.2
  38.6 1.9 collective-permute-done.2.other_ref
  40.4 1.5 shard_map.75
  41.9 2.4 %collective-permute-start.3 = (bf16[896,128]{1,0:T(8,128)(2,1)}, bf16[896,128]{1,0:T(8,128)(2,1)}, u32[]{:S(2)}, u32[]{:S(2)}) collective-permute-start(bf16[896,128]{1,0:T(8,128)(2,1)} %get-tuple-element.40), channel_id=1, source_target_pairs={{0,64},{64,128},{128,192},{192,256},{256,320},{320,384},{384,448},... | collective-permute-start | bytes 688136 | tf_op jit(solution)/shard_map/ppermute | solution.py:22
  44.4 4.8 %all-to-all-start.1 = ((bf16[4,32,2,224]{3,2,1,0:T(2,128)(2,1)}), bf16[4,32,2,224]{3,2,1,0:T(2,128)(2,1)S(1)}, u32[]{:S(2)}, u32[]{:S(2)}) async-start(bf16[4,32,2,224]{3,2,1,0:T(2,128)(2,1)} %bitcast.28), calls=%async_computation.1 | async-start | bytes 262144 | tf_op jit(solution)/shard_map/all_to_all | solution.py:186
  49.2 5.3 %collective-permute-start.7 = (bf16[896,128]{1,0:T(8,128)(2,1)}, bf16[896,128]{1,0:T(8,128)(2,1)S(1)}, u32[]{:S(2)}, u32[]{:S(2)}) collective-permute-start(bf16[896,128]{1,0:T(8,128)(2,1)} %get-tuple-element.48), channel_id=1, source_target_pairs={{0,452},{64,0},{128,64},{192,128},{256,192},{320,256},{384,320},{4... | collective-permute-start | bytes 688136 | tf_op jit(solution)/shard_map/ppermute | solution.py:22
  54.5 1.1 shard_map.76
  56.3 1.1 add_convert_fusion.4
  57.4 1.9 collective-permute-start.4
  60.2 5.5 %collective-permute-start.8 = (bf16[896,128]{1,0:T(8,128)(2,1)}, bf16[896,128]{1,0:T(8,128)(2,1)}, u32[]{:S(2)}, u32[]{:S(2)}) collective-permute-start(bf16[896,128]{1,0:T(8,128)(2,1)} %add_convert_fusion.1), channel_id=1, source_target_pairs={{0,452},{64,0},{128,64},{192,128},{256,192},{320,256},{384,320},{4... | collective-permute-start | bytes 688136 | tf_op jit(solution)/shard_map/ppermute | solution.py:22
  65.7 1.8 collective-permute-done.4
  68.2 1.9 collective-permute-start.5
  70.1 0.9 broadcast_in_dim.5
  71.0 10.0 %all-to-all-start.2 = ((bf16[16,32,512]{2,1,0:T(8,128)(2,1)}), bf16[16,32,512]{2,1,0:T(8,128)(2,1)S(1)}, u32[]{:S(2)}, u32[]{:S(2)}) async-start(bf16[16,32,512]{2,1,0:T(8,128)(2,1)} %broadcast_in_dim.5), calls=%async_computation.2 | async-start | bytes 1048576 | tf_op jit(solution)/shard_map/all_to_all | solution.py:156
  81.0 1.7 add_convert_fusion
  82.7 5.1 %collective-permute-start.9 = (bf16[896,128]{1,0:T(8,128)(2,1)}, bf16[896,128]{1,0:T(8,128)(2,1)}, u32[]{:S(2)}, u32[]{:S(2)}) collective-permute-start(bf16[896,128]{1,0:T(8,128)(2,1)} %add_convert_fusion), channel_id=1, source_target_pairs={{0,452},{64,0},{128,64},{192,128},{256,192},{320,256},{384,320},{4... | collective-permute-start | bytes 688136 | tf_op jit(solution)/shard_map/ppermute | solution.py:22
  87.9 1.7 add_convert_fusion.2
  89.6 1.9 collective-permute-start.6
  91.6 0.8 copy.18
  92.4 6.6 %collective-permute-done.6 = bf16[896,128]{1,0:T(8,128)(2,1)} collective-permute-done((bf16[896,128]{1,0:T(8,128)(2,1)}, bf16[896,128]{1,0:T(8,128)(2,1)}, u32[]{:S(2)}, u32[]{:S(2)}) %collective-permute-start.6) | collective-permute-done | bytes 229408 | tf_op jit(solution)/shard_map/ppermute | solution.py:22
  99.0 1.1 convert_add_fusion
  101.0 1.9 collective-permute-start.10
  103.0 3.9 %collective-permute-start.14 = (bf16[896,128]{1,0:T(8,128)(2,1)S(1)}, bf16[896,128]{1,0:T(8,128)(2,1)S(1)}, u32[]{:S(2)}, u32[]{:S(2)}) collective-permute-start(bf16[896,128]{1,0:T(8,128)(2,1)S(1)} %pad_maximum_fusion.3.refs_4_), channel_id=1, source_target_pairs={{0,64},{64,128},{128,192},{192,256},{256,320},{320,384},{384,448},... | collective-permute-start | bytes 688136 | tf_op jit(solution)/shard_map/ppermute | solution.py:22
  106.9 2.8 %collective-permute-done.10.refs_5_ = bf16[896,128]{1,0:T(8,128)(2,1)S(1)} collective-permute-done((bf16[896,128]{1,0:T(8,128)(2,1)S(1)}, bf16[896,128]{1,0:T(8,128)(2,1)S(1)}, u32[]{:S(2)}, u32[]{:S(2)}) %collective-permute-start.10) | collective-permute-done | bytes 229408 | tf_op jit(solution)/shard_map/ppermute | solution.py:22
  109.7 2.3 %collective-permute-start.11 = (bf16[896,128]{1,0:T(8,128)(2,1)S(1)}, bf16[896,128]{1,0:T(8,128)(2,1)S(1)}, u32[]{:S(2)}, u32[]{:S(2)}) collective-permute-start(bf16[896,128]{1,0:T(8,128)(2,1)S(1)} %collective-permute-done.10.refs_5_), channel_id=1, source_target_pairs={{0,452},{64,0},{128,64},{192,128},{256,192},{320,256},{384,320},{4... | collective-permute-start | bytes 688136 | tf_op jit(solution)/shard_map/ppermute | solution.py:22
  112.1 3.5 %collective-permute-start.15 = (bf16[896,128]{1,0:T(8,128)(2,1)S(1)}, bf16[896,128]{1,0:T(8,128)(2,1)S(1)}, u32[]{:S(2)}, u32[]{:S(2)}) collective-permute-start(bf16[896,128]{1,0:T(8,128)(2,1)S(1)} %collective-permute-done.14.refs_6_), channel_id=1, source_target_pairs={{0,64},{64,128},{128,192},{192,256},{256,320},{320,384},{384,448},... | collective-permute-start | bytes 688136 | tf_op jit(solution)/shard_map/ppermute | solution.py:22
  115.6 3.7 %collective-permute-done.11.refs_4_ = bf16[896,128]{1,0:T(8,128)(2,1)S(1)} collective-permute-done((bf16[896,128]{1,0:T(8,128)(2,1)S(1)}, bf16[896,128]{1,0:T(8,128)(2,1)S(1)}, u32[]{:S(2)}, u32[]{:S(2)}) %collective-permute-start.11) | collective-permute-done | bytes 229408 | tf_op jit(solution)/shard_map/ppermute | solution.py:22
  119.3 2.3 %collective-permute-start.12 = (bf16[896,128]{1,0:T(8,128)(2,1)S(1)}, bf16[896,128]{1,0:T(8,128)(2,1)}, u32[]{:S(2)}, u32[]{:S(2)}) collective-permute-start(bf16[896,128]{1,0:T(8,128)(2,1)S(1)} %collective-permute-done.11.refs_4_), channel_id=1, source_target_pairs={{0,452},{64,0},{128,64},{192,128},{256,192},{320,256},{384,320},{4... | collective-permute-start | bytes 688136 | tf_op jit(solution)/shard_map/ppermute | solution.py:22
  121.9 3.2 %collective-permute-start.16 = (bf16[896,128]{1,0:T(8,128)(2,1)S(1)}, bf16[896,128]{1,0:T(8,128)(2,1)}, u32[]{:S(2)}, u32[]{:S(2)}) collective-permute-start(bf16[896,128]{1,0:T(8,128)(2,1)S(1)} %collective-permute-done.15.refs_5_), channel_id=1, source_target_pairs={{0,64},{64,128},{128,192},{192,256},{256,320},{320,384},{384,448},... | collective-permute-start | bytes 688136 | tf_op jit(solution)/shard_map/ppermute | solution.py:22
  125.9 3.8 %collective-permute-done.12.refs_4_ = bf16[896,128]{1,0:T(8,128)(2,1)} collective-permute-done((bf16[896,128]{1,0:T(8,128)(2,1)S(1)}, bf16[896,128]{1,0:T(8,128)(2,1)}, u32[]{:S(2)}, u32[]{:S(2)}) %collective-permute-start.12) | collective-permute-done | bytes 229408 | tf_op jit(solution)/shard_map/ppermute | solution.py:22
  129.6 2.5 %collective-permute-start.13 = (bf16[896,128]{1,0:T(8,128)(2,1)}, bf16[896,128]{1,0:T(8,128)(2,1)S(1)}, u32[]{:S(2)}, u32[]{:S(2)}) collective-permute-start(bf16[896,128]{1,0:T(8,128)(2,1)} %collective-permute-done.12.refs_4_), channel_id=1, source_target_pairs={{0,452},{64,0},{128,64},{192,128},{256,192},{320,256},{384,320},{4... | collective-permute-start | bytes 688136 | tf_op jit(solution)/shard_map/ppermute | solution.py:22
  132.7 2.9 %collective-permute-start.17 = (bf16[896,128]{1,0:T(8,128)(2,1)}, bf16[896,128]{1,0:T(8,128)(2,1)S(1)}, u32[]{:S(2)}, u32[]{:S(2)}) collective-permute-start(bf16[896,128]{1,0:T(8,128)(2,1)} %collective-permute-done.16.refs_5_), channel_id=1, source_target_pairs={{0,64},{64,128},{128,192},{192,256},{256,320},{320,384},{384,448},... | collective-permute-start | bytes 688136 | tf_op jit(solution)/shard_map/ppermute | solution.py:22
  135.6 1.1 shard_map.77
  137.5 1.8 shard_map.79
  139.3 1.5 shard_map.80
  140.8 1.2 collective-permute-done.17.refs_6_
  142.1 7.4 %all-to-all-start.3 = ((bf16[32,32,512]{2,1,0:T(8,128)(2,1)}), bf16[32,32,512]{2,1,0:T(8,128)(2,1)}, u32[]{:S(2)}, u32[]{:S(2)}) async-start(bf16[32,32,512]{2,1,0:T(8,128)(2,1)} %bitcast.6), calls=%async_computation.3 | async-start | bytes 2097152 | tf_op jit(solution)/shard_map/all_to_all | solution.py:236
  149.5 3.1 %collective-permute-start.18 = (bf16[896,128]{1,0:T(8,128)(2,1)S(1)}, bf16[896,128]{1,0:T(8,128)(2,1)S(1)}, u32[]{:S(2)}, u32[]{:S(2)}) collective-permute-start(bf16[896,128]{1,0:T(8,128)(2,1)S(1)} %collective-permute-done.13.tile_ref.refs_5_), channel_id=1, source_target_pairs={{0,452},{64,0},{128,64},{192,128},{256,192},{320,256},{384,320},{4... | collective-permute-start | bytes 688136 | tf_op jit(solution)/shard_map/ppermute | solution.py:22
  152.6 2.8 %collective-permute-start.20 = (bf16[896,128]{1,0:T(8,128)(2,1)S(1)}, bf16[896,128]{1,0:T(8,128)(2,1)S(1)}, u32[]{:S(2)}, u32[]{:S(2)}) collective-permute-start(bf16[896,128]{1,0:T(8,128)(2,1)S(1)} %collective-permute-done.17.refs_6_), channel_id=1, source_target_pairs={{0,64},{64,128},{128,192},{192,256},{256,320},{320,384},{384,448},... | collective-permute-start | bytes 688136 | tf_op jit(solution)/shard_map/ppermute | solution.py:22
  155.3 3.7 %collective-permute-done.18.refs_7_ = bf16[896,128]{1,0:T(8,128)(2,1)S(1)} collective-permute-done((bf16[896,128]{1,0:T(8,128)(2,1)S(1)}, bf16[896,128]{1,0:T(8,128)(2,1)S(1)}, u32[]{:S(2)}, u32[]{:S(2)}) %collective-permute-start.18) | collective-permute-done | bytes 229408 | tf_op jit(solution)/shard_map/ppermute | solution.py:22
  159.0 4.3 %collective-permute-start.19 = (bf16[896,128]{1,0:T(8,128)(2,1)S(1)}, bf16[896,128]{1,0:T(8,128)(2,1)S(1)}, u32[]{:S(2)}, u32[]{:S(2)}) collective-permute-start(bf16[896,128]{1,0:T(8,128)(2,1)S(1)} %collective-permute-done.18.refs_7_), channel_id=1, source_target_pairs={{0,452},{64,0},{128,64},{192,128},{256,192},{320,256},{384,320},{4... | collective-permute-start | bytes 688136 | tf_op jit(solution)/shard_map/ppermute | solution.py:22
  164.0 1.9 collective-permute-start.21
  166.6 1.9 collective-permute-start.23
  168.6 5.2 %collective-permute-done.21.refs_4_ = bf16[896,128]{1,0:T(8,128)(2,1)} collective-permute-done((bf16[896,128]{1,0:T(8,128)(2,1)S(1)}, bf16[896,128]{1,0:T(8,128)(2,1)}, u32[]{:S(2)}, u32[]{:S(2)}) %collective-permute-start.21) | collective-permute-done | bytes 229408 | tf_op jit(solution)/shard_map/ppermute | solution.py:22
  173.8 1.9 collective-permute-start.24
  175.7 3.9 %collective-permute-start.25 = (bf16[896,128]{1,0:T(8,128)(2,1)}, bf16[896,128]{1,0:T(8,128)(2,1)}, u32[]{:S(2)}, u32[]{:S(2)}) collective-permute-start(bf16[896,128]{1,0:T(8,128)(2,1)} %collective-permute-done.21.refs_4_), channel_id=1, source_target_pairs={{0,64},{64,128},{128,192},{192,256},{256,320},{320,384},{384,448},... | collective-permute-start | bytes 688136 | tf_op jit(solution)/shard_map/ppermute | solution.py:22
  179.6 2.2 %collective-permute-done.24.refs_4_ = bf16[896,128]{1,0:T(8,128)(2,1)} collective-permute-done((bf16[896,128]{1,0:T(8,128)(2,1)S(1)}, bf16[896,128]{1,0:T(8,128)(2,1)}, u32[]{:S(2)}, u32[]{:S(2)}) %collective-permute-start.24) | collective-permute-done | bytes 229408 | tf_op jit(solution)/shard_map/ppermute | solution.py:22
  181.8 3.1 %collective-permute-start.26 = (bf16[896,128]{1,0:T(8,128)(2,1)}, bf16[896,128]{1,0:T(8,128)(2,1)}, u32[]{:S(2)}, u32[]{:S(2)}) collective-permute-start(bf16[896,128]{1,0:T(8,128)(2,1)} %collective-permute-done.24.refs_4_), channel_id=1, source_target_pairs={{0,452},{64,0},{128,64},{192,128},{256,192},{320,256},{384,320},{4... | collective-permute-start | bytes 688136 | tf_op jit(solution)/shard_map/ppermute | solution.py:22
  185.7 4.8 %all-to-all-start.4 = ((bf16[128,2,1,224]{3,1,2,0:T(2,128)(2,1)}), bf16[128,2,1,224]{3,1,2,0:T(2,128)(2,1)}, u32[]{:S(2)}, u32[]{:S(2)}) async-start(bf16[128,2,1,224]{3,1,2,0:T(2,128)(2,1)} %copy.19), calls=%async_computation.4 | async-start | bytes 262144 | tf_op jit(solution)/shard_map/all_to_all | solution.py:253
  190.5 1.4 reduce_sum.12
  191.9 12.1 %collective-permute-start.22 = (bf16[32,512]{1,0:T(8,128)(2,1)S(1)}, bf16[32,512]{1,0:T(8,128)(2,1)S(1)}, u32[]{:S(2)}, u32[]{:S(2)}) collective-permute-start(bf16[32,512]{1,0:T(8,128)(2,1)S(1)} %reduce_sum.12), channel_id=1, source_target_pairs={{0,44},{16,52},{32,60},{48,0},{8,8},{24,16},{40,24},{56,32},{64,11... | collective-permute-start | bytes 98312 | tf_op jit(solution)/shard_map/ppermute | solution.py:251
  204.1 1.8 maximum_select_fusion.refs_2_.refs_3_.refs_4_.refs_1_
  205.9 0.9 copy-done.1
  206.8 0.9 copy-done.3
  208.7 1.2 shard_map.82.refs_0_
  209.9 0.9 copy.20
  211.8 2.4 %shard_map.83 = (f32[224,512]{1,0:T(8,128)}, f32[224,512]{1,0:T(8,128)}) custom-call(s32[1]{0:T(128)} %bitcast.5.half_ref, f32[448,512]{1,0:T(8,128)S(1)} %shard_map.82.refs_0_, bf16[1024,512]{1,0:T(8,128)(2,1)S(1)} %maximum_select_fusion.refs_2_.refs_3_.refs_4_.refs_1_, bf16[1024,512]{1,0:T(8,128)(2,1)S(1)} %maximum_select_fusion.refs_2_.refs_3_.refs_4_.refs_1_, ...), custom_call_target="tpu_custom_call" | custom-call | tf_op jit(solution)/shard_map/pallas_call | solution.py:123
  (69 shorter events, 11.7 us)
Async XLA Ops:
  0.6 13.8 %collective-permute-start = (bf16[32,512]{1,0:T(8,128)(2,1)}, bf16[32,512]{1,0:T(8,128)(2,1)S(1)}, u32[]{:S(2)}, u32[]{:S(2)}) collective-permute-start(bf16[32,512]{1,0:T(8,128)(2,1)} %param.4), channel_id=1, source_target_pairs={{324,0},{388,16},{452,32},{0,48},{64,8},{128,24},{192,40},{256,56}... | collective-permute-start | bytes 98312 | tf_op jit(solution)/shard_map/ppermute | solution.py:178
  15.3 21.3 %all-to-all-start = ((bf16[16,32,512]{2,1,0:T(8,128)(2,1)}), bf16[16,32,512]{2,1,0:T(8,128)(2,1)S(1)}, u32[]{:S(2)}, u32[]{:S(2)}) async-start(bf16[16,32,512]{2,1,0:T(8,128)(2,1)} %broadcast_in_dim.4), calls=%async_computation | async-start | bytes 1048576 | tf_op jit(solution)/shard_map/all_to_all | solution.py:156
  24.0 12.6 %collective-permute-start.1 = (bf16[32,512]{1,0:T(8,128)(2,1)}, bf16[32,512]{1,0:T(8,128)(2,1)S(1)}, u32[]{:S(2)}, u32[]{:S(2)}) collective-permute-start(bf16[32,512]{1,0:T(8,128)(2,1)} %param.4), channel_id=1, source_target_pairs={{324,4},{388,20},{452,36},{0,52},{64,12},{128,28},{192,44},{256,60... | collective-permute-start | bytes 98312 | tf_op jit(solution)/shard_map/ppermute | solution.py:179
  31.0 2.3 %copy-start.16 = (bf16[32,1792]{1,0:T(8,128)(2,1)S(1)}, bf16[32,1792]{1,0:T(8,128)(2,1)}, u32[]{:S(2)}) copy-start(bf16[32,1792]{1,0:T(8,128)(2,1)} %param.7) | copy-start | bytes 344068
  36.7 3.8 %collective-permute-start.2 = (bf16[512,512]{1,0:T(8,128)(2,1)S(1)}, bf16[512,512]{1,0:T(8,128)(2,1)S(1)}, u32[]{:S(2)}, u32[]{:S(2)}) collective-permute-start(bf16[512,512]{1,0:T(8,128)(2,1)S(1)} %bitcast.29), channel_id=1, source_target_pairs={{0,8},{8,0},{1,9},{9,1},{2,10},{10,2},{3,11},{11,3},{4,12},{12,4},... | collective-permute-start | bytes 1572872 | tf_op jit(solution)/shard_map/ppermute | solution.py:61
  41.9 14.4 %collective-permute-start.3 = (bf16[896,128]{1,0:T(8,128)(2,1)}, bf16[896,128]{1,0:T(8,128)(2,1)}, u32[]{:S(2)}, u32[]{:S(2)}) collective-permute-start(bf16[896,128]{1,0:T(8,128)(2,1)} %get-tuple-element.40), channel_id=1, source_target_pairs={{0,64},{64,128},{128,192},{192,256},{256,320},{320,384},{384,448},... | collective-permute-start | bytes 688136 | tf_op jit(solution)/shard_map/ppermute | solution.py:22
  44.4 25.8 %all-to-all-start.1 = ((bf16[4,32,2,224]{3,2,1,0:T(2,128)(2,1)}), bf16[4,32,2,224]{3,2,1,0:T(2,128)(2,1)S(1)}, u32[]{:S(2)}, u32[]{:S(2)}) async-start(bf16[4,32,2,224]{3,2,1,0:T(2,128)(2,1)} %bitcast.28), calls=%async_computation.1 | async-start | bytes 262144 | tf_op jit(solution)/shard_map/all_to_all | solution.py:186
  49.2 10.2 %collective-permute-start.7 = (bf16[896,128]{1,0:T(8,128)(2,1)}, bf16[896,128]{1,0:T(8,128)(2,1)S(1)}, u32[]{:S(2)}, u32[]{:S(2)}) collective-permute-start(bf16[896,128]{1,0:T(8,128)(2,1)} %get-tuple-element.48), channel_id=1, source_target_pairs={{0,452},{64,0},{128,64},{192,128},{256,192},{320,256},{384,320},{4... | collective-permute-start | bytes 688136 | tf_op jit(solution)/shard_map/ppermute | solution.py:22
  55.6 0.7 copy-start.6
  56.3 3.1 %copy-start.8 = (bf16[896,128]{1,0:T(8,128)(2,1)}, bf16[896,128]{1,0:T(8,128)(2,1)S(1)}, u32[]{:S(2)}) copy-start(bf16[896,128]{1,0:T(8,128)(2,1)S(1)} %get-tuple-element.50) | copy-start | bytes 688132
  57.4 10.0 %collective-permute-start.4 = (bf16[896,128]{1,0:T(8,128)(2,1)S(1)}, bf16[896,128]{1,0:T(8,128)(2,1)S(1)}, u32[]{:S(2)}, u32[]{:S(2)}) collective-permute-start(bf16[896,128]{1,0:T(8,128)(2,1)S(1)} %add_convert_fusion.4), channel_id=1, source_target_pairs={{0,64},{64,128},{128,192},{192,256},{256,320},{320,384},{384,448},... | collective-permute-start | bytes 688136 | tf_op jit(solution)/shard_map/ppermute | solution.py:22
  59.4 21.6 %copy-start.9 = (bf16[896,128]{1,0:T(8,128)(2,1)S(1)}, bf16[896,128]{1,0:T(8,128)(2,1)}, u32[]{:S(2)}) copy-start(bf16[896,128]{1,0:T(8,128)(2,1)} %copy-done.8) | copy-start | bytes 688132
  59.4 28.4 %copy-start.7 = (bf16[896,128]{1,0:T(8,128)(2,1)S(1)}, bf16[896,128]{1,0:T(8,128)(2,1)}, u32[]{:S(2)}) copy-start(bf16[896,128]{1,0:T(8,128)(2,1)} %copy-done.6) | copy-start | bytes 688132
  60.2 20.8 %collective-permute-start.8 = (bf16[896,128]{1,0:T(8,128)(2,1)}, bf16[896,128]{1,0:T(8,128)(2,1)}, u32[]{:S(2)}, u32[]{:S(2)}) collective-permute-start(bf16[896,128]{1,0:T(8,128)(2,1)} %add_convert_fusion.1), channel_id=1, source_target_pairs={{0,452},{64,0},{128,64},{192,128},{256,192},{320,256},{384,320},{4... | collective-permute-start | bytes 688136 | tf_op jit(solution)/shard_map/ppermute | solution.py:22
  68.2 19.6 %collective-permute-start.5 = (bf16[896,128]{1,0:T(8,128)(2,1)}, bf16[896,128]{1,0:T(8,128)(2,1)}, u32[]{:S(2)}, u32[]{:S(2)}) collective-permute-start(bf16[896,128]{1,0:T(8,128)(2,1)} %add_convert_fusion.3), channel_id=1, source_target_pairs={{0,64},{64,128},{128,192},{192,256},{256,320},{320,384},{384,448},... | collective-permute-start | bytes 688136 | tf_op jit(solution)/shard_map/ppermute | solution.py:22
  71.0 21.4 %all-to-all-start.2 = ((bf16[16,32,512]{2,1,0:T(8,128)(2,1)}), bf16[16,32,512]{2,1,0:T(8,128)(2,1)S(1)}, u32[]{:S(2)}, u32[]{:S(2)}) async-start(bf16[16,32,512]{2,1,0:T(8,128)(2,1)} %broadcast_in_dim.5), calls=%async_computation.2 | async-start | bytes 1048576 | tf_op jit(solution)/shard_map/all_to_all | solution.py:156
  82.7 9.7 %collective-permute-start.9 = (bf16[896,128]{1,0:T(8,128)(2,1)}, bf16[896,128]{1,0:T(8,128)(2,1)}, u32[]{:S(2)}, u32[]{:S(2)}) collective-permute-start(bf16[896,128]{1,0:T(8,128)(2,1)} %add_convert_fusion), channel_id=1, source_target_pairs={{0,452},{64,0},{128,64},{192,128},{256,192},{320,256},{384,320},{4... | collective-permute-start | bytes 688136 | tf_op jit(solution)/shard_map/ppermute | solution.py:22
  89.6 9.4 %collective-permute-start.6 = (bf16[896,128]{1,0:T(8,128)(2,1)}, bf16[896,128]{1,0:T(8,128)(2,1)}, u32[]{:S(2)}, u32[]{:S(2)}) collective-permute-start(bf16[896,128]{1,0:T(8,128)(2,1)} %add_convert_fusion.2), channel_id=1, source_target_pairs={{0,64},{64,128},{128,192},{192,256},{256,320},{320,384},{384,448},... | collective-permute-start | bytes 688136 | tf_op jit(solution)/shard_map/ppermute | solution.py:22
  92.4 8.6 %copy-start.12 = (bf16[16,32,512]{2,1,0:T(8,128)(2,1)}, bf16[16,32,512]{2,1,0:T(8,128)(2,1)S(1)}, u32[]{:S(2)}) copy-start(bf16[16,32,512]{2,1,0:T(8,128)(2,1)S(1)} %all-to-all-done.2) | copy-start | bytes 1572868
  92.4 7.7 %copy-start.14 = (f32[128,448]{0,1:T(8,128)S(1)}, f32[128,448]{0,1:T(8,128)}, u32[]{:S(2)}) copy-start(f32[128,448]{0,1:T(8,128)} %copy.18) | copy-start | bytes 688132
  101.0 8.7 %collective-permute-start.10 = (bf16[896,128]{1,0:T(8,128)(2,1)S(1)}, bf16[896,128]{1,0:T(8,128)(2,1)S(1)}, u32[]{:S(2)}, u32[]{:S(2)}) collective-permute-start(bf16[896,128]{1,0:T(8,128)(2,1)S(1)} %pad_maximum_fusion.3.refs_4_), channel_id=1, source_target_pairs={{0,452},{64,0},{128,64},{192,128},{256,192},{320,256},{384,320},{4... | collective-permute-start | bytes 688136 | tf_op jit(solution)/shard_map/ppermute | solution.py:22
  103.0 9.1 %collective-permute-start.14 = (bf16[896,128]{1,0:T(8,128)(2,1)S(1)}, bf16[896,128]{1,0:T(8,128)(2,1)S(1)}, u32[]{:S(2)}, u32[]{:S(2)}) collective-permute-start(bf16[896,128]{1,0:T(8,128)(2,1)S(1)} %pad_maximum_fusion.3.refs_4_), channel_id=1, source_target_pairs={{0,64},{64,128},{128,192},{192,256},{256,320},{320,384},{384,448},... | collective-permute-start | bytes 688136 | tf_op jit(solution)/shard_map/ppermute | solution.py:22
  109.7 9.6 %collective-permute-start.11 = (bf16[896,128]{1,0:T(8,128)(2,1)S(1)}, bf16[896,128]{1,0:T(8,128)(2,1)S(1)}, u32[]{:S(2)}, u32[]{:S(2)}) collective-permute-start(bf16[896,128]{1,0:T(8,128)(2,1)S(1)} %collective-permute-done.10.refs_5_), channel_id=1, source_target_pairs={{0,452},{64,0},{128,64},{192,128},{256,192},{320,256},{384,320},{4... | collective-permute-start | bytes 688136 | tf_op jit(solution)/shard_map/ppermute | solution.py:22
  112.1 9.8 %collective-permute-start.15 = (bf16[896,128]{1,0:T(8,128)(2,1)S(1)}, bf16[896,128]{1,0:T(8,128)(2,1)S(1)}, u32[]{:S(2)}, u32[]{:S(2)}) collective-permute-start(bf16[896,128]{1,0:T(8,128)(2,1)S(1)} %collective-permute-done.14.refs_6_), channel_id=1, source_target_pairs={{0,64},{64,128},{128,192},{192,256},{256,320},{320,384},{384,448},... | collective-permute-start | bytes 688136 | tf_op jit(solution)/shard_map/ppermute | solution.py:22
  119.3 10.3 %collective-permute-start.12 = (bf16[896,128]{1,0:T(8,128)(2,1)S(1)}, bf16[896,128]{1,0:T(8,128)(2,1)}, u32[]{:S(2)}, u32[]{:S(2)}) collective-permute-start(bf16[896,128]{1,0:T(8,128)(2,1)S(1)} %collective-permute-done.11.refs_4_), channel_id=1, source_target_pairs={{0,452},{64,0},{128,64},{192,128},{256,192},{320,256},{384,320},{4... | collective-permute-start | bytes 688136 | tf_op jit(solution)/shard_map/ppermute | solution.py:22
  121.9 10.8 %collective-permute-start.16 = (bf16[896,128]{1,0:T(8,128)(2,1)S(1)}, bf16[896,128]{1,0:T(8,128)(2,1)}, u32[]{:S(2)}, u32[]{:S(2)}) collective-permute-start(bf16[896,128]{1,0:T(8,128)(2,1)S(1)} %collective-permute-done.15.refs_5_), channel_id=1, source_target_pairs={{0,64},{64,128},{128,192},{192,256},{256,320},{320,384},{384,448},... | collective-permute-start | bytes 688136 | tf_op jit(solution)/shard_map/ppermute | solution.py:22
  125.2 0.7 copy-start.10
  129.6 9.7 %collective-permute-start.13 = (bf16[896,128]{1,0:T(8,128)(2,1)}, bf16[896,128]{1,0:T(8,128)(2,1)S(1)}, u32[]{:S(2)}, u32[]{:S(2)}) collective-permute-start(bf16[896,128]{1,0:T(8,128)(2,1)} %collective-permute-done.12.refs_4_), channel_id=1, source_target_pairs={{0,452},{64,0},{128,64},{192,128},{256,192},{320,256},{384,320},{4... | collective-permute-start | bytes 688136 | tf_op jit(solution)/shard_map/ppermute | solution.py:22
  132.7 9.3 %collective-permute-start.17 = (bf16[896,128]{1,0:T(8,128)(2,1)}, bf16[896,128]{1,0:T(8,128)(2,1)S(1)}, u32[]{:S(2)}, u32[]{:S(2)}) collective-permute-start(bf16[896,128]{1,0:T(8,128)(2,1)} %collective-permute-done.16.refs_5_), channel_id=1, source_target_pairs={{0,64},{64,128},{128,192},{192,256},{256,320},{320,384},{384,448},... | collective-permute-start | bytes 688136 | tf_op jit(solution)/shard_map/ppermute | solution.py:22
  135.6 1.1 copy-start.11
  139.3 45.6 %copy-start.15 = (bf16[448,128]{1,0:T(8,128)(2,1)S(1)}, bf16[448,128]{1,0:T(8,128)(2,1)}, u32[]{:S(2)}) copy-start(bf16[448,128]{1,0:T(8,128)(2,1)} %get-tuple-element.64) | copy-start | bytes 344068
  140.8 25.8 %copy-start.13 = (bf16[16,32,512]{2,1,0:T(8,128)(2,1)S(1)}, bf16[16,32,512]{2,1,0:T(8,128)(2,1)}, u32[]{:S(2)}) copy-start(bf16[16,32,512]{2,1,0:T(8,128)(2,1)} %copy-done.12) | copy-start | bytes 1572868
  142.1 31.7 %all-to-all-start.3 = ((bf16[32,32,512]{2,1,0:T(8,128)(2,1)}), bf16[32,32,512]{2,1,0:T(8,128)(2,1)}, u32[]{:S(2)}, u32[]{:S(2)}) async-start(bf16[32,32,512]{2,1,0:T(8,128)(2,1)} %bitcast.6), calls=%async_computation.3 | async-start | bytes 2097152 | tf_op jit(solution)/shard_map/all_to_all | solution.py:236
  149.5 9.6 %collective-permute-start.18 = (bf16[896,128]{1,0:T(8,128)(2,1)S(1)}, bf16[896,128]{1,0:T(8,128)(2,1)S(1)}, u32[]{:S(2)}, u32[]{:S(2)}) collective-permute-start(bf16[896,128]{1,0:T(8,128)(2,1)S(1)} %collective-permute-done.13.tile_ref.refs_5_), channel_id=1, source_target_pairs={{0,452},{64,0},{128,64},{192,128},{256,192},{320,256},{384,320},{4... | collective-permute-start | bytes 688136 | tf_op jit(solution)/shard_map/ppermute | solution.py:22
  152.6 11.4 %collective-permute-start.20 = (bf16[896,128]{1,0:T(8,128)(2,1)S(1)}, bf16[896,128]{1,0:T(8,128)(2,1)S(1)}, u32[]{:S(2)}, u32[]{:S(2)}) collective-permute-start(bf16[896,128]{1,0:T(8,128)(2,1)S(1)} %collective-permute-done.17.refs_6_), channel_id=1, source_target_pairs={{0,64},{64,128},{128,192},{192,256},{256,320},{320,384},{384,448},... | collective-permute-start | bytes 688136 | tf_op jit(solution)/shard_map/ppermute | solution.py:22
  159.0 9.5 %collective-permute-start.19 = (bf16[896,128]{1,0:T(8,128)(2,1)S(1)}, bf16[896,128]{1,0:T(8,128)(2,1)S(1)}, u32[]{:S(2)}, u32[]{:S(2)}) collective-permute-start(bf16[896,128]{1,0:T(8,128)(2,1)S(1)} %collective-permute-done.18.refs_7_), channel_id=1, source_target_pairs={{0,452},{64,0},{128,64},{192,128},{256,192},{320,256},{384,320},{4... | collective-permute-start | bytes 688136 | tf_op jit(solution)/shard_map/ppermute | solution.py:22
  163.3 0.7 copy-start
  164.0 9.7 %collective-permute-start.21 = (bf16[896,128]{1,0:T(8,128)(2,1)S(1)}, bf16[896,128]{1,0:T(8,128)(2,1)}, u32[]{:S(2)}, u32[]{:S(2)}) collective-permute-start(bf16[896,128]{1,0:T(8,128)(2,1)S(1)} %collective-permute-done.20.refs_8_), channel_id=1, source_target_pairs={{0,64},{64,128},{128,192},{192,256},{256,320},{320,384},{384,448},... | collective-permute-start | bytes 688136 | tf_op jit(solution)/shard_map/ppermute | solution.py:22
  165.9 0.7 copy-start.2
  166.6 37.4 %collective-permute-start.23 = (bf16[512,512]{1,0:T(8,128)(2,1)S(1)}, bf16[512,512]{1,0:T(8,128)(2,1)}, u32[]{:S(2)}, u32[]{:S(2)}) collective-permute-start(bf16[512,512]{1,0:T(8,128)(2,1)S(1)} %bitcast.33), channel_id=1, source_target_pairs={{0,8},{8,0},{1,9},{9,1},{2,10},{10,2},{3,11},{11,3},{4,12},{12,4},... | collective-permute-start | bytes 1572872 | tf_op jit(solution)/shard_map/ppermute | solution.py:61
  168.5 35.5 %copy-start.4 = (bf16[896,128]{1,0:T(8,128)(2,1)}, bf16[896,128]{1,0:T(8,128)(2,1)S(1)}, u32[]{:S(2)}) copy-start(bf16[896,128]{1,0:T(8,128)(2,1)S(1)} %collective-permute-done.19.refs_3_) | copy-start | bytes 688132
  173.8 8.0 %collective-permute-start.24 = (bf16[896,128]{1,0:T(8,128)(2,1)S(1)}, bf16[896,128]{1,0:T(8,128)(2,1)}, u32[]{:S(2)}, u32[]{:S(2)}) collective-permute-start(bf16[896,128]{1,0:T(8,128)(2,1)S(1)} %collective-permute-done.19.refs_3_), channel_id=1, source_target_pairs={{0,452},{64,0},{128,64},{192,128},{256,192},{320,256},{384,320},{4... | collective-permute-start | bytes 688136 | tf_op jit(solution)/shard_map/ppermute | solution.py:22
  175.7 36.1 %collective-permute-start.25 = (bf16[896,128]{1,0:T(8,128)(2,1)}, bf16[896,128]{1,0:T(8,128)(2,1)}, u32[]{:S(2)}, u32[]{:S(2)}) collective-permute-start(bf16[896,128]{1,0:T(8,128)(2,1)} %collective-permute-done.21.refs_4_), channel_id=1, source_target_pairs={{0,64},{64,128},{128,192},{192,256},{256,320},{320,384},{384,448},... | collective-permute-start | bytes 688136 | tf_op jit(solution)/shard_map/ppermute | solution.py:22
  181.8 30.0 %collective-permute-start.26 = (bf16[896,128]{1,0:T(8,128)(2,1)}, bf16[896,128]{1,0:T(8,128)(2,1)}, u32[]{:S(2)}, u32[]{:S(2)}) collective-permute-start(bf16[896,128]{1,0:T(8,128)(2,1)} %collective-permute-done.24.refs_4_), channel_id=1, source_target_pairs={{0,452},{64,0},{128,64},{192,128},{256,192},{320,256},{384,320},{4... | collective-permute-start | bytes 688136 | tf_op jit(solution)/shard_map/ppermute | solution.py:22
  185.7 24.2 %all-to-all-start.4 = ((bf16[128,2,1,224]{3,1,2,0:T(2,128)(2,1)}), bf16[128,2,1,224]{3,1,2,0:T(2,128)(2,1)}, u32[]{:S(2)}, u32[]{:S(2)}) async-start(bf16[128,2,1,224]{3,1,2,0:T(2,128)(2,1)} %copy.19), calls=%async_computation.4 | async-start | bytes 262144 | tf_op jit(solution)/shard_map/all_to_all | solution.py:253
  191.9 18.0 %collective-permute-start.22 = (bf16[32,512]{1,0:T(8,128)(2,1)S(1)}, bf16[32,512]{1,0:T(8,128)(2,1)S(1)}, u32[]{:S(2)}, u32[]{:S(2)}) collective-permute-start(bf16[32,512]{1,0:T(8,128)(2,1)S(1)} %reduce_sum.12), channel_id=1, source_target_pairs={{0,44},{16,52},{32,60},{48,0},{8,8},{24,16},{40,24},{56,32},{64,11... | collective-permute-start | bytes 98312 | tf_op jit(solution)/shard_map/ppermute | solution.py:251
  205.9 0.9 copy-start.1
  206.8 0.9 copy-start.3
  207.8 0.9 copy-start.5

commit v8 on v6

--- a/solution.py
+++ b/solution.py
@@ -94,7 +94,7 @@
     for at, tile_ref in enumerate(tile_refs):
         wide_ref[:, at * 128 : (at + 1) * 128] = tile_ref[...]
         product = dot_f32(weights_ref[...], tile_ref[...])
-        terms_ref[at * 128 : (at + 1) * 128, :] = product.T.astype(jnp.bfloat16)
+        terms_ref[slot(at) * 128 : (slot(at) + 1) * 128, :] = product.T.astype(jnp.bfloat16)
     sums_ref[...] = dot_f32(wide_ref[...], tokens_ref[0:896, :])
 
 
@@ -151,25 +151,19 @@
     )(core, half, own, other, sums, tile)
 
 
-def last_terms_kernel(core_ref, weights_ref, terms_ref, tile_ref, keep_ref, send_ref, all_ref):
+def last_terms_kernel(weights_ref, terms_ref, tile_ref, all_ref):
     all_ref[0:896, :] = terms_ref[...]
     all_ref[896:1024, :] = dot_f32(weights_ref[...], tile_ref[...]).T.astype(jnp.bfloat16)
-    core = core_ref[0]
-    rows = keep_ref.shape[0]
-    keep_ref[...] = all_ref[pl.ds(pl.multiple_of(core * rows, rows), rows), :]
-    send_ref[...] = all_ref[pl.ds(pl.multiple_of((1 - core) * rows, rows), rows), :]
-
-
-def last_terms(core, weights, terms, tile):
-    shape = (ROWS * 64, weights.shape[0])
+
+
+def last_terms(weights, terms, tile):
     return pl.pallas_call(
         last_terms_kernel,
-        in_specs=[SMEM_SPEC] + [VMEM_SPEC] * 3,
-        out_specs=[VMEM_SPEC] * 2,
-        out_shape=[jax.ShapeDtypeStruct(shape, jnp.bfloat16)] * 2,
-        scratch_shapes=[pltpu.VMEM((ROWS * 128, shape[1]), jnp.bfloat16)],
-        compiler_params=PARAMS,
-    )(core, weights, terms, tile)
+        in_specs=[VMEM_SPEC] * 3,
+        out_specs=VMEM_SPEC,
+        out_shape=jax.ShapeDtypeStruct((ROWS * 128, weights.shape[0]), jnp.bfloat16),
+        compiler_params=PARAMS,
+    )(weights, terms, tile)
 
 
 def add_tiles(*tiles):
@@ -236,10 +230,9 @@
     keep, send = last_sums(core, half, own_tokens, other_tokens, sums, left_4)
     terms, send = lax.optimization_barrier((terms, send))
     received = lax.ppermute(send, "h", [(0, 1), (1, 0)])
-    keep_terms, send_terms = last_terms(core, weights, terms, left_4)
-    terms = add_tiles(keep_terms, swap_cores(send_terms))
+    terms = last_terms(weights, terms, left_4)
     terms = lax.all_to_all(
-        terms.reshape(16, -1, features), ("y", "x"), split_axis=0, concat_axis=0, tiled=True
+        terms.reshape(32, -1, features), ("y", "c", "x"), split_axis=0, concat_axis=0, tiled=True
     )
     grad_tokens = jnp.sum(terms.astype(jnp.float32), 0).astype(jnp.bfloat16)
     grad_tokens, hidden = lax.optimization_barrier((grad_tokens, hidden))

time: 184 us -> 182 us (0.989)
  the two profiles are of different devices: /device:TPU:233 before, /device:TPU:235 now
where the time goes in v8:
time: 182 us; the launch traced here: 181 us
  starting transfers between devices  88.3 us (49%)
  waiting for transfers between devices  71.7 us (39%)
  local copies, waits for them, and re-layouts  8.88 us (5%)
  Pallas kernels  7.38 us (4%)
  other arithmetic  3.45 us (2%)
    ppermute x14, starting transfers between devices, ring_shift(): return lax.ppermute(value, ('r', 'h'), pairs)  49.2 us
    ppermute x1, waiting for transfers between devices, local(): lax.ppermute(grad_tokens, ('r', 'y', 'c', 'h'), result_pairs())  28.8 us
    all_to_all x1, starting transfers between devices, local(): lax.all_to_all(terms.reshape(32, -1, features), ('y', 'c', 'x'), split_ax...  15.2 us
    ppermute x14, waiting for transfers between devices, ring_shift(): return lax.ppermute(value, ('r', 'h'), pairs)  13.7 us
    all_to_all x1, waiting for transfers between devices, local(): lax.all_to_all(terms.reshape(32, -1, features), ('y', 'c', 'x'), split_ax...  12.5 us
    ppermute x1, waiting for transfers between devices, local(): piece = lax.ppermute(tokens, ('r', 'y', 'c', 'h'), token_pairs())  8.6 us
    all_to_all x1, starting transfers between devices, local(): lax.all_to_all(copies, ('y', 'x'), split_axis=0, concat_axis=0, tiled=True)  5.29 us
    all_to_all x1, waiting for transfers between devices, local(): lax.all_to_all(copies, ('y', 'x'), split_axis=0, concat_axis=0, tiled=True)  5.05 us
  transfers between devices with their start and end apart: 22, of which 16 were waited for; matrix products, arithmetic and copies ran while one was open for 4% of the time, Pallas kernels for 3%

profile of v8, /device:TPU:235, one launch (start us, length us, event | category | flops | bytes accessed | tf_op | source)
XLA Modules:
  0.0 180.7 jit_solution(3110520055082692059)
XLA Ops:
  0.6 2.1 %collective-permute-start = (bf16[32,512]{1,0:T(8,128)(2,1)}, bf16[32,512]{1,0:T(8,128)(2,1)S(1)}, u32[]{:S(2)}, u32[]{:S(2)}) collective-permute-start(bf16[32,512]{1,0:T(8,128)(2,1)} %param.4), channel_id=1, source_target_pairs={{324,0},{388,16},{452,32},{0,48},{64,8},{128,24},{192,40},{256,56}... | collective-permute-start | bytes 98312 | tf_op jit(solution)/shard_map/ppermute | solution.py:187
  2.7 8.6 %collective-permute-done = bf16[32,512]{1,0:T(8,128)(2,1)S(1)} collective-permute-done((bf16[32,512]{1,0:T(8,128)(2,1)}, bf16[32,512]{1,0:T(8,128)(2,1)S(1)}, u32[]{:S(2)}, u32[]{:S(2)}) %collective-permute-start) | collective-permute-done | bytes 32800 | tf_op jit(solution)/shard_map/ppermute | solution.py:187
  11.3 0.8 broadcast_in_dim.2
  12.2 5.3 %all-to-all-start = ((bf16[16,32,512]{2,1,0:T(8,128)(2,1)}), bf16[16,32,512]{2,1,0:T(8,128)(2,1)S(1)}, u32[]{:S(2)}, u32[]{:S(2)}) async-start(bf16[16,32,512]{2,1,0:T(8,128)(2,1)} %broadcast_in_dim.2), calls=%async_computation | async-start | bytes 1048576 | tf_op jit(solution)/shard_map/all_to_all | solution.py:189
  17.5 1.1 reshape.34
  18.6 0.8 copy.23
  19.3 1.8 constant_dynamic-slice_fusion.2
  21.1 0.4 pad_maximum_fusion.weights_ref
  21.6 5.0 %all-to-all-done = bf16[16,32,512]{2,1,0:T(8,128)(2,1)S(1)} async-done(((bf16[16,32,512]{2,1,0:T(8,128)(2,1)}), bf16[16,32,512]{2,1,0:T(8,128)(2,1)S(1)}, u32[]{:S(2)}, u32[]{:S(2)}) %all-to-all-start) | async-done | bytes 524320 | tf_op jit(solution)/shard_map/all_to_all | solution.py:189
  26.6 2.7 %collective-permute-start.1 = (bf16[512,512]{1,0:T(8,128)(2,1)S(1)}, bf16[512,512]{1,0:T(8,128)(2,1)S(1)}, u32[]{:S(2)}, u32[]{:S(2)}) collective-permute-start(bf16[512,512]{1,0:T(8,128)(2,1)S(1)} %bitcast.30), channel_id=1, source_target_pairs={{0,8},{8,0},{1,9},{9,1},{2,10},{10,2},{3,11},{11,3},{4,12},{12,4},... | collective-permute-start | bytes 1572872 | tf_op jit(solution)/shard_map/ppermute | solution.py:61
  29.3 1.5 collective-permute-done.1.other_ref
  30.8 0.6 shard_map.75
  31.4 6.6 %collective-permute-start.2 = (bf16[896,128]{1,0:T(8,128)(2,1)S(1)}, bf16[896,128]{1,0:T(8,128)(2,1)S(1)}, u32[]{:S(2)}, u32[]{:S(2)}) collective-permute-start(bf16[896,128]{1,0:T(8,128)(2,1)S(1)} %get-tuple-element.30), channel_id=1, source_target_pairs={{0,64},{64,128},{128,192},{192,256},{256,320},{320,384},{384,448},... | collective-permute-start | bytes 688136 | tf_op jit(solution)/shard_map/ppermute | solution.py:22
  38.0 4.5 %all-to-all-start.1 = ((bf16[4,32,2,224]{3,2,1,0:T(2,128)(2,1)}), bf16[4,32,2,224]{3,2,1,0:T(2,128)(2,1)S(1)}, u32[]{:S(2)}, u32[]{:S(2)}) async-start(bf16[4,32,2,224]{3,2,1,0:T(2,128)(2,1)} %bitcast.29), calls=%async_computation.1 | async-start | bytes 262144 | tf_op jit(solution)/shard_map/all_to_all | solution.py:194
  42.5 1.9 %collective-permute-start.5 = (bf16[896,128]{1,0:T(8,128)(2,1)S(1)}, bf16[896,128]{1,0:T(8,128)(2,1)S(1)}, u32[]{:S(2)}, u32[]{:S(2)}) collective-permute-start(bf16[896,128]{1,0:T(8,128)(2,1)S(1)} %get-tuple-element.37), channel_id=1, source_target_pairs={{0,452},{64,0},{128,64},{192,128},{256,192},{320,256},{384,320},{4... | collective-permute-start | bytes 688136 | tf_op jit(solution)/shard_map/ppermute | solution.py:22
  44.4 1.1 shard_map.76
  45.5 0.1 add_convert_fusion.4
  45.6 4.6 %collective-permute-start.3 = (bf16[896,128]{1,0:T(8,128)(2,1)S(1)}, bf16[896,128]{1,0:T(8,128)(2,1)S(1)}, u32[]{:S(2)}, u32[]{:S(2)}) collective-permute-start(bf16[896,128]{1,0:T(8,128)(2,1)S(1)} %add_convert_fusion.4), channel_id=1, source_target_pairs={{0,64},{64,128},{128,192},{192,256},{256,320},{320,384},{384,448},... | collective-permute-start | bytes 688136 | tf_op jit(solution)/shard_map/ppermute | solution.py:22
  50.2 1.3 collective-permute-done.5
  51.5 0.1 add_convert_fusion.1
  51.5 1.9 %collective-permute-start.6 = (bf16[896,128]{1,0:T(8,128)(2,1)S(1)}, bf16[896,128]{1,0:T(8,128)(2,1)S(1)}, u32[]{:S(2)}, u32[]{:S(2)}) collective-permute-start(bf16[896,128]{1,0:T(8,128)(2,1)S(1)} %add_convert_fusion.1), channel_id=1, source_target_pairs={{0,452},{64,0},{128,64},{192,128},{256,192},{320,256},{384,320},{4... | collective-permute-start | bytes 688136 | tf_op jit(solution)/shard_map/ppermute | solution.py:22
  53.5 0.1 collective-permute-done.3
  53.6 0.1 add_convert_fusion.3
  53.6 5.3 %collective-permute-start.4 = (bf16[896,128]{1,0:T(8,128)(2,1)S(1)}, bf16[896,128]{1,0:T(8,128)(2,1)S(1)}, u32[]{:S(2)}, u32[]{:S(2)}) collective-permute-start(bf16[896,128]{1,0:T(8,128)(2,1)S(1)} %add_convert_fusion.3), channel_id=1, source_target_pairs={{0,64},{64,128},{128,192},{192,256},{256,320},{320,384},{384,448},... | collective-permute-start | bytes 688136 | tf_op jit(solution)/shard_map/ppermute | solution.py:22
  59.0 0.5 collective-permute-done.6
  59.5 0.1 add_convert_fusion
  59.6 1.9 %collective-permute-start.7 = (bf16[896,128]{1,0:T(8,128)(2,1)S(1)}, bf16[896,128]{1,0:T(8,128)(2,1)S(1)}, u32[]{:S(2)}, u32[]{:S(2)}) collective-permute-start(bf16[896,128]{1,0:T(8,128)(2,1)S(1)} %add_convert_fusion), channel_id=1, source_target_pairs={{0,452},{64,0},{128,64},{192,128},{256,192},{320,256},{384,320},{4... | collective-permute-start | bytes 688136 | tf_op jit(solution)/shard_map/ppermute | solution.py:22
  61.5 0.4 collective-permute-done.4
  62.0 5.0 %collective-permute-start.8 = (bf16[896,128]{1,0:T(8,128)(2,1)S(1)}, bf16[896,128]{1,0:T(8,128)(2,1)}, u32[]{:S(2)}, u32[]{:S(2)}) collective-permute-start(bf16[896,128]{1,0:T(8,128)(2,1)S(1)} %add_convert_fusion.2), channel_id=1, source_target_pairs={{0,64},{64,128},{128,192},{192,256},{256,320},{320,384},{384,448},... | collective-permute-start | bytes 688136 | tf_op jit(solution)/shard_map/ppermute | solution.py:22
  67.0 0.1 reshape.40
  67.1 0.1 copy.18
  67.3 0.3 collective-permute-done.7
  67.5 2.4 %collective-permute-done.8 = bf16[896,128]{1,0:T(8,128)(2,1)} collective-permute-done((bf16[896,128]{1,0:T(8,128)(2,1)S(1)}, bf16[896,128]{1,0:T(8,128)(2,1)}, u32[]{:S(2)}, u32[]{:S(2)}) %collective-permute-start.8) | collective-permute-done | bytes 229408 | tf_op jit(solution)/shard_map/ppermute | solution.py:22
  70.0 1.0 convert_add_fusion.1
  71.0 0.2 multiply_convert_fusion
  71.3 1.9 %collective-permute-start.12 = (bf16[896,128]{1,0:T(8,128)(2,1)S(1)}, bf16[896,128]{1,0:T(8,128)(2,1)S(1)}, u32[]{:S(2)}, u32[]{:S(2)}) collective-permute-start(bf16[896,128]{1,0:T(8,128)(2,1)S(1)} %pad_maximum_fusion.3.refs_3_), channel_id=1, source_target_pairs={{0,452},{64,0},{128,64},{192,128},{256,192},{320,256},{384,320},{4... | collective-permute-start | bytes 688136 | tf_op jit(solution)/shard_map/ppermute | solution.py:22
  73.2 5.1 %collective-permute-start.9 = (bf16[896,128]{1,0:T(8,128)(2,1)S(1)}, bf16[896,128]{1,0:T(8,128)(2,1)S(1)}, u32[]{:S(2)}, u32[]{:S(2)}) collective-permute-start(bf16[896,128]{1,0:T(8,128)(2,1)S(1)} %pad_maximum_fusion.3.refs_3_), channel_id=1, source_target_pairs={{0,64},{64,128},{128,192},{192,256},{256,320},{320,384},{384,448},... | collective-permute-start | bytes 688136 | tf_op jit(solution)/shard_map/ppermute | solution.py:22
  78.3 1.5 collective-permute-done.12.refs_4_
  79.8 1.9 %collective-permute-start.13 = (bf16[896,128]{1,0:T(8,128)(2,1)S(1)}, bf16[896,128]{1,0:T(8,128)(2,1)S(1)}, u32[]{:S(2)}, u32[]{:S(2)}) collective-permute-start(bf16[896,128]{1,0:T(8,128)(2,1)S(1)} %collective-permute-done.12.refs_4_), channel_id=1, source_target_pairs={{0,452},{64,0},{128,64},{192,128},{256,192},{320,256},{384,320},{4... | collective-permute-start | bytes 688136 | tf_op jit(solution)/shard_map/ppermute | solution.py:22
  81.7 4.6 %collective-permute-start.10 = (bf16[896,128]{1,0:T(8,128)(2,1)S(1)}, bf16[896,128]{1,0:T(8,128)(2,1)S(1)}, u32[]{:S(2)}, u32[]{:S(2)}) collective-permute-start(bf16[896,128]{1,0:T(8,128)(2,1)S(1)} %collective-permute-done.9.refs_2_), channel_id=1, source_target_pairs={{0,64},{64,128},{128,192},{192,256},{256,320},{320,384},{384,448},... | collective-permute-start | bytes 688136 | tf_op jit(solution)/shard_map/ppermute | solution.py:22
  86.3 1.5 collective-permute-done.13.refs_5_
  87.8 1.9 %collective-permute-start.14 = (bf16[896,128]{1,0:T(8,128)(2,1)S(1)}, bf16[896,128]{1,0:T(8,128)(2,1)}, u32[]{:S(2)}, u32[]{:S(2)}) collective-permute-start(bf16[896,128]{1,0:T(8,128)(2,1)S(1)} %collective-permute-done.13.refs_5_), channel_id=1, source_target_pairs={{0,452},{64,0},{128,64},{192,128},{256,192},{320,256},{384,320},{4... | collective-permute-start | bytes 688136 | tf_op jit(solution)/shard_map/ppermute | solution.py:22
  89.7 4.6 %collective-permute-start.11 = (bf16[896,128]{1,0:T(8,128)(2,1)S(1)}, bf16[896,128]{1,0:T(8,128)(2,1)}, u32[]{:S(2)}, u32[]{:S(2)}) collective-permute-start(bf16[896,128]{1,0:T(8,128)(2,1)S(1)} %collective-permute-done.10.refs_1_), channel_id=1, source_target_pairs={{0,64},{64,128},{128,192},{192,256},{256,320},{320,384},{384,448},... | collective-permute-start | bytes 688136 | tf_op jit(solution)/shard_map/ppermute | solution.py:22
  94.3 2.1 %collective-permute-done.14.refs_6_ = bf16[896,128]{1,0:T(8,128)(2,1)} collective-permute-done((bf16[896,128]{1,0:T(8,128)(2,1)S(1)}, bf16[896,128]{1,0:T(8,128)(2,1)}, u32[]{:S(2)}, u32[]{:S(2)}) %collective-permute-start.14) | collective-permute-done | bytes 229408 | tf_op jit(solution)/shard_map/ppermute | solution.py:22
  96.4 1.9 %collective-permute-start.15 = (bf16[896,128]{1,0:T(8,128)(2,1)}, bf16[896,128]{1,0:T(8,128)(2,1)S(1)}, u32[]{:S(2)}, u32[]{:S(2)}) collective-permute-start(bf16[896,128]{1,0:T(8,128)(2,1)} %collective-permute-done.14.refs_6_), channel_id=1, source_target_pairs={{0,452},{64,0},{128,64},{192,128},{256,192},{320,256},{384,320},{4... | collective-permute-start | bytes 688136 | tf_op jit(solution)/shard_map/ppermute | solution.py:22
  98.3 3.8 %shard_map.77 = (bf16[896,512]{1,0:T(8,128)(2,1)S(1)}, f32[896,512]{1,0:T(8,128)S(1)}) custom-call(s32[1]{0:T(128)} %bitcast.2.core_ref, bf16[512,512]{1,0:T(8,128)(2,1)S(1)} %bitcast.33, bf16[512,512]{1,0:T(8,128)(2,1)S(1)} %collective-permute-done.1.other_ref, bf16[512,896]{1,0:T(8,128)(2,1)S(1)} %pad_maximum_fusion.weights_ref, ...), custom_call_target="tpu_custom_call" | custom-call | tf_op jit(solution)/shard_map/pallas_call | solution.py:103
  102.1 3.7 %collective-permute-done.15.tile_ref = bf16[896,128]{1,0:T(8,128)(2,1)S(1)} collective-permute-done((bf16[896,128]{1,0:T(8,128)(2,1)}, bf16[896,128]{1,0:T(8,128)(2,1)S(1)}, u32[]{:S(2)}, u32[]{:S(2)}) %collective-permute-start.15) | collective-permute-done | bytes 229408 | tf_op jit(solution)/shard_map/ppermute | solution.py:22
  105.8 0.4 shard_map.78
  106.2 0.8 copy-done
  107.0 1.5 shard_map.79
  108.5 15.2 %all-to-all-start.2 = ((bf16[32,32,512]{2,1,0:T(8,128)(2,1)}), bf16[32,32,512]{2,1,0:T(8,128)(2,1)}, u32[]{:S(2)}, u32[]{:S(2)}) async-start(bf16[32,32,512]{2,1,0:T(8,128)(2,1)} %bitcast.5), calls=%async_computation.2 | async-start | bytes 2097152 | tf_op jit(solution)/shard_map/all_to_all | solution.py:234
  123.7 2.3 %collective-permute-start.17 = (bf16[448,512]{1,0:T(8,128)(2,1)S(1)}, bf16[448,512]{1,0:T(8,128)(2,1)S(1)}, u32[]{:S(2)}, u32[]{:S(2)}) collective-permute-start(bf16[448,512]{1,0:T(8,128)(2,1)S(1)} %copy-done.1), channel_id=1, source_target_pairs={{0,4},{4,0},{1,5},{5,1},{2,6},{6,2},{3,7},{7,3},{8,12},{12,8},{9,1... | collective-permute-start | bytes 1376264 | tf_op jit(solution)/shard_map/ppermute | solution.py:232
  126.0 12.5 %all-to-all-done.2 = bf16[32,32,512]{2,1,0:T(8,128)(2,1)} async-done(((bf16[32,32,512]{2,1,0:T(8,128)(2,1)}), bf16[32,32,512]{2,1,0:T(8,128)(2,1)}, u32[]{:S(2)}, u32[]{:S(2)}) %all-to-all-start.2) | async-done | bytes 1048608 | tf_op jit(solution)/shard_map/all_to_all | solution.py:234
  138.6 1.4 reduce_sum.12
  139.9 0.8 copy.19
  140.7 4.6 %all-to-all-start.3 = ((bf16[128,2,1,224]{3,1,2,0:T(2,128)(2,1)}), bf16[128,2,1,224]{3,1,2,0:T(2,128)(2,1)S(1)}, u32[]{:S(2)}, u32[]{:S(2)}) async-start(bf16[128,2,1,224]{3,1,2,0:T(2,128)(2,1)} %copy.19), calls=%async_computation.3 | async-start | bytes 262144 | tf_op jit(solution)/shard_map/all_to_all | solution.py:239
  145.3 2.4 %collective-permute-start.16 = (bf16[32,512]{1,0:T(8,128)(2,1)S(1)}, bf16[32,512]{1,0:T(8,128)(2,1)S(1)}, u32[]{:S(2)}, u32[]{:S(2)}) collective-permute-start(bf16[32,512]{1,0:T(8,128)(2,1)S(1)} %reduce_sum.12), channel_id=1, source_target_pairs={{0,44},{16,52},{32,60},{48,0},{8,8},{24,16},{40,24},{56,32},{64,11... | collective-permute-start | bytes 98312 | tf_op jit(solution)/shard_map/ppermute | solution.py:242
  147.7 1.5 all-to-all-done.3
  149.3 28.8 %collective-permute-done.16 = bf16[32,512]{1,0:T(8,128)(2,1)S(1)} collective-permute-done((bf16[32,512]{1,0:T(8,128)(2,1)S(1)}, bf16[32,512]{1,0:T(8,128)(2,1)S(1)}, u32[]{:S(2)}, u32[]{:S(2)}) %collective-permute-start.16) | collective-permute-done | bytes 32800 | tf_op jit(solution)/shard_map/ppermute | solution.py:242
  178.1 0.1 copy.21
  178.2 0.8 reshape.39
  179.0 0.1 convert_add_fusion
  179.1 1.0 slice_bitcast_fusion
  180.1 0.6 copy.25
  (15 shorter events, 0.2 us)
Async XLA Ops:
  0.6 10.7 %collective-permute-start = (bf16[32,512]{1,0:T(8,128)(2,1)}, bf16[32,512]{1,0:T(8,128)(2,1)S(1)}, u32[]{:S(2)}, u32[]{:S(2)}) collective-permute-start(bf16[32,512]{1,0:T(8,128)(2,1)} %param.4), channel_id=1, source_target_pairs={{324,0},{388,16},{452,32},{0,48},{64,8},{128,24},{192,40},{256,56}... | collective-permute-start | bytes 98312 | tf_op jit(solution)/shard_map/ppermute | solution.py:187
  12.2 14.4 %all-to-all-start = ((bf16[16,32,512]{2,1,0:T(8,128)(2,1)}), bf16[16,32,512]{2,1,0:T(8,128)(2,1)S(1)}, u32[]{:S(2)}, u32[]{:S(2)}) async-start(bf16[16,32,512]{2,1,0:T(8,128)(2,1)} %broadcast_in_dim.2), calls=%async_computation | async-start | bytes 1048576 | tf_op jit(solution)/shard_map/all_to_all | solution.py:189
  26.6 4.2 %collective-permute-start.1 = (bf16[512,512]{1,0:T(8,128)(2,1)S(1)}, bf16[512,512]{1,0:T(8,128)(2,1)S(1)}, u32[]{:S(2)}, u32[]{:S(2)}) collective-permute-start(bf16[512,512]{1,0:T(8,128)(2,1)S(1)} %bitcast.30), channel_id=1, source_target_pairs={{0,8},{8,0},{1,9},{9,1},{2,10},{10,2},{3,11},{11,3},{4,12},{12,4},... | collective-permute-start | bytes 1572872 | tf_op jit(solution)/shard_map/ppermute | solution.py:61
  31.4 14.1 %collective-permute-start.2 = (bf16[896,128]{1,0:T(8,128)(2,1)S(1)}, bf16[896,128]{1,0:T(8,128)(2,1)S(1)}, u32[]{:S(2)}, u32[]{:S(2)}) collective-permute-start(bf16[896,128]{1,0:T(8,128)(2,1)S(1)} %get-tuple-element.30), channel_id=1, source_target_pairs={{0,64},{64,128},{128,192},{192,256},{256,320},{320,384},{384,448},... | collective-permute-start | bytes 688136 | tf_op jit(solution)/shard_map/ppermute | solution.py:22
  38.0 24.0 %all-to-all-start.1 = ((bf16[4,32,2,224]{3,2,1,0:T(2,128)(2,1)}), bf16[4,32,2,224]{3,2,1,0:T(2,128)(2,1)S(1)}, u32[]{:S(2)}, u32[]{:S(2)}) async-start(bf16[4,32,2,224]{3,2,1,0:T(2,128)(2,1)} %bitcast.29), calls=%async_computation.1 | async-start | bytes 262144 | tf_op jit(solution)/shard_map/all_to_all | solution.py:194
  42.5 9.0 %collective-permute-start.5 = (bf16[896,128]{1,0:T(8,128)(2,1)S(1)}, bf16[896,128]{1,0:T(8,128)(2,1)S(1)}, u32[]{:S(2)}, u32[]{:S(2)}) collective-permute-start(bf16[896,128]{1,0:T(8,128)(2,1)S(1)} %get-tuple-element.37), channel_id=1, source_target_pairs={{0,452},{64,0},{128,64},{192,128},{256,192},{320,256},{384,320},{4... | collective-permute-start | bytes 688136 | tf_op jit(solution)/shard_map/ppermute | solution.py:22
  45.6 8.0 %collective-permute-start.3 = (bf16[896,128]{1,0:T(8,128)(2,1)S(1)}, bf16[896,128]{1,0:T(8,128)(2,1)S(1)}, u32[]{:S(2)}, u32[]{:S(2)}) collective-permute-start(bf16[896,128]{1,0:T(8,128)(2,1)S(1)} %add_convert_fusion.4), channel_id=1, source_target_pairs={{0,64},{64,128},{128,192},{192,256},{256,320},{320,384},{384,448},... | collective-permute-start | bytes 688136 | tf_op jit(solution)/shard_map/ppermute | solution.py:22
  51.5 8.0 %collective-permute-start.6 = (bf16[896,128]{1,0:T(8,128)(2,1)S(1)}, bf16[896,128]{1,0:T(8,128)(2,1)S(1)}, u32[]{:S(2)}, u32[]{:S(2)}) collective-permute-start(bf16[896,128]{1,0:T(8,128)(2,1)S(1)} %add_convert_fusion.1), channel_id=1, source_target_pairs={{0,452},{64,0},{128,64},{192,128},{256,192},{320,256},{384,320},{4... | collective-permute-start | bytes 688136 | tf_op jit(solution)/shard_map/ppermute | solution.py:22
  53.6 8.3 %collective-permute-start.4 = (bf16[896,128]{1,0:T(8,128)(2,1)S(1)}, bf16[896,128]{1,0:T(8,128)(2,1)S(1)}, u32[]{:S(2)}, u32[]{:S(2)}) collective-permute-start(bf16[896,128]{1,0:T(8,128)(2,1)S(1)} %add_convert_fusion.3), channel_id=1, source_target_pairs={{0,64},{64,128},{128,192},{192,256},{256,320},{320,384},{384,448},... | collective-permute-start | bytes 688136 | tf_op jit(solution)/shard_map/ppermute | solution.py:22
  59.6 8.0 %collective-permute-start.7 = (bf16[896,128]{1,0:T(8,128)(2,1)S(1)}, bf16[896,128]{1,0:T(8,128)(2,1)S(1)}, u32[]{:S(2)}, u32[]{:S(2)}) collective-permute-start(bf16[896,128]{1,0:T(8,128)(2,1)S(1)} %add_convert_fusion), channel_id=1, source_target_pairs={{0,452},{64,0},{128,64},{192,128},{256,192},{320,256},{384,320},{4... | collective-permute-start | bytes 688136 | tf_op jit(solution)/shard_map/ppermute | solution.py:22
  62.0 8.0 %collective-permute-start.8 = (bf16[896,128]{1,0:T(8,128)(2,1)S(1)}, bf16[896,128]{1,0:T(8,128)(2,1)}, u32[]{:S(2)}, u32[]{:S(2)}) collective-permute-start(bf16[896,128]{1,0:T(8,128)(2,1)S(1)} %add_convert_fusion.2), channel_id=1, source_target_pairs={{0,64},{64,128},{128,192},{192,256},{256,320},{320,384},{384,448},... | collective-permute-start | bytes 688136 | tf_op jit(solution)/shard_map/ppermute | solution.py:22
  71.3 8.5 %collective-permute-start.12 = (bf16[896,128]{1,0:T(8,128)(2,1)S(1)}, bf16[896,128]{1,0:T(8,128)(2,1)S(1)}, u32[]{:S(2)}, u32[]{:S(2)}) collective-permute-start(bf16[896,128]{1,0:T(8,128)(2,1)S(1)} %pad_maximum_fusion.3.refs_3_), channel_id=1, source_target_pairs={{0,452},{64,0},{128,64},{192,128},{256,192},{320,256},{384,320},{4... | collective-permute-start | bytes 688136 | tf_op jit(solution)/shard_map/ppermute | solution.py:22
  73.2 8.5 %collective-permute-start.9 = (bf16[896,128]{1,0:T(8,128)(2,1)S(1)}, bf16[896,128]{1,0:T(8,128)(2,1)S(1)}, u32[]{:S(2)}, u32[]{:S(2)}) collective-permute-start(bf16[896,128]{1,0:T(8,128)(2,1)S(1)} %pad_maximum_fusion.3.refs_3_), channel_id=1, source_target_pairs={{0,64},{64,128},{128,192},{192,256},{256,320},{320,384},{384,448},... | collective-permute-start | bytes 688136 | tf_op jit(solution)/shard_map/ppermute | solution.py:22
  79.8 8.0 %collective-permute-start.13 = (bf16[896,128]{1,0:T(8,128)(2,1)S(1)}, bf16[896,128]{1,0:T(8,128)(2,1)S(1)}, u32[]{:S(2)}, u32[]{:S(2)}) collective-permute-start(bf16[896,128]{1,0:T(8,128)(2,1)S(1)} %collective-permute-done.12.refs_4_), channel_id=1, source_target_pairs={{0,452},{64,0},{128,64},{192,128},{256,192},{320,256},{384,320},{4... | collective-permute-start | bytes 688136 | tf_op jit(solution)/shard_map/ppermute | solution.py:22
  81.7 8.0 %collective-permute-start.10 = (bf16[896,128]{1,0:T(8,128)(2,1)S(1)}, bf16[896,128]{1,0:T(8,128)(2,1)S(1)}, u32[]{:S(2)}, u32[]{:S(2)}) collective-permute-start(bf16[896,128]{1,0:T(8,128)(2,1)S(1)} %collective-permute-done.9.refs_2_), channel_id=1, source_target_pairs={{0,64},{64,128},{128,192},{192,256},{256,320},{320,384},{384,448},... | collective-permute-start | bytes 688136 | tf_op jit(solution)/shard_map/ppermute | solution.py:22
  87.8 8.6 %collective-permute-start.14 = (bf16[896,128]{1,0:T(8,128)(2,1)S(1)}, bf16[896,128]{1,0:T(8,128)(2,1)}, u32[]{:S(2)}, u32[]{:S(2)}) collective-permute-start(bf16[896,128]{1,0:T(8,128)(2,1)S(1)} %collective-permute-done.13.refs_5_), channel_id=1, source_target_pairs={{0,452},{64,0},{128,64},{192,128},{256,192},{320,256},{384,320},{4... | collective-permute-start | bytes 688136 | tf_op jit(solution)/shard_map/ppermute | solution.py:22
  89.7 8.6 %collective-permute-start.11 = (bf16[896,128]{1,0:T(8,128)(2,1)S(1)}, bf16[896,128]{1,0:T(8,128)(2,1)}, u32[]{:S(2)}, u32[]{:S(2)}) collective-permute-start(bf16[896,128]{1,0:T(8,128)(2,1)S(1)} %collective-permute-done.10.refs_1_), channel_id=1, source_target_pairs={{0,64},{64,128},{128,192},{192,256},{256,320},{320,384},{384,448},... | collective-permute-start | bytes 688136 | tf_op jit(solution)/shard_map/ppermute | solution.py:22
  96.4 9.5 %collective-permute-start.15 = (bf16[896,128]{1,0:T(8,128)(2,1)}, bf16[896,128]{1,0:T(8,128)(2,1)S(1)}, u32[]{:S(2)}, u32[]{:S(2)}) collective-permute-start(bf16[896,128]{1,0:T(8,128)(2,1)} %collective-permute-done.14.refs_6_), channel_id=1, source_target_pairs={{0,452},{64,0},{128,64},{192,128},{256,192},{320,256},{384,320},{4... | collective-permute-start | bytes 688136 | tf_op jit(solution)/shard_map/ppermute | solution.py:22
  106.2 0.8 copy-start
  107.0 16.7 %copy-start.1 = (bf16[448,512]{1,0:T(8,128)(2,1)S(1)}, bf16[448,512]{1,0:T(8,128)(2,1)}, u32[]{:S(2)}) copy-start(bf16[448,512]{1,0:T(8,128)(2,1)} %copy-done) | copy-start | bytes 1376260
  108.5 30.1 %all-to-all-start.2 = ((bf16[32,32,512]{2,1,0:T(8,128)(2,1)}), bf16[32,32,512]{2,1,0:T(8,128)(2,1)}, u32[]{:S(2)}, u32[]{:S(2)}) async-start(bf16[32,32,512]{2,1,0:T(8,128)(2,1)} %bitcast.5), calls=%async_computation.2 | async-start | bytes 2097152 | tf_op jit(solution)/shard_map/all_to_all | solution.py:234
  123.7 55.3 %collective-permute-start.17 = (bf16[448,512]{1,0:T(8,128)(2,1)S(1)}, bf16[448,512]{1,0:T(8,128)(2,1)S(1)}, u32[]{:S(2)}, u32[]{:S(2)}) collective-permute-start(bf16[448,512]{1,0:T(8,128)(2,1)S(1)} %copy-done.1), channel_id=1, source_target_pairs={{0,4},{4,0},{1,5},{5,1},{2,6},{6,2},{3,7},{7,3},{8,12},{12,8},{9,1... | collective-permute-start | bytes 1376264 | tf_op jit(solution)/shard_map/ppermute | solution.py:232
  140.7 8.5 %all-to-all-start.3 = ((bf16[128,2,1,224]{3,1,2,0:T(2,128)(2,1)}), bf16[128,2,1,224]{3,1,2,0:T(2,128)(2,1)S(1)}, u32[]{:S(2)}, u32[]{:S(2)}) async-start(bf16[128,2,1,224]{3,1,2,0:T(2,128)(2,1)} %copy.19), calls=%async_computation.3 | async-start | bytes 262144 | tf_op jit(solution)/shard_map/all_to_all | solution.py:239
  145.3 32.8 %collective-permute-start.16 = (bf16[32,512]{1,0:T(8,128)(2,1)S(1)}, bf16[32,512]{1,0:T(8,128)(2,1)S(1)}, u32[]{:S(2)}, u32[]{:S(2)}) collective-permute-start(bf16[32,512]{1,0:T(8,128)(2,1)S(1)} %reduce_sum.12), channel_id=1, source_target_pairs={{0,44},{16,52},{32,60},{48,0},{8,8},{24,16},{40,24},{56,32},{64,11... | collective-permute-start | bytes 98312 | tf_op jit(solution)/shard_map/ppermute | solution.py:242

commit v9 on v8

v9 whole, which is shorter than its diff:
```python
import functools

import jax
import jax.numpy as jnp
from jax import lax
from jax.experimental import pallas as pl
from jax.experimental.pallas import tpu as pltpu
from jax.sharding import Mesh, PartitionSpec as P

RING = 16
ROWS = 8
FORWARD = ((3, -1), (3, 0), (3, 1), (0, -1), (0, 0), (0, 1), (-3, -1), (-3, 0))
BACKWARD = ((-3, 0), (-2, 0), (-1, 0), (0, 0), (1, 0), (2, 0), (3, 0), (3, -1))


def ring_index(z):
    z %= RING
    return (z % ROWS) * 2 + z // ROWS


def ring_shift(value, step):
    pairs = [(ring_index(z), ring_index(z + step)) for z in range(RING)]
    return lax.ppermute(value, ("r", "h"), pairs)


def place(z, col):
    z %= RING
    return ((z % ROWS) * ROWS + col) * 2 + z // ROWS


def slot(at):
    return (at % 4) * 2 + at // 4


def token_pairs():
    pairs = []
    for z in range(RING):
        for at, (ahead, block) in enumerate(FORWARD):
            pairs.append((place(z + ahead, (z + block) % ROWS), place(z, slot(at))))
    return pairs


def result_pairs():
    pairs = []
    for z in range(RING):
        for at, (ahead, block) in enumerate(BACKWARD):
            tile = (z + ahead) % RING
            row = (z + block) % ROWS
            pairs.append((place(z, slot(at)), place(row + ROWS * (tile // ROWS), tile % ROWS)))
    return pairs


def dot_f32(left, right, dims=((1,), (0,))):
    return lax.dot_general(left, right, (dims, ((), ())), preferred_element_type=jnp.float32)


SMEM_SPEC = pl.BlockSpec(memory_space=pltpu.SMEM)
VMEM_SPEC = pl.BlockSpec(memory_space=pltpu.VMEM)
PARAMS = pltpu.CompilerParams(vmem_limit_bytes=16 << 20)


def swap_cores(value):
    return lax.ppermute(value, "c", [(0, 1), (1, 0)])


def join_cores(core, own_ref, other_ref, both_ref):
    rows = own_ref.shape[0]
    both_ref[pl.ds(pl.multiple_of(core * rows, rows), rows), :] = own_ref[...]
    both_ref[pl.ds(pl.multiple_of((1 - core) * rows, rows), rows), :] = other_ref[...]


def tile_product(tokens_ref, ats, weights_refs):
    total = 0.0
    for at, weights_ref in zip(ats, weights_refs):
        total = total + dot_f32(tokens_ref[at * 128 : (at + 1) * 128, :], weights_ref[...])
    return total.T


def sends_kernel(core_ref, own_ref, other_ref, below_ref, here_ref, above_ref, up_ref, down_ref, tokens_ref):
    join_cores(core_ref[0], own_ref, other_ref, tokens_ref)
    weights_refs = (below_ref, here_ref, above_ref)
    up_ref[...] = tile_product(tokens_ref, (0, 1, 2), weights_refs).astype(jnp.bfloat16)
    down_ref[...] = tile_product(tokens_ref, (6, 7), weights_refs).astype(jnp.bfloat16)


def own_kernel(core_ref, own_ref, other_ref, below_ref, here_ref, above_ref, out_ref, *refs):
    tokens_ref = refs[-1]
    join_cores(core_ref[0], own_ref, other_ref, tokens_ref)
    out_ref[...] = tile_product(tokens_ref, (3, 4, 5), (below_ref, here_ref, above_ref))
    for tokens_out_ref, ats in zip(refs, ((0, 3, 6), (2, 5), (7, 4, 1))):
        for row, at in enumerate(ats):
            tokens_out_ref[row * 128 : (row + 1) * 128, :] = tokens_ref[at * 128 : (at + 1) * 128, :]


def forward(kernel, outs, core, own, other, weights):
    return pl.pallas_call(
        kernel,
        in_specs=[SMEM_SPEC] + [VMEM_SPEC] * 5,
        out_specs=[VMEM_SPEC] * len(outs),
        out_shape=outs,
        scratch_shapes=[pltpu.VMEM((ROWS * 128, own.shape[1]), jnp.bfloat16)],
        compiler_params=PARAMS,
    )(core, own, other, *weights)


def forward_sends(core, own, other, weights):
    tile = jax.ShapeDtypeStruct((weights[0].shape[1], 128), jnp.bfloat16)
    return forward(sends_kernel, [tile, tile], core, own, other, weights)


def own_sums(core, own, other, weights):
    features, cols = weights[0].shape
    outs = [jax.ShapeDtypeStruct((cols, 128), jnp.float32)]
    outs += [jax.ShapeDtypeStruct((128 * count, features), jnp.bfloat16) for count in (3, 2, 3)]
    return forward(own_kernel, outs, core, own, other, weights)


def near_kernel(weights_ref, mine_ref, right_ref, left_ref, *refs):
    tile_refs = refs[:5]
    terms_ref, sums_ref, tokens_ref, wide_ref = refs[5:]
    sources = ((right_ref, 2), (left_ref, 1), (mine_ref, 1), (right_ref, 1), (left_ref, 0))
    for at, (tile_ref, (source_ref, row)) in enumerate(zip(tile_refs, sources)):
        tokens_ref[at * 128 : (at + 1) * 128, :] = source_ref[row * 128 : (row + 1) * 128, :]
        wide_ref[:, at * 128 : (at + 1) * 128] = tile_ref[...]
        product = dot_f32(weights_ref[...], tile_ref[...])
        terms_ref[at * 128 : (at + 1) * 128, :] = product.T.astype(jnp.bfloat16)
    sums_ref[...] = dot_f32(wide_ref[...], tokens_ref[...])


def near_products(weights, mine, right, left, tiles):
    features, cols = weights.shape
    return pl.pallas_call(
        near_kernel,
        in_specs=[VMEM_SPEC] * 9,
        out_specs=[VMEM_SPEC] * 2,
        out_shape=[
            jax.ShapeDtypeStruct((5 * 128, features), jnp.bfloat16),
            jax.ShapeDtypeStruct((cols, features), jnp.float32),
        ],
        scratch_shapes=[
            pltpu.VMEM((5 * 128, features), jnp.bfloat16),
            pltpu.VMEM((cols, 5 * 128), jnp.bfloat16),
        ],
        compiler_params=PARAMS,
    )(weights, mine, right, left, *tiles)


def third_kernel(here_ref, below_ref, mine_ref, terms_ref, sums_ref, low_ref, high_ref, *refs):
    all_ref, out_ref, tokens_ref, wide_ref = refs
    for at in range(1, 6):
        all_ref[slot(at) * 128 : (slot(at) + 1) * 128, :] = terms_ref[(at - 1) * 128 : at * 128, :]
    for at, tile_ref, weights_ref in ((0, low_ref, here_ref), (6, high_ref, here_ref), (7, high_ref, below_ref)):
        product = dot_f32(weights_ref[...], tile_ref[...])
        all_ref[slot(at) * 128 : (slot(at) + 1) * 128, :] = product.T.astype(jnp.bfloat16)
    tokens_ref[0:128, :] = mine_ref[0:128, :]
    tokens_ref[128:256, :] = mine_ref[256:384, :]
    wide_ref[:, 0:128] = low_ref[...]
    wide_ref[:, 128:256] = high_ref[...]
    out_ref[...] = sums_ref[...] + dot_f32(wide_ref[...], tokens_ref[...])


def third_products(here, below, mine, terms, sums, low, high):
    features, cols = here.shape
    return pl.pallas_call(
        third_kernel,
        in_specs=[VMEM_SPEC] * 7,
        out_specs=[VMEM_SPEC] * 2,
        out_shape=[
            jax.ShapeDtypeStruct((ROWS * 128, features), jnp.bfloat16),
            jax.ShapeDtypeStruct((cols, features), jnp.float32),
        ],
        scratch_shapes=[
            pltpu.VMEM((256, features), jnp.bfloat16),
            pltpu.VMEM((cols, 256), jnp.bfloat16),
        ],
        compiler_params=PARAMS,
    )(here, below, mine, terms, sums, low, high)


def last_kernel(half_ref, right_ref, sums_ref, tile_ref, keep_ref, send_ref):
    rows = keep_ref.shape[0]
    half = half_ref[0]
    send_rows = pl.ds(pl.multiple_of((1 - half) * rows, 16), rows)
    keep_rows = pl.ds(pl.multiple_of(half * rows, 16), rows)
    tokens = right_ref[0:128, :]
    send = sums_ref[send_rows, :] + dot_f32(tile_ref[send_rows, :], tokens)
    send_ref[...] = send.astype(jnp.bfloat16)
    keep_ref[...] = sums_ref[keep_rows, :] + dot_f32(tile_ref[keep_rows, :], tokens)


def last_sums(half, right, sums, tile):
    cols, features = sums.shape
    shape = (cols // 2, features)
    return pl.pallas_call(
        last_kernel,
        in_specs=[SMEM_SPEC] + [VMEM_SPEC] * 3,
        out_specs=[VMEM_SPEC] * 2,
        out_shape=[jax.ShapeDtypeStruct(shape, jnp.float32), jax.ShapeDtypeStruct(shape, jnp.bfloat16)],
        compiler_params=PARAMS,
    )(half, right, sums, tile)


def local(tokens, gate_weight, up_weight, grad_hidden):
    own_x = lax.axis_index("x")
    core = lax.axis_index("c").astype(jnp.int32).reshape(1)
    half = lax.axis_index("h").astype(jnp.int32).reshape(1)
    features, hidden_cols = gate_weight.shape
    part = hidden_cols // 8

    def own_columns(weight, which):
        return lax.dynamic_slice(weight, (0, (which * 4 + own_x) * part), (features, part))

    weights = jnp.concatenate(
        [own_columns(weight, which) for which in (0, 1) for weight in (gate_weight, up_weight)], 1
    )

    piece = lax.ppermute(tokens, ("r", "y", "c", "h"), token_pairs())
    piece, weights = lax.optimization_barrier((piece, weights))
    below = ring_shift(weights, 1)
    above = ring_shift(weights, -1)
    copies = jnp.broadcast_to(piece[None], (16,) + piece.shape)
    own_tokens = lax.all_to_all(copies, ("y", "x"), split_axis=0, concat_axis=0, tiled=True)
    own_tokens = own_tokens.reshape(-1, features)
    cotangent = grad_hidden.reshape(-1, 2, 4, part).transpose(2, 0, 1, 3)
    own_tokens, cotangent, below, above = lax.optimization_barrier((own_tokens, cotangent, below, above))
    other_tokens = swap_cores(own_tokens)
    cotangent = lax.all_to_all(cotangent, "x", split_axis=0, concat_axis=0, tiled=True)

    rows = (below, weights, above)
    up, down = forward_sends(core, own_tokens, other_tokens, rows)
    from_below = ring_shift(up, 3)
    from_above = ring_shift(down, -3)
    total, to_left, to_right, mine = own_sums(core, own_tokens, other_tokens, rows)
    right_tokens = ring_shift(to_left, -1)
    left_tokens = ring_shift(to_right, 1)
    from_below, from_above, cotangent = lax.optimization_barrier((from_below, from_above, cotangent))
    cotangent = cotangent.reshape(-1, 2 * part).T.astype(jnp.float32)
    total = total + from_below.astype(jnp.float32) + from_above.astype(jnp.float32)
    gate_pre = jnp.concatenate([total[:part], total[2 * part : 3 * part]], 0)
    up_pre = jnp.concatenate([total[part : 2 * part], total[3 * part :]], 0)

    sigmoid = jax.nn.sigmoid(gate_pre)
    silu = gate_pre * sigmoid
    hidden = (silu * up_pre).astype(jnp.bfloat16)
    grad_gate = (cotangent * up_pre * sigmoid * (1.0 + gate_pre * (1.0 - sigmoid))).astype(jnp.bfloat16)
    grad_up = (cotangent * silu).astype(jnp.bfloat16)
    grads = jnp.concatenate([grad_gate[:part], grad_up[:part], grad_gate[part:], grad_up[part:]], 0)

    left_1 = ring_shift(grads, -1)
    right_1 = ring_shift(grads, 1)
    left_2 = ring_shift(left_1, -1)
    right_2 = ring_shift(right_1, 1)
    left_3 = ring_shift(left_2, -1)
    right_3 = ring_shift(right_2, 1)
    terms, sums = near_products(
        weights, mine, right_tokens, left_tokens, [right_2, right_1, grads, left_1, left_2]
    )
    left_3, right_3, terms, sums = lax.optimization_barrier((left_3, right_3, terms, sums))
    left_4 = ring_shift(left_3, -1)
    terms, sums = third_products(weights, below, mine, terms, sums, right_3, left_3)
    left_4, terms = lax.optimization_barrier((left_4, terms))
    terms = lax.all_to_all(
        terms.reshape(32, -1, features), ("y", "c", "x"), split_axis=0, concat_axis=0, tiled=True
    )
    keep, send = last_sums(half, right_tokens, sums, left_4)
    received = lax.ppermute(send, "h", [(0, 1), (1, 0)])
    grad_tokens = jnp.sum(terms.astype(jnp.float32), 0).astype(jnp.bfloat16)
    grad_tokens, hidden = lax.optimization_barrier((grad_tokens, hidden))
    hidden = lax.all_to_all(
        hidden.T.reshape(-1, 2, 1, part), "x", split_axis=0, concat_axis=2, tiled=True
    )
    grad_tokens = lax.ppermute(grad_tokens, ("r", "y", "c", "h"), result_pairs())
    grad_tokens, hidden, keep = lax.optimization_barrier((grad_tokens, hidden, keep))
    grad_weights = keep + received.astype(jnp.float32)
    return hidden.reshape(-1, hidden_cols), grad_tokens, grad_weights[:part].T, grad_weights[part:].T


def solution(mesh):
    fine = Mesh(mesh.devices.reshape(8, 4, 2, 2, 4), ("r", "y", "c", "h", "x"))
    return jax.shard_map(
        local,
        mesh=fine,
        in_specs=(
            P(("r", "h", "x"), ("y", "c")),
            P("r", ("y", "c")),
            P("r", ("y", "c")),
            P(("r", "h", "x"), ("y", "c")),
        ),
        out_specs=(
            P(("r", "h", "x"), ("y", "c")),
            P(("y", "c", "h", "x"), "r"),
            P("r", ("y", "c", "h", "x")),
            P("r", ("y", "c", "h", "x")),
        ),
        check_vma=False,
    )
```

time: 182 us -> 194 us (1.066)
  the two profiles are of different devices: /device:TPU:235 before, /device:TPU:58 now
where the time goes in v9:
time: 194 us; the launch traced here: 192 us
  starting transfers between devices  98.7 us (51%)
  waiting for transfers between devices  64.7 us (33%)
  local copies, waits for them, and re-layouts  14 us (7%)
  Pallas kernels  8.85 us (5%)
  other arithmetic  5.09 us (3%)
    ppermute x13, starting transfers between devices, ring_shift(): return lax.ppermute(value, ('r', 'h'), pairs)  45.1 us
    ppermute x1, waiting for transfers between devices, local(): lax.ppermute(grad_tokens, ('r', 'y', 'c', 'h'), result_pairs())  34.2 us
    ppermute x13, waiting for transfers between devices, ring_shift(): return lax.ppermute(value, ('r', 'h'), pairs)  16.4 us
    ppermute x1, starting transfers between devices, local(): piece = lax.ppermute(tokens, ('r', 'y', 'c', 'h'), token_pairs())  12.1 us
    all_to_all x1, starting transfers between devices, local(): lax.all_to_all(terms.reshape(32, -1, features), ('y', 'c', 'x'), split_ax...  10.1 us
    ppermute x1, starting transfers between devices, local(): received = lax.ppermute(send, 'h', [(0, 1), (1, 0)])  9.4 us
    all_to_all x1, starting transfers between devices, local(): lax.all_to_all(copies, ('y', 'x'), split_axis=0, concat_axis=0, tiled=True)  6.96 us
    all_to_all x1, waiting for transfers between devices, local(): lax.all_to_all(copies, ('y', 'x'), split_axis=0, concat_axis=0, tiled=True)  6.66 us
  transfers between devices with their start and end apart: 21, of which 15 were waited for; matrix products, arithmetic and copies ran while one was open for 4% of the time, Pallas kernels for 3%

profile of v9, /device:TPU:58, one launch (start us, length us, event | category | flops | bytes accessed | tf_op | source)
XLA Modules:
  0.0 192.4 jit_solution(12049005797134623494)
XLA Ops:
  0.6 12.1 %collective-permute-start = (bf16[32,512]{1,0:T(8,128)(2,1)}, bf16[32,512]{1,0:T(8,128)(2,1)S(1)}, u32[]{:S(2)}, u32[]{:S(2)}) collective-permute-start(bf16[32,512]{1,0:T(8,128)(2,1)} %param.4), channel_id=1, source_target_pairs={{248,0},{192,16},{200,32},{56,48},{0,8},{8,24},{380,40},{324,56},{... | collective-permute-start | bytes 98312 | tf_op jit(solution)/shard_map/ppermute | solution.py:217
  12.7 1.8 constant_dynamic-slice_fusion.2
  14.5 0.4 pad_maximum_fusion.here_ref.weights_ref
  15.0 2.5 %collective-permute-start.2 = (bf16[512,896]{1,0:T(8,128)(2,1)S(1)}, bf16[512,896]{1,0:T(8,128)(2,1)S(1)}, u32[]{:S(2)}, u32[]{:S(2)}) collective-permute-start(bf16[512,896]{1,0:T(8,128)(2,1)S(1)} %pad_maximum_fusion.here_ref.weights_ref), channel_id=1, source_target_pairs={{0,452},{64,0},{128,64},{192,128},{256,192},{320,256},{384,320},{4... | collective-permute-start | bytes 2752520 | tf_op jit(solution)/shard_map/ppermute | solution.py:23
  17.5 3.4 %collective-permute-start.1 = (bf16[512,896]{1,0:T(8,128)(2,1)S(1)}, bf16[512,896]{1,0:T(8,128)(2,1)S(1)}, u32[]{:S(2)}, u32[]{:S(2)}) collective-permute-start(bf16[512,896]{1,0:T(8,128)(2,1)S(1)} %pad_maximum_fusion.here_ref.weights_ref), channel_id=1, source_target_pairs={{0,64},{64,128},{128,192},{192,256},{256,320},{320,384},{384,448},... | collective-permute-start | bytes 2752520 | tf_op jit(solution)/shard_map/ppermute | solution.py:23
  20.8 0.8 broadcast_in_dim.2
  21.7 7.0 %all-to-all-start = ((bf16[16,32,512]{2,1,0:T(8,128)(2,1)}), bf16[16,32,512]{2,1,0:T(8,128)(2,1)S(1)}, u32[]{:S(2)}, u32[]{:S(2)}) async-start(bf16[16,32,512]{2,1,0:T(8,128)(2,1)} %broadcast_in_dim.2), calls=%async_computation | async-start | bytes 1048576 | tf_op jit(solution)/shard_map/all_to_all | solution.py:222
  28.6 0.2 reshape.35
  28.9 0.7 copy.23
  29.6 6.7 %all-to-all-done = bf16[16,32,512]{2,1,0:T(8,128)(2,1)S(1)} async-done(((bf16[16,32,512]{2,1,0:T(8,128)(2,1)}), bf16[16,32,512]{2,1,0:T(8,128)(2,1)S(1)}, u32[]{:S(2)}, u32[]{:S(2)}) %all-to-all-start) | async-done | bytes 524320 | tf_op jit(solution)/shard_map/all_to_all | solution.py:222
  36.3 2.5 %collective-permute-done.2.above_ref = bf16[512,896]{1,0:T(8,128)(2,1)S(1)} collective-permute-done((bf16[512,896]{1,0:T(8,128)(2,1)S(1)}, bf16[512,896]{1,0:T(8,128)(2,1)S(1)}, u32[]{:S(2)}, u32[]{:S(2)}) %collective-permute-start.2) | collective-permute-done | bytes 917536 | tf_op jit(solution)/shard_map/ppermute | solution.py:23
  38.7 2.0 %collective-permute-done.1.below_ref = bf16[512,896]{1,0:T(8,128)(2,1)S(1)} collective-permute-done((bf16[512,896]{1,0:T(8,128)(2,1)S(1)}, bf16[512,896]{1,0:T(8,128)(2,1)S(1)}, u32[]{:S(2)}, u32[]{:S(2)}) %collective-permute-start.1) | collective-permute-done | bytes 917536 | tf_op jit(solution)/shard_map/ppermute | solution.py:23
  40.8 1.9 collective-permute-start.3
  42.7 2.0 %collective-permute-done.3.other_ref = bf16[512,512]{1,0:T(8,128)(2,1)} collective-permute-done((bf16[512,512]{1,0:T(8,128)(2,1)S(1)}, bf16[512,512]{1,0:T(8,128)(2,1)}, u32[]{:S(2)}, u32[]{:S(2)}) %collective-permute-start.3) | collective-permute-done | bytes 524320 | tf_op jit(solution)/shard_map/ppermute | solution.py:63
  44.7 2.8 %shard_map.75 = (bf16[896,128]{1,0:T(8,128)(2,1)}, bf16[896,128]{1,0:T(8,128)(2,1)}) custom-call(s32[1]{0:T(128)} %bitcast.core_ref, bf16[512,512]{1,0:T(8,128)(2,1)S(1)} %bitcast.31, bf16[512,512]{1,0:T(8,128)(2,1)} %collective-permute-done.3.other_ref, bf16[512,896]{1,0:T(8,128)(2,1)S(1)} %collective-permute-done.1.below_ref, ...), custom_call_target="tpu_custom_call" | custom-call | tf_op jit(solution)/shard_map/pallas_call | solution.py:96
  47.5 5.4 %collective-permute-start.4 = (bf16[896,128]{1,0:T(8,128)(2,1)}, bf16[896,128]{1,0:T(8,128)(2,1)}, u32[]{:S(2)}, u32[]{:S(2)}) collective-permute-start(bf16[896,128]{1,0:T(8,128)(2,1)} %get-tuple-element.41), channel_id=1, source_target_pairs={{0,192},{64,256},{128,320},{192,384},{256,448},{320,4},{384,68},{4... | collective-permute-start | bytes 688136 | tf_op jit(solution)/shard_map/ppermute | solution.py:23
  52.9 3.4 %collective-permute-start.5 = (bf16[896,128]{1,0:T(8,128)(2,1)}, bf16[896,128]{1,0:T(8,128)(2,1)}, u32[]{:S(2)}, u32[]{:S(2)}) collective-permute-start(bf16[896,128]{1,0:T(8,128)(2,1)} %get-tuple-element.42), channel_id=1, source_target_pairs={{0,324},{64,388},{128,452},{192,0},{256,64},{320,128},{384,192},{4... | collective-permute-start | bytes 688136 | tf_op jit(solution)/shard_map/ppermute | solution.py:23
  56.3 4.8 %all-to-all-start.1 = ((bf16[4,32,2,224]{3,2,1,0:T(2,128)(2,1)}), bf16[4,32,2,224]{3,2,1,0:T(2,128)(2,1)}, u32[]{:S(2)}, u32[]{:S(2)}) async-start(bf16[4,32,2,224]{3,2,1,0:T(2,128)(2,1)} %bitcast.29), calls=%async_computation.1 | async-start | bytes 262144 | tf_op jit(solution)/shard_map/all_to_all | solution.py:227
  61.2 1.8 shard_map.76
  63.0 0.7 copy-done.2
  63.8 0.8 copy-done.5
  64.5 0.7 copy-done.8
  65.3 0.5 all-to-all-done.1
  65.8 5.4 %collective-permute-done.5 = bf16[896,128]{1,0:T(8,128)(2,1)} collective-permute-done((bf16[896,128]{1,0:T(8,128)(2,1)}, bf16[896,128]{1,0:T(8,128)(2,1)}, u32[]{:S(2)}, u32[]{:S(2)}) %collective-permute-start.5) | collective-permute-done | bytes 229408 | tf_op jit(solution)/shard_map/ppermute | solution.py:23
  71.2 1.2 convert_add_fusion.1
  72.5 0.8 fusion.5
  73.2 1.0 reshape.40
  74.3 0.1 copy.18
  74.4 1.9 multiply_convert_fusion
  76.3 2.4 %collective-permute-start.9 = (bf16[896,128]{1,0:T(8,128)(2,1)S(1)}, bf16[896,128]{1,0:T(8,128)(2,1)S(1)}, u32[]{:S(2)}, u32[]{:S(2)}) collective-permute-start(bf16[896,128]{1,0:T(8,128)(2,1)S(1)} %pad_maximum_fusion.3.refs_2_), channel_id=1, source_target_pairs={{0,64},{64,128},{128,192},{192,256},{256,320},{320,384},{384,448},... | collective-permute-start | bytes 688136 | tf_op jit(solution)/shard_map/ppermute | solution.py:23
  78.7 4.9 %collective-permute-start.6 = (bf16[896,128]{1,0:T(8,128)(2,1)S(1)}, bf16[896,128]{1,0:T(8,128)(2,1)S(1)}, u32[]{:S(2)}, u32[]{:S(2)}) collective-permute-start(bf16[896,128]{1,0:T(8,128)(2,1)S(1)} %pad_maximum_fusion.3.refs_2_), channel_id=1, source_target_pairs={{0,452},{64,0},{128,64},{192,128},{256,192},{320,256},{384,320},{4... | collective-permute-start | bytes 688136 | tf_op jit(solution)/shard_map/ppermute | solution.py:23
  83.6 2.8 %collective-permute-done.9.refs_1_ = bf16[896,128]{1,0:T(8,128)(2,1)S(1)} collective-permute-done((bf16[896,128]{1,0:T(8,128)(2,1)S(1)}, bf16[896,128]{1,0:T(8,128)(2,1)S(1)}, u32[]{:S(2)}, u32[]{:S(2)}) %collective-permute-start.9) | collective-permute-done | bytes 229408 | tf_op jit(solution)/shard_map/ppermute | solution.py:23
  86.4 2.6 %collective-permute-start.10 = (bf16[896,128]{1,0:T(8,128)(2,1)S(1)}, bf16[896,128]{1,0:T(8,128)(2,1)S(1)}, u32[]{:S(2)}, u32[]{:S(2)}) collective-permute-start(bf16[896,128]{1,0:T(8,128)(2,1)S(1)} %collective-permute-done.9.refs_1_), channel_id=1, source_target_pairs={{0,64},{64,128},{128,192},{192,256},{256,320},{320,384},{384,448},... | collective-permute-start | bytes 688136 | tf_op jit(solution)/shard_map/ppermute | solution.py:23
  89.0 0.5 collective-permute-done.6.refs_3_
  89.5 3.7 %collective-permute-start.7 = (bf16[896,128]{1,0:T(8,128)(2,1)S(1)}, bf16[896,128]{1,0:T(8,128)(2,1)S(1)}, u32[]{:S(2)}, u32[]{:S(2)}) collective-permute-start(bf16[896,128]{1,0:T(8,128)(2,1)S(1)} %collective-permute-done.6.refs_3_), channel_id=1, source_target_pairs={{0,452},{64,0},{128,64},{192,128},{256,192},{320,256},{384,320},{4... | collective-permute-start | bytes 688136 | tf_op jit(solution)/shard_map/ppermute | solution.py:23
  93.2 5.1 %collective-permute-start.12 = (bf16[384,512]{1,0:T(8,128)(2,1)S(1)}, bf16[384,512]{1,0:T(8,128)(2,1)S(1)}, u32[]{:S(2)}, u32[]{:S(2)}) collective-permute-start(bf16[384,512]{1,0:T(8,128)(2,1)S(1)} %copy-done.9), channel_id=1, source_target_pairs={{0,452},{64,0},{128,64},{192,128},{256,192},{320,256},{384,320},{4... | collective-permute-start | bytes 1179656 | tf_op jit(solution)/shard_map/ppermute | solution.py:23
  98.3 1.9 collective-permute-start.13
  100.3 1.9 collective-permute-start.11
  102.2 3.9 %collective-permute-start.8 = (bf16[896,128]{1,0:T(8,128)(2,1)S(1)}, bf16[896,128]{1,0:T(8,128)(2,1)S(1)}, u32[]{:S(2)}, u32[]{:S(2)}) collective-permute-start(bf16[896,128]{1,0:T(8,128)(2,1)S(1)} %collective-permute-done.7.refs_4_), channel_id=1, source_target_pairs={{0,452},{64,0},{128,64},{192,128},{256,192},{320,256},{384,320},{4... | collective-permute-start | bytes 688136 | tf_op jit(solution)/shard_map/ppermute | solution.py:23
  106.2 1.9 %collective-permute-done.13.left_ref = bf16[256,512]{1,0:T(8,128)(2,1)S(1)} collective-permute-done((bf16[256,512]{1,0:T(8,128)(2,1)S(1)}, bf16[256,512]{1,0:T(8,128)(2,1)S(1)}, u32[]{:S(2)}, u32[]{:S(2)}) %collective-permute-start.13) | collective-permute-done | bytes 262176 | tf_op jit(solution)/shard_map/ppermute | solution.py:23
  108.1 2.1 %shard_map.77 = (bf16[640,512]{1,0:T(8,128)(2,1)S(1)}, f32[896,512]{1,0:T(8,128)S(1)}) custom-call(bf16[512,896]{1,0:T(8,128)(2,1)S(1)} %pad_maximum_fusion.here_ref.weights_ref, bf16[384,512]{1,0:T(8,128)(2,1)S(1)} %copy-done.3, bf16[384,512]{1,0:T(8,128)(2,1)S(1)} %collective-permute-done.12.right_ref, ...), custom_call_target="tpu_custom_call" | custom-call | tf_op jit(solution)/shard_map/pallas_call | solution.py:132
  110.2 0.4 collective-permute-done.11.low_ref
  110.6 0.3 collective-permute-done.8.high_ref
  110.9 3.9 %collective-permute-start.14 = (bf16[896,128]{1,0:T(8,128)(2,1)S(1)}, bf16[896,128]{1,0:T(8,128)(2,1)S(1)}, u32[]{:S(2)}, u32[]{:S(2)}) collective-permute-start(bf16[896,128]{1,0:T(8,128)(2,1)S(1)} %collective-permute-done.8.high_ref), channel_id=1, source_target_pairs={{0,452},{64,0},{128,64},{192,128},{256,192},{320,256},{384,320},{4... | collective-permute-start | bytes 688136 | tf_op jit(solution)/shard_map/ppermute | solution.py:23
  114.8 1.2 shard_map.78
  116.0 1.3 copy-done
  117.2 1.0 copy-done.4
  118.2 0.6 collective-permute-done.14.tile_ref
  118.8 0.7 copy-done.6
  119.5 10.1 %all-to-all-start.2 = ((bf16[32,32,512]{2,1,0:T(8,128)(2,1)}), bf16[32,32,512]{2,1,0:T(8,128)(2,1)}, u32[]{:S(2)}, u32[]{:S(2)}) async-start(bf16[32,32,512]{2,1,0:T(8,128)(2,1)} %bitcast.33), calls=%async_computation.2 | async-start | bytes 2097152 | tf_op jit(solution)/shard_map/all_to_all | solution.py:262
  129.6 1.0 shard_map.79
  130.6 9.4 %collective-permute-start.16 = (bf16[448,512]{1,0:T(8,128)(2,1)}, bf16[448,512]{1,0:T(8,128)(2,1)S(1)}, u32[]{:S(2)}, u32[]{:S(2)}) collective-permute-start(bf16[448,512]{1,0:T(8,128)(2,1)} %get-tuple-element.67), channel_id=1, source_target_pairs={{0,4},{4,0},{1,5},{5,1},{2,6},{6,2},{3,7},{7,3},{8,12},{12,8},{9,1... | collective-permute-start | bytes 1376264 | tf_op jit(solution)/shard_map/ppermute | solution.py:266
  140.0 2.8 %all-to-all-done.2 = bf16[32,32,512]{2,1,0:T(8,128)(2,1)} async-done(((bf16[32,32,512]{2,1,0:T(8,128)(2,1)}), bf16[32,32,512]{2,1,0:T(8,128)(2,1)}, u32[]{:S(2)}, u32[]{:S(2)}) %all-to-all-start.2) | async-done | bytes 1048608 | tf_op jit(solution)/shard_map/all_to_all | solution.py:262
  142.8 1.4 reduce_sum.12
  144.2 0.8 copy.19
  145.0 6.0 %all-to-all-start.3 = ((bf16[128,2,1,224]{3,1,2,0:T(2,128)(2,1)}), bf16[128,2,1,224]{3,1,2,0:T(2,128)(2,1)S(1)}, u32[]{:S(2)}, u32[]{:S(2)}) async-start(bf16[128,2,1,224]{3,1,2,0:T(2,128)(2,1)} %copy.19), calls=%async_computation.3 | async-start | bytes 262144 | tf_op jit(solution)/shard_map/all_to_all | solution.py:269
  151.0 2.5 %collective-permute-start.15 = (bf16[32,512]{1,0:T(8,128)(2,1)S(1)}, bf16[32,512]{1,0:T(8,128)(2,1)S(1)}, u32[]{:S(2)}, u32[]{:S(2)}) collective-permute-start(bf16[32,512]{1,0:T(8,128)(2,1)S(1)} %reduce_sum.12), channel_id=1, source_target_pairs={{0,44},{16,52},{32,60},{48,0},{8,8},{24,16},{40,24},{56,472},{64,1... | collective-permute-start | bytes 98312 | tf_op jit(solution)/shard_map/ppermute | solution.py:272
  153.4 2.1 %all-to-all-done.3 = bf16[128,2,1,224]{3,1,2,0:T(2,128)(2,1)S(1)} async-done(((bf16[128,2,1,224]{3,1,2,0:T(2,128)(2,1)}), bf16[128,2,1,224]{3,1,2,0:T(2,128)(2,1)S(1)}, u32[]{:S(2)}, u32[]{:S(2)}) %all-to-all-start.3) | async-done | bytes 114720 | tf_op jit(solution)/shard_map/all_to_all | solution.py:269
  155.5 34.2 %collective-permute-done.15 = bf16[32,512]{1,0:T(8,128)(2,1)S(1)} collective-permute-done((bf16[32,512]{1,0:T(8,128)(2,1)S(1)}, bf16[32,512]{1,0:T(8,128)(2,1)S(1)}, u32[]{:S(2)}, u32[]{:S(2)}) %collective-permute-start.15) | collective-permute-done | bytes 32800 | tf_op jit(solution)/shard_map/ppermute | solution.py:272
  189.7 0.1 copy.21
  189.8 0.8 reshape.39
  190.7 0.1 convert_add_fusion
  190.8 1.0 slice_bitcast_fusion
  191.8 0.6 copy.25
  (28 shorter events, 0.1 us)
Async XLA Ops:
  0.6 14.3 %collective-permute-start = (bf16[32,512]{1,0:T(8,128)(2,1)}, bf16[32,512]{1,0:T(8,128)(2,1)S(1)}, u32[]{:S(2)}, u32[]{:S(2)}) collective-permute-start(bf16[32,512]{1,0:T(8,128)(2,1)} %param.4), channel_id=1, source_target_pairs={{248,0},{192,16},{200,32},{56,48},{0,8},{8,24},{380,40},{324,56},{... | collective-permute-start | bytes 98312 | tf_op jit(solution)/shard_map/ppermute | solution.py:217
  14.5 14.1 %copy-start.11 = (bf16[32,1792]{1,0:T(8,128)(2,1)S(1)}, bf16[32,1792]{1,0:T(8,128)(2,1)}, u32[]{:S(2)}) copy-start(bf16[32,1792]{1,0:T(8,128)(2,1)} %param.7) | copy-start | bytes 344068
  15.0 23.8 %collective-permute-start.2 = (bf16[512,896]{1,0:T(8,128)(2,1)S(1)}, bf16[512,896]{1,0:T(8,128)(2,1)S(1)}, u32[]{:S(2)}, u32[]{:S(2)}) collective-permute-start(bf16[512,896]{1,0:T(8,128)(2,1)S(1)} %pad_maximum_fusion.here_ref.weights_ref), channel_id=1, source_target_pairs={{0,452},{64,0},{128,64},{192,128},{256,192},{320,256},{384,320},{4... | collective-permute-start | bytes 2752520 | tf_op jit(solution)/shard_map/ppermute | solution.py:23
  17.5 23.3 %collective-permute-start.1 = (bf16[512,896]{1,0:T(8,128)(2,1)S(1)}, bf16[512,896]{1,0:T(8,128)(2,1)S(1)}, u32[]{:S(2)}, u32[]{:S(2)}) collective-permute-start(bf16[512,896]{1,0:T(8,128)(2,1)S(1)} %pad_maximum_fusion.here_ref.weights_ref), channel_id=1, source_target_pairs={{0,64},{64,128},{128,192},{192,256},{256,320},{320,384},{384,448},... | collective-permute-start | bytes 2752520 | tf_op jit(solution)/shard_map/ppermute | solution.py:23
  21.7 14.6 %all-to-all-start = ((bf16[16,32,512]{2,1,0:T(8,128)(2,1)}), bf16[16,32,512]{2,1,0:T(8,128)(2,1)S(1)}, u32[]{:S(2)}, u32[]{:S(2)}) async-start(bf16[16,32,512]{2,1,0:T(8,128)(2,1)} %broadcast_in_dim.2), calls=%async_computation | async-start | bytes 1048576 | tf_op jit(solution)/shard_map/all_to_all | solution.py:222
  40.8 3.9 %collective-permute-start.3 = (bf16[512,512]{1,0:T(8,128)(2,1)S(1)}, bf16[512,512]{1,0:T(8,128)(2,1)}, u32[]{:S(2)}, u32[]{:S(2)}) collective-permute-start(bf16[512,512]{1,0:T(8,128)(2,1)S(1)} %bitcast.30), channel_id=1, source_target_pairs={{0,8},{8,0},{1,9},{9,1},{2,10},{10,2},{3,11},{11,3},{4,12},{12,4},... | collective-permute-start | bytes 1572872 | tf_op jit(solution)/shard_map/ppermute | solution.py:63
  47.5 18.3 %collective-permute-start.4 = (bf16[896,128]{1,0:T(8,128)(2,1)}, bf16[896,128]{1,0:T(8,128)(2,1)}, u32[]{:S(2)}, u32[]{:S(2)}) collective-permute-start(bf16[896,128]{1,0:T(8,128)(2,1)} %get-tuple-element.41), channel_id=1, source_target_pairs={{0,192},{64,256},{128,320},{192,384},{256,448},{320,4},{384,68},{4... | collective-permute-start | bytes 688136 | tf_op jit(solution)/shard_map/ppermute | solution.py:23
  52.9 18.3 %collective-permute-start.5 = (bf16[896,128]{1,0:T(8,128)(2,1)}, bf16[896,128]{1,0:T(8,128)(2,1)}, u32[]{:S(2)}, u32[]{:S(2)}) collective-permute-start(bf16[896,128]{1,0:T(8,128)(2,1)} %get-tuple-element.42), channel_id=1, source_target_pairs={{0,324},{64,388},{128,452},{192,0},{256,64},{320,128},{384,192},{4... | collective-permute-start | bytes 688136 | tf_op jit(solution)/shard_map/ppermute | solution.py:23
  56.3 9.5 %all-to-all-start.1 = ((bf16[4,32,2,224]{3,2,1,0:T(2,128)(2,1)}), bf16[4,32,2,224]{3,2,1,0:T(2,128)(2,1)}, u32[]{:S(2)}, u32[]{:S(2)}) async-start(bf16[4,32,2,224]{3,2,1,0:T(2,128)(2,1)} %bitcast.29), calls=%async_computation.1 | async-start | bytes 262144 | tf_op jit(solution)/shard_map/all_to_all | solution.py:227
  63.0 0.8 copy-start.2
  63.8 0.8 copy-start.5
  64.5 0.7 copy-start.8
  72.5 20.7 %copy-start.9 = (bf16[384,512]{1,0:T(8,128)(2,1)S(1)}, bf16[384,512]{1,0:T(8,128)(2,1)}, u32[]{:S(2)}) copy-start(bf16[384,512]{1,0:T(8,128)(2,1)} %copy-done.8) | copy-start | bytes 1179652
  72.5 35.6 %copy-start.3 = (bf16[384,512]{1,0:T(8,128)(2,1)S(1)}, bf16[384,512]{1,0:T(8,128)(2,1)}, u32[]{:S(2)}) copy-start(bf16[384,512]{1,0:T(8,128)(2,1)} %copy-done.2) | copy-start | bytes 1179652
  76.3 10.1 %collective-permute-start.9 = (bf16[896,128]{1,0:T(8,128)(2,1)S(1)}, bf16[896,128]{1,0:T(8,128)(2,1)S(1)}, u32[]{:S(2)}, u32[]{:S(2)}) collective-permute-start(bf16[896,128]{1,0:T(8,128)(2,1)S(1)} %pad_maximum_fusion.3.refs_2_), channel_id=1, source_target_pairs={{0,64},{64,128},{128,192},{192,256},{256,320},{320,384},{384,448},... | collective-permute-start | bytes 688136 | tf_op jit(solution)/shard_map/ppermute | solution.py:23
  78.7 10.8 %collective-permute-start.6 = (bf16[896,128]{1,0:T(8,128)(2,1)S(1)}, bf16[896,128]{1,0:T(8,128)(2,1)S(1)}, u32[]{:S(2)}, u32[]{:S(2)}) collective-permute-start(bf16[896,128]{1,0:T(8,128)(2,1)S(1)} %pad_maximum_fusion.3.refs_2_), channel_id=1, source_target_pairs={{0,452},{64,0},{128,64},{192,128},{256,192},{320,256},{384,320},{4... | collective-permute-start | bytes 688136 | tf_op jit(solution)/shard_map/ppermute | solution.py:23
  86.4 13.9 %collective-permute-start.10 = (bf16[896,128]{1,0:T(8,128)(2,1)S(1)}, bf16[896,128]{1,0:T(8,128)(2,1)S(1)}, u32[]{:S(2)}, u32[]{:S(2)}) collective-permute-start(bf16[896,128]{1,0:T(8,128)(2,1)S(1)} %collective-permute-done.9.refs_1_), channel_id=1, source_target_pairs={{0,64},{64,128},{128,192},{192,256},{256,320},{320,384},{384,448},... | collective-permute-start | bytes 688136 | tf_op jit(solution)/shard_map/ppermute | solution.py:23
  89.5 12.7 %collective-permute-start.7 = (bf16[896,128]{1,0:T(8,128)(2,1)S(1)}, bf16[896,128]{1,0:T(8,128)(2,1)S(1)}, u32[]{:S(2)}, u32[]{:S(2)}) collective-permute-start(bf16[896,128]{1,0:T(8,128)(2,1)S(1)} %collective-permute-done.6.refs_3_), channel_id=1, source_target_pairs={{0,452},{64,0},{128,64},{192,128},{256,192},{320,256},{384,320},{4... | collective-permute-start | bytes 688136 | tf_op jit(solution)/shard_map/ppermute | solution.py:23
  93.2 14.9 %collective-permute-start.12 = (bf16[384,512]{1,0:T(8,128)(2,1)S(1)}, bf16[384,512]{1,0:T(8,128)(2,1)S(1)}, u32[]{:S(2)}, u32[]{:S(2)}) collective-permute-start(bf16[384,512]{1,0:T(8,128)(2,1)S(1)} %copy-done.9), channel_id=1, source_target_pairs={{0,452},{64,0},{128,64},{192,128},{256,192},{320,256},{384,320},{4... | collective-permute-start | bytes 1179656 | tf_op jit(solution)/shard_map/ppermute | solution.py:23
  98.3 9.8 %collective-permute-start.13 = (bf16[256,512]{1,0:T(8,128)(2,1)S(1)}, bf16[256,512]{1,0:T(8,128)(2,1)S(1)}, u32[]{:S(2)}, u32[]{:S(2)}) collective-permute-start(bf16[256,512]{1,0:T(8,128)(2,1)S(1)} %get-tuple-element.50), channel_id=1, source_target_pairs={{0,64},{64,128},{128,192},{192,256},{256,320},{320,384},{384,448},... | collective-permute-start | bytes 786440 | tf_op jit(solution)/shard_map/ppermute | solution.py:23
  100.3 10.3 %collective-permute-start.11 = (bf16[896,128]{1,0:T(8,128)(2,1)S(1)}, bf16[896,128]{1,0:T(8,128)(2,1)S(1)}, u32[]{:S(2)}, u32[]{:S(2)}) collective-permute-start(bf16[896,128]{1,0:T(8,128)(2,1)S(1)} %collective-permute-done.10.refs_0_), channel_id=1, source_target_pairs={{0,64},{64,128},{128,192},{192,256},{256,320},{320,384},{384,448},... | collective-permute-start | bytes 688136 | tf_op jit(solution)/shard_map/ppermute | solution.py:23
  102.2 8.6 %collective-permute-start.8 = (bf16[896,128]{1,0:T(8,128)(2,1)S(1)}, bf16[896,128]{1,0:T(8,128)(2,1)S(1)}, u32[]{:S(2)}, u32[]{:S(2)}) collective-permute-start(bf16[896,128]{1,0:T(8,128)(2,1)S(1)} %collective-permute-done.7.refs_4_), channel_id=1, source_target_pairs={{0,452},{64,0},{128,64},{192,128},{256,192},{320,256},{384,320},{4... | collective-permute-start | bytes 688136 | tf_op jit(solution)/shard_map/ppermute | solution.py:23
  110.9 7.9 %collective-permute-start.14 = (bf16[896,128]{1,0:T(8,128)(2,1)S(1)}, bf16[896,128]{1,0:T(8,128)(2,1)S(1)}, u32[]{:S(2)}, u32[]{:S(2)}) collective-permute-start(bf16[896,128]{1,0:T(8,128)(2,1)S(1)} %collective-permute-done.8.high_ref), channel_id=1, source_target_pairs={{0,452},{64,0},{128,64},{192,128},{256,192},{320,256},{384,320},{4... | collective-permute-start | bytes 688136 | tf_op jit(solution)/shard_map/ppermute | solution.py:23
  116.0 1.3 copy-start
  117.2 1.0 copy-start.4
  118.8 0.7 copy-start.6
  119.5 10.1 %copy-start.1 = (f32[896,512]{1,0:T(8,128)S(1)}, f32[896,512]{1,0:T(8,128)}, u32[]{:S(2)}) copy-start(f32[896,512]{1,0:T(8,128)} %copy-done) | copy-start | bytes 5505028
  119.5 10.1 %copy-start.7 = (bf16[896,128]{1,0:T(8,128)(2,1)S(1)}, bf16[896,128]{1,0:T(8,128)(2,1)}, u32[]{:S(2)}) copy-start(bf16[896,128]{1,0:T(8,128)(2,1)} %copy-done.6) | copy-start | bytes 688132
  119.5 23.4 %all-to-all-start.2 = ((bf16[32,32,512]{2,1,0:T(8,128)(2,1)}), bf16[32,32,512]{2,1,0:T(8,128)(2,1)}, u32[]{:S(2)}, u32[]{:S(2)}) async-start(bf16[32,32,512]{2,1,0:T(8,128)(2,1)} %bitcast.33), calls=%async_computation.2 | async-start | bytes 2097152 | tf_op jit(solution)/shard_map/all_to_all | solution.py:262
  129.5 14.7 %copy-start.10 = (bf16[448,128]{1,0:T(8,128)(2,1)S(1)}, bf16[448,128]{1,0:T(8,128)(2,1)}, u32[]{:S(2)}) copy-start(bf16[448,128]{1,0:T(8,128)(2,1)} %get-tuple-element.60) | copy-start | bytes 344068
  130.6 60.1 %collective-permute-start.16 = (bf16[448,512]{1,0:T(8,128)(2,1)}, bf16[448,512]{1,0:T(8,128)(2,1)S(1)}, u32[]{:S(2)}, u32[]{:S(2)}) collective-permute-start(bf16[448,512]{1,0:T(8,128)(2,1)} %get-tuple-element.67), channel_id=1, source_target_pairs={{0,4},{4,0},{1,5},{5,1},{2,6},{6,2},{3,7},{7,3},{8,12},{12,8},{9,1... | collective-permute-start | bytes 1376264 | tf_op jit(solution)/shard_map/ppermute | solution.py:266
  145.0 10.5 %all-to-all-start.3 = ((bf16[128,2,1,224]{3,1,2,0:T(2,128)(2,1)}), bf16[128,2,1,224]{3,1,2,0:T(2,128)(2,1)S(1)}, u32[]{:S(2)}, u32[]{:S(2)}) async-start(bf16[128,2,1,224]{3,1,2,0:T(2,128)(2,1)} %copy.19), calls=%async_computation.3 | async-start | bytes 262144 | tf_op jit(solution)/shard_map/all_to_all | solution.py:269
  151.0 38.7 %collective-permute-start.15 = (bf16[32,512]{1,0:T(8,128)(2,1)S(1)}, bf16[32,512]{1,0:T(8,128)(2,1)S(1)}, u32[]{:S(2)}, u32[]{:S(2)}) collective-permute-start(bf16[32,512]{1,0:T(8,128)(2,1)S(1)} %reduce_sum.12), channel_id=1, source_target_pairs={{0,44},{16,52},{32,60},{48,0},{8,8},{24,16},{40,24},{56,472},{64,1... | collective-permute-start | bytes 98312 | tf_op jit(solution)/shard_map/ppermute | solution.py:272

commit v10 on v9

--- a/solution.py
+++ b/solution.py
@@ -113,6 +113,35 @@
     outs = [jax.ShapeDtypeStruct((cols, 128), jnp.float32)]
     outs += [jax.ShapeDtypeStruct((128 * count, features), jnp.bfloat16) for count in (3, 2, 3)]
     return forward(own_kernel, outs, core, own, other, weights)
+
+
+def pointwise_kernel(total_ref, below_ref, above_ref, cotangent_ref, grads_ref, hidden_ref):
+    part = total_ref.shape[0] // 4
+    total = total_ref[...] + below_ref[...].astype(jnp.float32) + above_ref[...].astype(jnp.float32)
+    for at in range(2):
+        gate = total[2 * at * part : (2 * at + 1) * part, :]
+        up = total[(2 * at + 1) * part : (2 * at + 2) * part, :]
+        cotangent = cotangent_ref[at * part : (at + 1) * part, :].astype(jnp.float32)
+        sigmoid = jax.nn.sigmoid(gate)
+        silu = gate * sigmoid
+        hidden_ref[at * part : (at + 1) * part, :] = (silu * up).astype(jnp.bfloat16)
+        grad_gate = cotangent * up * sigmoid * (1.0 + gate * (1.0 - sigmoid))
+        grads_ref[2 * at * part : (2 * at + 1) * part, :] = grad_gate.astype(jnp.bfloat16)
+        grads_ref[(2 * at + 1) * part : (2 * at + 2) * part, :] = (cotangent * silu).astype(jnp.bfloat16)
+
+
+def pointwise(total, below, above, cotangent):
+    return pl.pallas_call(
+        pointwise_kernel,
+        in_specs=[VMEM_SPEC] * 4,
+        out_specs=[VMEM_SPEC] * 2,
+        out_shape=[
+            jax.ShapeDtypeStruct(total.shape, jnp.bfloat16),
+            jax.ShapeDtypeStruct(cotangent.shape, jnp.bfloat16),
+        ],
+        compiler_params=PARAMS,
+        cost_estimate=pl.CostEstimate(flops=20_000_000_000, bytes_accessed=2_000_000, transcendentals=57344),
+    )(total, below, above, cotangent)
 
 
 def near_kernel(weights_ref, mine_ref, right_ref, left_ref, *refs):
@@ -215,7 +244,6 @@
     )
 
     piece = lax.ppermute(tokens, ("r", "y", "c", "h"), token_pairs())
-    piece, weights = lax.optimization_barrier((piece, weights))
     below = ring_shift(weights, 1)
     above = ring_shift(weights, -1)
     copies = jnp.broadcast_to(piece[None], (16,) + piece.shape)
@@ -224,27 +252,17 @@
     cotangent = grad_hidden.reshape(-1, 2, 4, part).transpose(2, 0, 1, 3)
     own_tokens, cotangent, below, above = lax.optimization_barrier((own_tokens, cotangent, below, above))
     other_tokens = swap_cores(own_tokens)
-    cotangent = lax.all_to_all(cotangent, "x", split_axis=0, concat_axis=0, tiled=True)
-
     rows = (below, weights, above)
     up, down = forward_sends(core, own_tokens, other_tokens, rows)
     from_below = ring_shift(up, 3)
     from_above = ring_shift(down, -3)
+    cotangent = lax.all_to_all(cotangent, "x", split_axis=0, concat_axis=0, tiled=True)
+    cotangent = cotangent.reshape(-1, 2 * part).T
     total, to_left, to_right, mine = own_sums(core, own_tokens, other_tokens, rows)
     right_tokens = ring_shift(to_left, -1)
     left_tokens = ring_shift(to_right, 1)
-    from_below, from_above, cotangent = lax.optimization_barrier((from_below, from_above, cotangent))
-    cotangent = cotangent.reshape(-1, 2 * part).T.astype(jnp.float32)
-    total = total + from_below.astype(jnp.float32) + from_above.astype(jnp.float32)
-    gate_pre = jnp.concatenate([total[:part], total[2 * part : 3 * part]], 0)
-    up_pre = jnp.concatenate([total[part : 2 * part], total[3 * part :]], 0)
-
-    sigmoid = jax.nn.sigmoid(gate_pre)
-    silu = gate_pre * sigmoid
-    hidden = (silu * up_pre).astype(jnp.bfloat16)
-    grad_gate = (cotangent * up_pre * sigmoid * (1.0 + gate_pre * (1.0 - sigmoid))).astype(jnp.bfloat16)
-    grad_up = (cotangent * silu).astype(jnp.bfloat16)
-    grads = jnp.concatenate([grad_gate[:part], grad_up[:part], grad_gate[part:], grad_up[part:]], 0)
+    grads, hidden = pointwise(total, from_below, from_above, cotangent)
+    grads, right_tokens, left_tokens = lax.optimization_barrier((grads, right_tokens, left_tokens))
 
     left_1 = ring_shift(grads, -1)
     right_1 = ring_shift(grads, 1)

time: 194 us -> 200 us (1.031)
  the two profiles are of different devices: /device:TPU:58 before, /device:TPU:49 now
where the time goes in v10:
time: 200 us; the launch traced here: 199 us
  starting transfers between devices  92.3 us (46%)
  waiting for transfers between devices  71.7 us (36%)
  local copies, waits for them, and re-layouts  13.2 us (7%)
  Pallas kernels  11 us (6%)
  blocking collectives  8.17 us (4%)
    ppermute x13, starting transfers between devices, ring_shift(): return lax.ppermute(value, ('r', 'h'), pairs)  43.2 us
    ppermute x1, waiting for transfers between devices, local(): lax.ppermute(grad_tokens, ('r', 'y', 'c', 'h'), result_pairs())  28.5 us
    ppermute x1, waiting for transfers between devices, local(): piece = lax.ppermute(tokens, ('r', 'y', 'c', 'h'), token_pairs())  18.7 us
    all_to_all x1, starting transfers between devices, local(): lax.all_to_all(terms.reshape(32, -1, features), ('y', 'c', 'x'), split_ax...  13.2 us
    ppermute x1, starting transfers between devices, local(): piece = lax.ppermute(tokens, ('r', 'y', 'c', 'h'), token_pairs())  11.8 us
    ppermute x1, starting transfers between devices, local(): received = lax.ppermute(send, 'h', [(0, 1), (1, 0)])  9.61 us
    ppermute x13, waiting for transfers between devices, ring_shift(): return lax.ppermute(value, ('r', 'h'), pairs)  9.3 us
    all_to_all x1, blocking collectives, local(): lax.all_to_all(cotangent, 'x', split_axis=0, concat_axis=0, tiled=True)  8.17 us
  transfers between devices with their start and end apart: 20, of which 12 were waited for; matrix products, arithmetic and copies ran while one was open for 4% of the time, Pallas kernels for 4%

profile of v10, /device:TPU:49, one launch (start us, length us, event | category | flops | bytes accessed | tf_op | source)
XLA Modules:
  0.0 199.2 jit_solution(3873374076971079921)
XLA Ops:
  0.6 1.8 constant_dynamic-slice_fusion.2
  2.5 0.0 copy-start.6
  2.5 0.4 pad_maximum_fusion.here_ref.weights_ref
  2.9 1.9 collective-permute-start.2
  4.8 3.5 %collective-permute-start.1 = (bf16[512,896]{1,0:T(8,128)(2,1)S(1)}, bf16[512,896]{1,0:T(8,128)(2,1)S(1)}, u32[]{:S(2)}, u32[]{:S(2)}) collective-permute-start(bf16[512,896]{1,0:T(8,128)(2,1)S(1)} %pad_maximum_fusion.here_ref.weights_ref), channel_id=1, source_target_pairs={{0,64},{64,128},{128,192},{192,256},{256,320},{320,384},{384,448},... | collective-permute-start | bytes 2752520 | tf_op jit(solution)/shard_map/ppermute | solution.py:23
  8.4 11.8 %collective-permute-start = (bf16[32,512]{1,0:T(8,128)(2,1)S(1)}, bf16[32,512]{1,0:T(8,128)(2,1)S(1)}, u32[]{:S(2)}, u32[]{:S(2)}) collective-permute-start(bf16[32,512]{1,0:T(8,128)(2,1)S(1)} %copy-done.7), channel_id=1, source_target_pairs={{248,0},{192,16},{200,32},{56,48},{0,8},{8,24},{380,40},{324,56},{... | collective-permute-start | bytes 98312 | tf_op jit(solution)/shard_map/ppermute | solution.py:246
  20.2 18.7 %collective-permute-done = bf16[32,512]{1,0:T(8,128)(2,1)S(1)} collective-permute-done((bf16[32,512]{1,0:T(8,128)(2,1)S(1)}, bf16[32,512]{1,0:T(8,128)(2,1)S(1)}, u32[]{:S(2)}, u32[]{:S(2)}) %collective-permute-start) | collective-permute-done | bytes 32800 | tf_op jit(solution)/shard_map/ppermute | solution.py:246
  38.9 0.8 broadcast_in_dim.2
  39.8 6.7 %all-to-all-start = ((bf16[16,32,512]{2,1,0:T(8,128)(2,1)}), bf16[16,32,512]{2,1,0:T(8,128)(2,1)S(1)}, u32[]{:S(2)}, u32[]{:S(2)}) async-start(bf16[16,32,512]{2,1,0:T(8,128)(2,1)} %broadcast_in_dim.2), calls=%async_computation | async-start | bytes 1048576 | tf_op jit(solution)/shard_map/all_to_all | solution.py:250
  46.5 0.2 reshape.35
  46.7 0.8 copy.23
  47.5 5.7 %all-to-all-done = bf16[16,32,512]{2,1,0:T(8,128)(2,1)S(1)} async-done(((bf16[16,32,512]{2,1,0:T(8,128)(2,1)}), bf16[16,32,512]{2,1,0:T(8,128)(2,1)S(1)}, u32[]{:S(2)}, u32[]{:S(2)}) %all-to-all-start) | async-done | bytes 524320 | tf_op jit(solution)/shard_map/all_to_all | solution.py:250
  53.2 0.0 collective-permute-done.2.above_ref
  53.2 0.0 collective-permute-done.1.below_ref
  53.2 1.9 collective-permute-start.3
  55.1 2.0 %collective-permute-done.3.other_ref = bf16[512,512]{1,0:T(8,128)(2,1)} collective-permute-done((bf16[512,512]{1,0:T(8,128)(2,1)S(1)}, bf16[512,512]{1,0:T(8,128)(2,1)}, u32[]{:S(2)}, u32[]{:S(2)}) %collective-permute-start.3) | collective-permute-done | bytes 524320 | tf_op jit(solution)/shard_map/ppermute | solution.py:63
  57.1 2.8 %shard_map.76 = (bf16[896,128]{1,0:T(8,128)(2,1)}, bf16[896,128]{1,0:T(8,128)(2,1)}) custom-call(s32[1]{0:T(128)} %bitcast.core_ref, bf16[512,512]{1,0:T(8,128)(2,1)S(1)} %bitcast.21, bf16[512,512]{1,0:T(8,128)(2,1)} %collective-permute-done.3.other_ref, bf16[512,896]{1,0:T(8,128)(2,1)S(1)} %collective-permute-done.1.below_ref, ...), custom_call_target="tpu_custom_call" | custom-call | tf_op jit(solution)/shard_map/pallas_call | solution.py:96
  59.9 1.9 collective-permute-start.4
  61.8 6.4 %collective-permute-start.5 = (bf16[896,128]{1,0:T(8,128)(2,1)}, bf16[896,128]{1,0:T(8,128)(2,1)}, u32[]{:S(2)}, u32[]{:S(2)}) collective-permute-start(bf16[896,128]{1,0:T(8,128)(2,1)} %get-tuple-element.41), channel_id=1, source_target_pairs={{0,324},{64,388},{128,452},{192,0},{256,64},{320,128},{384,192},{4... | collective-permute-start | bytes 688136 | tf_op jit(solution)/shard_map/ppermute | solution.py:23
  68.2 8.2 %all_to_all.33 = bf16[4,32,2,224]{3,2,1,0:T(2,128)(2,1)} all-to-all(bf16[4,32,2,224]{3,2,1,0:T(2,128)(2,1)S(1)} %bitcast.25), channel_id=1, replica_groups=mesh['r'=8,'y'=4,'c'=2,'h'=2,'x'=4] {'x'}, dimensions={0} | all-to-all | bytes 229376 | tf_op jit(solution)/shard_map/all_to_all | solution.py:259
  76.4 1.7 reshape.36
  78.0 1.7 copy.18
  79.7 1.9 shard_map.75
  81.6 3.8 %collective-permute-start.7 = (bf16[256,512]{1,0:T(8,128)(2,1)S(1)}, bf16[256,512]{1,0:T(8,128)(2,1)S(1)}, u32[]{:S(2)}, u32[]{:S(2)}) collective-permute-start(bf16[256,512]{1,0:T(8,128)(2,1)S(1)} %get-tuple-element.45), channel_id=1, source_target_pairs={{0,64},{64,128},{128,192},{192,256},{256,320},{320,384},{384,448},... | collective-permute-start | bytes 786440 | tf_op jit(solution)/shard_map/ppermute | solution.py:23
  85.4 2.7 %collective-permute-start.6 = (bf16[384,512]{1,0:T(8,128)(2,1)S(1)}, bf16[384,512]{1,0:T(8,128)(2,1)S(1)}, u32[]{:S(2)}, u32[]{:S(2)}) collective-permute-start(bf16[384,512]{1,0:T(8,128)(2,1)S(1)} %get-tuple-element.44), channel_id=1, source_target_pairs={{0,452},{64,0},{128,64},{192,128},{256,192},{320,256},{384,320},{4... | collective-permute-start | bytes 1179656 | tf_op jit(solution)/shard_map/ppermute | solution.py:23
  88.1 0.0 collective-permute-done.4.below_ref
  88.1 0.0 copy-start.3
  88.1 0.7 copy-done.3
  88.8 0.0 collective-permute-done.5.above_ref
  88.8 0.9 copy-done.4
  89.7 1.1 shard_map.77
  90.8 0.3 collective-permute-done.7.left_ref
  91.1 4.9 %collective-permute-done.6.right_ref = bf16[384,512]{1,0:T(8,128)(2,1)S(1)} collective-permute-done((bf16[384,512]{1,0:T(8,128)(2,1)S(1)}, bf16[384,512]{1,0:T(8,128)(2,1)S(1)}, u32[]{:S(2)}, u32[]{:S(2)}) %collective-permute-start.6) | collective-permute-done | bytes 393248 | tf_op jit(solution)/shard_map/ppermute | solution.py:23
  96.0 2.2 %collective-permute-start.11 = (bf16[896,128]{1,0:T(8,128)(2,1)S(1)}, bf16[896,128]{1,0:T(8,128)(2,1)S(1)}, u32[]{:S(2)}, u32[]{:S(2)}) collective-permute-start(bf16[896,128]{1,0:T(8,128)(2,1)S(1)} %get-tuple-element.46.refs_2_), channel_id=1, source_target_pairs={{0,64},{64,128},{128,192},{192,256},{256,320},{320,384},{384,448},... | collective-permute-start | bytes 688136 | tf_op jit(solution)/shard_map/ppermute | solution.py:23
  98.2 3.1 %collective-permute-start.8 = (bf16[896,128]{1,0:T(8,128)(2,1)S(1)}, bf16[896,128]{1,0:T(8,128)(2,1)S(1)}, u32[]{:S(2)}, u32[]{:S(2)}) collective-permute-start(bf16[896,128]{1,0:T(8,128)(2,1)S(1)} %get-tuple-element.46.refs_2_), channel_id=1, source_target_pairs={{0,452},{64,0},{128,64},{192,128},{256,192},{320,256},{384,320},{4... | collective-permute-start | bytes 688136 | tf_op jit(solution)/shard_map/ppermute | solution.py:23
  101.3 1.5 collective-permute-done.11.refs_1_
  102.8 2.2 %collective-permute-start.12 = (bf16[896,128]{1,0:T(8,128)(2,1)S(1)}, bf16[896,128]{1,0:T(8,128)(2,1)S(1)}, u32[]{:S(2)}, u32[]{:S(2)}) collective-permute-start(bf16[896,128]{1,0:T(8,128)(2,1)S(1)} %collective-permute-done.11.refs_1_), channel_id=1, source_target_pairs={{0,64},{64,128},{128,192},{192,256},{256,320},{320,384},{384,448},... | collective-permute-start | bytes 688136 | tf_op jit(solution)/shard_map/ppermute | solution.py:23
  105.0 0.3 collective-permute-done.8.refs_3_
  105.3 4.5 %collective-permute-start.9 = (bf16[896,128]{1,0:T(8,128)(2,1)S(1)}, bf16[896,128]{1,0:T(8,128)(2,1)S(1)}, u32[]{:S(2)}, u32[]{:S(2)}) collective-permute-start(bf16[896,128]{1,0:T(8,128)(2,1)S(1)} %collective-permute-done.8.refs_3_), channel_id=1, source_target_pairs={{0,452},{64,0},{128,64},{192,128},{256,192},{320,256},{384,320},{4... | collective-permute-start | bytes 688136 | tf_op jit(solution)/shard_map/ppermute | solution.py:23
  109.8 1.5 collective-permute-done.12.refs_0_
  111.2 1.9 collective-permute-start.13
  113.1 0.0 collective-permute-done.9.refs_4_
  113.1 4.6 %collective-permute-start.10 = (bf16[896,128]{1,0:T(8,128)(2,1)S(1)}, bf16[896,128]{1,0:T(8,128)(2,1)S(1)}, u32[]{:S(2)}, u32[]{:S(2)}) collective-permute-start(bf16[896,128]{1,0:T(8,128)(2,1)S(1)} %collective-permute-done.9.refs_4_), channel_id=1, source_target_pairs={{0,452},{64,0},{128,64},{192,128},{256,192},{320,256},{384,320},{4... | collective-permute-start | bytes 688136 | tf_op jit(solution)/shard_map/ppermute | solution.py:23
  117.7 2.1 %shard_map.78 = (bf16[640,512]{1,0:T(8,128)(2,1)S(1)}, f32[896,512]{1,0:T(8,128)S(1)}) custom-call(bf16[512,896]{1,0:T(8,128)(2,1)S(1)} %pad_maximum_fusion.here_ref.weights_ref, bf16[384,512]{1,0:T(8,128)(2,1)S(1)} %get-tuple-element.47.mine_ref, bf16[384,512]{1,0:T(8,128)(2,1)S(1)} %collective-permute-done.6.right_ref, ...), custom_call_target="tpu_custom_call" | custom-call | tf_op jit(solution)/shard_map/pallas_call | solution.py:161
  119.8 0.0 collective-permute-done.13.low_ref
  119.8 0.9 collective-permute-done.10.high_ref
  120.7 4.6 %collective-permute-start.14 = (bf16[896,128]{1,0:T(8,128)(2,1)S(1)}, bf16[896,128]{1,0:T(8,128)(2,1)S(1)}, u32[]{:S(2)}, u32[]{:S(2)}) collective-permute-start(bf16[896,128]{1,0:T(8,128)(2,1)S(1)} %collective-permute-done.10.high_ref), channel_id=1, source_target_pairs={{0,452},{64,0},{128,64},{192,128},{256,192},{320,256},{384,320},{4... | collective-permute-start | bytes 688136 | tf_op jit(solution)/shard_map/ppermute | solution.py:23
  125.2 2.1 %shard_map.79 = (bf16[1024,512]{1,0:T(8,128)(2,1)}, f32[896,512]{1,0:T(8,128)S(1)}) custom-call(bf16[512,896]{1,0:T(8,128)(2,1)S(1)} %pad_maximum_fusion.here_ref.weights_ref, bf16[512,896]{1,0:T(8,128)(2,1)S(1)} %collective-permute-done.1.below_ref, bf16[384,512]{1,0:T(8,128)(2,1)S(1)} %get-tuple-element.47.mine_ref, ...), custom_call_target="tpu_custom_call" | custom-call | tf_op jit(solution)/shard_map/pallas_call | solution.py:193
  127.3 1.2 copy-done
  128.6 13.2 %all-to-all-start.2 = ((bf16[32,32,512]{2,1,0:T(8,128)(2,1)}), bf16[32,32,512]{2,1,0:T(8,128)(2,1)}, u32[]{:S(2)}, u32[]{:S(2)}) async-start(bf16[32,32,512]{2,1,0:T(8,128)(2,1)} %bitcast.4), calls=%async_computation.2 | async-start | bytes 2097152 | tf_op jit(solution)/shard_map/all_to_all | solution.py:280
  141.8 1.0 shard_map.80
  142.9 9.6 %collective-permute-start.16 = (bf16[448,512]{1,0:T(8,128)(2,1)}, bf16[448,512]{1,0:T(8,128)(2,1)S(1)}, u32[]{:S(2)}, u32[]{:S(2)}) collective-permute-start(bf16[448,512]{1,0:T(8,128)(2,1)} %get-tuple-element.67), channel_id=1, source_target_pairs={{0,4},{4,0},{1,5},{5,1},{2,6},{6,2},{3,7},{7,3},{8,12},{12,8},{9,1... | collective-permute-start | bytes 1376264 | tf_op jit(solution)/shard_map/ppermute | solution.py:284
  152.5 4.9 %all-to-all-done.2 = bf16[32,32,512]{2,1,0:T(8,128)(2,1)} async-done(((bf16[32,32,512]{2,1,0:T(8,128)(2,1)}), bf16[32,32,512]{2,1,0:T(8,128)(2,1)}, u32[]{:S(2)}, u32[]{:S(2)}) %all-to-all-start.2) | async-done | bytes 1048608 | tf_op jit(solution)/shard_map/all_to_all | solution.py:280
  157.4 1.4 reduce_sum.12
  158.7 0.8 copy.19
  159.5 3.3 %all-to-all-start.3 = ((bf16[128,2,1,224]{3,1,2,0:T(2,128)(2,1)}), bf16[128,2,1,224]{3,1,2,0:T(2,128)(2,1)S(1)}, u32[]{:S(2)}, u32[]{:S(2)}) async-start(bf16[128,2,1,224]{3,1,2,0:T(2,128)(2,1)} %copy.19), calls=%async_computation.3 | async-start | bytes 262144 | tf_op jit(solution)/shard_map/all_to_all | solution.py:287
  162.9 2.5 %collective-permute-start.15 = (bf16[32,512]{1,0:T(8,128)(2,1)S(1)}, bf16[32,512]{1,0:T(8,128)(2,1)S(1)}, u32[]{:S(2)}, u32[]{:S(2)}) collective-permute-start(bf16[32,512]{1,0:T(8,128)(2,1)S(1)} %reduce_sum.12), channel_id=1, source_target_pairs={{0,44},{16,52},{32,60},{48,0},{8,8},{24,16},{40,24},{56,472},{64,1... | collective-permute-start | bytes 98312 | tf_op jit(solution)/shard_map/ppermute | solution.py:290
  165.3 2.6 %all-to-all-done.3 = bf16[128,2,1,224]{3,1,2,0:T(2,128)(2,1)S(1)} async-done(((bf16[128,2,1,224]{3,1,2,0:T(2,128)(2,1)}), bf16[128,2,1,224]{3,1,2,0:T(2,128)(2,1)S(1)}, u32[]{:S(2)}, u32[]{:S(2)}) %all-to-all-start.3) | async-done | bytes 114720 | tf_op jit(solution)/shard_map/all_to_all | solution.py:287
  168.0 28.5 %collective-permute-done.15 = bf16[32,512]{1,0:T(8,128)(2,1)S(1)} collective-permute-done((bf16[32,512]{1,0:T(8,128)(2,1)S(1)}, bf16[32,512]{1,0:T(8,128)(2,1)S(1)}, u32[]{:S(2)}, u32[]{:S(2)}) %collective-permute-start.15) | collective-permute-done | bytes 32800 | tf_op jit(solution)/shard_map/ppermute | solution.py:290
  196.5 0.1 copy.21
  196.6 0.8 reshape.40
  197.4 0.1 convert_add_fusion
  197.6 1.0 slice_bitcast_fusion
  198.5 0.6 copy.25
  (14 shorter events, 0.0 us)
Async XLA Ops:
  0.6 7.8 %copy-start.7 = (bf16[32,512]{1,0:T(8,128)(2,1)S(1)}, bf16[32,512]{1,0:T(8,128)(2,1)}, u32[]{:S(2)}) copy-start(bf16[32,512]{1,0:T(8,128)(2,1)} %param.4) | copy-start | bytes 98308
  2.5 44.0 %copy-start.6 = (bf16[32,1792]{1,0:T(8,128)(2,1)S(1)}, bf16[32,1792]{1,0:T(8,128)(2,1)}, u32[]{:S(2)}) copy-start(bf16[32,1792]{1,0:T(8,128)(2,1)} %param.7) | copy-start | bytes 344068
  2.9 50.3 %collective-permute-start.2 = (bf16[512,896]{1,0:T(8,128)(2,1)S(1)}, bf16[512,896]{1,0:T(8,128)(2,1)S(1)}, u32[]{:S(2)}, u32[]{:S(2)}) collective-permute-start(bf16[512,896]{1,0:T(8,128)(2,1)S(1)} %pad_maximum_fusion.here_ref.weights_ref), channel_id=1, source_target_pairs={{0,452},{64,0},{128,64},{192,128},{256,192},{320,256},{384,320},{4... | collective-permute-start | bytes 2752520 | tf_op jit(solution)/shard_map/ppermute | solution.py:23
  4.8 48.4 %collective-permute-start.1 = (bf16[512,896]{1,0:T(8,128)(2,1)S(1)}, bf16[512,896]{1,0:T(8,128)(2,1)S(1)}, u32[]{:S(2)}, u32[]{:S(2)}) collective-permute-start(bf16[512,896]{1,0:T(8,128)(2,1)S(1)} %pad_maximum_fusion.here_ref.weights_ref), channel_id=1, source_target_pairs={{0,64},{64,128},{128,192},{192,256},{256,320},{320,384},{384,448},... | collective-permute-start | bytes 2752520 | tf_op jit(solution)/shard_map/ppermute | solution.py:23
  8.4 30.5 %collective-permute-start = (bf16[32,512]{1,0:T(8,128)(2,1)S(1)}, bf16[32,512]{1,0:T(8,128)(2,1)S(1)}, u32[]{:S(2)}, u32[]{:S(2)}) collective-permute-start(bf16[32,512]{1,0:T(8,128)(2,1)S(1)} %copy-done.7), channel_id=1, source_target_pairs={{248,0},{192,16},{200,32},{56,48},{0,8},{8,24},{380,40},{324,56},{... | collective-permute-start | bytes 98312 | tf_op jit(solution)/shard_map/ppermute | solution.py:246
  39.8 13.4 %all-to-all-start = ((bf16[16,32,512]{2,1,0:T(8,128)(2,1)}), bf16[16,32,512]{2,1,0:T(8,128)(2,1)S(1)}, u32[]{:S(2)}, u32[]{:S(2)}) async-start(bf16[16,32,512]{2,1,0:T(8,128)(2,1)} %broadcast_in_dim.2), calls=%async_computation | async-start | bytes 1048576 | tf_op jit(solution)/shard_map/all_to_all | solution.py:250
  53.2 3.9 %collective-permute-start.3 = (bf16[512,512]{1,0:T(8,128)(2,1)S(1)}, bf16[512,512]{1,0:T(8,128)(2,1)}, u32[]{:S(2)}, u32[]{:S(2)}) collective-permute-start(bf16[512,512]{1,0:T(8,128)(2,1)S(1)} %bitcast.20), channel_id=1, source_target_pairs={{0,8},{8,0},{1,9},{9,1},{2,10},{10,2},{3,11},{11,3},{4,12},{12,4},... | collective-permute-start | bytes 1572872 | tf_op jit(solution)/shard_map/ppermute | solution.py:63
  57.1 11.1 %copy-start.5 = (bf16[32,2,4,224]{3,1,0,2:T(2,128)(2,1)S(1)}, bf16[32,2,4,224]{3,1,0,2:T(2,128)(2,1)}, u32[]{:S(2)}) copy-start(bf16[32,2,4,224]{3,1,0,2:T(2,128)(2,1)} %copy.23) | copy-start | bytes 344068
  59.9 28.2 %collective-permute-start.4 = (bf16[896,128]{1,0:T(8,128)(2,1)}, bf16[896,128]{1,0:T(8,128)(2,1)S(1)}, u32[]{:S(2)}, u32[]{:S(2)}) collective-permute-start(bf16[896,128]{1,0:T(8,128)(2,1)} %get-tuple-element.40), channel_id=1, source_target_pairs={{0,192},{64,256},{128,320},{192,384},{256,448},{320,4},{384,68},{4... | collective-permute-start | bytes 688136 | tf_op jit(solution)/shard_map/ppermute | solution.py:23
  61.8 26.9 %collective-permute-start.5 = (bf16[896,128]{1,0:T(8,128)(2,1)}, bf16[896,128]{1,0:T(8,128)(2,1)}, u32[]{:S(2)}, u32[]{:S(2)}) collective-permute-start(bf16[896,128]{1,0:T(8,128)(2,1)} %get-tuple-element.41), channel_id=1, source_target_pairs={{0,324},{64,388},{128,452},{192,0},{256,64},{320,128},{384,192},{4... | collective-permute-start | bytes 688136 | tf_op jit(solution)/shard_map/ppermute | solution.py:23
  79.7 9.0 %copy-start.2 = (bf16[128,448]{0,1:T(8,128)(2,1)S(1)}, bf16[128,448]{0,1:T(8,128)(2,1)}, u32[]{:S(2)}) copy-start(bf16[128,448]{0,1:T(8,128)(2,1)} %copy.18) | copy-start | bytes 344068
  81.6 9.5 %collective-permute-start.7 = (bf16[256,512]{1,0:T(8,128)(2,1)S(1)}, bf16[256,512]{1,0:T(8,128)(2,1)S(1)}, u32[]{:S(2)}, u32[]{:S(2)}) collective-permute-start(bf16[256,512]{1,0:T(8,128)(2,1)S(1)} %get-tuple-element.45), channel_id=1, source_target_pairs={{0,64},{64,128},{128,192},{192,256},{256,320},{320,384},{384,448},... | collective-permute-start | bytes 786440 | tf_op jit(solution)/shard_map/ppermute | solution.py:23
  85.4 10.6 %collective-permute-start.6 = (bf16[384,512]{1,0:T(8,128)(2,1)S(1)}, bf16[384,512]{1,0:T(8,128)(2,1)S(1)}, u32[]{:S(2)}, u32[]{:S(2)}) collective-permute-start(bf16[384,512]{1,0:T(8,128)(2,1)S(1)} %get-tuple-element.44), channel_id=1, source_target_pairs={{0,452},{64,0},{128,64},{192,128},{256,192},{320,256},{384,320},{4... | collective-permute-start | bytes 1179656 | tf_op jit(solution)/shard_map/ppermute | solution.py:23
  88.1 0.7 copy-start.3
  88.8 0.9 copy-start.4
  96.0 6.8 %collective-permute-start.11 = (bf16[896,128]{1,0:T(8,128)(2,1)S(1)}, bf16[896,128]{1,0:T(8,128)(2,1)S(1)}, u32[]{:S(2)}, u32[]{:S(2)}) collective-permute-start(bf16[896,128]{1,0:T(8,128)(2,1)S(1)} %get-tuple-element.46.refs_2_), channel_id=1, source_target_pairs={{0,64},{64,128},{128,192},{192,256},{256,320},{320,384},{384,448},... | collective-permute-start | bytes 688136 | tf_op jit(solution)/shard_map/ppermute | solution.py:23
  98.2 7.1 %collective-permute-start.8 = (bf16[896,128]{1,0:T(8,128)(2,1)S(1)}, bf16[896,128]{1,0:T(8,128)(2,1)S(1)}, u32[]{:S(2)}, u32[]{:S(2)}) collective-permute-start(bf16[896,128]{1,0:T(8,128)(2,1)S(1)} %get-tuple-element.46.refs_2_), channel_id=1, source_target_pairs={{0,452},{64,0},{128,64},{192,128},{256,192},{320,256},{384,320},{4... | collective-permute-start | bytes 688136 | tf_op jit(solution)/shard_map/ppermute | solution.py:23
  102.8 8.4 %collective-permute-start.12 = (bf16[896,128]{1,0:T(8,128)(2,1)S(1)}, bf16[896,128]{1,0:T(8,128)(2,1)S(1)}, u32[]{:S(2)}, u32[]{:S(2)}) collective-permute-start(bf16[896,128]{1,0:T(8,128)(2,1)S(1)} %collective-permute-done.11.refs_1_), channel_id=1, source_target_pairs={{0,64},{64,128},{128,192},{192,256},{256,320},{320,384},{384,448},... | collective-permute-start | bytes 688136 | tf_op jit(solution)/shard_map/ppermute | solution.py:23
  105.3 7.9 %collective-permute-start.9 = (bf16[896,128]{1,0:T(8,128)(2,1)S(1)}, bf16[896,128]{1,0:T(8,128)(2,1)S(1)}, u32[]{:S(2)}, u32[]{:S(2)}) collective-permute-start(bf16[896,128]{1,0:T(8,128)(2,1)S(1)} %collective-permute-done.8.refs_3_), channel_id=1, source_target_pairs={{0,452},{64,0},{128,64},{192,128},{256,192},{320,256},{384,320},{4... | collective-permute-start | bytes 688136 | tf_op jit(solution)/shard_map/ppermute | solution.py:23
  111.2 8.6 %collective-permute-start.13 = (bf16[896,128]{1,0:T(8,128)(2,1)S(1)}, bf16[896,128]{1,0:T(8,128)(2,1)S(1)}, u32[]{:S(2)}, u32[]{:S(2)}) collective-permute-start(bf16[896,128]{1,0:T(8,128)(2,1)S(1)} %collective-permute-done.12.refs_0_), channel_id=1, source_target_pairs={{0,64},{64,128},{128,192},{192,256},{256,320},{320,384},{384,448},... | collective-permute-start | bytes 688136 | tf_op jit(solution)/shard_map/ppermute | solution.py:23
  113.1 7.5 %collective-permute-start.10 = (bf16[896,128]{1,0:T(8,128)(2,1)S(1)}, bf16[896,128]{1,0:T(8,128)(2,1)S(1)}, u32[]{:S(2)}, u32[]{:S(2)}) collective-permute-start(bf16[896,128]{1,0:T(8,128)(2,1)S(1)} %collective-permute-done.9.refs_4_), channel_id=1, source_target_pairs={{0,452},{64,0},{128,64},{192,128},{256,192},{320,256},{384,320},{4... | collective-permute-start | bytes 688136 | tf_op jit(solution)/shard_map/ppermute | solution.py:23
  120.7 7.9 %collective-permute-start.14 = (bf16[896,128]{1,0:T(8,128)(2,1)S(1)}, bf16[896,128]{1,0:T(8,128)(2,1)S(1)}, u32[]{:S(2)}, u32[]{:S(2)}) collective-permute-start(bf16[896,128]{1,0:T(8,128)(2,1)S(1)} %collective-permute-done.10.high_ref), channel_id=1, source_target_pairs={{0,452},{64,0},{128,64},{192,128},{256,192},{320,256},{384,320},{4... | collective-permute-start | bytes 688136 | tf_op jit(solution)/shard_map/ppermute | solution.py:23
  127.3 1.2 copy-start
  128.6 13.2 %copy-start.1 = (f32[896,512]{1,0:T(8,128)S(1)}, f32[896,512]{1,0:T(8,128)}, u32[]{:S(2)}) copy-start(f32[896,512]{1,0:T(8,128)} %copy-done) | copy-start | bytes 5505028
  128.6 28.8 %all-to-all-start.2 = ((bf16[32,32,512]{2,1,0:T(8,128)(2,1)}), bf16[32,32,512]{2,1,0:T(8,128)(2,1)}, u32[]{:S(2)}, u32[]{:S(2)}) async-start(bf16[32,32,512]{2,1,0:T(8,128)(2,1)} %bitcast.4), calls=%async_computation.2 | async-start | bytes 2097152 | tf_op jit(solution)/shard_map/all_to_all | solution.py:280
  142.9 54.5 %collective-permute-start.16 = (bf16[448,512]{1,0:T(8,128)(2,1)}, bf16[448,512]{1,0:T(8,128)(2,1)S(1)}, u32[]{:S(2)}, u32[]{:S(2)}) collective-permute-start(bf16[448,512]{1,0:T(8,128)(2,1)} %get-tuple-element.67), channel_id=1, source_target_pairs={{0,4},{4,0},{1,5},{5,1},{2,6},{6,2},{3,7},{7,3},{8,12},{12,8},{9,1... | collective-permute-start | bytes 1376264 | tf_op jit(solution)/shard_map/ppermute | solution.py:284
  159.5 8.4 %all-to-all-start.3 = ((bf16[128,2,1,224]{3,1,2,0:T(2,128)(2,1)}), bf16[128,2,1,224]{3,1,2,0:T(2,128)(2,1)S(1)}, u32[]{:S(2)}, u32[]{:S(2)}) async-start(bf16[128,2,1,224]{3,1,2,0:T(2,128)(2,1)} %copy.19), calls=%async_computation.3 | async-start | bytes 262144 | tf_op jit(solution)/shard_map/all_to_all | solution.py:287
  162.9 33.6 %collective-permute-start.15 = (bf16[32,512]{1,0:T(8,128)(2,1)S(1)}, bf16[32,512]{1,0:T(8,128)(2,1)S(1)}, u32[]{:S(2)}, u32[]{:S(2)}) collective-permute-start(bf16[32,512]{1,0:T(8,128)(2,1)S(1)} %reduce_sum.12), channel_id=1, source_target_pairs={{0,44},{16,52},{32,60},{48,0},{8,8},{24,16},{40,24},{56,472},{64,1... | collective-permute-start | bytes 98312 | tf_op jit(solution)/shard_map/ppermute | solution.py:290

commit v11 on v8

--- a/solution.py
+++ b/solution.py
@@ -52,6 +52,7 @@
     return lax.dot_general(left, right, (dims, ((), ())), preferred_element_type=jnp.float32)
 
 
+ANY_SPEC = pl.BlockSpec(memory_space=pl.ANY)
 SMEM_SPEC = pl.BlockSpec(memory_space=pltpu.SMEM)
 VMEM_SPEC = pl.BlockSpec(memory_space=pltpu.VMEM)
 PARAMS = pltpu.CompilerParams(vmem_limit_bytes=16 << 20)
@@ -87,14 +88,21 @@
     )(core, own, other, weights)
 
 
+def term_rows(at):
+    return [((at % 4 * 4 + x) * 2 + at // 4) * 32 for x in range(4)]
+
+
 def near_kernel(core_ref, own_ref, other_ref, weights_ref, *refs):
     tile_refs = refs[:7]
     terms_ref, sums_ref, tokens_ref, wide_ref = refs[7:]
     join_cores(core_ref[0], own_ref, other_ref, tokens_ref)
     for at, tile_ref in enumerate(tile_refs):
         wide_ref[:, at * 128 : (at + 1) * 128] = tile_ref[...]
-        product = dot_f32(weights_ref[...], tile_ref[...])
-        terms_ref[slot(at) * 128 : (slot(at) + 1) * 128, :] = product.T.astype(jnp.bfloat16)
+        product = dot_f32(weights_ref[...], tile_ref[...]).T.astype(jnp.bfloat16)
+        for part, first in enumerate(term_rows(at)):
+            terms_ref[first : first + 32, :] = product[part * 32 : (part + 1) * 32, :]
+    for first in term_rows(7):
+        terms_ref[first : first + 32, :] = jnp.zeros((32, terms_ref.shape[1]), jnp.bfloat16)
     sums_ref[...] = dot_f32(wide_ref[...], tokens_ref[0:896, :])
 
 
@@ -105,7 +113,7 @@
         in_specs=[SMEM_SPEC] + [VMEM_SPEC] * 10,
         out_specs=[VMEM_SPEC] * 2,
         out_shape=[
-            jax.ShapeDtypeStruct((7 * 128, features), jnp.bfloat16),
+            jax.ShapeDtypeStruct((ROWS * 128, features), jnp.bfloat16),
             jax.ShapeDtypeStruct((cols, features), jnp.float32),
         ],
         scratch_shapes=[
@@ -151,19 +159,53 @@
     )(core, half, own, other, sums, tile)
 
 
-def last_terms_kernel(weights_ref, terms_ref, tile_ref, all_ref):
-    all_ref[0:896, :] = terms_ref[...]
-    all_ref[896:1024, :] = dot_f32(weights_ref[...], tile_ref[...]).T.astype(jnp.bfloat16)
+def last_terms_kernel(weights_ref, tile_ref, terms_ref, all_ref, block_ref, sem_ref):
+    del terms_ref
+    block_ref[...] = dot_f32(weights_ref[...], tile_ref[...]).T.astype(jnp.bfloat16)
+    copies = [
+        pltpu.make_async_copy(
+            block_ref.at[part * 32 : (part + 1) * 32, :], all_ref.at[first : first + 32, :], sem_ref.at[part]
+        )
+        for part, first in enumerate(term_rows(7))
+    ]
+    for copy in copies:
+        copy.start()
+    for copy in copies:
+        copy.wait()
 
 
 def last_terms(weights, terms, tile):
     return pl.pallas_call(
         last_terms_kernel,
-        in_specs=[VMEM_SPEC] * 3,
-        out_specs=VMEM_SPEC,
-        out_shape=jax.ShapeDtypeStruct((ROWS * 128, weights.shape[0]), jnp.bfloat16),
-        compiler_params=PARAMS,
-    )(weights, terms, tile)
+        in_specs=[VMEM_SPEC] * 2 + [ANY_SPEC],
+        out_specs=ANY_SPEC,
+        out_shape=jax.ShapeDtypeStruct(terms.shape, terms.dtype),
+        input_output_aliases={2: 0},
+        scratch_shapes=[pltpu.VMEM((128, terms.shape[1]), jnp.bfloat16), pltpu.SemaphoreType.DMA((4,))],
+        compiler_params=PARAMS,
+    )(weights, tile, terms)
+
+
+def total_kernel(core_ref, parts_ref, keep_ref, send_ref, total_ref):
+    total_ref[...] = jnp.sum(parts_ref[...].astype(jnp.float32), 0)
+    rows = keep_ref.shape[0]
+    core = core_ref[0]
+    keep_ref[...] = total_ref[pl.ds(pl.multiple_of(core * rows, rows), rows), :]
+    send = total_ref[pl.ds(pl.multiple_of((1 - core) * rows, rows), rows), :]
+    send_ref[...] = send.astype(jnp.bfloat16)
+
+
+def sum_parts(core, parts):
+    _, rows, features = parts.shape
+    shape = (rows // 2, features)
+    return pl.pallas_call(
+        total_kernel,
+        in_specs=[SMEM_SPEC, VMEM_SPEC],
+        out_specs=[VMEM_SPEC] * 2,
+        out_shape=[jax.ShapeDtypeStruct(shape, jnp.float32), jax.ShapeDtypeStruct(shape, jnp.bfloat16)],
+        scratch_shapes=[pltpu.VMEM((rows, features), jnp.float32)],
+        compiler_params=PARAMS,
+    )(core, parts)
 
 
 def add_tiles(*tiles):
@@ -232,9 +274,10 @@
     received = lax.ppermute(send, "h", [(0, 1), (1, 0)])
     terms = last_terms(weights, terms, left_4)
     terms = lax.all_to_all(
-        terms.reshape(32, -1, features), ("y", "c", "x"), split_axis=0, concat_axis=0, tiled=True
-    )
-    grad_tokens = jnp.sum(terms.astype(jnp.float32), 0).astype(jnp.bfloat16)
+        terms.reshape(16, -1, features), ("y", "x"), split_axis=0, concat_axis=0, tiled=True
+    )
+    keep_terms, send_terms = sum_parts(core, terms)
+    grad_tokens = (keep_terms + swap_cores(send_terms).astype(jnp.float32)).astype(jnp.bfloat16)
     grad_tokens, hidden = lax.optimization_barrier((grad_tokens, hidden))
     hidden = lax.all_to_all(
         hidden.T.reshape(-1, 2, 1, part), "x", split_axis=0, concat_axis=2, tiled=True

time: 182 us -> 178 us (0.978)
  the two profiles are of different devices: /device:TPU:235 before, /device:TPU:160 now
where the time goes in v11:
time: 178 us; the launch traced here: 177 us
  starting transfers between devices  87.9 us (49%)
  waiting for transfers between devices  67.5 us (38%)
  local copies, waits for them, and re-layouts  8.89 us (5%)
  Pallas kernels  8.2 us (5%)
  other arithmetic  3.1 us (2%)
    ppermute x14, starting transfers between devices, ring_shift(): return lax.ppermute(value, ('r', 'h'), pairs)  48.2 us
    ppermute x1, waiting for transfers between devices, local(): lax.ppermute(grad_tokens, ('r', 'y', 'c', 'h'), result_pairs())  26.3 us
    ppermute x14, waiting for transfers between devices, ring_shift(): return lax.ppermute(value, ('r', 'h'), pairs)  18.5 us
    ppermute x1, starting transfers between devices, local(): received = lax.ppermute(send, 'h', [(0, 1), (1, 0)])  9.56 us
    all_to_all x1, waiting for transfers between devices, local(): lax.all_to_all(copies, ('y', 'x'), split_axis=0, concat_axis=0, tiled=True)  8.34 us
    ppermute x1, starting transfers between devices, local(): piece = lax.ppermute(tokens, ('r', 'y', 'c', 'h'), token_pairs())  7.74 us
    all_to_all x1, starting transfers between devices, local(): lax.all_to_all(terms.reshape(16, -1, features), ('y', 'x'), split_axis=0,...  5.51 us
    pallas_call x1, Pallas kernels, near_products(): pl.pallas_call(near_kernel, in_specs=[SMEM_SPEC] + [VMEM_SPEC] * 10, out_...  4.76 us
  transfers between devices with their start and end apart: 23, of which 16 were waited for; matrix products, arithmetic and copies ran while one was open for 3% of the time, Pallas kernels for 3%

profile of v11, /device:TPU:160, one launch (start us, length us, event | category | flops | bytes accessed | tf_op | source)
XLA Modules:
  0.0 176.6 jit_solution(5511866457670541652)
XLA Ops:
  0.6 7.7 %collective-permute-start = (bf16[32,512]{1,0:T(8,128)(2,1)}, bf16[32,512]{1,0:T(8,128)(2,1)S(1)}, u32[]{:S(2)}, u32[]{:S(2)}) collective-permute-start(bf16[32,512]{1,0:T(8,128)(2,1)} %param.4), channel_id=1, source_target_pairs={{324,0},{388,16},{452,32},{0,48},{64,8},{128,24},{192,40},{256,56}... | collective-permute-start | bytes 98312 | tf_op jit(solution)/shard_map/ppermute | solution.py:229
  8.4 3.5 %collective-permute-done = bf16[32,512]{1,0:T(8,128)(2,1)S(1)} collective-permute-done((bf16[32,512]{1,0:T(8,128)(2,1)}, bf16[32,512]{1,0:T(8,128)(2,1)S(1)}, u32[]{:S(2)}, u32[]{:S(2)}) %collective-permute-start) | collective-permute-done | bytes 32800 | tf_op jit(solution)/shard_map/ppermute | solution.py:229
  11.8 0.8 broadcast_in_dim.2
  12.7 4.4 %all-to-all-start = ((bf16[16,32,512]{2,1,0:T(8,128)(2,1)}), bf16[16,32,512]{2,1,0:T(8,128)(2,1)S(1)}, u32[]{:S(2)}, u32[]{:S(2)}) async-start(bf16[16,32,512]{2,1,0:T(8,128)(2,1)} %broadcast_in_dim.2), calls=%async_computation | async-start | bytes 1048576 | tf_op jit(solution)/shard_map/all_to_all | solution.py:231
  17.1 1.1 reshape.35
  18.2 0.8 copy.24
  19.0 1.8 %constant_dynamic-slice_fusion.2 = (bf16[512,224]{1,0:T(8,128)(2,1)S(1)}, bf16[512,224]{1,0:T(8,128)(2,1)S(1)}, bf16[512,224]{1,0:T(8,128)(2,1)S(1)}, bf16[512,224]{1,0:T(8,128)(2,1)S(1)}) fusion(bf16[512,1792]{1,0:T(8,128)(2,1)} %param.6, s32[]{:T(128)S(6)} %select_n.8, s32[]{:T(128)S(6)} %select_n.9, bf16[512,1792]{1,0:T(8,128)(2,1)} %param.5), kind=kLoop, calls=%fused_computation.26 | loop fusion | bytes 1835016 | tf_op jit(solution)/shard_map/dynamic_slice | solution.py:223
  20.8 0.4 pad_maximum_fusion.weights_ref
  21.2 8.3 %all-to-all-done = bf16[16,32,512]{2,1,0:T(8,128)(2,1)S(1)} async-done(((bf16[16,32,512]{2,1,0:T(8,128)(2,1)}), bf16[16,32,512]{2,1,0:T(8,128)(2,1)S(1)}, u32[]{:S(2)}, u32[]{:S(2)}) %all-to-all-start) | async-done | bytes 524320 | tf_op jit(solution)/shard_map/all_to_all | solution.py:231
  29.5 1.9 %collective-permute-start.1 = (bf16[512,512]{1,0:T(8,128)(2,1)S(1)}, bf16[512,512]{1,0:T(8,128)(2,1)S(1)}, u32[]{:S(2)}, u32[]{:S(2)}) collective-permute-start(bf16[512,512]{1,0:T(8,128)(2,1)S(1)} %bitcast.30), channel_id=1, source_target_pairs={{0,8},{8,0},{1,9},{9,1},{2,10},{10,2},{3,11},{11,3},{4,12},{12,4},... | collective-permute-start | bytes 1572872 | tf_op jit(solution)/shard_map/ppermute | solution.py:62
  31.5 1.9 %collective-permute-done.1.other_ref = bf16[512,512]{1,0:T(8,128)(2,1)S(1)} collective-permute-done((bf16[512,512]{1,0:T(8,128)(2,1)S(1)}, bf16[512,512]{1,0:T(8,128)(2,1)S(1)}, u32[]{:S(2)}, u32[]{:S(2)}) %collective-permute-start.1) | collective-permute-done | bytes 524320 | tf_op jit(solution)/shard_map/ppermute | solution.py:62
  33.3 0.6 shard_map.75
  33.9 3.7 %collective-permute-start.2 = (bf16[896,128]{1,0:T(8,128)(2,1)S(1)}, bf16[896,128]{1,0:T(8,128)(2,1)S(1)}, u32[]{:S(2)}, u32[]{:S(2)}) collective-permute-start(bf16[896,128]{1,0:T(8,128)(2,1)S(1)} %get-tuple-element.32), channel_id=1, source_target_pairs={{0,64},{64,128},{128,192},{192,256},{256,320},{320,384},{384,448},... | collective-permute-start | bytes 688136 | tf_op jit(solution)/shard_map/ppermute | solution.py:22
  37.6 3.3 %all-to-all-start.1 = ((bf16[4,32,2,224]{3,2,1,0:T(2,128)(2,1)}), bf16[4,32,2,224]{3,2,1,0:T(2,128)(2,1)S(1)}, u32[]{:S(2)}, u32[]{:S(2)}) async-start(bf16[4,32,2,224]{3,2,1,0:T(2,128)(2,1)} %bitcast.29), calls=%async_computation.1 | async-start | bytes 262144 | tf_op jit(solution)/shard_map/all_to_all | solution.py:236
  41.0 2.1 %collective-permute-start.5 = (bf16[896,128]{1,0:T(8,128)(2,1)S(1)}, bf16[896,128]{1,0:T(8,128)(2,1)S(1)}, u32[]{:S(2)}, u32[]{:S(2)}) collective-permute-start(bf16[896,128]{1,0:T(8,128)(2,1)S(1)} %get-tuple-element.39), channel_id=1, source_target_pairs={{0,452},{64,0},{128,64},{192,128},{256,192},{320,256},{384,320},{4... | collective-permute-start | bytes 688136 | tf_op jit(solution)/shard_map/ppermute | solution.py:22
  43.1 1.1 shard_map.76
  44.2 0.1 add_convert_fusion.4
  44.3 3.7 %collective-permute-start.3 = (bf16[896,128]{1,0:T(8,128)(2,1)S(1)}, bf16[896,128]{1,0:T(8,128)(2,1)S(1)}, u32[]{:S(2)}, u32[]{:S(2)}) collective-permute-start(bf16[896,128]{1,0:T(8,128)(2,1)S(1)} %add_convert_fusion.4), channel_id=1, source_target_pairs={{0,64},{64,128},{128,192},{192,256},{256,320},{320,384},{384,448},... | collective-permute-start | bytes 688136 | tf_op jit(solution)/shard_map/ppermute | solution.py:22
  48.1 2.5 %collective-permute-done.5 = bf16[896,128]{1,0:T(8,128)(2,1)S(1)} collective-permute-done((bf16[896,128]{1,0:T(8,128)(2,1)S(1)}, bf16[896,128]{1,0:T(8,128)(2,1)S(1)}, u32[]{:S(2)}, u32[]{:S(2)}) %collective-permute-start.5) | collective-permute-done | bytes 229408 | tf_op jit(solution)/shard_map/ppermute | solution.py:22
  50.6 2.1 %collective-permute-start.6 = (bf16[896,128]{1,0:T(8,128)(2,1)S(1)}, bf16[896,128]{1,0:T(8,128)(2,1)S(1)}, u32[]{:S(2)}, u32[]{:S(2)}) collective-permute-start(bf16[896,128]{1,0:T(8,128)(2,1)S(1)} %add_convert_fusion.1), channel_id=1, source_target_pairs={{0,452},{64,0},{128,64},{192,128},{256,192},{320,256},{384,320},{4... | collective-permute-start | bytes 688136 | tf_op jit(solution)/shard_map/ppermute | solution.py:22
  52.7 0.9 collective-permute-done.3
  53.6 0.1 add_convert_fusion.3
  53.7 6.4 %collective-permute-start.4 = (bf16[896,128]{1,0:T(8,128)(2,1)S(1)}, bf16[896,128]{1,0:T(8,128)(2,1)S(1)}, u32[]{:S(2)}, u32[]{:S(2)}) collective-permute-start(bf16[896,128]{1,0:T(8,128)(2,1)S(1)} %add_convert_fusion.3), channel_id=1, source_target_pairs={{0,64},{64,128},{128,192},{192,256},{256,320},{320,384},{384,448},... | collective-permute-start | bytes 688136 | tf_op jit(solution)/shard_map/ppermute | solution.py:22
  60.0 2.7 %collective-permute-done.6 = bf16[896,128]{1,0:T(8,128)(2,1)S(1)} collective-permute-done((bf16[896,128]{1,0:T(8,128)(2,1)S(1)}, bf16[896,128]{1,0:T(8,128)(2,1)S(1)}, u32[]{:S(2)}, u32[]{:S(2)}) %collective-permute-start.6) | collective-permute-done | bytes 229408 | tf_op jit(solution)/shard_map/ppermute | solution.py:22
  62.8 1.9 %collective-permute-start.7 = (bf16[896,128]{1,0:T(8,128)(2,1)S(1)}, bf16[896,128]{1,0:T(8,128)(2,1)S(1)}, u32[]{:S(2)}, u32[]{:S(2)}) collective-permute-start(bf16[896,128]{1,0:T(8,128)(2,1)S(1)} %add_convert_fusion), channel_id=1, source_target_pairs={{0,452},{64,0},{128,64},{192,128},{256,192},{320,256},{384,320},{4... | collective-permute-start | bytes 688136 | tf_op jit(solution)/shard_map/ppermute | solution.py:22
  64.7 0.1 add_convert_fusion.2
  64.8 4.5 %collective-permute-start.8 = (bf16[896,128]{1,0:T(8,128)(2,1)S(1)}, bf16[896,128]{1,0:T(8,128)(2,1)}, u32[]{:S(2)}, u32[]{:S(2)}) collective-permute-start(bf16[896,128]{1,0:T(8,128)(2,1)S(1)} %add_convert_fusion.2), channel_id=1, source_target_pairs={{0,64},{64,128},{128,192},{192,256},{256,320},{320,384},{384,448},... | collective-permute-start | bytes 688136 | tf_op jit(solution)/shard_map/ppermute | solution.py:22
  69.3 0.1 reshape.40
  69.4 0.1 copy.19
  69.6 1.8 %collective-permute-done.7 = bf16[896,128]{1,0:T(8,128)(2,1)S(1)} collective-permute-done((bf16[896,128]{1,0:T(8,128)(2,1)S(1)}, bf16[896,128]{1,0:T(8,128)(2,1)S(1)}, u32[]{:S(2)}, u32[]{:S(2)}) %collective-permute-start.7) | collective-permute-done | bytes 229408 | tf_op jit(solution)/shard_map/ppermute | solution.py:22
  71.4 1.6 collective-permute-done.8
  73.0 1.0 convert_add_fusion.1
  74.0 0.2 multiply_convert_fusion
  74.3 4.2 %collective-permute-start.9 = (bf16[896,128]{1,0:T(8,128)(2,1)S(1)}, bf16[896,128]{1,0:T(8,128)(2,1)S(1)}, u32[]{:S(2)}, u32[]{:S(2)}) collective-permute-start(bf16[896,128]{1,0:T(8,128)(2,1)S(1)} %pad_maximum_fusion.3.refs_3_), channel_id=1, source_target_pairs={{0,452},{64,0},{128,64},{192,128},{256,192},{320,256},{384,320},{4... | collective-permute-start | bytes 688136 | tf_op jit(solution)/shard_map/ppermute | solution.py:22
  78.4 2.5 %collective-permute-start.13 = (bf16[896,128]{1,0:T(8,128)(2,1)S(1)}, bf16[896,128]{1,0:T(8,128)(2,1)S(1)}, u32[]{:S(2)}, u32[]{:S(2)}) collective-permute-start(bf16[896,128]{1,0:T(8,128)(2,1)S(1)} %pad_maximum_fusion.3.refs_3_), channel_id=1, source_target_pairs={{0,64},{64,128},{128,192},{192,256},{256,320},{320,384},{384,448},... | collective-permute-start | bytes 688136 | tf_op jit(solution)/shard_map/ppermute | solution.py:22
  81.0 2.1 %collective-permute-done.9.refs_4_ = bf16[896,128]{1,0:T(8,128)(2,1)S(1)} collective-permute-done((bf16[896,128]{1,0:T(8,128)(2,1)S(1)}, bf16[896,128]{1,0:T(8,128)(2,1)S(1)}, u32[]{:S(2)}, u32[]{:S(2)}) %collective-permute-start.9) | collective-permute-done | bytes 229408 | tf_op jit(solution)/shard_map/ppermute | solution.py:22
  83.0 3.3 %collective-permute-start.10 = (bf16[896,128]{1,0:T(8,128)(2,1)S(1)}, bf16[896,128]{1,0:T(8,128)(2,1)S(1)}, u32[]{:S(2)}, u32[]{:S(2)}) collective-permute-start(bf16[896,128]{1,0:T(8,128)(2,1)S(1)} %collective-permute-done.9.refs_4_), channel_id=1, source_target_pairs={{0,452},{64,0},{128,64},{192,128},{256,192},{320,256},{384,320},{4... | collective-permute-start | bytes 688136 | tf_op jit(solution)/shard_map/ppermute | solution.py:22
  86.4 4.2 %collective-permute-start.14 = (bf16[896,128]{1,0:T(8,128)(2,1)S(1)}, bf16[896,128]{1,0:T(8,128)(2,1)S(1)}, u32[]{:S(2)}, u32[]{:S(2)}) collective-permute-start(bf16[896,128]{1,0:T(8,128)(2,1)S(1)} %collective-permute-done.13.refs_2_), channel_id=1, source_target_pairs={{0,64},{64,128},{128,192},{192,256},{256,320},{320,384},{384,448},... | collective-permute-start | bytes 688136 | tf_op jit(solution)/shard_map/ppermute | solution.py:22
  90.6 2.0 %collective-permute-done.10.refs_5_ = bf16[896,128]{1,0:T(8,128)(2,1)S(1)} collective-permute-done((bf16[896,128]{1,0:T(8,128)(2,1)S(1)}, bf16[896,128]{1,0:T(8,128)(2,1)S(1)}, u32[]{:S(2)}, u32[]{:S(2)}) %collective-permute-start.10) | collective-permute-done | bytes 229408 | tf_op jit(solution)/shard_map/ppermute | solution.py:22
  92.6 1.9 %collective-permute-start.11 = (bf16[896,128]{1,0:T(8,128)(2,1)S(1)}, bf16[896,128]{1,0:T(8,128)(2,1)}, u32[]{:S(2)}, u32[]{:S(2)}) collective-permute-start(bf16[896,128]{1,0:T(8,128)(2,1)S(1)} %collective-permute-done.10.refs_5_), channel_id=1, source_target_pairs={{0,452},{64,0},{128,64},{192,128},{256,192},{320,256},{384,320},{4... | collective-permute-start | bytes 688136 | tf_op jit(solution)/shard_map/ppermute | solution.py:22
  94.5 5.7 %collective-permute-start.15 = (bf16[896,128]{1,0:T(8,128)(2,1)S(1)}, bf16[896,128]{1,0:T(8,128)(2,1)}, u32[]{:S(2)}, u32[]{:S(2)}) collective-permute-start(bf16[896,128]{1,0:T(8,128)(2,1)S(1)} %collective-permute-done.14.refs_1_), channel_id=1, source_target_pairs={{0,64},{64,128},{128,192},{192,256},{256,320},{320,384},{384,448},... | collective-permute-start | bytes 688136 | tf_op jit(solution)/shard_map/ppermute | solution.py:22
  100.2 2.1 %collective-permute-done.11.refs_6_ = bf16[896,128]{1,0:T(8,128)(2,1)} collective-permute-done((bf16[896,128]{1,0:T(8,128)(2,1)S(1)}, bf16[896,128]{1,0:T(8,128)(2,1)}, u32[]{:S(2)}, u32[]{:S(2)}) %collective-permute-start.11) | collective-permute-done | bytes 229408 | tf_op jit(solution)/shard_map/ppermute | solution.py:22
  102.4 1.9 %collective-permute-start.12 = (bf16[896,128]{1,0:T(8,128)(2,1)}, bf16[896,128]{1,0:T(8,128)(2,1)S(1)}, u32[]{:S(2)}, u32[]{:S(2)}) collective-permute-start(bf16[896,128]{1,0:T(8,128)(2,1)} %collective-permute-done.11.refs_6_), channel_id=1, source_target_pairs={{0,452},{64,0},{128,64},{192,128},{256,192},{320,256},{384,320},{4... | collective-permute-start | bytes 688136 | tf_op jit(solution)/shard_map/ppermute | solution.py:22
  104.3 4.8 %shard_map.77 = (bf16[1024,512]{1,0:T(8,128)(2,1)}, f32[896,512]{1,0:T(8,128)S(1)}) custom-call(s32[1]{0:T(128)} %bitcast.core_ref, bf16[512,512]{1,0:T(8,128)(2,1)S(1)} %bitcast.33, bf16[512,512]{1,0:T(8,128)(2,1)S(1)} %collective-permute-done.1.other_ref, bf16[512,896]{1,0:T(8,128)(2,1)S(1)} %pad_maximum_fusion.weights_ref, ...), custom_call_target="tpu_custom_call" | custom-call | tf_op jit(solution)/shard_map/pallas_call | solution.py:111
  109.1 2.9 %collective-permute-done.12.tile_ref = bf16[896,128]{1,0:T(8,128)(2,1)S(1)} collective-permute-done((bf16[896,128]{1,0:T(8,128)(2,1)}, bf16[896,128]{1,0:T(8,128)(2,1)S(1)}, u32[]{:S(2)}, u32[]{:S(2)}) %collective-permute-start.12) | collective-permute-done | bytes 229408 | tf_op jit(solution)/shard_map/ppermute | solution.py:22
  111.9 0.4 shard_map.78
  112.4 0.8 copy-done
  113.1 1.2 shard_map.79
  114.3 5.5 %all-to-all-start.2 = ((bf16[16,64,512]{2,1,0:T(8,128)(2,1)}), bf16[16,64,512]{2,1,0:T(8,128)(2,1)S(1)}, u32[]{:S(2)}, u32[]{:S(2)}) async-start(bf16[16,64,512]{2,1,0:T(8,128)(2,1)} %bitcast.5), calls=%async_computation.2 | async-start | bytes 2097152 | tf_op jit(solution)/shard_map/all_to_all | solution.py:276
  119.8 9.6 %collective-permute-start.18 = (bf16[448,512]{1,0:T(8,128)(2,1)S(1)}, bf16[448,512]{1,0:T(8,128)(2,1)}, u32[]{:S(2)}, u32[]{:S(2)}) collective-permute-start(bf16[448,512]{1,0:T(8,128)(2,1)S(1)} %copy-done.1), channel_id=1, source_target_pairs={{0,4},{4,0},{1,5},{5,1},{2,6},{6,2},{3,7},{7,3},{8,12},{12,8},{9,1... | collective-permute-start | bytes 1376264 | tf_op jit(solution)/shard_map/ppermute | solution.py:274
  129.4 3.8 %all-to-all-done.2.parts_ref = bf16[16,64,512]{2,1,0:T(8,128)(2,1)S(1)} async-done(((bf16[16,64,512]{2,1,0:T(8,128)(2,1)}), bf16[16,64,512]{2,1,0:T(8,128)(2,1)S(1)}, u32[]{:S(2)}, u32[]{:S(2)}) %all-to-all-start.2) | async-done | bytes 1048608 | tf_op jit(solution)/shard_map/all_to_all | solution.py:276
  133.2 0.2 shard_map.80
  133.4 1.9 %collective-permute-start.16 = (bf16[32,512]{1,0:T(8,128)(2,1)S(1)}, bf16[32,512]{1,0:T(8,128)(2,1)S(1)}, u32[]{:S(2)}, u32[]{:S(2)}) collective-permute-start(bf16[32,512]{1,0:T(8,128)(2,1)S(1)} %get-tuple-element.48), channel_id=1, source_target_pairs={{0,8},{8,0},{1,9},{9,1},{2,10},{10,2},{3,11},{11,3},{4,12},{12,4},... | collective-permute-start | bytes 98312 | tf_op jit(solution)/shard_map/ppermute | solution.py:62
  135.3 1.2 collective-permute-done.16
  136.5 0.8 copy.20
  137.3 3.3 %all-to-all-start.3 = ((bf16[128,2,1,224]{3,1,2,0:T(2,128)(2,1)}), bf16[128,2,1,224]{3,1,2,0:T(2,128)(2,1)S(1)}, u32[]{:S(2)}, u32[]{:S(2)}) async-start(bf16[128,2,1,224]{3,1,2,0:T(2,128)(2,1)} %copy.20), calls=%async_computation.3 | async-start | bytes 262144 | tf_op jit(solution)/shard_map/all_to_all | solution.py:282
  140.6 1.9 %collective-permute-start.17 = (bf16[32,512]{1,0:T(8,128)(2,1)S(1)}, bf16[32,512]{1,0:T(8,128)(2,1)S(1)}, u32[]{:S(2)}, u32[]{:S(2)}) collective-permute-start(bf16[32,512]{1,0:T(8,128)(2,1)S(1)} %add_convert_fusion.5), channel_id=1, source_target_pairs={{0,44},{16,52},{32,60},{48,0},{8,8},{24,16},{40,24},{56,32},{64,11... | collective-permute-start | bytes 98312 | tf_op jit(solution)/shard_map/ppermute | solution.py:285
  142.5 4.0 %all-to-all-done.3 = bf16[128,2,1,224]{3,1,2,0:T(2,128)(2,1)S(1)} async-done(((bf16[128,2,1,224]{3,1,2,0:T(2,128)(2,1)}), bf16[128,2,1,224]{3,1,2,0:T(2,128)(2,1)S(1)}, u32[]{:S(2)}, u32[]{:S(2)}) %all-to-all-start.3) | async-done | bytes 114720 | tf_op jit(solution)/shard_map/all_to_all | solution.py:282
  146.6 26.3 %collective-permute-done.17 = bf16[32,512]{1,0:T(8,128)(2,1)S(1)} collective-permute-done((bf16[32,512]{1,0:T(8,128)(2,1)S(1)}, bf16[32,512]{1,0:T(8,128)(2,1)S(1)}, u32[]{:S(2)}, u32[]{:S(2)}) %collective-permute-start.17) | collective-permute-done | bytes 32800 | tf_op jit(solution)/shard_map/ppermute | solution.py:285
  172.9 1.1 convert_add_fusion
  174.1 1.0 slice_bitcast_fusion
  175.0 0.1 copy.22
  175.1 0.8 reshape.39
  176.0 0.6 copy.27
  (18 shorter events, 0.3 us)
Async XLA Ops:
  0.6 11.2 %collective-permute-start = (bf16[32,512]{1,0:T(8,128)(2,1)}, bf16[32,512]{1,0:T(8,128)(2,1)S(1)}, u32[]{:S(2)}, u32[]{:S(2)}) collective-permute-start(bf16[32,512]{1,0:T(8,128)(2,1)} %param.4), channel_id=1, source_target_pairs={{324,0},{388,16},{452,32},{0,48},{64,8},{128,24},{192,40},{256,56}... | collective-permute-start | bytes 98312 | tf_op jit(solution)/shard_map/ppermute | solution.py:229
  12.7 16.9 %all-to-all-start = ((bf16[16,32,512]{2,1,0:T(8,128)(2,1)}), bf16[16,32,512]{2,1,0:T(8,128)(2,1)S(1)}, u32[]{:S(2)}, u32[]{:S(2)}) async-start(bf16[16,32,512]{2,1,0:T(8,128)(2,1)} %broadcast_in_dim.2), calls=%async_computation | async-start | bytes 1048576 | tf_op jit(solution)/shard_map/all_to_all | solution.py:231
  29.5 3.8 %collective-permute-start.1 = (bf16[512,512]{1,0:T(8,128)(2,1)S(1)}, bf16[512,512]{1,0:T(8,128)(2,1)S(1)}, u32[]{:S(2)}, u32[]{:S(2)}) collective-permute-start(bf16[512,512]{1,0:T(8,128)(2,1)S(1)} %bitcast.30), channel_id=1, source_target_pairs={{0,8},{8,0},{1,9},{9,1},{2,10},{10,2},{3,11},{11,3},{4,12},{12,4},... | collective-permute-start | bytes 1572872 | tf_op jit(solution)/shard_map/ppermute | solution.py:62
  33.9 10.3 %collective-permute-start.2 = (bf16[896,128]{1,0:T(8,128)(2,1)S(1)}, bf16[896,128]{1,0:T(8,128)(2,1)S(1)}, u32[]{:S(2)}, u32[]{:S(2)}) collective-permute-start(bf16[896,128]{1,0:T(8,128)(2,1)S(1)} %get-tuple-element.32), channel_id=1, source_target_pairs={{0,64},{64,128},{128,192},{192,256},{256,320},{320,384},{384,448},... | collective-permute-start | bytes 688136 | tf_op jit(solution)/shard_map/ppermute | solution.py:22
  37.6 27.1 %all-to-all-start.1 = ((bf16[4,32,2,224]{3,2,1,0:T(2,128)(2,1)}), bf16[4,32,2,224]{3,2,1,0:T(2,128)(2,1)S(1)}, u32[]{:S(2)}, u32[]{:S(2)}) async-start(bf16[4,32,2,224]{3,2,1,0:T(2,128)(2,1)} %bitcast.29), calls=%async_computation.1 | async-start | bytes 262144 | tf_op jit(solution)/shard_map/all_to_all | solution.py:236
  41.0 9.6 %collective-permute-start.5 = (bf16[896,128]{1,0:T(8,128)(2,1)S(1)}, bf16[896,128]{1,0:T(8,128)(2,1)S(1)}, u32[]{:S(2)}, u32[]{:S(2)}) collective-permute-start(bf16[896,128]{1,0:T(8,128)(2,1)S(1)} %get-tuple-element.39), channel_id=1, source_target_pairs={{0,452},{64,0},{128,64},{192,128},{256,192},{320,256},{384,320},{4... | collective-permute-start | bytes 688136 | tf_op jit(solution)/shard_map/ppermute | solution.py:22
  44.3 9.3 %collective-permute-start.3 = (bf16[896,128]{1,0:T(8,128)(2,1)S(1)}, bf16[896,128]{1,0:T(8,128)(2,1)S(1)}, u32[]{:S(2)}, u32[]{:S(2)}) collective-permute-start(bf16[896,128]{1,0:T(8,128)(2,1)S(1)} %add_convert_fusion.4), channel_id=1, source_target_pairs={{0,64},{64,128},{128,192},{192,256},{256,320},{320,384},{384,448},... | collective-permute-start | bytes 688136 | tf_op jit(solution)/shard_map/ppermute | solution.py:22
  50.6 12.1 %collective-permute-start.6 = (bf16[896,128]{1,0:T(8,128)(2,1)S(1)}, bf16[896,128]{1,0:T(8,128)(2,1)S(1)}, u32[]{:S(2)}, u32[]{:S(2)}) collective-permute-start(bf16[896,128]{1,0:T(8,128)(2,1)S(1)} %add_convert_fusion.1), channel_id=1, source_target_pairs={{0,452},{64,0},{128,64},{192,128},{256,192},{320,256},{384,320},{4... | collective-permute-start | bytes 688136 | tf_op jit(solution)/shard_map/ppermute | solution.py:22
  53.7 11.0 %collective-permute-start.4 = (bf16[896,128]{1,0:T(8,128)(2,1)S(1)}, bf16[896,128]{1,0:T(8,128)(2,1)S(1)}, u32[]{:S(2)}, u32[]{:S(2)}) collective-permute-start(bf16[896,128]{1,0:T(8,128)(2,1)S(1)} %add_convert_fusion.3), channel_id=1, source_target_pairs={{0,64},{64,128},{128,192},{192,256},{256,320},{320,384},{384,448},... | collective-permute-start | bytes 688136 | tf_op jit(solution)/shard_map/ppermute | solution.py:22
  62.8 8.6 %collective-permute-start.7 = (bf16[896,128]{1,0:T(8,128)(2,1)S(1)}, bf16[896,128]{1,0:T(8,128)(2,1)S(1)}, u32[]{:S(2)}, u32[]{:S(2)}) collective-permute-start(bf16[896,128]{1,0:T(8,128)(2,1)S(1)} %add_convert_fusion), channel_id=1, source_target_pairs={{0,452},{64,0},{128,64},{192,128},{256,192},{320,256},{384,320},{4... | collective-permute-start | bytes 688136 | tf_op jit(solution)/shard_map/ppermute | solution.py:22
  64.8 8.2 %collective-permute-start.8 = (bf16[896,128]{1,0:T(8,128)(2,1)S(1)}, bf16[896,128]{1,0:T(8,128)(2,1)}, u32[]{:S(2)}, u32[]{:S(2)}) collective-permute-start(bf16[896,128]{1,0:T(8,128)(2,1)S(1)} %add_convert_fusion.2), channel_id=1, source_target_pairs={{0,64},{64,128},{128,192},{192,256},{256,320},{320,384},{384,448},... | collective-permute-start | bytes 688136 | tf_op jit(solution)/shard_map/ppermute | solution.py:22
  74.3 8.8 %collective-permute-start.9 = (bf16[896,128]{1,0:T(8,128)(2,1)S(1)}, bf16[896,128]{1,0:T(8,128)(2,1)S(1)}, u32[]{:S(2)}, u32[]{:S(2)}) collective-permute-start(bf16[896,128]{1,0:T(8,128)(2,1)S(1)} %pad_maximum_fusion.3.refs_3_), channel_id=1, source_target_pairs={{0,452},{64,0},{128,64},{192,128},{256,192},{320,256},{384,320},{4... | collective-permute-start | bytes 688136 | tf_op jit(solution)/shard_map/ppermute | solution.py:22
  78.4 7.9 %collective-permute-start.13 = (bf16[896,128]{1,0:T(8,128)(2,1)S(1)}, bf16[896,128]{1,0:T(8,128)(2,1)S(1)}, u32[]{:S(2)}, u32[]{:S(2)}) collective-permute-start(bf16[896,128]{1,0:T(8,128)(2,1)S(1)} %pad_maximum_fusion.3.refs_3_), channel_id=1, source_target_pairs={{0,64},{64,128},{128,192},{192,256},{256,320},{320,384},{384,448},... | collective-permute-start | bytes 688136 | tf_op jit(solution)/shard_map/ppermute | solution.py:22
  83.0 9.6 %collective-permute-start.10 = (bf16[896,128]{1,0:T(8,128)(2,1)S(1)}, bf16[896,128]{1,0:T(8,128)(2,1)S(1)}, u32[]{:S(2)}, u32[]{:S(2)}) collective-permute-start(bf16[896,128]{1,0:T(8,128)(2,1)S(1)} %collective-permute-done.9.refs_4_), channel_id=1, source_target_pairs={{0,452},{64,0},{128,64},{192,128},{256,192},{320,256},{384,320},{4... | collective-permute-start | bytes 688136 | tf_op jit(solution)/shard_map/ppermute | solution.py:22
  86.4 8.2 %collective-permute-start.14 = (bf16[896,128]{1,0:T(8,128)(2,1)S(1)}, bf16[896,128]{1,0:T(8,128)(2,1)S(1)}, u32[]{:S(2)}, u32[]{:S(2)}) collective-permute-start(bf16[896,128]{1,0:T(8,128)(2,1)S(1)} %collective-permute-done.13.refs_2_), channel_id=1, source_target_pairs={{0,64},{64,128},{128,192},{192,256},{256,320},{320,384},{384,448},... | collective-permute-start | bytes 688136 | tf_op jit(solution)/shard_map/ppermute | solution.py:22
  92.6 9.8 %collective-permute-start.11 = (bf16[896,128]{1,0:T(8,128)(2,1)S(1)}, bf16[896,128]{1,0:T(8,128)(2,1)}, u32[]{:S(2)}, u32[]{:S(2)}) collective-permute-start(bf16[896,128]{1,0:T(8,128)(2,1)S(1)} %collective-permute-done.10.refs_5_), channel_id=1, source_target_pairs={{0,452},{64,0},{128,64},{192,128},{256,192},{320,256},{384,320},{4... | collective-permute-start | bytes 688136 | tf_op jit(solution)/shard_map/ppermute | solution.py:22
  94.5 9.8 %collective-permute-start.15 = (bf16[896,128]{1,0:T(8,128)(2,1)S(1)}, bf16[896,128]{1,0:T(8,128)(2,1)}, u32[]{:S(2)}, u32[]{:S(2)}) collective-permute-start(bf16[896,128]{1,0:T(8,128)(2,1)S(1)} %collective-permute-done.14.refs_1_), channel_id=1, source_target_pairs={{0,64},{64,128},{128,192},{192,256},{256,320},{320,384},{384,448},... | collective-permute-start | bytes 688136 | tf_op jit(solution)/shard_map/ppermute | solution.py:22
  102.4 9.5 %collective-permute-start.12 = (bf16[896,128]{1,0:T(8,128)(2,1)}, bf16[896,128]{1,0:T(8,128)(2,1)S(1)}, u32[]{:S(2)}, u32[]{:S(2)}) collective-permute-start(bf16[896,128]{1,0:T(8,128)(2,1)} %collective-permute-done.11.refs_6_), channel_id=1, source_target_pairs={{0,452},{64,0},{128,64},{192,128},{256,192},{320,256},{384,320},{4... | collective-permute-start | bytes 688136 | tf_op jit(solution)/shard_map/ppermute | solution.py:22
  112.3 0.8 copy-start
  114.3 5.5 %copy-start.1 = (bf16[448,512]{1,0:T(8,128)(2,1)S(1)}, bf16[448,512]{1,0:T(8,128)(2,1)}, u32[]{:S(2)}) copy-start(bf16[448,512]{1,0:T(8,128)(2,1)} %copy-done) | copy-start | bytes 1376260
  114.3 18.9 %all-to-all-start.2 = ((bf16[16,64,512]{2,1,0:T(8,128)(2,1)}), bf16[16,64,512]{2,1,0:T(8,128)(2,1)S(1)}, u32[]{:S(2)}, u32[]{:S(2)}) async-start(bf16[16,64,512]{2,1,0:T(8,128)(2,1)} %bitcast.5), calls=%async_computation.2 | async-start | bytes 2097152 | tf_op jit(solution)/shard_map/all_to_all | solution.py:276
  119.8 53.1 %collective-permute-start.18 = (bf16[448,512]{1,0:T(8,128)(2,1)S(1)}, bf16[448,512]{1,0:T(8,128)(2,1)}, u32[]{:S(2)}, u32[]{:S(2)}) collective-permute-start(bf16[448,512]{1,0:T(8,128)(2,1)S(1)} %copy-done.1), channel_id=1, source_target_pairs={{0,4},{4,0},{1,5},{5,1},{2,6},{6,2},{3,7},{7,3},{8,12},{12,8},{9,1... | collective-permute-start | bytes 1376264 | tf_op jit(solution)/shard_map/ppermute | solution.py:274
  133.4 3.1 %collective-permute-start.16 = (bf16[32,512]{1,0:T(8,128)(2,1)S(1)}, bf16[32,512]{1,0:T(8,128)(2,1)S(1)}, u32[]{:S(2)}, u32[]{:S(2)}) collective-permute-start(bf16[32,512]{1,0:T(8,128)(2,1)S(1)} %get-tuple-element.48), channel_id=1, source_target_pairs={{0,8},{8,0},{1,9},{9,1},{2,10},{10,2},{3,11},{11,3},{4,12},{12,4},... | collective-permute-start | bytes 98312 | tf_op jit(solution)/shard_map/ppermute | solution.py:62
  137.3 9.3 %all-to-all-start.3 = ((bf16[128,2,1,224]{3,1,2,0:T(2,128)(2,1)}), bf16[128,2,1,224]{3,1,2,0:T(2,128)(2,1)S(1)}, u32[]{:S(2)}, u32[]{:S(2)}) async-start(bf16[128,2,1,224]{3,1,2,0:T(2,128)(2,1)} %copy.20), calls=%async_computation.3 | async-start | bytes 262144 | tf_op jit(solution)/shard_map/all_to_all | solution.py:282
  140.6 32.3 %collective-permute-start.17 = (bf16[32,512]{1,0:T(8,128)(2,1)S(1)}, bf16[32,512]{1,0:T(8,128)(2,1)S(1)}, u32[]{:S(2)}, u32[]{:S(2)}) collective-permute-start(bf16[32,512]{1,0:T(8,128)(2,1)S(1)} %add_convert_fusion.5), channel_id=1, source_target_pairs={{0,44},{16,52},{32,60},{48,0},{8,8},{24,16},{40,24},{56,32},{64,11... | collective-permute-start | bytes 98312 | tf_op jit(solution)/shard_map/ppermute | solution.py:285

commit v12 on v11

--- a/solution.py
+++ b/solution.py
@@ -182,7 +182,7 @@
         out_shape=jax.ShapeDtypeStruct(terms.shape, terms.dtype),
         input_output_aliases={2: 0},
         scratch_shapes=[pltpu.VMEM((128, terms.shape[1]), jnp.bfloat16), pltpu.SemaphoreType.DMA((4,))],
-        compiler_params=PARAMS,
+        compiler_params=pltpu.CompilerParams(vmem_limit_bytes=6 << 20),
     )(weights, tile, terms)
 
 
@@ -193,6 +193,38 @@
     keep_ref[...] = total_ref[pl.ds(pl.multiple_of(core * rows, rows), rows), :]
     send = total_ref[pl.ds(pl.multiple_of((1 - core) * rows, rows), rows), :]
     send_ref[...] = send.astype(jnp.bfloat16)
+
+
+def finish_kernel(keep_ref, received_ref, gate_ref, up_ref):
+    rows = gate_ref.shape[0]
+    gate_ref[...] = keep_ref[:rows, :] + received_ref[:rows, :].astype(jnp.float32)
+    up_ref[...] = keep_ref[rows:, :] + received_ref[rows:, :].astype(jnp.float32)
+
+
+def finish(keep, received):
+    shape = jax.ShapeDtypeStruct((keep.shape[0] // 2, keep.shape[1]), jnp.float32)
+    return pl.pallas_call(
+        finish_kernel,
+        in_specs=[VMEM_SPEC] * 2,
+        out_specs=[VMEM_SPEC] * 2,
+        out_shape=[shape, shape],
+        compiler_params=PARAMS,
+    )(keep, received)
+
+
+def copy_kernel(in_ref, out_ref):
+    out_ref[...] = in_ref[...]
+
+
+def copied(value, flops):
+    return pl.pallas_call(
+        copy_kernel,
+        in_specs=[VMEM_SPEC],
+        out_specs=VMEM_SPEC,
+        out_shape=jax.ShapeDtypeStruct(value.shape, value.dtype),
+        compiler_params=PARAMS,
+        cost_estimate=pl.CostEstimate(flops=flops, bytes_accessed=1, transcendentals=0),
+    )(value)
 
 
 def sum_parts(core, parts):
@@ -283,9 +315,11 @@
         hidden.T.reshape(-1, 2, 1, part), "x", split_axis=0, concat_axis=2, tiled=True
     )
     grad_tokens = lax.ppermute(grad_tokens, ("r", "y", "c", "h"), result_pairs())
+    grad_tokens = copied(grad_tokens, 1_000_000_000)
+    hidden = hidden.reshape(-1, hidden_cols)
     grad_tokens, hidden, keep = lax.optimization_barrier((grad_tokens, hidden, keep))
-    grad_weights = keep + received.astype(jnp.float32)
-    return hidden.reshape(-1, hidden_cols), grad_tokens, grad_weights[:part].T, grad_weights[part:].T
+    gate_grad, up_grad = finish(keep, received)
+    return hidden, grad_tokens, gate_grad.T, up_grad.T
 
 
 def solution(mesh):

time: 178 us -> 176 us (0.989)
  local copies, waits for them, and re-layouts: 8.89 us -> 6.54 us
    all_to_all x1, waiting for transfers between devices: 4.01 us -> 0.01 us  [local(): lax.all_to_all(hidden.T.reshape(-1, 2, 1, part), 'x', split_axis=0, conca...]
    ppermute x1, waiting for transfers between devices: 26.3 us -> 30.3 us  [local(): lax.ppermute(grad_tokens, ('r', 'y', 'c', 'h'), result_pairs())]
  transfers between devices with their start and end apart: 23 -> 23, of which waited for: 16 -> 15; matrix products, arithmetic and copies ran while one was open for 3% -> 4% of each run, Pallas kernels for 3% -> 4%
where the time goes in v12:
time: 176 us; the launch traced here: 175 us
  starting transfers between devices  87.9 us (50%)
  waiting for transfers between devices  67.5 us (38%)
  Pallas kernels  9.82 us (6%)
  local copies, waits for them, and re-layouts  6.54 us (4%)
  other arithmetic  1.95 us (1%)
    ppermute x14, starting transfers between devices, ring_shift(): return lax.ppermute(value, ('r', 'h'), pairs)  48.2 us
    ppermute x1, waiting for transfers between devices, local(): lax.ppermute(grad_tokens, ('r', 'y', 'c', 'h'), result_pairs())  30.3 us
    ppermute x14, waiting for transfers between devices, ring_shift(): return lax.ppermute(value, ('r', 'h'), pairs)  18.5 us
    ppermute x1, starting transfers between devices, local(): received = lax.ppermute(send, 'h', [(0, 1), (1, 0)])  9.56 us
    all_to_all x1, waiting for transfers between devices, local(): lax.all_to_all(copies, ('y', 'x'), split_axis=0, concat_axis=0, tiled=True)  8.34 us
    ppermute x1, starting transfers between devices, local(): piece = lax.ppermute(tokens, ('r', 'y', 'c', 'h'), token_pairs())  7.74 us
    all_to_all x1, starting transfers between devices, local(): lax.all_to_all(terms.reshape(16, -1, features), ('y', 'x'), split_axis=0,...  5.51 us
    pallas_call x1, Pallas kernels, near_products(): pl.pallas_call(near_kernel, in_specs=[SMEM_SPEC] + [VMEM_SPEC] * 10, out_...  4.76 us
  transfers between devices with their start and end apart: 23, of which 15 were waited for; matrix products, arithmetic and copies ran while one was open for 4% of the time, Pallas kernels for 4%

profile of v12, /device:TPU:160, one launch (start us, length us, event | category | flops | bytes accessed | tf_op | source)
XLA Modules:
  0.0 174.7 jit_solution(7236237912799819839)
XLA Ops:
  0.6 7.7 %collective-permute-start = (bf16[32,512]{1,0:T(8,128)(2,1)}, bf16[32,512]{1,0:T(8,128)(2,1)S(1)}, u32[]{:S(2)}, u32[]{:S(2)}) collective-permute-start(bf16[32,512]{1,0:T(8,128)(2,1)} %param.4), channel_id=1, source_target_pairs={{324,0},{388,16},{452,32},{0,48},{64,8},{128,24},{192,40},{256,56}... | collective-permute-start | bytes 98312 | tf_op jit(solution)/shard_map/ppermute | solution.py:261
  8.4 3.5 %collective-permute-done = bf16[32,512]{1,0:T(8,128)(2,1)S(1)} collective-permute-done((bf16[32,512]{1,0:T(8,128)(2,1)}, bf16[32,512]{1,0:T(8,128)(2,1)S(1)}, u32[]{:S(2)}, u32[]{:S(2)}) %collective-permute-start) | collective-permute-done | bytes 32800 | tf_op jit(solution)/shard_map/ppermute | solution.py:261
  11.8 0.8 broadcast_in_dim.2
  12.7 4.4 %all-to-all-start = ((bf16[16,32,512]{2,1,0:T(8,128)(2,1)}), bf16[16,32,512]{2,1,0:T(8,128)(2,1)S(1)}, u32[]{:S(2)}, u32[]{:S(2)}) async-start(bf16[16,32,512]{2,1,0:T(8,128)(2,1)} %broadcast_in_dim.2), calls=%async_computation | async-start | bytes 1048576 | tf_op jit(solution)/shard_map/all_to_all | solution.py:263
  17.1 1.1 reshape.36
  18.2 0.8 copy.24
  19.0 1.8 %constant_dynamic-slice_fusion.2 = (bf16[512,224]{1,0:T(8,128)(2,1)S(1)}, bf16[512,224]{1,0:T(8,128)(2,1)S(1)}, bf16[512,224]{1,0:T(8,128)(2,1)S(1)}, bf16[512,224]{1,0:T(8,128)(2,1)S(1)}) fusion(bf16[512,1792]{1,0:T(8,128)(2,1)} %param.6, s32[]{:T(128)S(6)} %select_n.8, s32[]{:T(128)S(6)} %select_n.9, bf16[512,1792]{1,0:T(8,128)(2,1)} %param.5), kind=kLoop, calls=%fused_computation.23 | loop fusion | bytes 1835016 | tf_op jit(solution)/shard_map/dynamic_slice | solution.py:255
  20.8 0.4 pad_maximum_fusion.weights_ref
  21.2 8.3 %all-to-all-done = bf16[16,32,512]{2,1,0:T(8,128)(2,1)S(1)} async-done(((bf16[16,32,512]{2,1,0:T(8,128)(2,1)}), bf16[16,32,512]{2,1,0:T(8,128)(2,1)S(1)}, u32[]{:S(2)}, u32[]{:S(2)}) %all-to-all-start) | async-done | bytes 524320 | tf_op jit(solution)/shard_map/all_to_all | solution.py:263
  29.5 1.9 %collective-permute-start.1 = (bf16[512,512]{1,0:T(8,128)(2,1)S(1)}, bf16[512,512]{1,0:T(8,128)(2,1)S(1)}, u32[]{:S(2)}, u32[]{:S(2)}) collective-permute-start(bf16[512,512]{1,0:T(8,128)(2,1)S(1)} %bitcast.28), channel_id=1, source_target_pairs={{0,8},{8,0},{1,9},{9,1},{2,10},{10,2},{3,11},{11,3},{4,12},{12,4},... | collective-permute-start | bytes 1572872 | tf_op jit(solution)/shard_map/ppermute | solution.py:62
  31.5 1.9 %collective-permute-done.1.other_ref = bf16[512,512]{1,0:T(8,128)(2,1)S(1)} collective-permute-done((bf16[512,512]{1,0:T(8,128)(2,1)S(1)}, bf16[512,512]{1,0:T(8,128)(2,1)S(1)}, u32[]{:S(2)}, u32[]{:S(2)}) %collective-permute-start.1) | collective-permute-done | bytes 524320 | tf_op jit(solution)/shard_map/ppermute | solution.py:62
  33.3 0.6 shard_map.75
  33.9 3.7 %collective-permute-start.2 = (bf16[896,128]{1,0:T(8,128)(2,1)S(1)}, bf16[896,128]{1,0:T(8,128)(2,1)S(1)}, u32[]{:S(2)}, u32[]{:S(2)}) collective-permute-start(bf16[896,128]{1,0:T(8,128)(2,1)S(1)} %get-tuple-element.34), channel_id=1, source_target_pairs={{0,64},{64,128},{128,192},{192,256},{256,320},{320,384},{384,448},... | collective-permute-start | bytes 688136 | tf_op jit(solution)/shard_map/ppermute | solution.py:22
  37.6 3.3 %all-to-all-start.1 = ((bf16[4,32,2,224]{3,2,1,0:T(2,128)(2,1)}), bf16[4,32,2,224]{3,2,1,0:T(2,128)(2,1)S(1)}, u32[]{:S(2)}, u32[]{:S(2)}) async-start(bf16[4,32,2,224]{3,2,1,0:T(2,128)(2,1)} %bitcast.27), calls=%async_computation.1 | async-start | bytes 262144 | tf_op jit(solution)/shard_map/all_to_all | solution.py:268
  41.0 2.1 %collective-permute-start.5 = (bf16[896,128]{1,0:T(8,128)(2,1)S(1)}, bf16[896,128]{1,0:T(8,128)(2,1)S(1)}, u32[]{:S(2)}, u32[]{:S(2)}) collective-permute-start(bf16[896,128]{1,0:T(8,128)(2,1)S(1)} %get-tuple-element.41), channel_id=1, source_target_pairs={{0,452},{64,0},{128,64},{192,128},{256,192},{320,256},{384,320},{4... | collective-permute-start | bytes 688136 | tf_op jit(solution)/shard_map/ppermute | solution.py:22
  43.1 1.1 shard_map.76
  44.2 0.1 add_convert_fusion.4
  44.3 3.7 %collective-permute-start.3 = (bf16[896,128]{1,0:T(8,128)(2,1)S(1)}, bf16[896,128]{1,0:T(8,128)(2,1)S(1)}, u32[]{:S(2)}, u32[]{:S(2)}) collective-permute-start(bf16[896,128]{1,0:T(8,128)(2,1)S(1)} %add_convert_fusion.4), channel_id=1, source_target_pairs={{0,64},{64,128},{128,192},{192,256},{256,320},{320,384},{384,448},... | collective-permute-start | bytes 688136 | tf_op jit(solution)/shard_map/ppermute | solution.py:22
  48.1 2.5 %collective-permute-done.5 = bf16[896,128]{1,0:T(8,128)(2,1)S(1)} collective-permute-done((bf16[896,128]{1,0:T(8,128)(2,1)S(1)}, bf16[896,128]{1,0:T(8,128)(2,1)S(1)}, u32[]{:S(2)}, u32[]{:S(2)}) %collective-permute-start.5) | collective-permute-done | bytes 229408 | tf_op jit(solution)/shard_map/ppermute | solution.py:22
  50.5 0.1 add_convert_fusion.1
  50.6 2.1 %collective-permute-start.6 = (bf16[896,128]{1,0:T(8,128)(2,1)S(1)}, bf16[896,128]{1,0:T(8,128)(2,1)S(1)}, u32[]{:S(2)}, u32[]{:S(2)}) collective-permute-start(bf16[896,128]{1,0:T(8,128)(2,1)S(1)} %add_convert_fusion.1), channel_id=1, source_target_pairs={{0,452},{64,0},{128,64},{192,128},{256,192},{320,256},{384,320},{4... | collective-permute-start | bytes 688136 | tf_op jit(solution)/shard_map/ppermute | solution.py:22
  52.7 0.9 collective-permute-done.3
  53.6 0.1 add_convert_fusion.3
  53.7 6.4 %collective-permute-start.4 = (bf16[896,128]{1,0:T(8,128)(2,1)S(1)}, bf16[896,128]{1,0:T(8,128)(2,1)S(1)}, u32[]{:S(2)}, u32[]{:S(2)}) collective-permute-start(bf16[896,128]{1,0:T(8,128)(2,1)S(1)} %add_convert_fusion.3), channel_id=1, source_target_pairs={{0,64},{64,128},{128,192},{192,256},{256,320},{320,384},{384,448},... | collective-permute-start | bytes 688136 | tf_op jit(solution)/shard_map/ppermute | solution.py:22
  60.0 2.7 %collective-permute-done.6 = bf16[896,128]{1,0:T(8,128)(2,1)S(1)} collective-permute-done((bf16[896,128]{1,0:T(8,128)(2,1)S(1)}, bf16[896,128]{1,0:T(8,128)(2,1)S(1)}, u32[]{:S(2)}, u32[]{:S(2)}) %collective-permute-start.6) | collective-permute-done | bytes 229408 | tf_op jit(solution)/shard_map/ppermute | solution.py:22
  62.7 0.1 add_convert_fusion
  62.8 1.9 %collective-permute-start.7 = (bf16[896,128]{1,0:T(8,128)(2,1)S(1)}, bf16[896,128]{1,0:T(8,128)(2,1)S(1)}, u32[]{:S(2)}, u32[]{:S(2)}) collective-permute-start(bf16[896,128]{1,0:T(8,128)(2,1)S(1)} %add_convert_fusion), channel_id=1, source_target_pairs={{0,452},{64,0},{128,64},{192,128},{256,192},{320,256},{384,320},{4... | collective-permute-start | bytes 688136 | tf_op jit(solution)/shard_map/ppermute | solution.py:22
  64.7 0.1 add_convert_fusion.2
  64.8 4.5 %collective-permute-start.8 = (bf16[896,128]{1,0:T(8,128)(2,1)S(1)}, bf16[896,128]{1,0:T(8,128)(2,1)}, u32[]{:S(2)}, u32[]{:S(2)}) collective-permute-start(bf16[896,128]{1,0:T(8,128)(2,1)S(1)} %add_convert_fusion.2), channel_id=1, source_target_pairs={{0,64},{64,128},{128,192},{192,256},{256,320},{320,384},{384,448},... | collective-permute-start | bytes 688136 | tf_op jit(solution)/shard_map/ppermute | solution.py:22
  69.3 0.1 reshape.41
  69.4 0.1 copy.19
  69.6 1.8 %collective-permute-done.7 = bf16[896,128]{1,0:T(8,128)(2,1)S(1)} collective-permute-done((bf16[896,128]{1,0:T(8,128)(2,1)S(1)}, bf16[896,128]{1,0:T(8,128)(2,1)S(1)}, u32[]{:S(2)}, u32[]{:S(2)}) %collective-permute-start.7) | collective-permute-done | bytes 229408 | tf_op jit(solution)/shard_map/ppermute | solution.py:22
  71.4 1.6 collective-permute-done.8
  73.0 1.0 convert_add_fusion
  74.0 0.2 multiply_convert_fusion
  74.3 4.2 %collective-permute-start.9 = (bf16[896,128]{1,0:T(8,128)(2,1)S(1)}, bf16[896,128]{1,0:T(8,128)(2,1)S(1)}, u32[]{:S(2)}, u32[]{:S(2)}) collective-permute-start(bf16[896,128]{1,0:T(8,128)(2,1)S(1)} %pad_maximum_fusion.3.refs_3_), channel_id=1, source_target_pairs={{0,452},{64,0},{128,64},{192,128},{256,192},{320,256},{384,320},{4... | collective-permute-start | bytes 688136 | tf_op jit(solution)/shard_map/ppermute | solution.py:22
  78.4 2.5 %collective-permute-start.13 = (bf16[896,128]{1,0:T(8,128)(2,1)S(1)}, bf16[896,128]{1,0:T(8,128)(2,1)S(1)}, u32[]{:S(2)}, u32[]{:S(2)}) collective-permute-start(bf16[896,128]{1,0:T(8,128)(2,1)S(1)} %pad_maximum_fusion.3.refs_3_), channel_id=1, source_target_pairs={{0,64},{64,128},{128,192},{192,256},{256,320},{320,384},{384,448},... | collective-permute-start | bytes 688136 | tf_op jit(solution)/shard_map/ppermute | solution.py:22
  81.0 2.1 %collective-permute-done.9.refs_4_ = bf16[896,128]{1,0:T(8,128)(2,1)S(1)} collective-permute-done((bf16[896,128]{1,0:T(8,128)(2,1)S(1)}, bf16[896,128]{1,0:T(8,128)(2,1)S(1)}, u32[]{:S(2)}, u32[]{:S(2)}) %collective-permute-start.9) | collective-permute-done | bytes 229408 | tf_op jit(solution)/shard_map/ppermute | solution.py:22
  83.0 3.3 %collective-permute-start.10 = (bf16[896,128]{1,0:T(8,128)(2,1)S(1)}, bf16[896,128]{1,0:T(8,128)(2,1)S(1)}, u32[]{:S(2)}, u32[]{:S(2)}) collective-permute-start(bf16[896,128]{1,0:T(8,128)(2,1)S(1)} %collective-permute-done.9.refs_4_), channel_id=1, source_target_pairs={{0,452},{64,0},{128,64},{192,128},{256,192},{320,256},{384,320},{4... | collective-permute-start | bytes 688136 | tf_op jit(solution)/shard_map/ppermute | solution.py:22
  86.3 0.0 collective-permute-done.13.refs_2_
  86.4 4.2 %collective-permute-start.14 = (bf16[896,128]{1,0:T(8,128)(2,1)S(1)}, bf16[896,128]{1,0:T(8,128)(2,1)S(1)}, u32[]{:S(2)}, u32[]{:S(2)}) collective-permute-start(bf16[896,128]{1,0:T(8,128)(2,1)S(1)} %collective-permute-done.13.refs_2_), channel_id=1, source_target_pairs={{0,64},{64,128},{128,192},{192,256},{256,320},{320,384},{384,448},... | collective-permute-start | bytes 688136 | tf_op jit(solution)/shard_map/ppermute | solution.py:22
  90.6 2.0 %collective-permute-done.10.refs_5_ = bf16[896,128]{1,0:T(8,128)(2,1)S(1)} collective-permute-done((bf16[896,128]{1,0:T(8,128)(2,1)S(1)}, bf16[896,128]{1,0:T(8,128)(2,1)S(1)}, u32[]{:S(2)}, u32[]{:S(2)}) %collective-permute-start.10) | collective-permute-done | bytes 229408 | tf_op jit(solution)/shard_map/ppermute | solution.py:22
  92.6 1.9 %collective-permute-start.11 = (bf16[896,128]{1,0:T(8,128)(2,1)S(1)}, bf16[896,128]{1,0:T(8,128)(2,1)}, u32[]{:S(2)}, u32[]{:S(2)}) collective-permute-start(bf16[896,128]{1,0:T(8,128)(2,1)S(1)} %collective-permute-done.10.refs_5_), channel_id=1, source_target_pairs={{0,452},{64,0},{128,64},{192,128},{256,192},{320,256},{384,320},{4... | collective-permute-start | bytes 688136 | tf_op jit(solution)/shard_map/ppermute | solution.py:22
  94.5 5.7 %collective-permute-start.15 = (bf16[896,128]{1,0:T(8,128)(2,1)S(1)}, bf16[896,128]{1,0:T(8,128)(2,1)}, u32[]{:S(2)}, u32[]{:S(2)}) collective-permute-start(bf16[896,128]{1,0:T(8,128)(2,1)S(1)} %collective-permute-done.14.refs_1_), channel_id=1, source_target_pairs={{0,64},{64,128},{128,192},{192,256},{256,320},{320,384},{384,448},... | collective-permute-start | bytes 688136 | tf_op jit(solution)/shard_map/ppermute | solution.py:22
  100.2 2.1 %collective-permute-done.11.refs_6_ = bf16[896,128]{1,0:T(8,128)(2,1)} collective-permute-done((bf16[896,128]{1,0:T(8,128)(2,1)S(1)}, bf16[896,128]{1,0:T(8,128)(2,1)}, u32[]{:S(2)}, u32[]{:S(2)}) %collective-permute-start.11) | collective-permute-done | bytes 229408 | tf_op jit(solution)/shard_map/ppermute | solution.py:22
  102.4 1.9 %collective-permute-start.12 = (bf16[896,128]{1,0:T(8,128)(2,1)}, bf16[896,128]{1,0:T(8,128)(2,1)S(1)}, u32[]{:S(2)}, u32[]{:S(2)}) collective-permute-start(bf16[896,128]{1,0:T(8,128)(2,1)} %collective-permute-done.11.refs_6_), channel_id=1, source_target_pairs={{0,452},{64,0},{128,64},{192,128},{256,192},{320,256},{384,320},{4... | collective-permute-start | bytes 688136 | tf_op jit(solution)/shard_map/ppermute | solution.py:22
  104.3 4.8 %shard_map.77 = (bf16[1024,512]{1,0:T(8,128)(2,1)}, f32[896,512]{1,0:T(8,128)S(1)}) custom-call(s32[1]{0:T(128)} %bitcast.core_ref, bf16[512,512]{1,0:T(8,128)(2,1)S(1)} %bitcast.31, bf16[512,512]{1,0:T(8,128)(2,1)S(1)} %collective-permute-done.1.other_ref, bf16[512,896]{1,0:T(8,128)(2,1)S(1)} %pad_maximum_fusion.weights_ref, ...), custom_call_target="tpu_custom_call" | custom-call | tf_op jit(solution)/shard_map/pallas_call | solution.py:111
  109.1 2.9 %collective-permute-done.12.tile_ref = bf16[896,128]{1,0:T(8,128)(2,1)S(1)} collective-permute-done((bf16[896,128]{1,0:T(8,128)(2,1)}, bf16[896,128]{1,0:T(8,128)(2,1)S(1)}, u32[]{:S(2)}, u32[]{:S(2)}) %collective-permute-start.12) | collective-permute-done | bytes 229408 | tf_op jit(solution)/shard_map/ppermute | solution.py:22
  111.9 0.4 shard_map.78
  112.4 1.2 shard_map.79
  113.6 5.5 %all-to-all-start.2 = ((bf16[16,64,512]{2,1,0:T(8,128)(2,1)}), bf16[16,64,512]{2,1,0:T(8,128)(2,1)S(1)}, u32[]{:S(2)}, u32[]{:S(2)}) async-start(bf16[16,64,512]{2,1,0:T(8,128)(2,1)} %bitcast.5), calls=%async_computation.2 | async-start | bytes 2097152 | tf_op jit(solution)/shard_map/all_to_all | solution.py:308
  119.1 9.6 %collective-permute-start.18 = (bf16[448,512]{1,0:T(8,128)(2,1)S(1)}, bf16[448,512]{1,0:T(8,128)(2,1)S(1)}, u32[]{:S(2)}, u32[]{:S(2)}) collective-permute-start(bf16[448,512]{1,0:T(8,128)(2,1)S(1)} %copy-done.1), channel_id=1, source_target_pairs={{0,4},{4,0},{1,5},{5,1},{2,6},{6,2},{3,7},{7,3},{8,12},{12,8},{9,1... | collective-permute-start | bytes 1376264 | tf_op jit(solution)/shard_map/ppermute | solution.py:306
  128.7 3.8 %all-to-all-done.2.parts_ref = bf16[16,64,512]{2,1,0:T(8,128)(2,1)S(1)} async-done(((bf16[16,64,512]{2,1,0:T(8,128)(2,1)}), bf16[16,64,512]{2,1,0:T(8,128)(2,1)S(1)}, u32[]{:S(2)}, u32[]{:S(2)}) %all-to-all-start.2) | async-done | bytes 1048608 | tf_op jit(solution)/shard_map/all_to_all | solution.py:308
  132.4 0.2 shard_map.80
  132.6 1.9 %collective-permute-start.16 = (bf16[32,512]{1,0:T(8,128)(2,1)S(1)}, bf16[32,512]{1,0:T(8,128)(2,1)S(1)}, u32[]{:S(2)}, u32[]{:S(2)}) collective-permute-start(bf16[32,512]{1,0:T(8,128)(2,1)S(1)} %get-tuple-element.50), channel_id=1, source_target_pairs={{0,8},{8,0},{1,9},{9,1},{2,10},{10,2},{3,11},{11,3},{4,12},{12,4},... | collective-permute-start | bytes 98312 | tf_op jit(solution)/shard_map/ppermute | solution.py:62
  134.6 1.2 collective-permute-done.16
  135.7 1.9 %collective-permute-start.17 = (bf16[32,512]{1,0:T(8,128)(2,1)S(1)}, bf16[32,512]{1,0:T(8,128)(2,1)S(1)}, u32[]{:S(2)}, u32[]{:S(2)}) collective-permute-start(bf16[32,512]{1,0:T(8,128)(2,1)S(1)} %add_convert_fusion.5), channel_id=1, source_target_pairs={{0,44},{16,52},{32,60},{48,0},{8,8},{24,16},{40,24},{56,32},{64,11... | collective-permute-start | bytes 98312 | tf_op jit(solution)/shard_map/ppermute | solution.py:317
  137.7 0.8 copy.20
  138.5 3.3 %all-to-all-start.3 = ((bf16[128,2,1,224]{3,1,2,0:T(2,128)(2,1)}), bf16[128,2,1,224]{3,1,2,0:T(2,128)(2,1)S(1)}, u32[]{:S(2)}, u32[]{:S(2)}) async-start(bf16[128,2,1,224]{3,1,2,0:T(2,128)(2,1)} %copy.20), calls=%async_computation.3 | async-start | bytes 262144 | tf_op jit(solution)/shard_map/all_to_all | solution.py:314
  141.8 30.3 %collective-permute-done.17.in_ref = bf16[32,512]{1,0:T(8,128)(2,1)S(1)} collective-permute-done((bf16[32,512]{1,0:T(8,128)(2,1)S(1)}, bf16[32,512]{1,0:T(8,128)(2,1)S(1)}, u32[]{:S(2)}, u32[]{:S(2)}) %collective-permute-start.17) | collective-permute-done | bytes 32800 | tf_op jit(solution)/shard_map/ppermute | solution.py:317
  172.1 0.6 shard_map.81
  172.8 0.1 copy.22
  172.9 0.8 reshape.40
  173.7 1.0 shard_map.82
  (17 shorter events, 0.1 us)
Async XLA Ops:
  0.6 11.2 %collective-permute-start = (bf16[32,512]{1,0:T(8,128)(2,1)}, bf16[32,512]{1,0:T(8,128)(2,1)S(1)}, u32[]{:S(2)}, u32[]{:S(2)}) collective-permute-start(bf16[32,512]{1,0:T(8,128)(2,1)} %param.4), channel_id=1, source_target_pairs={{324,0},{388,16},{452,32},{0,48},{64,8},{128,24},{192,40},{256,56}... | collective-permute-start | bytes 98312 | tf_op jit(solution)/shard_map/ppermute | solution.py:261
  12.7 16.9 %all-to-all-start = ((bf16[16,32,512]{2,1,0:T(8,128)(2,1)}), bf16[16,32,512]{2,1,0:T(8,128)(2,1)S(1)}, u32[]{:S(2)}, u32[]{:S(2)}) async-start(bf16[16,32,512]{2,1,0:T(8,128)(2,1)} %broadcast_in_dim.2), calls=%async_computation | async-start | bytes 1048576 | tf_op jit(solution)/shard_map/all_to_all | solution.py:263
  29.5 3.8 %collective-permute-start.1 = (bf16[512,512]{1,0:T(8,128)(2,1)S(1)}, bf16[512,512]{1,0:T(8,128)(2,1)S(1)}, u32[]{:S(2)}, u32[]{:S(2)}) collective-permute-start(bf16[512,512]{1,0:T(8,128)(2,1)S(1)} %bitcast.28), channel_id=1, source_target_pairs={{0,8},{8,0},{1,9},{9,1},{2,10},{10,2},{3,11},{11,3},{4,12},{12,4},... | collective-permute-start | bytes 1572872 | tf_op jit(solution)/shard_map/ppermute | solution.py:62
  33.9 10.3 %collective-permute-start.2 = (bf16[896,128]{1,0:T(8,128)(2,1)S(1)}, bf16[896,128]{1,0:T(8,128)(2,1)S(1)}, u32[]{:S(2)}, u32[]{:S(2)}) collective-permute-start(bf16[896,128]{1,0:T(8,128)(2,1)S(1)} %get-tuple-element.34), channel_id=1, source_target_pairs={{0,64},{64,128},{128,192},{192,256},{256,320},{320,384},{384,448},... | collective-permute-start | bytes 688136 | tf_op jit(solution)/shard_map/ppermute | solution.py:22
  37.6 27.1 %all-to-all-start.1 = ((bf16[4,32,2,224]{3,2,1,0:T(2,128)(2,1)}), bf16[4,32,2,224]{3,2,1,0:T(2,128)(2,1)S(1)}, u32[]{:S(2)}, u32[]{:S(2)}) async-start(bf16[4,32,2,224]{3,2,1,0:T(2,128)(2,1)} %bitcast.27), calls=%async_computation.1 | async-start | bytes 262144 | tf_op jit(solution)/shard_map/all_to_all | solution.py:268
  41.0 9.6 %collective-permute-start.5 = (bf16[896,128]{1,0:T(8,128)(2,1)S(1)}, bf16[896,128]{1,0:T(8,128)(2,1)S(1)}, u32[]{:S(2)}, u32[]{:S(2)}) collective-permute-start(bf16[896,128]{1,0:T(8,128)(2,1)S(1)} %get-tuple-element.41), channel_id=1, source_target_pairs={{0,452},{64,0},{128,64},{192,128},{256,192},{320,256},{384,320},{4... | collective-permute-start | bytes 688136 | tf_op jit(solution)/shard_map/ppermute | solution.py:22
  44.3 9.3 %collective-permute-start.3 = (bf16[896,128]{1,0:T(8,128)(2,1)S(1)}, bf16[896,128]{1,0:T(8,128)(2,1)S(1)}, u32[]{:S(2)}, u32[]{:S(2)}) collective-permute-start(bf16[896,128]{1,0:T(8,128)(2,1)S(1)} %add_convert_fusion.4), channel_id=1, source_target_pairs={{0,64},{64,128},{128,192},{192,256},{256,320},{320,384},{384,448},... | collective-permute-start | bytes 688136 | tf_op jit(solution)/shard_map/ppermute | solution.py:22
  50.6 12.1 %collective-permute-start.6 = (bf16[896,128]{1,0:T(8,128)(2,1)S(1)}, bf16[896,128]{1,0:T(8,128)(2,1)S(1)}, u32[]{:S(2)}, u32[]{:S(2)}) collective-permute-start(bf16[896,128]{1,0:T(8,128)(2,1)S(1)} %add_convert_fusion.1), channel_id=1, source_target_pairs={{0,452},{64,0},{128,64},{192,128},{256,192},{320,256},{384,320},{4... | collective-permute-start | bytes 688136 | tf_op jit(solution)/shard_map/ppermute | solution.py:22
  53.7 11.0 %collective-permute-start.4 = (bf16[896,128]{1,0:T(8,128)(2,1)S(1)}, bf16[896,128]{1,0:T(8,128)(2,1)S(1)}, u32[]{:S(2)}, u32[]{:S(2)}) collective-permute-start(bf16[896,128]{1,0:T(8,128)(2,1)S(1)} %add_convert_fusion.3), channel_id=1, source_target_pairs={{0,64},{64,128},{128,192},{192,256},{256,320},{320,384},{384,448},... | collective-permute-start | bytes 688136 | tf_op jit(solution)/shard_map/ppermute | solution.py:22
  62.8 8.6 %collective-permute-start.7 = (bf16[896,128]{1,0:T(8,128)(2,1)S(1)}, bf16[896,128]{1,0:T(8,128)(2,1)S(1)}, u32[]{:S(2)}, u32[]{:S(2)}) collective-permute-start(bf16[896,128]{1,0:T(8,128)(2,1)S(1)} %add_convert_fusion), channel_id=1, source_target_pairs={{0,452},{64,0},{128,64},{192,128},{256,192},{320,256},{384,320},{4... | collective-permute-start | bytes 688136 | tf_op jit(solution)/shard_map/ppermute | solution.py:22
  64.8 8.2 %collective-permute-start.8 = (bf16[896,128]{1,0:T(8,128)(2,1)S(1)}, bf16[896,128]{1,0:T(8,128)(2,1)}, u32[]{:S(2)}, u32[]{:S(2)}) collective-permute-start(bf16[896,128]{1,0:T(8,128)(2,1)S(1)} %add_convert_fusion.2), channel_id=1, source_target_pairs={{0,64},{64,128},{128,192},{192,256},{256,320},{320,384},{384,448},... | collective-permute-start | bytes 688136 | tf_op jit(solution)/shard_map/ppermute | solution.py:22
  74.3 8.8 %collective-permute-start.9 = (bf16[896,128]{1,0:T(8,128)(2,1)S(1)}, bf16[896,128]{1,0:T(8,128)(2,1)S(1)}, u32[]{:S(2)}, u32[]{:S(2)}) collective-permute-start(bf16[896,128]{1,0:T(8,128)(2,1)S(1)} %pad_maximum_fusion.3.refs_3_), channel_id=1, source_target_pairs={{0,452},{64,0},{128,64},{192,128},{256,192},{320,256},{384,320},{4... | collective-permute-start | bytes 688136 | tf_op jit(solution)/shard_map/ppermute | solution.py:22
  78.4 7.9 %collective-permute-start.13 = (bf16[896,128]{1,0:T(8,128)(2,1)S(1)}, bf16[896,128]{1,0:T(8,128)(2,1)S(1)}, u32[]{:S(2)}, u32[]{:S(2)}) collective-permute-start(bf16[896,128]{1,0:T(8,128)(2,1)S(1)} %pad_maximum_fusion.3.refs_3_), channel_id=1, source_target_pairs={{0,64},{64,128},{128,192},{192,256},{256,320},{320,384},{384,448},... | collective-permute-start | bytes 688136 | tf_op jit(solution)/shard_map/ppermute | solution.py:22
  83.0 9.6 %collective-permute-start.10 = (bf16[896,128]{1,0:T(8,128)(2,1)S(1)}, bf16[896,128]{1,0:T(8,128)(2,1)S(1)}, u32[]{:S(2)}, u32[]{:S(2)}) collective-permute-start(bf16[896,128]{1,0:T(8,128)(2,1)S(1)} %collective-permute-done.9.refs_4_), channel_id=1, source_target_pairs={{0,452},{64,0},{128,64},{192,128},{256,192},{320,256},{384,320},{4... | collective-permute-start | bytes 688136 | tf_op jit(solution)/shard_map/ppermute | solution.py:22
  86.4 8.2 %collective-permute-start.14 = (bf16[896,128]{1,0:T(8,128)(2,1)S(1)}, bf16[896,128]{1,0:T(8,128)(2,1)S(1)}, u32[]{:S(2)}, u32[]{:S(2)}) collective-permute-start(bf16[896,128]{1,0:T(8,128)(2,1)S(1)} %collective-permute-done.13.refs_2_), channel_id=1, source_target_pairs={{0,64},{64,128},{128,192},{192,256},{256,320},{320,384},{384,448},... | collective-permute-start | bytes 688136 | tf_op jit(solution)/shard_map/ppermute | solution.py:22
  92.6 9.8 %collective-permute-start.11 = (bf16[896,128]{1,0:T(8,128)(2,1)S(1)}, bf16[896,128]{1,0:T(8,128)(2,1)}, u32[]{:S(2)}, u32[]{:S(2)}) collective-permute-start(bf16[896,128]{1,0:T(8,128)(2,1)S(1)} %collective-permute-done.10.refs_5_), channel_id=1, source_target_pairs={{0,452},{64,0},{128,64},{192,128},{256,192},{320,256},{384,320},{4... | collective-permute-start | bytes 688136 | tf_op jit(solution)/shard_map/ppermute | solution.py:22
  94.5 9.8 %collective-permute-start.15 = (bf16[896,128]{1,0:T(8,128)(2,1)S(1)}, bf16[896,128]{1,0:T(8,128)(2,1)}, u32[]{:S(2)}, u32[]{:S(2)}) collective-permute-start(bf16[896,128]{1,0:T(8,128)(2,1)S(1)} %collective-permute-done.14.refs_1_), channel_id=1, source_target_pairs={{0,64},{64,128},{128,192},{192,256},{256,320},{320,384},{384,448},... | collective-permute-start | bytes 688136 | tf_op jit(solution)/shard_map/ppermute | solution.py:22
  102.4 9.5 %collective-permute-start.12 = (bf16[896,128]{1,0:T(8,128)(2,1)}, bf16[896,128]{1,0:T(8,128)(2,1)S(1)}, u32[]{:S(2)}, u32[]{:S(2)}) collective-permute-start(bf16[896,128]{1,0:T(8,128)(2,1)} %collective-permute-done.11.refs_6_), channel_id=1, source_target_pairs={{0,452},{64,0},{128,64},{192,128},{256,192},{320,256},{384,320},{4... | collective-permute-start | bytes 688136 | tf_op jit(solution)/shard_map/ppermute | solution.py:22
  112.3 1.2 copy-start
  113.5 5.5 %copy-start.1 = (bf16[448,512]{1,0:T(8,128)(2,1)S(1)}, bf16[448,512]{1,0:T(8,128)(2,1)}, u32[]{:S(2)}) copy-start(bf16[448,512]{1,0:T(8,128)(2,1)} %copy-done) | copy-start | bytes 1376260
  113.6 18.9 %all-to-all-start.2 = ((bf16[16,64,512]{2,1,0:T(8,128)(2,1)}), bf16[16,64,512]{2,1,0:T(8,128)(2,1)S(1)}, u32[]{:S(2)}, u32[]{:S(2)}) async-start(bf16[16,64,512]{2,1,0:T(8,128)(2,1)} %bitcast.5), calls=%async_computation.2 | async-start | bytes 2097152 | tf_op jit(solution)/shard_map/all_to_all | solution.py:308
  119.1 54.6 %collective-permute-start.18 = (bf16[448,512]{1,0:T(8,128)(2,1)S(1)}, bf16[448,512]{1,0:T(8,128)(2,1)S(1)}, u32[]{:S(2)}, u32[]{:S(2)}) collective-permute-start(bf16[448,512]{1,0:T(8,128)(2,1)S(1)} %copy-done.1), channel_id=1, source_target_pairs={{0,4},{4,0},{1,5},{5,1},{2,6},{6,2},{3,7},{7,3},{8,12},{12,8},{9,1... | collective-permute-start | bytes 1376264 | tf_op jit(solution)/shard_map/ppermute | solution.py:306
  132.6 3.1 %collective-permute-start.16 = (bf16[32,512]{1,0:T(8,128)(2,1)S(1)}, bf16[32,512]{1,0:T(8,128)(2,1)S(1)}, u32[]{:S(2)}, u32[]{:S(2)}) collective-permute-start(bf16[32,512]{1,0:T(8,128)(2,1)S(1)} %get-tuple-element.50), channel_id=1, source_target_pairs={{0,8},{8,0},{1,9},{9,1},{2,10},{10,2},{3,11},{11,3},{4,12},{12,4},... | collective-permute-start | bytes 98312 | tf_op jit(solution)/shard_map/ppermute | solution.py:62
  135.7 36.4 %collective-permute-start.17 = (bf16[32,512]{1,0:T(8,128)(2,1)S(1)}, bf16[32,512]{1,0:T(8,128)(2,1)S(1)}, u32[]{:S(2)}, u32[]{:S(2)}) collective-permute-start(bf16[32,512]{1,0:T(8,128)(2,1)S(1)} %add_convert_fusion.5), channel_id=1, source_target_pairs={{0,44},{16,52},{32,60},{48,0},{8,8},{24,16},{40,24},{56,32},{64,11... | collective-permute-start | bytes 98312 | tf_op jit(solution)/shard_map/ppermute | solution.py:317
  138.5 34.3 %all-to-all-start.3 = ((bf16[128,2,1,224]{3,1,2,0:T(2,128)(2,1)}), bf16[128,2,1,224]{3,1,2,0:T(2,128)(2,1)S(1)}, u32[]{:S(2)}, u32[]{:S(2)}) async-start(bf16[128,2,1,224]{3,1,2,0:T(2,128)(2,1)} %copy.20), calls=%async_computation.3 | async-start | bytes 262144 | tf_op jit(solution)/shard_map/all_to_all | solution.py:314

commit v13 on v12

--- a/solution.py
+++ b/solution.py
@@ -315,10 +315,11 @@
         hidden.T.reshape(-1, 2, 1, part), "x", split_axis=0, concat_axis=2, tiled=True
     )
     grad_tokens = lax.ppermute(grad_tokens, ("r", "y", "c", "h"), result_pairs())
+    hidden = hidden.reshape(-1, hidden_cols)
+    hidden, keep = lax.optimization_barrier((hidden, keep))
+    gate_grad, up_grad = finish(keep, received)
+    grad_tokens, gate_grad = lax.optimization_barrier((grad_tokens, gate_grad))
     grad_tokens = copied(grad_tokens, 1_000_000_000)
-    hidden = hidden.reshape(-1, hidden_cols)
-    grad_tokens, hidden, keep = lax.optimization_barrier((grad_tokens, hidden, keep))
-    gate_grad, up_grad = finish(keep, received)
     return hidden, grad_tokens, gate_grad.T, up_grad.T
 
 

time: 176 us -> 174 us (0.989)
  waiting for transfers between devices: 67.5 us -> 65.5 us
    ppermute x1, waiting for transfers between devices: 30.3 us -> 24.4 us  [local(): lax.ppermute(grad_tokens, ('r', 'y', 'c', 'h'), result_pairs())]
    all_to_all x1, waiting for transfers between devices: 0.01 us -> 4.01 us  [local(): lax.all_to_all(hidden.T.reshape(-1, 2, 1, part), 'x', split_axis=0, conca...]
  transfers between devices with their start and end apart: 23 -> 23, of which waited for: 15 -> 16; matrix products, arithmetic and copies ran while one was open for 4% -> 4% of each run, Pallas kernels for 4% -> 4%
where the time goes in v13:
time: 174 us; the launch traced here: 173 us
  starting transfers between devices  87.9 us (51%)
  waiting for transfers between devices  65.5 us (38%)
  Pallas kernels  9.82 us (6%)
  local copies, waits for them, and re-layouts  6.54 us (4%)
  other arithmetic  1.95 us (1%)
    ppermute x14, starting transfers between devices, ring_shift(): return lax.ppermute(value, ('r', 'h'), pairs)  48.2 us
    ppermute x1, waiting for transfers between devices, local(): lax.ppermute(grad_tokens, ('r', 'y', 'c', 'h'), result_pairs())  24.4 us
    ppermute x14, waiting for transfers between devices, ring_shift(): return lax.ppermute(value, ('r', 'h'), pairs)  18.5 us
    ppermute x1, starting transfers between devices, local(): received = lax.ppermute(send, 'h', [(0, 1), (1, 0)])  9.56 us
    all_to_all x1, waiting for transfers between devices, local(): lax.all_to_all(copies, ('y', 'x'), split_axis=0, concat_axis=0, tiled=True)  8.34 us
    ppermute x1, starting transfers between devices, local(): piece = lax.ppermute(tokens, ('r', 'y', 'c', 'h'), token_pairs())  7.74 us
    all_to_all x1, starting transfers between devices, local(): lax.all_to_all(terms.reshape(16, -1, features), ('y', 'x'), split_axis=0,...  5.51 us
    pallas_call x1, Pallas kernels, near_products(): pl.pallas_call(near_kernel, in_specs=[SMEM_SPEC] + [VMEM_SPEC] * 10, out_...  4.76 us
  transfers between devices with their start and end apart: 23, of which 16 were waited for; matrix products, arithmetic and copies ran while one was open for 4% of the time, Pallas kernels for 4%

profile of v13, /device:TPU:160, one launch (start us, length us, event | category | flops | bytes accessed | tf_op | source)
XLA Modules:
  0.0 172.8 jit_solution(9889130666401741108)
XLA Ops:
  0.6 7.7 %collective-permute-start = (bf16[32,512]{1,0:T(8,128)(2,1)}, bf16[32,512]{1,0:T(8,128)(2,1)S(1)}, u32[]{:S(2)}, u32[]{:S(2)}) collective-permute-start(bf16[32,512]{1,0:T(8,128)(2,1)} %param.4), channel_id=1, source_target_pairs={{324,0},{388,16},{452,32},{0,48},{64,8},{128,24},{192,40},{256,56}... | collective-permute-start | bytes 98312 | tf_op jit(solution)/shard_map/ppermute | solution.py:261
  8.4 3.5 %collective-permute-done = bf16[32,512]{1,0:T(8,128)(2,1)S(1)} collective-permute-done((bf16[32,512]{1,0:T(8,128)(2,1)}, bf16[32,512]{1,0:T(8,128)(2,1)S(1)}, u32[]{:S(2)}, u32[]{:S(2)}) %collective-permute-start) | collective-permute-done | bytes 32800 | tf_op jit(solution)/shard_map/ppermute | solution.py:261
  11.8 0.8 broadcast_in_dim.2
  12.7 4.4 %all-to-all-start = ((bf16[16,32,512]{2,1,0:T(8,128)(2,1)}), bf16[16,32,512]{2,1,0:T(8,128)(2,1)S(1)}, u32[]{:S(2)}, u32[]{:S(2)}) async-start(bf16[16,32,512]{2,1,0:T(8,128)(2,1)} %broadcast_in_dim.2), calls=%async_computation | async-start | bytes 1048576 | tf_op jit(solution)/shard_map/all_to_all | solution.py:263
  17.1 1.1 reshape.36
  18.2 0.8 copy.24
  19.0 1.8 %constant_dynamic-slice_fusion.2 = (bf16[512,224]{1,0:T(8,128)(2,1)S(1)}, bf16[512,224]{1,0:T(8,128)(2,1)S(1)}, bf16[512,224]{1,0:T(8,128)(2,1)S(1)}, bf16[512,224]{1,0:T(8,128)(2,1)S(1)}) fusion(bf16[512,1792]{1,0:T(8,128)(2,1)} %param.6, s32[]{:T(128)S(6)} %select_n.8, s32[]{:T(128)S(6)} %select_n.9, bf16[512,1792]{1,0:T(8,128)(2,1)} %param.5), kind=kLoop, calls=%fused_computation.23 | loop fusion | bytes 1835016 | tf_op jit(solution)/shard_map/dynamic_slice | solution.py:255
  20.8 0.4 pad_maximum_fusion.weights_ref
  21.2 8.3 %all-to-all-done = bf16[16,32,512]{2,1,0:T(8,128)(2,1)S(1)} async-done(((bf16[16,32,512]{2,1,0:T(8,128)(2,1)}), bf16[16,32,512]{2,1,0:T(8,128)(2,1)S(1)}, u32[]{:S(2)}, u32[]{:S(2)}) %all-to-all-start) | async-done | bytes 524320 | tf_op jit(solution)/shard_map/all_to_all | solution.py:263
  29.5 1.9 %collective-permute-start.1 = (bf16[512,512]{1,0:T(8,128)(2,1)S(1)}, bf16[512,512]{1,0:T(8,128)(2,1)S(1)}, u32[]{:S(2)}, u32[]{:S(2)}) collective-permute-start(bf16[512,512]{1,0:T(8,128)(2,1)S(1)} %bitcast.28), channel_id=1, source_target_pairs={{0,8},{8,0},{1,9},{9,1},{2,10},{10,2},{3,11},{11,3},{4,12},{12,4},... | collective-permute-start | bytes 1572872 | tf_op jit(solution)/shard_map/ppermute | solution.py:62
  31.5 1.9 %collective-permute-done.1.other_ref = bf16[512,512]{1,0:T(8,128)(2,1)S(1)} collective-permute-done((bf16[512,512]{1,0:T(8,128)(2,1)S(1)}, bf16[512,512]{1,0:T(8,128)(2,1)S(1)}, u32[]{:S(2)}, u32[]{:S(2)}) %collective-permute-start.1) | collective-permute-done | bytes 524320 | tf_op jit(solution)/shard_map/ppermute | solution.py:62
  33.3 0.6 shard_map.75
  33.9 3.7 %collective-permute-start.2 = (bf16[896,128]{1,0:T(8,128)(2,1)S(1)}, bf16[896,128]{1,0:T(8,128)(2,1)S(1)}, u32[]{:S(2)}, u32[]{:S(2)}) collective-permute-start(bf16[896,128]{1,0:T(8,128)(2,1)S(1)} %get-tuple-element.35), channel_id=1, source_target_pairs={{0,64},{64,128},{128,192},{192,256},{256,320},{320,384},{384,448},... | collective-permute-start | bytes 688136 | tf_op jit(solution)/shard_map/ppermute | solution.py:22
  37.6 3.3 %all-to-all-start.1 = ((bf16[4,32,2,224]{3,2,1,0:T(2,128)(2,1)}), bf16[4,32,2,224]{3,2,1,0:T(2,128)(2,1)S(1)}, u32[]{:S(2)}, u32[]{:S(2)}) async-start(bf16[4,32,2,224]{3,2,1,0:T(2,128)(2,1)} %bitcast.27), calls=%async_computation.1 | async-start | bytes 262144 | tf_op jit(solution)/shard_map/all_to_all | solution.py:268
  41.0 2.1 %collective-permute-start.5 = (bf16[896,128]{1,0:T(8,128)(2,1)S(1)}, bf16[896,128]{1,0:T(8,128)(2,1)S(1)}, u32[]{:S(2)}, u32[]{:S(2)}) collective-permute-start(bf16[896,128]{1,0:T(8,128)(2,1)S(1)} %get-tuple-element.42), channel_id=1, source_target_pairs={{0,452},{64,0},{128,64},{192,128},{256,192},{320,256},{384,320},{4... | collective-permute-start | bytes 688136 | tf_op jit(solution)/shard_map/ppermute | solution.py:22
  43.1 1.1 shard_map.76
  44.2 0.1 add_convert_fusion.4
  44.3 3.7 %collective-permute-start.3 = (bf16[896,128]{1,0:T(8,128)(2,1)S(1)}, bf16[896,128]{1,0:T(8,128)(2,1)S(1)}, u32[]{:S(2)}, u32[]{:S(2)}) collective-permute-start(bf16[896,128]{1,0:T(8,128)(2,1)S(1)} %add_convert_fusion.4), channel_id=1, source_target_pairs={{0,64},{64,128},{128,192},{192,256},{256,320},{320,384},{384,448},... | collective-permute-start | bytes 688136 | tf_op jit(solution)/shard_map/ppermute | solution.py:22
  48.1 2.5 %collective-permute-done.5 = bf16[896,128]{1,0:T(8,128)(2,1)S(1)} collective-permute-done((bf16[896,128]{1,0:T(8,128)(2,1)S(1)}, bf16[896,128]{1,0:T(8,128)(2,1)S(1)}, u32[]{:S(2)}, u32[]{:S(2)}) %collective-permute-start.5) | collective-permute-done | bytes 229408 | tf_op jit(solution)/shard_map/ppermute | solution.py:22
  50.5 0.1 add_convert_fusion.1
  50.6 2.1 %collective-permute-start.6 = (bf16[896,128]{1,0:T(8,128)(2,1)S(1)}, bf16[896,128]{1,0:T(8,128)(2,1)S(1)}, u32[]{:S(2)}, u32[]{:S(2)}) collective-permute-start(bf16[896,128]{1,0:T(8,128)(2,1)S(1)} %add_convert_fusion.1), channel_id=1, source_target_pairs={{0,452},{64,0},{128,64},{192,128},{256,192},{320,256},{384,320},{4... | collective-permute-start | bytes 688136 | tf_op jit(solution)/shard_map/ppermute | solution.py:22
  52.7 0.9 collective-permute-done.3
  53.6 0.1 add_convert_fusion.3
  53.7 6.4 %collective-permute-start.4 = (bf16[896,128]{1,0:T(8,128)(2,1)S(1)}, bf16[896,128]{1,0:T(8,128)(2,1)S(1)}, u32[]{:S(2)}, u32[]{:S(2)}) collective-permute-start(bf16[896,128]{1,0:T(8,128)(2,1)S(1)} %add_convert_fusion.3), channel_id=1, source_target_pairs={{0,64},{64,128},{128,192},{192,256},{256,320},{320,384},{384,448},... | collective-permute-start | bytes 688136 | tf_op jit(solution)/shard_map/ppermute | solution.py:22
  60.0 2.7 %collective-permute-done.6 = bf16[896,128]{1,0:T(8,128)(2,1)S(1)} collective-permute-done((bf16[896,128]{1,0:T(8,128)(2,1)S(1)}, bf16[896,128]{1,0:T(8,128)(2,1)S(1)}, u32[]{:S(2)}, u32[]{:S(2)}) %collective-permute-start.6) | collective-permute-done | bytes 229408 | tf_op jit(solution)/shard_map/ppermute | solution.py:22
  62.7 0.1 add_convert_fusion
  62.8 1.9 %collective-permute-start.7 = (bf16[896,128]{1,0:T(8,128)(2,1)S(1)}, bf16[896,128]{1,0:T(8,128)(2,1)S(1)}, u32[]{:S(2)}, u32[]{:S(2)}) collective-permute-start(bf16[896,128]{1,0:T(8,128)(2,1)S(1)} %add_convert_fusion), channel_id=1, source_target_pairs={{0,452},{64,0},{128,64},{192,128},{256,192},{320,256},{384,320},{4... | collective-permute-start | bytes 688136 | tf_op jit(solution)/shard_map/ppermute | solution.py:22
  64.7 0.1 add_convert_fusion.2
  64.8 4.5 %collective-permute-start.8 = (bf16[896,128]{1,0:T(8,128)(2,1)S(1)}, bf16[896,128]{1,0:T(8,128)(2,1)}, u32[]{:S(2)}, u32[]{:S(2)}) collective-permute-start(bf16[896,128]{1,0:T(8,128)(2,1)S(1)} %add_convert_fusion.2), channel_id=1, source_target_pairs={{0,64},{64,128},{128,192},{192,256},{256,320},{320,384},{384,448},... | collective-permute-start | bytes 688136 | tf_op jit(solution)/shard_map/ppermute | solution.py:22
  69.3 0.1 reshape.41
  69.4 0.1 copy.19
  69.6 1.8 %collective-permute-done.7 = bf16[896,128]{1,0:T(8,128)(2,1)S(1)} collective-permute-done((bf16[896,128]{1,0:T(8,128)(2,1)S(1)}, bf16[896,128]{1,0:T(8,128)(2,1)S(1)}, u32[]{:S(2)}, u32[]{:S(2)}) %collective-permute-start.7) | collective-permute-done | bytes 229408 | tf_op jit(solution)/shard_map/ppermute | solution.py:22
  71.4 1.6 collective-permute-done.8
  73.0 1.0 convert_add_fusion
  74.0 0.2 multiply_convert_fusion
  74.3 4.2 %collective-permute-start.9 = (bf16[896,128]{1,0:T(8,128)(2,1)S(1)}, bf16[896,128]{1,0:T(8,128)(2,1)S(1)}, u32[]{:S(2)}, u32[]{:S(2)}) collective-permute-start(bf16[896,128]{1,0:T(8,128)(2,1)S(1)} %pad_maximum_fusion.3.refs_3_), channel_id=1, source_target_pairs={{0,452},{64,0},{128,64},{192,128},{256,192},{320,256},{384,320},{4... | collective-permute-start | bytes 688136 | tf_op jit(solution)/shard_map/ppermute | solution.py:22
  78.4 2.5 %collective-permute-start.13 = (bf16[896,128]{1,0:T(8,128)(2,1)S(1)}, bf16[896,128]{1,0:T(8,128)(2,1)S(1)}, u32[]{:S(2)}, u32[]{:S(2)}) collective-permute-start(bf16[896,128]{1,0:T(8,128)(2,1)S(1)} %pad_maximum_fusion.3.refs_3_), channel_id=1, source_target_pairs={{0,64},{64,128},{128,192},{192,256},{256,320},{320,384},{384,448},... | collective-permute-start | bytes 688136 | tf_op jit(solution)/shard_map/ppermute | solution.py:22
  81.0 2.1 %collective-permute-done.9.refs_4_ = bf16[896,128]{1,0:T(8,128)(2,1)S(1)} collective-permute-done((bf16[896,128]{1,0:T(8,128)(2,1)S(1)}, bf16[896,128]{1,0:T(8,128)(2,1)S(1)}, u32[]{:S(2)}, u32[]{:S(2)}) %collective-permute-start.9) | collective-permute-done | bytes 229408 | tf_op jit(solution)/shard_map/ppermute | solution.py:22
  83.0 3.3 %collective-permute-start.10 = (bf16[896,128]{1,0:T(8,128)(2,1)S(1)}, bf16[896,128]{1,0:T(8,128)(2,1)S(1)}, u32[]{:S(2)}, u32[]{:S(2)}) collective-permute-start(bf16[896,128]{1,0:T(8,128)(2,1)S(1)} %collective-permute-done.9.refs_4_), channel_id=1, source_target_pairs={{0,452},{64,0},{128,64},{192,128},{256,192},{320,256},{384,320},{4... | collective-permute-start | bytes 688136 | tf_op jit(solution)/shard_map/ppermute | solution.py:22
  86.4 4.2 %collective-permute-start.14 = (bf16[896,128]{1,0:T(8,128)(2,1)S(1)}, bf16[896,128]{1,0:T(8,128)(2,1)S(1)}, u32[]{:S(2)}, u32[]{:S(2)}) collective-permute-start(bf16[896,128]{1,0:T(8,128)(2,1)S(1)} %collective-permute-done.13.refs_2_), channel_id=1, source_target_pairs={{0,64},{64,128},{128,192},{192,256},{256,320},{320,384},{384,448},... | collective-permute-start | bytes 688136 | tf_op jit(solution)/shard_map/ppermute | solution.py:22
  90.6 2.0 %collective-permute-done.10.refs_5_ = bf16[896,128]{1,0:T(8,128)(2,1)S(1)} collective-permute-done((bf16[896,128]{1,0:T(8,128)(2,1)S(1)}, bf16[896,128]{1,0:T(8,128)(2,1)S(1)}, u32[]{:S(2)}, u32[]{:S(2)}) %collective-permute-start.10) | collective-permute-done | bytes 229408 | tf_op jit(solution)/shard_map/ppermute | solution.py:22
  92.6 1.9 %collective-permute-start.11 = (bf16[896,128]{1,0:T(8,128)(2,1)S(1)}, bf16[896,128]{1,0:T(8,128)(2,1)}, u32[]{:S(2)}, u32[]{:S(2)}) collective-permute-start(bf16[896,128]{1,0:T(8,128)(2,1)S(1)} %collective-permute-done.10.refs_5_), channel_id=1, source_target_pairs={{0,452},{64,0},{128,64},{192,128},{256,192},{320,256},{384,320},{4... | collective-permute-start | bytes 688136 | tf_op jit(solution)/shard_map/ppermute | solution.py:22
  94.5 5.7 %collective-permute-start.15 = (bf16[896,128]{1,0:T(8,128)(2,1)S(1)}, bf16[896,128]{1,0:T(8,128)(2,1)}, u32[]{:S(2)}, u32[]{:S(2)}) collective-permute-start(bf16[896,128]{1,0:T(8,128)(2,1)S(1)} %collective-permute-done.14.refs_1_), channel_id=1, source_target_pairs={{0,64},{64,128},{128,192},{192,256},{256,320},{320,384},{384,448},... | collective-permute-start | bytes 688136 | tf_op jit(solution)/shard_map/ppermute | solution.py:22
  100.2 2.1 %collective-permute-done.11.refs_6_ = bf16[896,128]{1,0:T(8,128)(2,1)} collective-permute-done((bf16[896,128]{1,0:T(8,128)(2,1)S(1)}, bf16[896,128]{1,0:T(8,128)(2,1)}, u32[]{:S(2)}, u32[]{:S(2)}) %collective-permute-start.11) | collective-permute-done | bytes 229408 | tf_op jit(solution)/shard_map/ppermute | solution.py:22
  102.4 1.9 %collective-permute-start.12 = (bf16[896,128]{1,0:T(8,128)(2,1)}, bf16[896,128]{1,0:T(8,128)(2,1)S(1)}, u32[]{:S(2)}, u32[]{:S(2)}) collective-permute-start(bf16[896,128]{1,0:T(8,128)(2,1)} %collective-permute-done.11.refs_6_), channel_id=1, source_target_pairs={{0,452},{64,0},{128,64},{192,128},{256,192},{320,256},{384,320},{4... | collective-permute-start | bytes 688136 | tf_op jit(solution)/shard_map/ppermute | solution.py:22
  104.3 4.8 %shard_map.77 = (bf16[1024,512]{1,0:T(8,128)(2,1)}, f32[896,512]{1,0:T(8,128)S(1)}) custom-call(s32[1]{0:T(128)} %bitcast.core_ref, bf16[512,512]{1,0:T(8,128)(2,1)S(1)} %bitcast.31, bf16[512,512]{1,0:T(8,128)(2,1)S(1)} %collective-permute-done.1.other_ref, bf16[512,896]{1,0:T(8,128)(2,1)S(1)} %pad_maximum_fusion.weights_ref, ...), custom_call_target="tpu_custom_call" | custom-call | tf_op jit(solution)/shard_map/pallas_call | solution.py:111
  109.1 2.9 %collective-permute-done.12.tile_ref = bf16[896,128]{1,0:T(8,128)(2,1)S(1)} collective-permute-done((bf16[896,128]{1,0:T(8,128)(2,1)}, bf16[896,128]{1,0:T(8,128)(2,1)S(1)}, u32[]{:S(2)}, u32[]{:S(2)}) %collective-permute-start.12) | collective-permute-done | bytes 229408 | tf_op jit(solution)/shard_map/ppermute | solution.py:22
  111.9 0.4 shard_map.78
  112.4 1.2 shard_map.79
  113.6 5.5 %all-to-all-start.2 = ((bf16[16,64,512]{2,1,0:T(8,128)(2,1)}), bf16[16,64,512]{2,1,0:T(8,128)(2,1)S(1)}, u32[]{:S(2)}, u32[]{:S(2)}) async-start(bf16[16,64,512]{2,1,0:T(8,128)(2,1)} %bitcast.5), calls=%async_computation.2 | async-start | bytes 2097152 | tf_op jit(solution)/shard_map/all_to_all | solution.py:308
  119.1 9.6 %collective-permute-start.18 = (bf16[448,512]{1,0:T(8,128)(2,1)S(1)}, bf16[448,512]{1,0:T(8,128)(2,1)S(1)}, u32[]{:S(2)}, u32[]{:S(2)}) collective-permute-start(bf16[448,512]{1,0:T(8,128)(2,1)S(1)} %copy-done.1), channel_id=1, source_target_pairs={{0,4},{4,0},{1,5},{5,1},{2,6},{6,2},{3,7},{7,3},{8,12},{12,8},{9,1... | collective-permute-start | bytes 1376264 | tf_op jit(solution)/shard_map/ppermute | solution.py:306
  128.7 3.8 %all-to-all-done.2.parts_ref = bf16[16,64,512]{2,1,0:T(8,128)(2,1)S(1)} async-done(((bf16[16,64,512]{2,1,0:T(8,128)(2,1)}), bf16[16,64,512]{2,1,0:T(8,128)(2,1)S(1)}, u32[]{:S(2)}, u32[]{:S(2)}) %all-to-all-start.2) | async-done | bytes 1048608 | tf_op jit(solution)/shard_map/all_to_all | solution.py:308
  132.4 0.2 shard_map.80
  132.6 1.9 %collective-permute-start.16 = (bf16[32,512]{1,0:T(8,128)(2,1)S(1)}, bf16[32,512]{1,0:T(8,128)(2,1)S(1)}, u32[]{:S(2)}, u32[]{:S(2)}) collective-permute-start(bf16[32,512]{1,0:T(8,128)(2,1)S(1)} %get-tuple-element.51), channel_id=1, source_target_pairs={{0,8},{8,0},{1,9},{9,1},{2,10},{10,2},{3,11},{11,3},{4,12},{12,4},... | collective-permute-start | bytes 98312 | tf_op jit(solution)/shard_map/ppermute | solution.py:62
  134.6 1.2 collective-permute-done.16
  135.7 0.8 copy.20
  136.5 3.3 %all-to-all-start.3 = ((bf16[128,2,1,224]{3,1,2,0:T(2,128)(2,1)}), bf16[128,2,1,224]{3,1,2,0:T(2,128)(2,1)S(1)}, u32[]{:S(2)}, u32[]{:S(2)}) async-start(bf16[128,2,1,224]{3,1,2,0:T(2,128)(2,1)} %copy.20), calls=%async_computation.3 | async-start | bytes 262144 | tf_op jit(solution)/shard_map/all_to_all | solution.py:314
  139.9 1.9 %collective-permute-start.17 = (bf16[32,512]{1,0:T(8,128)(2,1)S(1)}, bf16[32,512]{1,0:T(8,128)(2,1)S(1)}, u32[]{:S(2)}, u32[]{:S(2)}) collective-permute-start(bf16[32,512]{1,0:T(8,128)(2,1)S(1)} %add_convert_fusion.5), channel_id=1, source_target_pairs={{0,44},{16,52},{32,60},{48,0},{8,8},{24,16},{40,24},{56,32},{64,11... | collective-permute-start | bytes 98312 | tf_op jit(solution)/shard_map/ppermute | solution.py:317
  141.8 4.0 %all-to-all-done.3 = bf16[128,2,1,224]{3,1,2,0:T(2,128)(2,1)S(1)} async-done(((bf16[128,2,1,224]{3,1,2,0:T(2,128)(2,1)}), bf16[128,2,1,224]{3,1,2,0:T(2,128)(2,1)S(1)}, u32[]{:S(2)}, u32[]{:S(2)}) %all-to-all-start.3) | async-done | bytes 114720 | tf_op jit(solution)/shard_map/all_to_all | solution.py:314
  145.8 0.1 copy.22
  145.9 0.8 reshape.40
  146.8 1.0 shard_map.81
  147.8 24.4 %collective-permute-done.17.in_ref = bf16[32,512]{1,0:T(8,128)(2,1)S(1)} collective-permute-done((bf16[32,512]{1,0:T(8,128)(2,1)S(1)}, bf16[32,512]{1,0:T(8,128)(2,1)S(1)}, u32[]{:S(2)}, u32[]{:S(2)}) %collective-permute-start.17) | collective-permute-done | bytes 32800 | tf_op jit(solution)/shard_map/ppermute | solution.py:317
  172.2 0.6 shard_map.82
  (17 shorter events, 0.1 us)
Async XLA Ops:
  0.6 11.2 %collective-permute-start = (bf16[32,512]{1,0:T(8,128)(2,1)}, bf16[32,512]{1,0:T(8,128)(2,1)S(1)}, u32[]{:S(2)}, u32[]{:S(2)}) collective-permute-start(bf16[32,512]{1,0:T(8,128)(2,1)} %param.4), channel_id=1, source_target_pairs={{324,0},{388,16},{452,32},{0,48},{64,8},{128,24},{192,40},{256,56}... | collective-permute-start | bytes 98312 | tf_op jit(solution)/shard_map/ppermute | solution.py:261
  12.7 16.9 %all-to-all-start = ((bf16[16,32,512]{2,1,0:T(8,128)(2,1)}), bf16[16,32,512]{2,1,0:T(8,128)(2,1)S(1)}, u32[]{:S(2)}, u32[]{:S(2)}) async-start(bf16[16,32,512]{2,1,0:T(8,128)(2,1)} %broadcast_in_dim.2), calls=%async_computation | async-start | bytes 1048576 | tf_op jit(solution)/shard_map/all_to_all | solution.py:263
  29.5 3.8 %collective-permute-start.1 = (bf16[512,512]{1,0:T(8,128)(2,1)S(1)}, bf16[512,512]{1,0:T(8,128)(2,1)S(1)}, u32[]{:S(2)}, u32[]{:S(2)}) collective-permute-start(bf16[512,512]{1,0:T(8,128)(2,1)S(1)} %bitcast.28), channel_id=1, source_target_pairs={{0,8},{8,0},{1,9},{9,1},{2,10},{10,2},{3,11},{11,3},{4,12},{12,4},... | collective-permute-start | bytes 1572872 | tf_op jit(solution)/shard_map/ppermute | solution.py:62
  33.9 10.3 %collective-permute-start.2 = (bf16[896,128]{1,0:T(8,128)(2,1)S(1)}, bf16[896,128]{1,0:T(8,128)(2,1)S(1)}, u32[]{:S(2)}, u32[]{:S(2)}) collective-permute-start(bf16[896,128]{1,0:T(8,128)(2,1)S(1)} %get-tuple-element.35), channel_id=1, source_target_pairs={{0,64},{64,128},{128,192},{192,256},{256,320},{320,384},{384,448},... | collective-permute-start | bytes 688136 | tf_op jit(solution)/shard_map/ppermute | solution.py:22
  37.6 27.1 %all-to-all-start.1 = ((bf16[4,32,2,224]{3,2,1,0:T(2,128)(2,1)}), bf16[4,32,2,224]{3,2,1,0:T(2,128)(2,1)S(1)}, u32[]{:S(2)}, u32[]{:S(2)}) async-start(bf16[4,32,2,224]{3,2,1,0:T(2,128)(2,1)} %bitcast.27), calls=%async_computation.1 | async-start | bytes 262144 | tf_op jit(solution)/shard_map/all_to_all | solution.py:268
  41.0 9.6 %collective-permute-start.5 = (bf16[896,128]{1,0:T(8,128)(2,1)S(1)}, bf16[896,128]{1,0:T(8,128)(2,1)S(1)}, u32[]{:S(2)}, u32[]{:S(2)}) collective-permute-start(bf16[896,128]{1,0:T(8,128)(2,1)S(1)} %get-tuple-element.42), channel_id=1, source_target_pairs={{0,452},{64,0},{128,64},{192,128},{256,192},{320,256},{384,320},{4... | collective-permute-start | bytes 688136 | tf_op jit(solution)/shard_map/ppermute | solution.py:22
  44.3 9.3 %collective-permute-start.3 = (bf16[896,128]{1,0:T(8,128)(2,1)S(1)}, bf16[896,128]{1,0:T(8,128)(2,1)S(1)}, u32[]{:S(2)}, u32[]{:S(2)}) collective-permute-start(bf16[896,128]{1,0:T(8,128)(2,1)S(1)} %add_convert_fusion.4), channel_id=1, source_target_pairs={{0,64},{64,128},{128,192},{192,256},{256,320},{320,384},{384,448},... | collective-permute-start | bytes 688136 | tf_op jit(solution)/shard_map/ppermute | solution.py:22
  50.6 12.1 %collective-permute-start.6 = (bf16[896,128]{1,0:T(8,128)(2,1)S(1)}, bf16[896,128]{1,0:T(8,128)(2,1)S(1)}, u32[]{:S(2)}, u32[]{:S(2)}) collective-permute-start(bf16[896,128]{1,0:T(8,128)(2,1)S(1)} %add_convert_fusion.1), channel_id=1, source_target_pairs={{0,452},{64,0},{128,64},{192,128},{256,192},{320,256},{384,320},{4... | collective-permute-start | bytes 688136 | tf_op jit(solution)/shard_map/ppermute | solution.py:22
  53.7 11.0 %collective-permute-start.4 = (bf16[896,128]{1,0:T(8,128)(2,1)S(1)}, bf16[896,128]{1,0:T(8,128)(2,1)S(1)}, u32[]{:S(2)}, u32[]{:S(2)}) collective-permute-start(bf16[896,128]{1,0:T(8,128)(2,1)S(1)} %add_convert_fusion.3), channel_id=1, source_target_pairs={{0,64},{64,128},{128,192},{192,256},{256,320},{320,384},{384,448},... | collective-permute-start | bytes 688136 | tf_op jit(solution)/shard_map/ppermute | solution.py:22
  62.8 8.6 %collective-permute-start.7 = (bf16[896,128]{1,0:T(8,128)(2,1)S(1)}, bf16[896,128]{1,0:T(8,128)(2,1)S(1)}, u32[]{:S(2)}, u32[]{:S(2)}) collective-permute-start(bf16[896,128]{1,0:T(8,128)(2,1)S(1)} %add_convert_fusion), channel_id=1, source_target_pairs={{0,452},{64,0},{128,64},{192,128},{256,192},{320,256},{384,320},{4... | collective-permute-start | bytes 688136 | tf_op jit(solution)/shard_map/ppermute | solution.py:22
  64.8 8.2 %collective-permute-start.8 = (bf16[896,128]{1,0:T(8,128)(2,1)S(1)}, bf16[896,128]{1,0:T(8,128)(2,1)}, u32[]{:S(2)}, u32[]{:S(2)}) collective-permute-start(bf16[896,128]{1,0:T(8,128)(2,1)S(1)} %add_convert_fusion.2), channel_id=1, source_target_pairs={{0,64},{64,128},{128,192},{192,256},{256,320},{320,384},{384,448},... | collective-permute-start | bytes 688136 | tf_op jit(solution)/shard_map/ppermute | solution.py:22
  74.3 8.8 %collective-permute-start.9 = (bf16[896,128]{1,0:T(8,128)(2,1)S(1)}, bf16[896,128]{1,0:T(8,128)(2,1)S(1)}, u32[]{:S(2)}, u32[]{:S(2)}) collective-permute-start(bf16[896,128]{1,0:T(8,128)(2,1)S(1)} %pad_maximum_fusion.3.refs_3_), channel_id=1, source_target_pairs={{0,452},{64,0},{128,64},{192,128},{256,192},{320,256},{384,320},{4... | collective-permute-start | bytes 688136 | tf_op jit(solution)/shard_map/ppermute | solution.py:22
  78.4 7.9 %collective-permute-start.13 = (bf16[896,128]{1,0:T(8,128)(2,1)S(1)}, bf16[896,128]{1,0:T(8,128)(2,1)S(1)}, u32[]{:S(2)}, u32[]{:S(2)}) collective-permute-start(bf16[896,128]{1,0:T(8,128)(2,1)S(1)} %pad_maximum_fusion.3.refs_3_), channel_id=1, source_target_pairs={{0,64},{64,128},{128,192},{192,256},{256,320},{320,384},{384,448},... | collective-permute-start | bytes 688136 | tf_op jit(solution)/shard_map/ppermute | solution.py:22
  83.0 9.6 %collective-permute-start.10 = (bf16[896,128]{1,0:T(8,128)(2,1)S(1)}, bf16[896,128]{1,0:T(8,128)(2,1)S(1)}, u32[]{:S(2)}, u32[]{:S(2)}) collective-permute-start(bf16[896,128]{1,0:T(8,128)(2,1)S(1)} %collective-permute-done.9.refs_4_), channel_id=1, source_target_pairs={{0,452},{64,0},{128,64},{192,128},{256,192},{320,256},{384,320},{4... | collective-permute-start | bytes 688136 | tf_op jit(solution)/shard_map/ppermute | solution.py:22
  86.4 8.2 %collective-permute-start.14 = (bf16[896,128]{1,0:T(8,128)(2,1)S(1)}, bf16[896,128]{1,0:T(8,128)(2,1)S(1)}, u32[]{:S(2)}, u32[]{:S(2)}) collective-permute-start(bf16[896,128]{1,0:T(8,128)(2,1)S(1)} %collective-permute-done.13.refs_2_), channel_id=1, source_target_pairs={{0,64},{64,128},{128,192},{192,256},{256,320},{320,384},{384,448},... | collective-permute-start | bytes 688136 | tf_op jit(solution)/shard_map/ppermute | solution.py:22
  92.6 9.8 %collective-permute-start.11 = (bf16[896,128]{1,0:T(8,128)(2,1)S(1)}, bf16[896,128]{1,0:T(8,128)(2,1)}, u32[]{:S(2)}, u32[]{:S(2)}) collective-permute-start(bf16[896,128]{1,0:T(8,128)(2,1)S(1)} %collective-permute-done.10.refs_5_), channel_id=1, source_target_pairs={{0,452},{64,0},{128,64},{192,128},{256,192},{320,256},{384,320},{4... | collective-permute-start | bytes 688136 | tf_op jit(solution)/shard_map/ppermute | solution.py:22
  94.5 9.8 %collective-permute-start.15 = (bf16[896,128]{1,0:T(8,128)(2,1)S(1)}, bf16[896,128]{1,0:T(8,128)(2,1)}, u32[]{:S(2)}, u32[]{:S(2)}) collective-permute-start(bf16[896,128]{1,0:T(8,128)(2,1)S(1)} %collective-permute-done.14.refs_1_), channel_id=1, source_target_pairs={{0,64},{64,128},{128,192},{192,256},{256,320},{320,384},{384,448},... | collective-permute-start | bytes 688136 | tf_op jit(solution)/shard_map/ppermute | solution.py:22
  102.4 9.5 %collective-permute-start.12 = (bf16[896,128]{1,0:T(8,128)(2,1)}, bf16[896,128]{1,0:T(8,128)(2,1)S(1)}, u32[]{:S(2)}, u32[]{:S(2)}) collective-permute-start(bf16[896,128]{1,0:T(8,128)(2,1)} %collective-permute-done.11.refs_6_), channel_id=1, source_target_pairs={{0,452},{64,0},{128,64},{192,128},{256,192},{320,256},{384,320},{4... | collective-permute-start | bytes 688136 | tf_op jit(solution)/shard_map/ppermute | solution.py:22
  112.3 1.2 copy-start
  113.5 5.5 %copy-start.1 = (bf16[448,512]{1,0:T(8,128)(2,1)S(1)}, bf16[448,512]{1,0:T(8,128)(2,1)}, u32[]{:S(2)}) copy-start(bf16[448,512]{1,0:T(8,128)(2,1)} %copy-done) | copy-start | bytes 1376260
  113.6 18.9 %all-to-all-start.2 = ((bf16[16,64,512]{2,1,0:T(8,128)(2,1)}), bf16[16,64,512]{2,1,0:T(8,128)(2,1)S(1)}, u32[]{:S(2)}, u32[]{:S(2)}) async-start(bf16[16,64,512]{2,1,0:T(8,128)(2,1)} %bitcast.5), calls=%async_computation.2 | async-start | bytes 2097152 | tf_op jit(solution)/shard_map/all_to_all | solution.py:308
  119.1 27.7 %collective-permute-start.18 = (bf16[448,512]{1,0:T(8,128)(2,1)S(1)}, bf16[448,512]{1,0:T(8,128)(2,1)S(1)}, u32[]{:S(2)}, u32[]{:S(2)}) collective-permute-start(bf16[448,512]{1,0:T(8,128)(2,1)S(1)} %copy-done.1), channel_id=1, source_target_pairs={{0,4},{4,0},{1,5},{5,1},{2,6},{6,2},{3,7},{7,3},{8,12},{12,8},{9,1... | collective-permute-start | bytes 1376264 | tf_op jit(solution)/shard_map/ppermute | solution.py:306
  132.6 3.1 %collective-permute-start.16 = (bf16[32,512]{1,0:T(8,128)(2,1)S(1)}, bf16[32,512]{1,0:T(8,128)(2,1)S(1)}, u32[]{:S(2)}, u32[]{:S(2)}) collective-permute-start(bf16[32,512]{1,0:T(8,128)(2,1)S(1)} %get-tuple-element.51), channel_id=1, source_target_pairs={{0,8},{8,0},{1,9},{9,1},{2,10},{10,2},{3,11},{11,3},{4,12},{12,4},... | collective-permute-start | bytes 98312 | tf_op jit(solution)/shard_map/ppermute | solution.py:62
  136.5 9.3 %all-to-all-start.3 = ((bf16[128,2,1,224]{3,1,2,0:T(2,128)(2,1)}), bf16[128,2,1,224]{3,1,2,0:T(2,128)(2,1)S(1)}, u32[]{:S(2)}, u32[]{:S(2)}) async-start(bf16[128,2,1,224]{3,1,2,0:T(2,128)(2,1)} %copy.20), calls=%async_computation.3 | async-start | bytes 262144 | tf_op jit(solution)/shard_map/all_to_all | solution.py:314
  139.9 32.3 %collective-permute-start.17 = (bf16[32,512]{1,0:T(8,128)(2,1)S(1)}, bf16[32,512]{1,0:T(8,128)(2,1)S(1)}, u32[]{:S(2)}, u32[]{:S(2)}) collective-permute-start(bf16[32,512]{1,0:T(8,128)(2,1)S(1)} %add_convert_fusion.5), channel_id=1, source_target_pairs={{0,44},{16,52},{32,60},{48,0},{8,8},{24,16},{40,24},{56,32},{64,11... | collective-permute-start | bytes 98312 | tf_op jit(solution)/shard_map/ppermute | solution.py:317

commit v14 on v13

--- a/solution.py
+++ b/solution.py
@@ -265,7 +265,6 @@
     cotangent = grad_hidden.reshape(-1, 2, 4, part).transpose(2, 0, 1, 3)
     own_tokens, cotangent, weights = lax.optimization_barrier((own_tokens, cotangent, weights))
     other_tokens = swap_cores(own_tokens)
-    cotangent = lax.all_to_all(cotangent, "x", split_axis=0, concat_axis=0, tiled=True)
     partial = {}
     for offsets in ((7, 0), (6, 1, 5, 2, 4, 3)):
         partial.update(zip(offsets, forward_tiles(offsets, core, own_tokens, other_tokens, weights)))
@@ -278,6 +277,7 @@
     right = add_tiles(ring_shift(right, 1), partial[4])
     left = ring_shift(left, -1)
     right, cotangent = lax.optimization_barrier((right, cotangent))
+    cotangent = lax.all_to_all(cotangent, "x", split_axis=0, concat_axis=0, tiled=True)
     right = ring_shift(right, 1)
     cotangent = cotangent.reshape(-1, 2 * part).T.astype(jnp.float32)
     total = partial[BEFORE].astype(jnp.float32) + left.astype(jnp.float32) + right.astype(jnp.float32)

time: 174 us -> 195 us (1.12)
  the two profiles are of different devices: /device:TPU:160 before, /device:TPU:26 now
where the time goes in v14:
time: 195 us; the launch traced here: 194 us
  starting transfers between devices  130 us (67%)
  waiting for transfers between devices  36.5 us (19%)
  Pallas kernels  9.82 us (5%)
  blocking collectives  8.37 us (4%)
  local copies, waits for them, and re-layouts  5.9 us (3%)
    ppermute x14, starting transfers between devices, ring_shift(): return lax.ppermute(value, ('r', 'h'), pairs)  52.5 us
    ppermute x1, starting transfers between devices, local(): received = lax.ppermute(send, 'h', [(0, 1), (1, 0)])  40.9 us
    ppermute x14, waiting for transfers between devices, ring_shift(): return lax.ppermute(value, ('r', 'h'), pairs)  14 us
    ppermute x1, starting transfers between devices, local(): piece = lax.ppermute(tokens, ('r', 'y', 'c', 'h'), token_pairs())  12 us
    ppermute x1, waiting for transfers between devices, local(): lax.ppermute(grad_tokens, ('r', 'y', 'c', 'h'), result_pairs())  10.4 us
    all_to_all x1, blocking collectives, local(): lax.all_to_all(cotangent, 'x', split_axis=0, concat_axis=0, tiled=True)  8.37 us
    all_to_all x1, starting transfers between devices, local(): lax.all_to_all(copies, ('y', 'x'), split_axis=0, concat_axis=0, tiled=True)  6.96 us
    all_to_all x1, starting transfers between devices, local(): lax.all_to_all(terms.reshape(16, -1, features), ('y', 'x'), split_axis=0,...  6.94 us
  transfers between devices with their start and end apart: 22, of which 13 were waited for; matrix products, arithmetic and copies ran while one was open for 3% of the time, Pallas kernels for 4%

profile of v14, /device:TPU:26, one launch (start us, length us, event | category | flops | bytes accessed | tf_op | source)
XLA Modules:
  0.0 193.6 jit_solution(6187536244887768655)
XLA Ops:
  0.6 12.0 %collective-permute-start = (bf16[32,512]{1,0:T(8,128)(2,1)}, bf16[32,512]{1,0:T(8,128)(2,1)S(1)}, u32[]{:S(2)}, u32[]{:S(2)}) collective-permute-start(bf16[32,512]{1,0:T(8,128)(2,1)} %param.4), channel_id=1, source_target_pairs={{324,0},{388,16},{452,32},{0,48},{64,8},{128,24},{192,40},{256,56}... | collective-permute-start | bytes 98312 | tf_op jit(solution)/shard_map/ppermute | solution.py:261
  12.6 3.4 %collective-permute-done = bf16[32,512]{1,0:T(8,128)(2,1)S(1)} collective-permute-done((bf16[32,512]{1,0:T(8,128)(2,1)}, bf16[32,512]{1,0:T(8,128)(2,1)S(1)}, u32[]{:S(2)}, u32[]{:S(2)}) %collective-permute-start) | collective-permute-done | bytes 32800 | tf_op jit(solution)/shard_map/ppermute | solution.py:261
  16.0 0.8 broadcast_in_dim.2
  16.8 7.0 %all-to-all-start = ((bf16[16,32,512]{2,1,0:T(8,128)(2,1)}), bf16[16,32,512]{2,1,0:T(8,128)(2,1)S(1)}, u32[]{:S(2)}, u32[]{:S(2)}) async-start(bf16[16,32,512]{2,1,0:T(8,128)(2,1)} %broadcast_in_dim.2), calls=%async_computation | async-start | bytes 1048576 | tf_op jit(solution)/shard_map/all_to_all | solution.py:263
  23.8 1.1 reshape.36
  24.9 0.1 copy.24
  25.0 1.8 constant_dynamic-slice_fusion.2
  26.8 0.4 pad_maximum_fusion.weights_ref
  27.3 3.4 %all-to-all-done = bf16[16,32,512]{2,1,0:T(8,128)(2,1)S(1)} async-done(((bf16[16,32,512]{2,1,0:T(8,128)(2,1)}), bf16[16,32,512]{2,1,0:T(8,128)(2,1)S(1)}, u32[]{:S(2)}, u32[]{:S(2)}) %all-to-all-start) | async-done | bytes 524320 | tf_op jit(solution)/shard_map/all_to_all | solution.py:263
  30.7 1.9 collective-permute-start.1
  32.6 1.9 collective-permute-done.1.other_ref
  34.5 0.6 shard_map.75
  35.1 3.7 %collective-permute-start.2 = (bf16[896,128]{1,0:T(8,128)(2,1)S(1)}, bf16[896,128]{1,0:T(8,128)(2,1)S(1)}, u32[]{:S(2)}, u32[]{:S(2)}) collective-permute-start(bf16[896,128]{1,0:T(8,128)(2,1)S(1)} %get-tuple-element.35), channel_id=1, source_target_pairs={{0,64},{64,128},{128,192},{192,256},{256,320},{320,384},{384,448},... | collective-permute-start | bytes 688136 | tf_op jit(solution)/shard_map/ppermute | solution.py:22
  38.8 5.1 %collective-permute-start.5 = (bf16[896,128]{1,0:T(8,128)(2,1)S(1)}, bf16[896,128]{1,0:T(8,128)(2,1)S(1)}, u32[]{:S(2)}, u32[]{:S(2)}) collective-permute-start(bf16[896,128]{1,0:T(8,128)(2,1)S(1)} %get-tuple-element.42), channel_id=1, source_target_pairs={{0,452},{64,0},{128,64},{192,128},{256,192},{320,256},{384,320},{4... | collective-permute-start | bytes 688136 | tf_op jit(solution)/shard_map/ppermute | solution.py:22
  43.8 1.1 shard_map.76
  45.0 2.8 %collective-permute-done.2 = bf16[896,128]{1,0:T(8,128)(2,1)S(1)} collective-permute-done((bf16[896,128]{1,0:T(8,128)(2,1)S(1)}, bf16[896,128]{1,0:T(8,128)(2,1)S(1)}, u32[]{:S(2)}, u32[]{:S(2)}) %collective-permute-start.2) | collective-permute-done | bytes 229408 | tf_op jit(solution)/shard_map/ppermute | solution.py:22
  47.8 0.1 add_convert_fusion.4
  47.9 1.9 collective-permute-start.3
  49.8 0.1 add_convert_fusion.1
  49.9 5.1 %collective-permute-start.6 = (bf16[896,128]{1,0:T(8,128)(2,1)S(1)}, bf16[896,128]{1,0:T(8,128)(2,1)S(1)}, u32[]{:S(2)}, u32[]{:S(2)}) collective-permute-start(bf16[896,128]{1,0:T(8,128)(2,1)S(1)} %add_convert_fusion.1), channel_id=1, source_target_pairs={{0,452},{64,0},{128,64},{192,128},{256,192},{320,256},{384,320},{4... | collective-permute-start | bytes 688136 | tf_op jit(solution)/shard_map/ppermute | solution.py:22
  55.0 3.1 %collective-permute-done.3 = bf16[896,128]{1,0:T(8,128)(2,1)S(1)} collective-permute-done((bf16[896,128]{1,0:T(8,128)(2,1)S(1)}, bf16[896,128]{1,0:T(8,128)(2,1)S(1)}, u32[]{:S(2)}, u32[]{:S(2)}) %collective-permute-start.3) | collective-permute-done | bytes 229408 | tf_op jit(solution)/shard_map/ppermute | solution.py:22
  58.1 0.1 add_convert_fusion.3
  58.2 1.9 collective-permute-start.4
  60.1 0.1 add_convert_fusion
  60.2 5.1 %collective-permute-start.7 = (bf16[896,128]{1,0:T(8,128)(2,1)S(1)}, bf16[896,128]{1,0:T(8,128)(2,1)S(1)}, u32[]{:S(2)}, u32[]{:S(2)}) collective-permute-start(bf16[896,128]{1,0:T(8,128)(2,1)S(1)} %add_convert_fusion), channel_id=1, source_target_pairs={{0,452},{64,0},{128,64},{192,128},{256,192},{320,256},{384,320},{4... | collective-permute-start | bytes 688136 | tf_op jit(solution)/shard_map/ppermute | solution.py:22
  65.3 2.2 %collective-permute-done.4 = bf16[896,128]{1,0:T(8,128)(2,1)S(1)} collective-permute-done((bf16[896,128]{1,0:T(8,128)(2,1)S(1)}, bf16[896,128]{1,0:T(8,128)(2,1)S(1)}, u32[]{:S(2)}, u32[]{:S(2)}) %collective-permute-start.4) | collective-permute-done | bytes 229408 | tf_op jit(solution)/shard_map/ppermute | solution.py:22
  67.5 0.8 add_convert_fusion.2
  68.3 1.9 collective-permute-start.8
  70.2 8.4 %all_to_all.30 = bf16[4,32,2,224]{3,2,1,0:T(2,128)(2,1)S(1)} all-to-all(bf16[4,32,2,224]{3,2,1,0:T(2,128)(2,1)S(1)} %bitcast.33), channel_id=1, replica_groups=mesh['r'=8,'y'=4,'c'=2,'h'=2,'x'=4] {'x'}, dimensions={0} | all-to-all | bytes 229376 | tf_op jit(solution)/shard_map/all_to_all | solution.py:280
  78.5 0.1 reshape.41
  78.7 0.1 copy.19
  78.8 0.1 convert_add_fusion
  78.9 0.2 multiply_convert_fusion
  79.2 5.1 %collective-permute-start.9 = (bf16[896,128]{1,0:T(8,128)(2,1)S(1)}, bf16[896,128]{1,0:T(8,128)(2,1)S(1)}, u32[]{:S(2)}, u32[]{:S(2)}) collective-permute-start(bf16[896,128]{1,0:T(8,128)(2,1)S(1)} %pad_maximum_fusion.3.refs_3_), channel_id=1, source_target_pairs={{0,452},{64,0},{128,64},{192,128},{256,192},{320,256},{384,320},{4... | collective-permute-start | bytes 688136 | tf_op jit(solution)/shard_map/ppermute | solution.py:22
  84.3 1.9 collective-permute-start.13
  86.2 1.6 collective-permute-done.9.refs_4_
  87.8 5.6 %collective-permute-start.10 = (bf16[896,128]{1,0:T(8,128)(2,1)S(1)}, bf16[896,128]{1,0:T(8,128)(2,1)S(1)}, u32[]{:S(2)}, u32[]{:S(2)}) collective-permute-start(bf16[896,128]{1,0:T(8,128)(2,1)S(1)} %collective-permute-done.9.refs_4_), channel_id=1, source_target_pairs={{0,452},{64,0},{128,64},{192,128},{256,192},{320,256},{384,320},{4... | collective-permute-start | bytes 688136 | tf_op jit(solution)/shard_map/ppermute | solution.py:22
  93.4 0.0 collective-permute-done.13.refs_2_
  93.4 1.9 collective-permute-start.14
  95.4 1.7 collective-permute-done.10.refs_5_
  97.1 5.6 %collective-permute-start.11 = (bf16[896,128]{1,0:T(8,128)(2,1)S(1)}, bf16[896,128]{1,0:T(8,128)(2,1)}, u32[]{:S(2)}, u32[]{:S(2)}) collective-permute-start(bf16[896,128]{1,0:T(8,128)(2,1)S(1)} %collective-permute-done.10.refs_5_), channel_id=1, source_target_pairs={{0,452},{64,0},{128,64},{192,128},{256,192},{320,256},{384,320},{4... | collective-permute-start | bytes 688136 | tf_op jit(solution)/shard_map/ppermute | solution.py:22
  102.7 0.3 collective-permute-done.14.refs_1_
  103.0 1.9 collective-permute-start.15
  104.9 2.2 %collective-permute-done.11.refs_6_ = bf16[896,128]{1,0:T(8,128)(2,1)} collective-permute-done((bf16[896,128]{1,0:T(8,128)(2,1)S(1)}, bf16[896,128]{1,0:T(8,128)(2,1)}, u32[]{:S(2)}, u32[]{:S(2)}) %collective-permute-start.11) | collective-permute-done | bytes 229408 | tf_op jit(solution)/shard_map/ppermute | solution.py:22
  107.2 5.7 %collective-permute-start.12 = (bf16[896,128]{1,0:T(8,128)(2,1)}, bf16[896,128]{1,0:T(8,128)(2,1)S(1)}, u32[]{:S(2)}, u32[]{:S(2)}) collective-permute-start(bf16[896,128]{1,0:T(8,128)(2,1)} %collective-permute-done.11.refs_6_), channel_id=1, source_target_pairs={{0,452},{64,0},{128,64},{192,128},{256,192},{320,256},{384,320},{4... | collective-permute-start | bytes 688136 | tf_op jit(solution)/shard_map/ppermute | solution.py:22
  112.9 4.8 %shard_map.77 = (bf16[1024,512]{1,0:T(8,128)(2,1)}, f32[896,512]{1,0:T(8,128)S(1)}) custom-call(s32[1]{0:T(128)} %bitcast.core_ref, bf16[512,512]{1,0:T(8,128)(2,1)S(1)} %bitcast.31, bf16[512,512]{1,0:T(8,128)(2,1)S(1)} %collective-permute-done.1.other_ref, bf16[512,896]{1,0:T(8,128)(2,1)S(1)} %pad_maximum_fusion.weights_ref, ...), custom_call_target="tpu_custom_call" | custom-call | tf_op jit(solution)/shard_map/pallas_call | solution.py:111
  117.6 0.4 shard_map.78
  118.0 0.0 copy-start
  118.1 1.2 shard_map.79
  119.2 0.0 copy-start.1
  119.2 6.9 %all-to-all-start.2 = ((bf16[16,64,512]{2,1,0:T(8,128)(2,1)}), bf16[16,64,512]{2,1,0:T(8,128)(2,1)S(1)}, u32[]{:S(2)}, u32[]{:S(2)}) async-start(bf16[16,64,512]{2,1,0:T(8,128)(2,1)} %bitcast.5), calls=%async_computation.2 | async-start | bytes 2097152 | tf_op jit(solution)/shard_map/all_to_all | solution.py:308
  126.2 40.9 %collective-permute-start.18 = (bf16[448,512]{1,0:T(8,128)(2,1)S(1)}, bf16[448,512]{1,0:T(8,128)(2,1)S(1)}, u32[]{:S(2)}, u32[]{:S(2)}) collective-permute-start(bf16[448,512]{1,0:T(8,128)(2,1)S(1)} %copy-done.1), channel_id=1, source_target_pairs={{0,4},{4,0},{1,5},{5,1},{2,6},{6,2},{3,7},{7,3},{8,12},{12,8},{9,1... | collective-permute-start | bytes 1376264 | tf_op jit(solution)/shard_map/ppermute | solution.py:306
  167.1 0.2 shard_map.80
  167.3 1.9 collective-permute-start.16
  169.3 1.2 collective-permute-done.16
  170.4 0.8 copy.20
  171.2 4.8 %all-to-all-start.3 = ((bf16[128,2,1,224]{3,1,2,0:T(2,128)(2,1)}), bf16[128,2,1,224]{3,1,2,0:T(2,128)(2,1)S(1)}, u32[]{:S(2)}, u32[]{:S(2)}) async-start(bf16[128,2,1,224]{3,1,2,0:T(2,128)(2,1)} %copy.20), calls=%async_computation.3 | async-start | bytes 262144 | tf_op jit(solution)/shard_map/all_to_all | solution.py:314
  176.0 2.4 %collective-permute-start.17 = (bf16[32,512]{1,0:T(8,128)(2,1)S(1)}, bf16[32,512]{1,0:T(8,128)(2,1)S(1)}, u32[]{:S(2)}, u32[]{:S(2)}) collective-permute-start(bf16[32,512]{1,0:T(8,128)(2,1)S(1)} %add_convert_fusion.5), channel_id=1, source_target_pairs={{0,44},{16,52},{32,60},{48,0},{8,8},{24,16},{40,24},{56,32},{64,11... | collective-permute-start | bytes 98312 | tf_op jit(solution)/shard_map/ppermute | solution.py:317
  178.4 2.1 %all-to-all-done.3 = bf16[128,2,1,224]{3,1,2,0:T(2,128)(2,1)S(1)} async-done(((bf16[128,2,1,224]{3,1,2,0:T(2,128)(2,1)}), bf16[128,2,1,224]{3,1,2,0:T(2,128)(2,1)S(1)}, u32[]{:S(2)}, u32[]{:S(2)}) %all-to-all-start.3) | async-done | bytes 114720 | tf_op jit(solution)/shard_map/all_to_all | solution.py:314
  180.6 0.1 copy.22
  180.7 0.8 reshape.40
  181.5 1.0 shard_map.81
  182.5 10.4 %collective-permute-done.17.in_ref = bf16[32,512]{1,0:T(8,128)(2,1)S(1)} collective-permute-done((bf16[32,512]{1,0:T(8,128)(2,1)S(1)}, bf16[32,512]{1,0:T(8,128)(2,1)S(1)}, u32[]{:S(2)}, u32[]{:S(2)}) %collective-permute-start.17) | collective-permute-done | bytes 32800 | tf_op jit(solution)/shard_map/ppermute | solution.py:317
  193.0 0.6 shard_map.82
  (16 shorter events, 0.1 us)
Async XLA Ops:
  0.6 15.4 %collective-permute-start = (bf16[32,512]{1,0:T(8,128)(2,1)}, bf16[32,512]{1,0:T(8,128)(2,1)S(1)}, u32[]{:S(2)}, u32[]{:S(2)}) collective-permute-start(bf16[32,512]{1,0:T(8,128)(2,1)} %param.4), channel_id=1, source_target_pairs={{324,0},{388,16},{452,32},{0,48},{64,8},{128,24},{192,40},{256,56}... | collective-permute-start | bytes 98312 | tf_op jit(solution)/shard_map/ppermute | solution.py:261
  16.8 13.9 %all-to-all-start = ((bf16[16,32,512]{2,1,0:T(8,128)(2,1)}), bf16[16,32,512]{2,1,0:T(8,128)(2,1)S(1)}, u32[]{:S(2)}, u32[]{:S(2)}) async-start(bf16[16,32,512]{2,1,0:T(8,128)(2,1)} %broadcast_in_dim.2), calls=%async_computation | async-start | bytes 1048576 | tf_op jit(solution)/shard_map/all_to_all | solution.py:263
  30.7 3.8 %collective-permute-start.1 = (bf16[512,512]{1,0:T(8,128)(2,1)S(1)}, bf16[512,512]{1,0:T(8,128)(2,1)S(1)}, u32[]{:S(2)}, u32[]{:S(2)}) collective-permute-start(bf16[512,512]{1,0:T(8,128)(2,1)S(1)} %bitcast.28), channel_id=1, source_target_pairs={{0,8},{8,0},{1,9},{9,1},{2,10},{10,2},{3,11},{11,3},{4,12},{12,4},... | collective-permute-start | bytes 1572872 | tf_op jit(solution)/shard_map/ppermute | solution.py:62
  35.1 12.7 %collective-permute-start.2 = (bf16[896,128]{1,0:T(8,128)(2,1)S(1)}, bf16[896,128]{1,0:T(8,128)(2,1)S(1)}, u32[]{:S(2)}, u32[]{:S(2)}) collective-permute-start(bf16[896,128]{1,0:T(8,128)(2,1)S(1)} %get-tuple-element.35), channel_id=1, source_target_pairs={{0,64},{64,128},{128,192},{192,256},{256,320},{320,384},{384,448},... | collective-permute-start | bytes 688136 | tf_op jit(solution)/shard_map/ppermute | solution.py:22
  38.8 11.0 %collective-permute-start.5 = (bf16[896,128]{1,0:T(8,128)(2,1)S(1)}, bf16[896,128]{1,0:T(8,128)(2,1)S(1)}, u32[]{:S(2)}, u32[]{:S(2)}) collective-permute-start(bf16[896,128]{1,0:T(8,128)(2,1)S(1)} %get-tuple-element.42), channel_id=1, source_target_pairs={{0,452},{64,0},{128,64},{192,128},{256,192},{320,256},{384,320},{4... | collective-permute-start | bytes 688136 | tf_op jit(solution)/shard_map/ppermute | solution.py:22
  47.9 10.2 %collective-permute-start.3 = (bf16[896,128]{1,0:T(8,128)(2,1)S(1)}, bf16[896,128]{1,0:T(8,128)(2,1)S(1)}, u32[]{:S(2)}, u32[]{:S(2)}) collective-permute-start(bf16[896,128]{1,0:T(8,128)(2,1)S(1)} %add_convert_fusion.4), channel_id=1, source_target_pairs={{0,64},{64,128},{128,192},{192,256},{256,320},{320,384},{384,448},... | collective-permute-start | bytes 688136 | tf_op jit(solution)/shard_map/ppermute | solution.py:22
  49.9 10.2 %collective-permute-start.6 = (bf16[896,128]{1,0:T(8,128)(2,1)S(1)}, bf16[896,128]{1,0:T(8,128)(2,1)S(1)}, u32[]{:S(2)}, u32[]{:S(2)}) collective-permute-start(bf16[896,128]{1,0:T(8,128)(2,1)S(1)} %add_convert_fusion.1), channel_id=1, source_target_pairs={{0,452},{64,0},{128,64},{192,128},{256,192},{320,256},{384,320},{4... | collective-permute-start | bytes 688136 | tf_op jit(solution)/shard_map/ppermute | solution.py:22
  58.2 9.3 %collective-permute-start.4 = (bf16[896,128]{1,0:T(8,128)(2,1)S(1)}, bf16[896,128]{1,0:T(8,128)(2,1)S(1)}, u32[]{:S(2)}, u32[]{:S(2)}) collective-permute-start(bf16[896,128]{1,0:T(8,128)(2,1)S(1)} %add_convert_fusion.3), channel_id=1, source_target_pairs={{0,64},{64,128},{128,192},{192,256},{256,320},{320,384},{384,448},... | collective-permute-start | bytes 688136 | tf_op jit(solution)/shard_map/ppermute | solution.py:22
  60.2 18.6 %collective-permute-start.7 = (bf16[896,128]{1,0:T(8,128)(2,1)S(1)}, bf16[896,128]{1,0:T(8,128)(2,1)S(1)}, u32[]{:S(2)}, u32[]{:S(2)}) collective-permute-start(bf16[896,128]{1,0:T(8,128)(2,1)S(1)} %add_convert_fusion), channel_id=1, source_target_pairs={{0,452},{64,0},{128,64},{192,128},{256,192},{320,256},{384,320},{4... | collective-permute-start | bytes 688136 | tf_op jit(solution)/shard_map/ppermute | solution.py:22
  68.3 10.5 %collective-permute-start.8 = (bf16[896,128]{1,0:T(8,128)(2,1)}, bf16[896,128]{1,0:T(8,128)(2,1)S(1)}, u32[]{:S(2)}, u32[]{:S(2)}) collective-permute-start(bf16[896,128]{1,0:T(8,128)(2,1)} %add_convert_fusion.2), channel_id=1, source_target_pairs={{0,64},{64,128},{128,192},{192,256},{256,320},{320,384},{384,448},... | collective-permute-start | bytes 688136 | tf_op jit(solution)/shard_map/ppermute | solution.py:22
  79.2 8.7 %collective-permute-start.9 = (bf16[896,128]{1,0:T(8,128)(2,1)S(1)}, bf16[896,128]{1,0:T(8,128)(2,1)S(1)}, u32[]{:S(2)}, u32[]{:S(2)}) collective-permute-start(bf16[896,128]{1,0:T(8,128)(2,1)S(1)} %pad_maximum_fusion.3.refs_3_), channel_id=1, source_target_pairs={{0,452},{64,0},{128,64},{192,128},{256,192},{320,256},{384,320},{4... | collective-permute-start | bytes 688136 | tf_op jit(solution)/shard_map/ppermute | solution.py:22
  84.3 9.1 %collective-permute-start.13 = (bf16[896,128]{1,0:T(8,128)(2,1)S(1)}, bf16[896,128]{1,0:T(8,128)(2,1)S(1)}, u32[]{:S(2)}, u32[]{:S(2)}) collective-permute-start(bf16[896,128]{1,0:T(8,128)(2,1)S(1)} %pad_maximum_fusion.3.refs_3_), channel_id=1, source_target_pairs={{0,64},{64,128},{128,192},{192,256},{256,320},{320,384},{384,448},... | collective-permute-start | bytes 688136 | tf_op jit(solution)/shard_map/ppermute | solution.py:22
  87.8 9.3 %collective-permute-start.10 = (bf16[896,128]{1,0:T(8,128)(2,1)S(1)}, bf16[896,128]{1,0:T(8,128)(2,1)S(1)}, u32[]{:S(2)}, u32[]{:S(2)}) collective-permute-start(bf16[896,128]{1,0:T(8,128)(2,1)S(1)} %collective-permute-done.9.refs_4_), channel_id=1, source_target_pairs={{0,452},{64,0},{128,64},{192,128},{256,192},{320,256},{384,320},{4... | collective-permute-start | bytes 688136 | tf_op jit(solution)/shard_map/ppermute | solution.py:22
  93.4 9.6 %collective-permute-start.14 = (bf16[896,128]{1,0:T(8,128)(2,1)S(1)}, bf16[896,128]{1,0:T(8,128)(2,1)S(1)}, u32[]{:S(2)}, u32[]{:S(2)}) collective-permute-start(bf16[896,128]{1,0:T(8,128)(2,1)S(1)} %collective-permute-done.13.refs_2_), channel_id=1, source_target_pairs={{0,64},{64,128},{128,192},{192,256},{256,320},{320,384},{384,448},... | collective-permute-start | bytes 688136 | tf_op jit(solution)/shard_map/ppermute | solution.py:22
  97.1 10.1 %collective-permute-start.11 = (bf16[896,128]{1,0:T(8,128)(2,1)S(1)}, bf16[896,128]{1,0:T(8,128)(2,1)}, u32[]{:S(2)}, u32[]{:S(2)}) collective-permute-start(bf16[896,128]{1,0:T(8,128)(2,1)S(1)} %collective-permute-done.10.refs_5_), channel_id=1, source_target_pairs={{0,452},{64,0},{128,64},{192,128},{256,192},{320,256},{384,320},{4... | collective-permute-start | bytes 688136 | tf_op jit(solution)/shard_map/ppermute | solution.py:22
  103.0 9.9 %collective-permute-start.15 = (bf16[896,128]{1,0:T(8,128)(2,1)S(1)}, bf16[896,128]{1,0:T(8,128)(2,1)}, u32[]{:S(2)}, u32[]{:S(2)}) collective-permute-start(bf16[896,128]{1,0:T(8,128)(2,1)S(1)} %collective-permute-done.14.refs_1_), channel_id=1, source_target_pairs={{0,64},{64,128},{128,192},{192,256},{256,320},{320,384},{384,448},... | collective-permute-start | bytes 688136 | tf_op jit(solution)/shard_map/ppermute | solution.py:22
  107.2 10.5 %collective-permute-start.12 = (bf16[896,128]{1,0:T(8,128)(2,1)}, bf16[896,128]{1,0:T(8,128)(2,1)S(1)}, u32[]{:S(2)}, u32[]{:S(2)}) collective-permute-start(bf16[896,128]{1,0:T(8,128)(2,1)} %collective-permute-done.11.refs_6_), channel_id=1, source_target_pairs={{0,452},{64,0},{128,64},{192,128},{256,192},{320,256},{384,320},{4... | collective-permute-start | bytes 688136 | tf_op jit(solution)/shard_map/ppermute | solution.py:22
  118.0 1.2 copy-start
  119.2 7.0 %copy-start.1 = (bf16[448,512]{1,0:T(8,128)(2,1)S(1)}, bf16[448,512]{1,0:T(8,128)(2,1)}, u32[]{:S(2)}) copy-start(bf16[448,512]{1,0:T(8,128)(2,1)} %copy-done) | copy-start | bytes 1376260
  119.2 47.9 %all-to-all-start.2 = ((bf16[16,64,512]{2,1,0:T(8,128)(2,1)}), bf16[16,64,512]{2,1,0:T(8,128)(2,1)S(1)}, u32[]{:S(2)}, u32[]{:S(2)}) async-start(bf16[16,64,512]{2,1,0:T(8,128)(2,1)} %bitcast.5), calls=%async_computation.2 | async-start | bytes 2097152 | tf_op jit(solution)/shard_map/all_to_all | solution.py:308
  126.2 55.3 %collective-permute-start.18 = (bf16[448,512]{1,0:T(8,128)(2,1)S(1)}, bf16[448,512]{1,0:T(8,128)(2,1)S(1)}, u32[]{:S(2)}, u32[]{:S(2)}) collective-permute-start(bf16[448,512]{1,0:T(8,128)(2,1)S(1)} %copy-done.1), channel_id=1, source_target_pairs={{0,4},{4,0},{1,5},{5,1},{2,6},{6,2},{3,7},{7,3},{8,12},{12,8},{9,1... | collective-permute-start | bytes 1376264 | tf_op jit(solution)/shard_map/ppermute | solution.py:306
  167.3 3.1 %collective-permute-start.16 = (bf16[32,512]{1,0:T(8,128)(2,1)S(1)}, bf16[32,512]{1,0:T(8,128)(2,1)S(1)}, u32[]{:S(2)}, u32[]{:S(2)}) collective-permute-start(bf16[32,512]{1,0:T(8,128)(2,1)S(1)} %get-tuple-element.51), channel_id=1, source_target_pairs={{0,8},{8,0},{1,9},{9,1},{2,10},{10,2},{3,11},{11,3},{4,12},{12,4},... | collective-permute-start | bytes 98312 | tf_op jit(solution)/shard_map/ppermute | solution.py:62
  171.2 9.3 %all-to-all-start.3 = ((bf16[128,2,1,224]{3,1,2,0:T(2,128)(2,1)}), bf16[128,2,1,224]{3,1,2,0:T(2,128)(2,1)S(1)}, u32[]{:S(2)}, u32[]{:S(2)}) async-start(bf16[128,2,1,224]{3,1,2,0:T(2,128)(2,1)} %copy.20), calls=%async_computation.3 | async-start | bytes 262144 | tf_op jit(solution)/shard_map/all_to_all | solution.py:314
  176.0 16.9 %collective-permute-start.17 = (bf16[32,512]{1,0:T(8,128)(2,1)S(1)}, bf16[32,512]{1,0:T(8,128)(2,1)S(1)}, u32[]{:S(2)}, u32[]{:S(2)}) collective-permute-start(bf16[32,512]{1,0:T(8,128)(2,1)S(1)} %add_convert_fusion.5), channel_id=1, source_target_pairs={{0,44},{16,52},{32,60},{48,0},{8,8},{24,16},{40,24},{56,32},{64,11... | collective-permute-start | bytes 98312 | tf_op jit(solution)/shard_map/ppermute | solution.py:317

commit v15 on v13

--- a/solution.py
+++ b/solution.py
@@ -155,7 +155,7 @@
             jax.ShapeDtypeStruct((cols // 2, features), jnp.bfloat16),
         ],
         scratch_shapes=[pltpu.VMEM((128, features), jnp.bfloat16)],
-        compiler_params=PARAMS,
+        compiler_params=pltpu.CompilerParams(vmem_limit_bytes=10 << 20),
     )(core, half, own, other, sums, tile)
 
 

time: 174 us -> 174 us (level)
  no operation moved by 1% of the time
where the time goes in v15:
time: 174 us; the launch traced here: 173 us
  starting transfers between devices  87.9 us (51%)
  waiting for transfers between devices  65.5 us (38%)
  Pallas kernels  9.82 us (6%)
  local copies, waits for them, and re-layouts  6.54 us (4%)
  other arithmetic  1.95 us (1%)
    ppermute x14, starting transfers between devices, ring_shift(): return lax.ppermute(value, ('r', 'h'), pairs)  48.2 us
    ppermute x1, waiting for transfers between devices, local(): lax.ppermute(grad_tokens, ('r', 'y', 'c', 'h'), result_pairs())  24.4 us
    ppermute x14, waiting for transfers between devices, ring_shift(): return lax.ppermute(value, ('r', 'h'), pairs)  18.5 us
    ppermute x1, starting transfers between devices, local(): received = lax.ppermute(send, 'h', [(0, 1), (1, 0)])  9.56 us
    all_to_all x1, waiting for transfers between devices, local(): lax.all_to_all(copies, ('y', 'x'), split_axis=0, concat_axis=0, tiled=True)  8.34 us
    ppermute x1, starting transfers between devices, local(): piece = lax.ppermute(tokens, ('r', 'y', 'c', 'h'), token_pairs())  7.74 us
    all_to_all x1, starting transfers between devices, local(): lax.all_to_all(terms.reshape(16, -1, features), ('y', 'x'), split_axis=0,...  5.51 us
    pallas_call x1, Pallas kernels, near_products(): pl.pallas_call(near_kernel, in_specs=[SMEM_SPEC] + [VMEM_SPEC] * 10, out_...  4.76 us
  transfers between devices with their start and end apart: 23, of which 16 were waited for; matrix products, arithmetic and copies ran while one was open for 4% of the time, Pallas kernels for 4%

profile of v15, /device:TPU:160, one launch (start us, length us, event | category | flops | bytes accessed | tf_op | source)
XLA Modules:
  0.0 172.8 jit_solution(15200801493892649735)
XLA Ops:
  0.6 7.7 %collective-permute-start = (bf16[32,512]{1,0:T(8,128)(2,1)}, bf16[32,512]{1,0:T(8,128)(2,1)S(1)}, u32[]{:S(2)}, u32[]{:S(2)}) collective-permute-start(bf16[32,512]{1,0:T(8,128)(2,1)} %param.4), channel_id=1, source_target_pairs={{324,0},{388,16},{452,32},{0,48},{64,8},{128,24},{192,40},{256,56}... | collective-permute-start | bytes 98312 | tf_op jit(solution)/shard_map/ppermute | solution.py:261
  8.4 3.5 %collective-permute-done = bf16[32,512]{1,0:T(8,128)(2,1)S(1)} collective-permute-done((bf16[32,512]{1,0:T(8,128)(2,1)}, bf16[32,512]{1,0:T(8,128)(2,1)S(1)}, u32[]{:S(2)}, u32[]{:S(2)}) %collective-permute-start) | collective-permute-done | bytes 32800 | tf_op jit(solution)/shard_map/ppermute | solution.py:261
  11.8 0.8 broadcast_in_dim.2
  12.7 4.4 %all-to-all-start = ((bf16[16,32,512]{2,1,0:T(8,128)(2,1)}), bf16[16,32,512]{2,1,0:T(8,128)(2,1)S(1)}, u32[]{:S(2)}, u32[]{:S(2)}) async-start(bf16[16,32,512]{2,1,0:T(8,128)(2,1)} %broadcast_in_dim.2), calls=%async_computation | async-start | bytes 1048576 | tf_op jit(solution)/shard_map/all_to_all | solution.py:263
  17.1 1.1 reshape.36
  18.2 0.8 copy.24
  19.0 1.8 %constant_dynamic-slice_fusion.2 = (bf16[512,224]{1,0:T(8,128)(2,1)S(1)}, bf16[512,224]{1,0:T(8,128)(2,1)S(1)}, bf16[512,224]{1,0:T(8,128)(2,1)S(1)}, bf16[512,224]{1,0:T(8,128)(2,1)S(1)}) fusion(bf16[512,1792]{1,0:T(8,128)(2,1)} %param.6, s32[]{:T(128)S(6)} %select_n.8, s32[]{:T(128)S(6)} %select_n.9, bf16[512,1792]{1,0:T(8,128)(2,1)} %param.5), kind=kLoop, calls=%fused_computation.23 | loop fusion | bytes 1835016 | tf_op jit(solution)/shard_map/dynamic_slice | solution.py:255
  20.8 0.4 pad_maximum_fusion.weights_ref
  21.2 8.3 %all-to-all-done = bf16[16,32,512]{2,1,0:T(8,128)(2,1)S(1)} async-done(((bf16[16,32,512]{2,1,0:T(8,128)(2,1)}), bf16[16,32,512]{2,1,0:T(8,128)(2,1)S(1)}, u32[]{:S(2)}, u32[]{:S(2)}) %all-to-all-start) | async-done | bytes 524320 | tf_op jit(solution)/shard_map/all_to_all | solution.py:263
  29.5 1.9 %collective-permute-start.1 = (bf16[512,512]{1,0:T(8,128)(2,1)S(1)}, bf16[512,512]{1,0:T(8,128)(2,1)S(1)}, u32[]{:S(2)}, u32[]{:S(2)}) collective-permute-start(bf16[512,512]{1,0:T(8,128)(2,1)S(1)} %bitcast.28), channel_id=1, source_target_pairs={{0,8},{8,0},{1,9},{9,1},{2,10},{10,2},{3,11},{11,3},{4,12},{12,4},... | collective-permute-start | bytes 1572872 | tf_op jit(solution)/shard_map/ppermute | solution.py:62
  31.5 1.9 %collective-permute-done.1.other_ref = bf16[512,512]{1,0:T(8,128)(2,1)S(1)} collective-permute-done((bf16[512,512]{1,0:T(8,128)(2,1)S(1)}, bf16[512,512]{1,0:T(8,128)(2,1)S(1)}, u32[]{:S(2)}, u32[]{:S(2)}) %collective-permute-start.1) | collective-permute-done | bytes 524320 | tf_op jit(solution)/shard_map/ppermute | solution.py:62
  33.3 0.6 shard_map.75
  33.9 3.7 %collective-permute-start.2 = (bf16[896,128]{1,0:T(8,128)(2,1)S(1)}, bf16[896,128]{1,0:T(8,128)(2,1)S(1)}, u32[]{:S(2)}, u32[]{:S(2)}) collective-permute-start(bf16[896,128]{1,0:T(8,128)(2,1)S(1)} %get-tuple-element.35), channel_id=1, source_target_pairs={{0,64},{64,128},{128,192},{192,256},{256,320},{320,384},{384,448},... | collective-permute-start | bytes 688136 | tf_op jit(solution)/shard_map/ppermute | solution.py:22
  37.6 3.3 %all-to-all-start.1 = ((bf16[4,32,2,224]{3,2,1,0:T(2,128)(2,1)}), bf16[4,32,2,224]{3,2,1,0:T(2,128)(2,1)S(1)}, u32[]{:S(2)}, u32[]{:S(2)}) async-start(bf16[4,32,2,224]{3,2,1,0:T(2,128)(2,1)} %bitcast.27), calls=%async_computation.1 | async-start | bytes 262144 | tf_op jit(solution)/shard_map/all_to_all | solution.py:268
  41.0 2.1 %collective-permute-start.5 = (bf16[896,128]{1,0:T(8,128)(2,1)S(1)}, bf16[896,128]{1,0:T(8,128)(2,1)S(1)}, u32[]{:S(2)}, u32[]{:S(2)}) collective-permute-start(bf16[896,128]{1,0:T(8,128)(2,1)S(1)} %get-tuple-element.42), channel_id=1, source_target_pairs={{0,452},{64,0},{128,64},{192,128},{256,192},{320,256},{384,320},{4... | collective-permute-start | bytes 688136 | tf_op jit(solution)/shard_map/ppermute | solution.py:22
  43.1 1.1 shard_map.76
  44.2 0.1 add_convert_fusion.4
  44.3 3.7 %collective-permute-start.3 = (bf16[896,128]{1,0:T(8,128)(2,1)S(1)}, bf16[896,128]{1,0:T(8,128)(2,1)S(1)}, u32[]{:S(2)}, u32[]{:S(2)}) collective-permute-start(bf16[896,128]{1,0:T(8,128)(2,1)S(1)} %add_convert_fusion.4), channel_id=1, source_target_pairs={{0,64},{64,128},{128,192},{192,256},{256,320},{320,384},{384,448},... | collective-permute-start | bytes 688136 | tf_op jit(solution)/shard_map/ppermute | solution.py:22
  48.1 2.5 %collective-permute-done.5 = bf16[896,128]{1,0:T(8,128)(2,1)S(1)} collective-permute-done((bf16[896,128]{1,0:T(8,128)(2,1)S(1)}, bf16[896,128]{1,0:T(8,128)(2,1)S(1)}, u32[]{:S(2)}, u32[]{:S(2)}) %collective-permute-start.5) | collective-permute-done | bytes 229408 | tf_op jit(solution)/shard_map/ppermute | solution.py:22
  50.5 0.1 add_convert_fusion.1
  50.6 2.1 %collective-permute-start.6 = (bf16[896,128]{1,0:T(8,128)(2,1)S(1)}, bf16[896,128]{1,0:T(8,128)(2,1)S(1)}, u32[]{:S(2)}, u32[]{:S(2)}) collective-permute-start(bf16[896,128]{1,0:T(8,128)(2,1)S(1)} %add_convert_fusion.1), channel_id=1, source_target_pairs={{0,452},{64,0},{128,64},{192,128},{256,192},{320,256},{384,320},{4... | collective-permute-start | bytes 688136 | tf_op jit(solution)/shard_map/ppermute | solution.py:22
  52.7 0.9 collective-permute-done.3
  53.6 0.1 add_convert_fusion.3
  53.7 6.4 %collective-permute-start.4 = (bf16[896,128]{1,0:T(8,128)(2,1)S(1)}, bf16[896,128]{1,0:T(8,128)(2,1)S(1)}, u32[]{:S(2)}, u32[]{:S(2)}) collective-permute-start(bf16[896,128]{1,0:T(8,128)(2,1)S(1)} %add_convert_fusion.3), channel_id=1, source_target_pairs={{0,64},{64,128},{128,192},{192,256},{256,320},{320,384},{384,448},... | collective-permute-start | bytes 688136 | tf_op jit(solution)/shard_map/ppermute | solution.py:22
  60.0 2.7 %collective-permute-done.6 = bf16[896,128]{1,0:T(8,128)(2,1)S(1)} collective-permute-done((bf16[896,128]{1,0:T(8,128)(2,1)S(1)}, bf16[896,128]{1,0:T(8,128)(2,1)S(1)}, u32[]{:S(2)}, u32[]{:S(2)}) %collective-permute-start.6) | collective-permute-done | bytes 229408 | tf_op jit(solution)/shard_map/ppermute | solution.py:22
  62.7 0.1 add_convert_fusion
  62.8 1.9 %collective-permute-start.7 = (bf16[896,128]{1,0:T(8,128)(2,1)S(1)}, bf16[896,128]{1,0:T(8,128)(2,1)S(1)}, u32[]{:S(2)}, u32[]{:S(2)}) collective-permute-start(bf16[896,128]{1,0:T(8,128)(2,1)S(1)} %add_convert_fusion), channel_id=1, source_target_pairs={{0,452},{64,0},{128,64},{192,128},{256,192},{320,256},{384,320},{4... | collective-permute-start | bytes 688136 | tf_op jit(solution)/shard_map/ppermute | solution.py:22
  64.7 0.1 add_convert_fusion.2
  64.8 4.5 %collective-permute-start.8 = (bf16[896,128]{1,0:T(8,128)(2,1)S(1)}, bf16[896,128]{1,0:T(8,128)(2,1)}, u32[]{:S(2)}, u32[]{:S(2)}) collective-permute-start(bf16[896,128]{1,0:T(8,128)(2,1)S(1)} %add_convert_fusion.2), channel_id=1, source_target_pairs={{0,64},{64,128},{128,192},{192,256},{256,320},{320,384},{384,448},... | collective-permute-start | bytes 688136 | tf_op jit(solution)/shard_map/ppermute | solution.py:22
  69.3 0.1 reshape.41
  69.4 0.1 copy.19
  69.6 1.8 %collective-permute-done.7 = bf16[896,128]{1,0:T(8,128)(2,1)S(1)} collective-permute-done((bf16[896,128]{1,0:T(8,128)(2,1)S(1)}, bf16[896,128]{1,0:T(8,128)(2,1)S(1)}, u32[]{:S(2)}, u32[]{:S(2)}) %collective-permute-start.7) | collective-permute-done | bytes 229408 | tf_op jit(solution)/shard_map/ppermute | solution.py:22
  71.4 1.6 collective-permute-done.8
  73.0 1.0 convert_add_fusion
  74.0 0.2 multiply_convert_fusion
  74.3 4.2 %collective-permute-start.9 = (bf16[896,128]{1,0:T(8,128)(2,1)S(1)}, bf16[896,128]{1,0:T(8,128)(2,1)S(1)}, u32[]{:S(2)}, u32[]{:S(2)}) collective-permute-start(bf16[896,128]{1,0:T(8,128)(2,1)S(1)} %pad_maximum_fusion.3.refs_3_), channel_id=1, source_target_pairs={{0,452},{64,0},{128,64},{192,128},{256,192},{320,256},{384,320},{4... | collective-permute-start | bytes 688136 | tf_op jit(solution)/shard_map/ppermute | solution.py:22
  78.4 2.5 %collective-permute-start.13 = (bf16[896,128]{1,0:T(8,128)(2,1)S(1)}, bf16[896,128]{1,0:T(8,128)(2,1)S(1)}, u32[]{:S(2)}, u32[]{:S(2)}) collective-permute-start(bf16[896,128]{1,0:T(8,128)(2,1)S(1)} %pad_maximum_fusion.3.refs_3_), channel_id=1, source_target_pairs={{0,64},{64,128},{128,192},{192,256},{256,320},{320,384},{384,448},... | collective-permute-start | bytes 688136 | tf_op jit(solution)/shard_map/ppermute | solution.py:22
  81.0 2.1 %collective-permute-done.9.refs_4_ = bf16[896,128]{1,0:T(8,128)(2,1)S(1)} collective-permute-done((bf16[896,128]{1,0:T(8,128)(2,1)S(1)}, bf16[896,128]{1,0:T(8,128)(2,1)S(1)}, u32[]{:S(2)}, u32[]{:S(2)}) %collective-permute-start.9) | collective-permute-done | bytes 229408 | tf_op jit(solution)/shard_map/ppermute | solution.py:22
  83.0 3.3 %collective-permute-start.10 = (bf16[896,128]{1,0:T(8,128)(2,1)S(1)}, bf16[896,128]{1,0:T(8,128)(2,1)S(1)}, u32[]{:S(2)}, u32[]{:S(2)}) collective-permute-start(bf16[896,128]{1,0:T(8,128)(2,1)S(1)} %collective-permute-done.9.refs_4_), channel_id=1, source_target_pairs={{0,452},{64,0},{128,64},{192,128},{256,192},{320,256},{384,320},{4... | collective-permute-start | bytes 688136 | tf_op jit(solution)/shard_map/ppermute | solution.py:22
  86.4 4.2 %collective-permute-start.14 = (bf16[896,128]{1,0:T(8,128)(2,1)S(1)}, bf16[896,128]{1,0:T(8,128)(2,1)S(1)}, u32[]{:S(2)}, u32[]{:S(2)}) collective-permute-start(bf16[896,128]{1,0:T(8,128)(2,1)S(1)} %collective-permute-done.13.refs_2_), channel_id=1, source_target_pairs={{0,64},{64,128},{128,192},{192,256},{256,320},{320,384},{384,448},... | collective-permute-start | bytes 688136 | tf_op jit(solution)/shard_map/ppermute | solution.py:22
  90.6 2.0 %collective-permute-done.10.refs_5_ = bf16[896,128]{1,0:T(8,128)(2,1)S(1)} collective-permute-done((bf16[896,128]{1,0:T(8,128)(2,1)S(1)}, bf16[896,128]{1,0:T(8,128)(2,1)S(1)}, u32[]{:S(2)}, u32[]{:S(2)}) %collective-permute-start.10) | collective-permute-done | bytes 229408 | tf_op jit(solution)/shard_map/ppermute | solution.py:22
  92.6 1.9 %collective-permute-start.11 = (bf16[896,128]{1,0:T(8,128)(2,1)S(1)}, bf16[896,128]{1,0:T(8,128)(2,1)}, u32[]{:S(2)}, u32[]{:S(2)}) collective-permute-start(bf16[896,128]{1,0:T(8,128)(2,1)S(1)} %collective-permute-done.10.refs_5_), channel_id=1, source_target_pairs={{0,452},{64,0},{128,64},{192,128},{256,192},{320,256},{384,320},{4... | collective-permute-start | bytes 688136 | tf_op jit(solution)/shard_map/ppermute | solution.py:22
  94.5 5.7 %collective-permute-start.15 = (bf16[896,128]{1,0:T(8,128)(2,1)S(1)}, bf16[896,128]{1,0:T(8,128)(2,1)}, u32[]{:S(2)}, u32[]{:S(2)}) collective-permute-start(bf16[896,128]{1,0:T(8,128)(2,1)S(1)} %collective-permute-done.14.refs_1_), channel_id=1, source_target_pairs={{0,64},{64,128},{128,192},{192,256},{256,320},{320,384},{384,448},... | collective-permute-start | bytes 688136 | tf_op jit(solution)/shard_map/ppermute | solution.py:22
  100.2 2.1 %collective-permute-done.11.refs_6_ = bf16[896,128]{1,0:T(8,128)(2,1)} collective-permute-done((bf16[896,128]{1,0:T(8,128)(2,1)S(1)}, bf16[896,128]{1,0:T(8,128)(2,1)}, u32[]{:S(2)}, u32[]{:S(2)}) %collective-permute-start.11) | collective-permute-done | bytes 229408 | tf_op jit(solution)/shard_map/ppermute | solution.py:22
  102.4 1.9 %collective-permute-start.12 = (bf16[896,128]{1,0:T(8,128)(2,1)}, bf16[896,128]{1,0:T(8,128)(2,1)S(1)}, u32[]{:S(2)}, u32[]{:S(2)}) collective-permute-start(bf16[896,128]{1,0:T(8,128)(2,1)} %collective-permute-done.11.refs_6_), channel_id=1, source_target_pairs={{0,452},{64,0},{128,64},{192,128},{256,192},{320,256},{384,320},{4... | collective-permute-start | bytes 688136 | tf_op jit(solution)/shard_map/ppermute | solution.py:22
  104.3 4.8 %shard_map.77 = (bf16[1024,512]{1,0:T(8,128)(2,1)}, f32[896,512]{1,0:T(8,128)S(1)}) custom-call(s32[1]{0:T(128)} %bitcast.core_ref, bf16[512,512]{1,0:T(8,128)(2,1)S(1)} %bitcast.31, bf16[512,512]{1,0:T(8,128)(2,1)S(1)} %collective-permute-done.1.other_ref, bf16[512,896]{1,0:T(8,128)(2,1)S(1)} %pad_maximum_fusion.weights_ref, ...), custom_call_target="tpu_custom_call" | custom-call | tf_op jit(solution)/shard_map/pallas_call | solution.py:111
  109.1 2.9 %collective-permute-done.12.tile_ref = bf16[896,128]{1,0:T(8,128)(2,1)S(1)} collective-permute-done((bf16[896,128]{1,0:T(8,128)(2,1)}, bf16[896,128]{1,0:T(8,128)(2,1)S(1)}, u32[]{:S(2)}, u32[]{:S(2)}) %collective-permute-start.12) | collective-permute-done | bytes 229408 | tf_op jit(solution)/shard_map/ppermute | solution.py:22
  111.9 0.4 shard_map.78
  112.4 1.2 shard_map.79
  113.6 5.5 %all-to-all-start.2 = ((bf16[16,64,512]{2,1,0:T(8,128)(2,1)}), bf16[16,64,512]{2,1,0:T(8,128)(2,1)S(1)}, u32[]{:S(2)}, u32[]{:S(2)}) async-start(bf16[16,64,512]{2,1,0:T(8,128)(2,1)} %bitcast.5), calls=%async_computation.2 | async-start | bytes 2097152 | tf_op jit(solution)/shard_map/all_to_all | solution.py:308
  119.1 9.6 %collective-permute-start.18 = (bf16[448,512]{1,0:T(8,128)(2,1)S(1)}, bf16[448,512]{1,0:T(8,128)(2,1)S(1)}, u32[]{:S(2)}, u32[]{:S(2)}) collective-permute-start(bf16[448,512]{1,0:T(8,128)(2,1)S(1)} %copy-done.1), channel_id=1, source_target_pairs={{0,4},{4,0},{1,5},{5,1},{2,6},{6,2},{3,7},{7,3},{8,12},{12,8},{9,1... | collective-permute-start | bytes 1376264 | tf_op jit(solution)/shard_map/ppermute | solution.py:306
  128.7 3.8 %all-to-all-done.2.parts_ref = bf16[16,64,512]{2,1,0:T(8,128)(2,1)S(1)} async-done(((bf16[16,64,512]{2,1,0:T(8,128)(2,1)}), bf16[16,64,512]{2,1,0:T(8,128)(2,1)S(1)}, u32[]{:S(2)}, u32[]{:S(2)}) %all-to-all-start.2) | async-done | bytes 1048608 | tf_op jit(solution)/shard_map/all_to_all | solution.py:308
  132.4 0.2 shard_map.80
  132.6 1.9 %collective-permute-start.16 = (bf16[32,512]{1,0:T(8,128)(2,1)S(1)}, bf16[32,512]{1,0:T(8,128)(2,1)S(1)}, u32[]{:S(2)}, u32[]{:S(2)}) collective-permute-start(bf16[32,512]{1,0:T(8,128)(2,1)S(1)} %get-tuple-element.51), channel_id=1, source_target_pairs={{0,8},{8,0},{1,9},{9,1},{2,10},{10,2},{3,11},{11,3},{4,12},{12,4},... | collective-permute-start | bytes 98312 | tf_op jit(solution)/shard_map/ppermute | solution.py:62
  134.6 1.2 collective-permute-done.16
  135.7 0.8 copy.20
  136.5 3.3 %all-to-all-start.3 = ((bf16[128,2,1,224]{3,1,2,0:T(2,128)(2,1)}), bf16[128,2,1,224]{3,1,2,0:T(2,128)(2,1)S(1)}, u32[]{:S(2)}, u32[]{:S(2)}) async-start(bf16[128,2,1,224]{3,1,2,0:T(2,128)(2,1)} %copy.20), calls=%async_computation.3 | async-start | bytes 262144 | tf_op jit(solution)/shard_map/all_to_all | solution.py:314
  139.9 1.9 %collective-permute-start.17 = (bf16[32,512]{1,0:T(8,128)(2,1)S(1)}, bf16[32,512]{1,0:T(8,128)(2,1)S(1)}, u32[]{:S(2)}, u32[]{:S(2)}) collective-permute-start(bf16[32,512]{1,0:T(8,128)(2,1)S(1)} %add_convert_fusion.5), channel_id=1, source_target_pairs={{0,44},{16,52},{32,60},{48,0},{8,8},{24,16},{40,24},{56,32},{64,11... | collective-permute-start | bytes 98312 | tf_op jit(solution)/shard_map/ppermute | solution.py:317
  141.8 4.0 %all-to-all-done.3 = bf16[128,2,1,224]{3,1,2,0:T(2,128)(2,1)S(1)} async-done(((bf16[128,2,1,224]{3,1,2,0:T(2,128)(2,1)}), bf16[128,2,1,224]{3,1,2,0:T(2,128)(2,1)S(1)}, u32[]{:S(2)}, u32[]{:S(2)}) %all-to-all-start.3) | async-done | bytes 114720 | tf_op jit(solution)/shard_map/all_to_all | solution.py:314
  145.8 0.1 copy.22
  145.9 0.8 reshape.40
  146.8 1.0 shard_map.81
  147.8 24.4 %collective-permute-done.17.in_ref = bf16[32,512]{1,0:T(8,128)(2,1)S(1)} collective-permute-done((bf16[32,512]{1,0:T(8,128)(2,1)S(1)}, bf16[32,512]{1,0:T(8,128)(2,1)S(1)}, u32[]{:S(2)}, u32[]{:S(2)}) %collective-permute-start.17) | collective-permute-done | bytes 32800 | tf_op jit(solution)/shard_map/ppermute | solution.py:317
  172.2 0.6 shard_map.82
  (17 shorter events, 0.1 us)
Async XLA Ops:
  0.6 11.2 %collective-permute-start = (bf16[32,512]{1,0:T(8,128)(2,1)}, bf16[32,512]{1,0:T(8,128)(2,1)S(1)}, u32[]{:S(2)}, u32[]{:S(2)}) collective-permute-start(bf16[32,512]{1,0:T(8,128)(2,1)} %param.4), channel_id=1, source_target_pairs={{324,0},{388,16},{452,32},{0,48},{64,8},{128,24},{192,40},{256,56}... | collective-permute-start | bytes 98312 | tf_op jit(solution)/shard_map/ppermute | solution.py:261
  12.7 16.9 %all-to-all-start = ((bf16[16,32,512]{2,1,0:T(8,128)(2,1)}), bf16[16,32,512]{2,1,0:T(8,128)(2,1)S(1)}, u32[]{:S(2)}, u32[]{:S(2)}) async-start(bf16[16,32,512]{2,1,0:T(8,128)(2,1)} %broadcast_in_dim.2), calls=%async_computation | async-start | bytes 1048576 | tf_op jit(solution)/shard_map/all_to_all | solution.py:263
  29.5 3.8 %collective-permute-start.1 = (bf16[512,512]{1,0:T(8,128)(2,1)S(1)}, bf16[512,512]{1,0:T(8,128)(2,1)S(1)}, u32[]{:S(2)}, u32[]{:S(2)}) collective-permute-start(bf16[512,512]{1,0:T(8,128)(2,1)S(1)} %bitcast.28), channel_id=1, source_target_pairs={{0,8},{8,0},{1,9},{9,1},{2,10},{10,2},{3,11},{11,3},{4,12},{12,4},... | collective-permute-start | bytes 1572872 | tf_op jit(solution)/shard_map/ppermute | solution.py:62
  33.9 10.3 %collective-permute-start.2 = (bf16[896,128]{1,0:T(8,128)(2,1)S(1)}, bf16[896,128]{1,0:T(8,128)(2,1)S(1)}, u32[]{:S(2)}, u32[]{:S(2)}) collective-permute-start(bf16[896,128]{1,0:T(8,128)(2,1)S(1)} %get-tuple-element.35), channel_id=1, source_target_pairs={{0,64},{64,128},{128,192},{192,256},{256,320},{320,384},{384,448},... | collective-permute-start | bytes 688136 | tf_op jit(solution)/shard_map/ppermute | solution.py:22
  37.6 27.1 %all-to-all-start.1 = ((bf16[4,32,2,224]{3,2,1,0:T(2,128)(2,1)}), bf16[4,32,2,224]{3,2,1,0:T(2,128)(2,1)S(1)}, u32[]{:S(2)}, u32[]{:S(2)}) async-start(bf16[4,32,2,224]{3,2,1,0:T(2,128)(2,1)} %bitcast.27), calls=%async_computation.1 | async-start | bytes 262144 | tf_op jit(solution)/shard_map/all_to_all | solution.py:268
  41.0 9.6 %collective-permute-start.5 = (bf16[896,128]{1,0:T(8,128)(2,1)S(1)}, bf16[896,128]{1,0:T(8,128)(2,1)S(1)}, u32[]{:S(2)}, u32[]{:S(2)}) collective-permute-start(bf16[896,128]{1,0:T(8,128)(2,1)S(1)} %get-tuple-element.42), channel_id=1, source_target_pairs={{0,452},{64,0},{128,64},{192,128},{256,192},{320,256},{384,320},{4... | collective-permute-start | bytes 688136 | tf_op jit(solution)/shard_map/ppermute | solution.py:22
  44.3 9.3 %collective-permute-start.3 = (bf16[896,128]{1,0:T(8,128)(2,1)S(1)}, bf16[896,128]{1,0:T(8,128)(2,1)S(1)}, u32[]{:S(2)}, u32[]{:S(2)}) collective-permute-start(bf16[896,128]{1,0:T(8,128)(2,1)S(1)} %add_convert_fusion.4), channel_id=1, source_target_pairs={{0,64},{64,128},{128,192},{192,256},{256,320},{320,384},{384,448},... | collective-permute-start | bytes 688136 | tf_op jit(solution)/shard_map/ppermute | solution.py:22
  50.6 12.1 %collective-permute-start.6 = (bf16[896,128]{1,0:T(8,128)(2,1)S(1)}, bf16[896,128]{1,0:T(8,128)(2,1)S(1)}, u32[]{:S(2)}, u32[]{:S(2)}) collective-permute-start(bf16[896,128]{1,0:T(8,128)(2,1)S(1)} %add_convert_fusion.1), channel_id=1, source_target_pairs={{0,452},{64,0},{128,64},{192,128},{256,192},{320,256},{384,320},{4... | collective-permute-start | bytes 688136 | tf_op jit(solution)/shard_map/ppermute | solution.py:22
  53.7 11.0 %collective-permute-start.4 = (bf16[896,128]{1,0:T(8,128)(2,1)S(1)}, bf16[896,128]{1,0:T(8,128)(2,1)S(1)}, u32[]{:S(2)}, u32[]{:S(2)}) collective-permute-start(bf16[896,128]{1,0:T(8,128)(2,1)S(1)} %add_convert_fusion.3), channel_id=1, source_target_pairs={{0,64},{64,128},{128,192},{192,256},{256,320},{320,384},{384,448},... | collective-permute-start | bytes 688136 | tf_op jit(solution)/shard_map/ppermute | solution.py:22
  62.8 8.6 %collective-permute-start.7 = (bf16[896,128]{1,0:T(8,128)(2,1)S(1)}, bf16[896,128]{1,0:T(8,128)(2,1)S(1)}, u32[]{:S(2)}, u32[]{:S(2)}) collective-permute-start(bf16[896,128]{1,0:T(8,128)(2,1)S(1)} %add_convert_fusion), channel_id=1, source_target_pairs={{0,452},{64,0},{128,64},{192,128},{256,192},{320,256},{384,320},{4... | collective-permute-start | bytes 688136 | tf_op jit(solution)/shard_map/ppermute | solution.py:22
  64.8 8.2 %collective-permute-start.8 = (bf16[896,128]{1,0:T(8,128)(2,1)S(1)}, bf16[896,128]{1,0:T(8,128)(2,1)}, u32[]{:S(2)}, u32[]{:S(2)}) collective-permute-start(bf16[896,128]{1,0:T(8,128)(2,1)S(1)} %add_convert_fusion.2), channel_id=1, source_target_pairs={{0,64},{64,128},{128,192},{192,256},{256,320},{320,384},{384,448},... | collective-permute-start | bytes 688136 | tf_op jit(solution)/shard_map/ppermute | solution.py:22
  74.3 8.8 %collective-permute-start.9 = (bf16[896,128]{1,0:T(8,128)(2,1)S(1)}, bf16[896,128]{1,0:T(8,128)(2,1)S(1)}, u32[]{:S(2)}, u32[]{:S(2)}) collective-permute-start(bf16[896,128]{1,0:T(8,128)(2,1)S(1)} %pad_maximum_fusion.3.refs_3_), channel_id=1, source_target_pairs={{0,452},{64,0},{128,64},{192,128},{256,192},{320,256},{384,320},{4... | collective-permute-start | bytes 688136 | tf_op jit(solution)/shard_map/ppermute | solution.py:22
  78.4 7.9 %collective-permute-start.13 = (bf16[896,128]{1,0:T(8,128)(2,1)S(1)}, bf16[896,128]{1,0:T(8,128)(2,1)S(1)}, u32[]{:S(2)}, u32[]{:S(2)}) collective-permute-start(bf16[896,128]{1,0:T(8,128)(2,1)S(1)} %pad_maximum_fusion.3.refs_3_), channel_id=1, source_target_pairs={{0,64},{64,128},{128,192},{192,256},{256,320},{320,384},{384,448},... | collective-permute-start | bytes 688136 | tf_op jit(solution)/shard_map/ppermute | solution.py:22
  83.0 9.6 %collective-permute-start.10 = (bf16[896,128]{1,0:T(8,128)(2,1)S(1)}, bf16[896,128]{1,0:T(8,128)(2,1)S(1)}, u32[]{:S(2)}, u32[]{:S(2)}) collective-permute-start(bf16[896,128]{1,0:T(8,128)(2,1)S(1)} %collective-permute-done.9.refs_4_), channel_id=1, source_target_pairs={{0,452},{64,0},{128,64},{192,128},{256,192},{320,256},{384,320},{4... | collective-permute-start | bytes 688136 | tf_op jit(solution)/shard_map/ppermute | solution.py:22
  86.4 8.2 %collective-permute-start.14 = (bf16[896,128]{1,0:T(8,128)(2,1)S(1)}, bf16[896,128]{1,0:T(8,128)(2,1)S(1)}, u32[]{:S(2)}, u32[]{:S(2)}) collective-permute-start(bf16[896,128]{1,0:T(8,128)(2,1)S(1)} %collective-permute-done.13.refs_2_), channel_id=1, source_target_pairs={{0,64},{64,128},{128,192},{192,256},{256,320},{320,384},{384,448},... | collective-permute-start | bytes 688136 | tf_op jit(solution)/shard_map/ppermute | solution.py:22
  92.6 9.8 %collective-permute-start.11 = (bf16[896,128]{1,0:T(8,128)(2,1)S(1)}, bf16[896,128]{1,0:T(8,128)(2,1)}, u32[]{:S(2)}, u32[]{:S(2)}) collective-permute-start(bf16[896,128]{1,0:T(8,128)(2,1)S(1)} %collective-permute-done.10.refs_5_), channel_id=1, source_target_pairs={{0,452},{64,0},{128,64},{192,128},{256,192},{320,256},{384,320},{4... | collective-permute-start | bytes 688136 | tf_op jit(solution)/shard_map/ppermute | solution.py:22
  94.5 9.8 %collective-permute-start.15 = (bf16[896,128]{1,0:T(8,128)(2,1)S(1)}, bf16[896,128]{1,0:T(8,128)(2,1)}, u32[]{:S(2)}, u32[]{:S(2)}) collective-permute-start(bf16[896,128]{1,0:T(8,128)(2,1)S(1)} %collective-permute-done.14.refs_1_), channel_id=1, source_target_pairs={{0,64},{64,128},{128,192},{192,256},{256,320},{320,384},{384,448},... | collective-permute-start | bytes 688136 | tf_op jit(solution)/shard_map/ppermute | solution.py:22
  102.4 9.5 %collective-permute-start.12 = (bf16[896,128]{1,0:T(8,128)(2,1)}, bf16[896,128]{1,0:T(8,128)(2,1)S(1)}, u32[]{:S(2)}, u32[]{:S(2)}) collective-permute-start(bf16[896,128]{1,0:T(8,128)(2,1)} %collective-permute-done.11.refs_6_), channel_id=1, source_target_pairs={{0,452},{64,0},{128,64},{192,128},{256,192},{320,256},{384,320},{4... | collective-permute-start | bytes 688136 | tf_op jit(solution)/shard_map/ppermute | solution.py:22
  112.3 1.2 copy-start
  113.5 5.5 %copy-start.1 = (bf16[448,512]{1,0:T(8,128)(2,1)S(1)}, bf16[448,512]{1,0:T(8,128)(2,1)}, u32[]{:S(2)}) copy-start(bf16[448,512]{1,0:T(8,128)(2,1)} %copy-done) | copy-start | bytes 1376260
  113.6 18.9 %all-to-all-start.2 = ((bf16[16,64,512]{2,1,0:T(8,128)(2,1)}), bf16[16,64,512]{2,1,0:T(8,128)(2,1)S(1)}, u32[]{:S(2)}, u32[]{:S(2)}) async-start(bf16[16,64,512]{2,1,0:T(8,128)(2,1)} %bitcast.5), calls=%async_computation.2 | async-start | bytes 2097152 | tf_op jit(solution)/shard_map/all_to_all | solution.py:308
  119.1 27.7 %collective-permute-start.18 = (bf16[448,512]{1,0:T(8,128)(2,1)S(1)}, bf16[448,512]{1,0:T(8,128)(2,1)S(1)}, u32[]{:S(2)}, u32[]{:S(2)}) collective-permute-start(bf16[448,512]{1,0:T(8,128)(2,1)S(1)} %copy-done.1), channel_id=1, source_target_pairs={{0,4},{4,0},{1,5},{5,1},{2,6},{6,2},{3,7},{7,3},{8,12},{12,8},{9,1... | collective-permute-start | bytes 1376264 | tf_op jit(solution)/shard_map/ppermute | solution.py:306
  132.6 3.1 %collective-permute-start.16 = (bf16[32,512]{1,0:T(8,128)(2,1)S(1)}, bf16[32,512]{1,0:T(8,128)(2,1)S(1)}, u32[]{:S(2)}, u32[]{:S(2)}) collective-permute-start(bf16[32,512]{1,0:T(8,128)(2,1)S(1)} %get-tuple-element.51), channel_id=1, source_target_pairs={{0,8},{8,0},{1,9},{9,1},{2,10},{10,2},{3,11},{11,3},{4,12},{12,4},... | collective-permute-start | bytes 98312 | tf_op jit(solution)/shard_map/ppermute | solution.py:62
  136.5 9.3 %all-to-all-start.3 = ((bf16[128,2,1,224]{3,1,2,0:T(2,128)(2,1)}), bf16[128,2,1,224]{3,1,2,0:T(2,128)(2,1)S(1)}, u32[]{:S(2)}, u32[]{:S(2)}) async-start(bf16[128,2,1,224]{3,1,2,0:T(2,128)(2,1)} %copy.20), calls=%async_computation.3 | async-start | bytes 262144 | tf_op jit(solution)/shard_map/all_to_all | solution.py:314
  139.9 32.3 %collective-permute-start.17 = (bf16[32,512]{1,0:T(8,128)(2,1)S(1)}, bf16[32,512]{1,0:T(8,128)(2,1)S(1)}, u32[]{:S(2)}, u32[]{:S(2)}) collective-permute-start(bf16[32,512]{1,0:T(8,128)(2,1)S(1)} %add_convert_fusion.5), channel_id=1, source_target_pairs={{0,44},{16,52},{32,60},{48,0},{8,8},{24,16},{40,24},{56,32},{64,11... | collective-permute-start | bytes 98312 | tf_op jit(solution)/shard_map/ppermute | solution.py:317
